TPU v7x, 32 devices: a whole 2x2x4 slice. The times are simulated.
32 devices in a mesh: grp: 2 (over x), ep: 16 (over z, y, core).
Axes of the slice: x: 2, y: 2, z: 4, core: 2. Of those that a mesh axis runs over, the one named last changes fastest.
Arguments:
- hidden_in: bfloat16 [2, 1024, 2048], P(None, ('grp', 'ep')), parts along dimension 1, may hold values from -12 to 12
- expert_ids: int32 [2, 1024, 8], P(None, ('grp', 'ep')), parts along dimension 1, may hold values from 0 to 15, all different within a row; in each aligned block of 32 rows (0 to 31, 32 to 63, ..., all dimensions but the last counted through in order) at most 32 rows name the same one
- route_share: int32 [2, 1024, 8], P(None, ('grp', 'ep')), parts along dimension 1, may hold values from 4 to 28
- norm_gain: float32 [2048], replicated, may hold values from 0.1 to 1.9
- gate_weight: bfloat16 [16, 2048, 768], P('ep'), may hold values from -0.125 to 0.125
- up_weight: bfloat16 [16, 2048, 768], P('ep'), may hold values from -0.125 to 0.125
- down_weight: bfloat16 [16, 768, 2048], P('ep'), may hold values from -0.21875 to 0.21875
- exponent_table: int32 [16, 3, 6], P('ep'), may hold values from -2 to 1
Outputs:
- mixed_out: bfloat16 [2, 1024, 2048], P(None, ('grp', 'ep')), parts along dimension 1
There are 2 independent parts, one for each index of `grp`. A program takes and returns all parts, laid end to end along the dimension named above; an argument that names none is the same for every part. Nothing has to cross between parts.
Inputs may be any that keep to these rules, and one draw needn't show every extreme that they name: `expert_ids`: each row names 8 different experts. Within each micro-batch, in each aligned block of 32 rows, no expert is named by more than 32 rows, and in some blocks one expert is named by exactly 32 rows.
All inputs are finite; a program needn't handle non-finite values.
Results may differ from a plain program's by a relative error of at most 0.0044.
Values may be sent and summed in bfloat16 or wider, within the bound.
No kernel may reach another device: no remote copies, remote signals or barrier semaphores. Data moves between devices by JAX's collectives and lax.ppermute only.
A program may use at most 64 MiB of HBM per device.

v0:
```python
import jax
import jax.numpy as jnp
from jax import lax
from jax.sharding import PartitionSpec as P

SCALE_GROUP = 128
EXP_DEV = 1


def normalize(rows_in, norm_gain):
    values = rows_in.astype(jnp.float32)
    power = jnp.mean(values * values, axis=-1, keepdims=True)
    return (values * lax.rsqrt(power + 1e-06) * norm_gain).astype(jnp.bfloat16)


def local(
    hidden_in,
    expert_ids,
    route_share,
    norm_gain,
    gate_weight,
    up_weight,
    down_weight,
    exponent_table,
):
    owners = lax.axis_size("ep")
    experts = owners * EXP_DEV
    batches, dev_rows, fanout = expert_ids.shape
    model_width = hidden_in.shape[2]
    capacity = min(dev_rows, 2 * dev_rows * fanout // experts)
    scale_factors = jnp.repeat(jnp.exp2(exponent_table[0].astype(jnp.float32)), SCALE_GROUP, axis=1)
    gate_matrix = gate_weight[0]
    up_matrix = up_weight[0]
    down_mat = down_weight[0]
    slot_ids = jnp.arange(experts * capacity, dtype=jnp.int32)
    expert_range = jnp.arange(experts, dtype=jnp.int32)

    def expert_rows(block_of_rows):
        gate_output = (
            jnp.dot(block_of_rows, gate_matrix, preferred_element_type=jnp.float32)
            * scale_factors[0]
        )
        up_output = (
            jnp.dot(block_of_rows, up_matrix, preferred_element_type=jnp.float32) * scale_factors[1]
        )
        hidden_state = (jax.nn.silu(gate_output) * up_output * scale_factors[2]).astype(
            jnp.bfloat16
        )
        return jnp.dot(hidden_state, down_mat, preferred_element_type=jnp.float32).astype(
            jnp.bfloat16
        )

    def mixing_for(batch):
        flat_ids = expert_ids[batch].reshape(-1)
        onehot = (flat_ids[:, None] == expert_range[None, :]).astype(jnp.int32)
        position = jnp.sum((jnp.cumsum(onehot, axis=0) - 1) * onehot, axis=1)
        slot_of = (flat_ids * capacity + position).reshape(dev_rows, fanout)
        matches = slot_of[:, :, None] == slot_ids[None, None, :]
        shares = route_share[batch].astype(jnp.float32) / 64.0
        mixing = jnp.sum(jnp.where(matches, shares[:, :, None], 0.0), axis=1).astype(jnp.bfloat16)
        picker = jnp.any(matches, axis=1).T.astype(jnp.bfloat16)
        return (mixing, picker)

    def serve(batch_list):
        count = len(batch_list)
        mixings = []
        pickers = []
        for batch in batch_list:
            mixing, picker = mixing_for(batch)
            mixings.append(mixing)
            pickers.append(picker)
        normed_list = [normalize(hidden_in[batch], norm_gain) for batch in batch_list]
        local_rows = normed_list[0]
        local_ids = jnp.concatenate([expert_ids[batch] for batch in batch_list], axis=0)
        all_rows = lax.all_gather(local_rows, "ep", axis=0, tiled=True)
        all_ids = lax.all_gather(local_ids, "ep", axis=0, tiled=True)
        all_rows = all_rows.reshape(owners, count, dev_rows, model_width)
        all_ids = all_ids.reshape(owners, count, dev_rows, fanout)
        owner = lax.axis_index("ep")
        block_base = (jnp.arange(owners, dtype=jnp.int32) * capacity)[:, None]
        ids_here = all_ids[:, 0].reshape(owners, dev_rows * fanout)
        mine = (ids_here == owner).astype(jnp.int32)
        place = jnp.where(mine > 0, block_base + jnp.cumsum(mine, axis=1) - 1, -1)
        place = place.reshape(owners * dev_rows, fanout)
        chooser = jnp.any(place[:, :, None] == slot_ids[None, None, :], axis=1).T.astype(
            jnp.bfloat16
        )
        rows_here = all_rows[:, 0].reshape(owners * dev_rows, model_width)
        built = jnp.dot(chooser, rows_here, preferred_element_type=jnp.float32).astype(jnp.bfloat16)
        buffers = built.reshape(experts, capacity, model_width)
        produced = expert_rows(buffers.reshape(-1, model_width)).reshape(
            experts, count * capacity, model_width
        )
        returned = lax.all_to_all(produced, "ep", split_axis=0, concat_axis=0, tiled=True)
        return (returned, mixings)

    outputs = []
    for batch in range(batches):
        returned, mixings = serve([batch])
        gathered = returned.reshape(experts * capacity, model_width)
        mixed = jnp.dot(mixings[0], gathered, preferred_element_type=jnp.float32)
        outputs.append((hidden_in[batch].astype(jnp.float32) + mixed).astype(jnp.bfloat16))
    return jnp.stack(outputs)


def solution(mesh):
    return jax.shard_map(
        local,
        mesh=mesh,
        in_specs=(
            P(None, ("grp", "ep"), None),
            P(None, ("grp", "ep"), None),
            P(None, ("grp", "ep"), None),
            P(),
            P("ep", None, None),
            P("ep", None, None),
            P("ep", None, None),
            P("ep", None, None),
        ),
        out_specs=P(None, ("grp", "ep"), None),
        check_vma=False,
    )
```

profile of v0, /device:TPU:13, one launch (start us, length us, event | category | flops | bytes accessed | tf_op | source)
XLA Modules:
  0.0 198.7 jit_solution(16054259629744714355)
XLA Ops:
  6.5 1.3 fusion.40
  7.8 1.8 fusion.42
  9.7 0.7 all-gather.7.cloned.1.call-update
  10.4 0.7 fusion.56
  11.2 16.5 %all-gather.1 = s32[1,512,8]{2,1,0:T(8,128)S(1)} all-gather(s32[1,32,8]{2,1,0:T(8,128)S(1)} %copy.36), channel_id=3, replica_groups=mesh['grp'=2,'ep'=16] {'ep'}, dimensions={1}, use_global_device_ids=true | all-gather | bytes 17408 | tf_op jit(solution)/shard_map/all_gather | solution.py:76
  27.7 0.7 compare_convert_fusion
  28.4 1.1 reshape.203
  30.5 0.9 reduce_window_sum.55
  31.4 22.5 %all-gather = s32[1,512,8]{2,1,0:T(8,128)S(1)} all-gather(s32[1,32,8]{2,1,0:T(8,128)S(1)} %copy.35), channel_id=2, replica_groups=mesh['grp'=2,'ep'=16] {'ep'}, dimensions={1}, use_global_device_ids=true | all-gather | bytes 17408 | tf_op jit(solution)/shard_map/all_gather | solution.py:76
  53.9 0.7 copy-done.2
  54.6 0.7 compare_convert_fusion.1
  55.3 1.1 reshape.201
  57.3 0.9 reduce_window_sum.52
  58.4 1.9 add_select_fusion.1
  60.3 3.2 %fusion = pred[512,512]{1,0:T(8,128)(4,1)S(1)} fusion(s32[512,8]{1,0:T(8,128)S(1)} %get-tuple-element.13), kind=kLoop, calls=%fused_computation.2 | loop fusion | flops 3932160 | bytes 278528 | tf_op jit(solution)/shard_map/reduce_or | solution.py:85
  63.8 3.0 %convolution_convert_fusion.1 = bf16[512,2048]{1,0:T(8,128)(2,1)S(1)} fusion(pred[512,512]{1,0:T(8,128)(4,1)S(1)} %fusion, bf16[512,2048]{1,0:T(8,128)(2,1)} %all-gather.5.cloned.1.call-done), kind=kOutput, calls=%fused_computation.19 | convolution fusion | flops 1074790400 | bytes 4456448 | tf_op jit(solution)/shard_map/dot_general | solution.py:89
  66.8 2.9 %fusion.8 = f32[512,768]{1,0:T(8,128)} fusion(bf16[512,2048]{1,0:T(8,128)(2,1)S(1)} %convolution_convert_fusion.1, bf16[1,2048,768]{2,1,0:T(8,128)(2,1)S(1)} %copy-done.6), kind=kOutput, calls=%fused_computation.10 | convolution fusion | flops 1610612736 | bytes 6815744 | tf_op jit(solution)/shard_map/dot_general | solution.py:44
  69.8 8.3 %fusion.14 = bf16[512,2048]{1,0:T(8,128)(2,1)} fusion(bf16[1,768,2048]{2,1,0:T(8,128)(2,1)S(1)} %copy-done, f32[512,768]{1,0:T(8,128)} %fusion.8, bf16[512,2048]{1,0:T(8,128)(2,1)} %copy-done.9, bf16[1,2048,768]{2,1,0:T(8,128)(2,1)} %param.12, f32[768]{0:T(1024)S(1)} %get-tuple-element.20, f32[768]{0:T(1024)S(1)} %get-tuple-element.21, ...), kind=kOutput, calls=%fused_computation.16 | convolution fusion | flops 3225812992 | bytes 12067840 | tf_op jit(solution)/shard_map/dot_general | solution.py:49
  78.1 7.0 %all-to-all-start = ((bf16[16,32,2048]{2,1,0:T(8,128)(2,1)}), bf16[16,32,2048]{2,1,0:T(8,128)(2,1)}, u32[]{:S(2)}, u32[]{:S(2)}) async-start(bf16[16,32,2048]{2,1,0:T(8,128)(2,1)} %bitcast.112), calls=%async_computation | async-start | bytes 4194304 | tf_op jit(solution)/shard_map/all_to_all | solution.py:94
  85.1 4.0 %fusion.1 = pred[512,512]{1,0:T(8,128)(4,1)} fusion(s32[512,8]{1,0:T(8,128)S(1)} %copy-done.3), kind=kLoop, calls=%fused_computation.3 | loop fusion | flops 3932160 | bytes 278528 | tf_op jit(solution)/shard_map/reduce_or | solution.py:85
  89.0 9.9 %all-gather.7.cloned.1.call-done = bf16[512,2048]{1,0:T(8,128)(2,1)} async-done(((bf16[32,2048]{1,0:T(8,128)(2,1)}), bf16[512,2048]{1,0:T(8,128)(2,1)}) %all-gather.7.cloned.1.call-update) | async-done | bytes 2097168 | tf_op jit(solution)/shard_map/all_gather | solution.py:75
  98.9 3.1 %convolution_convert_fusion = bf16[512,2048]{1,0:T(8,128)(2,1)S(1)} fusion(pred[512,512]{1,0:T(8,128)(4,1)} %fusion.1, bf16[512,2048]{1,0:T(8,128)(2,1)} %all-gather.7.cloned.1.call-done), kind=kOutput, calls=%fused_computation.18 | convolution fusion | flops 1074790400 | bytes 4456448 | tf_op jit(solution)/shard_map/dot_general | solution.py:89
  102.0 1.3 copy-done.8
  103.4 3.0 %fusion.6 = f32[512,768]{1,0:T(8,128)} fusion(bf16[512,2048]{1,0:T(8,128)(2,1)S(1)} %convolution_convert_fusion, bf16[1,2048,768]{2,1,0:T(8,128)(2,1)S(1)} %copy-done.7), kind=kOutput, calls=%fused_computation.8 | convolution fusion | flops 1610612736 | bytes 6815744 | tf_op jit(solution)/shard_map/dot_general | solution.py:44
  106.4 8.4 %fusion.17 = bf16[512,2048]{1,0:T(8,128)(2,1)} fusion(bf16[1,768,2048]{2,1,0:T(8,128)(2,1)S(1)} %copy-done, f32[512,768]{1,0:T(8,128)} %fusion.6, bf16[512,2048]{1,0:T(8,128)(2,1)} %copy-done.8, bf16[1,2048,768]{2,1,0:T(8,128)(2,1)} %param.12, f32[768]{0:T(1024)S(1)} %get-tuple-element.20, f32[768]{0:T(1024)S(1)} %get-tuple-element.21, ...), kind=kOutput, calls=%fused_computation.17 | convolution fusion | flops 3225812992 | bytes 12067840 | tf_op jit(solution)/shard_map/dot_general | solution.py:49
  114.8 22.0 %all-to-all-done = bf16[16,32,2048]{2,1,0:T(8,128)(2,1)} async-done(((bf16[16,32,2048]{2,1,0:T(8,128)(2,1)}), bf16[16,32,2048]{2,1,0:T(8,128)(2,1)}, u32[]{:S(2)}, u32[]{:S(2)}) %all-to-all-start) | async-done | bytes 2097184 | tf_op jit(solution)/shard_map/all_to_all | solution.py:94
  136.7 4.8 %all-to-all-start.1 = ((bf16[16,32,2048]{2,1,0:T(8,128)(2,1)}), bf16[16,32,2048]{2,1,0:T(8,128)(2,1)}, u32[]{:S(2)}, u32[]{:S(2)}) async-start(bf16[16,32,2048]{2,1,0:T(8,128)(2,1)} %bitcast.111), calls=%async_computation.1 | async-start | bytes 4194304 | tf_op jit(solution)/shard_map/all_to_all | solution.py:94
  144.3 0.9 select_reduce_fusion
  145.2 2.1 %fusion.23 = bf16[1,32,2048]{2,1,0:T(8,128)(2,1)S(1)} fusion(bf16[512,2048]{1,0:T(8,128)(2,1)} %bitcast.16, bf16[2,32,2048]{2,1,0:T(8,128)(2,1)S(1)} %copy-done.1, bf16[32,512]{1,0:T(8,128)(2,1)S(1)} %select_reduce_fusion.1), kind=kOutput, calls=%fused_computation.25 | convolution fusion | flops 67305472 | bytes 2392064 | tf_op jit(solution)/shard_map/dot_general | solution.py:101
  147.2 41.8 %all-to-all-done.1 = bf16[16,32,2048]{2,1,0:T(8,128)(2,1)} async-done(((bf16[16,32,2048]{2,1,0:T(8,128)(2,1)}), bf16[16,32,2048]{2,1,0:T(8,128)(2,1)}, u32[]{:S(2)}, u32[]{:S(2)}) %all-to-all-start.1) | async-done | bytes 2097184 | tf_op jit(solution)/shard_map/all_to_all | solution.py:94
  189.0 2.1 %fusion.22 = bf16[1,32,2048]{2,1,0:T(8,128)(2,1)S(1)} fusion(bf16[512,2048]{1,0:T(8,128)(2,1)} %bitcast.25, bf16[2,32,2048]{2,1,0:T(8,128)(2,1)S(1)} %copy-done.1, bf16[32,512]{1,0:T(8,128)(2,1)} %select_reduce_fusion), kind=kOutput, calls=%fused_computation.24 | convolution fusion | flops 67305472 | bytes 2392064 | tf_op jit(solution)/shard_map/dot_general | solution.py:101
  191.1 0.7 pad_maximum_fusion
  (70 shorter events, 5.1 us)
Async XLA Ops:
  6.5 63.2 %copy-start = (bf16[1,768,2048]{2,1,0:T(8,128)(2,1)S(1)}, bf16[1,768,2048]{2,1,0:T(8,128)(2,1)}, u32[]{:S(2)}) copy-start(bf16[1,768,2048]{2,1,0:T(8,128)(2,1)} %param.14) | copy-start | bytes 9437188
  6.5 57.2 %all-gather.5.cloned.1.call-start = ((), (), s32[]{:S(2)}) async-start(), calls=%async_computation.2 | async-start | bytes 2228224 | tf_op jit(solution)/shard_map/all_gather | solution.py:75
  9.7 89.2 %all-gather.7.cloned.1.call-start = ((), (), s32[]{:S(2)}) async-start(), calls=%async_computation.3 | async-start | bytes 2228224 | tf_op jit(solution)/shard_map/all_gather | solution.py:75
  29.5 34.0 %copy-start.5 = (s32[1,3,6]{2,0,1:T(1,128)S(1)}, s32[1,3,6]{2,0,1:T(1,128)}, u32[]{:S(2)}) copy-start(s32[1,3,6]{2,0,1:T(1,128)} %param.15) | copy-start | bytes 220
  53.9 0.7 copy-start.2
  63.8 3.0 %copy-start.6 = (bf16[1,2048,768]{2,1,0:T(8,128)(2,1)S(1)}, bf16[1,2048,768]{2,1,0:T(8,128)(2,1)}, u32[]{:S(2)}) copy-start(bf16[1,2048,768]{2,1,0:T(8,128)(2,1)} %param.13) | copy-start | bytes 9437188
  66.8 3.0 %copy-start.9 = (bf16[512,2048]{1,0:T(8,128)(2,1)}, bf16[512,2048]{1,0:T(8,128)(2,1)S(1)}, u32[]{:S(2)}) copy-start(bf16[512,2048]{1,0:T(8,128)(2,1)S(1)} %convolution_convert_fusion.1) | copy-start | bytes 6291460
  78.1 7.0 %copy-start.3 = (s32[512,8]{1,0:T(8,128)S(1)}, s32[512,8]{1,0:T(8,128)}, u32[]{:S(2)}) copy-start(s32[512,8]{1,0:T(8,128)} %get-tuple-element.14) | copy-start | bytes 49156
  78.1 58.7 %all-to-all-start = ((bf16[16,32,2048]{2,1,0:T(8,128)(2,1)}), bf16[16,32,2048]{2,1,0:T(8,128)(2,1)}, u32[]{:S(2)}, u32[]{:S(2)}) async-start(bf16[16,32,2048]{2,1,0:T(8,128)(2,1)} %bitcast.112), calls=%async_computation | async-start | bytes 4194304 | tf_op jit(solution)/shard_map/all_to_all | solution.py:94
  98.9 4.5 %copy-start.7 = (bf16[1,2048,768]{2,1,0:T(8,128)(2,1)S(1)}, bf16[1,2048,768]{2,1,0:T(8,128)(2,1)}, u32[]{:S(2)}) copy-start(bf16[1,2048,768]{2,1,0:T(8,128)(2,1)} %param.13) | copy-start | bytes 9437188
  102.0 1.3 copy-start.8
  136.7 6.1 %copy-start.4 = (s32[2,32,8]{1,2,0:T(8,128)S(1)}, s32[2,32,8]{1,2,0:T(8,128)}, u32[]{:S(2)}) copy-start(s32[2,32,8]{1,2,0:T(8,128)} %param.10) | copy-start | bytes 6148
  136.7 8.4 %copy-start.1 = (bf16[2,32,2048]{2,1,0:T(8,128)(2,1)S(1)}, bf16[2,32,2048]{2,1,0:T(8,128)(2,1)}, u32[]{:S(2)}) copy-start(bf16[2,32,2048]{2,1,0:T(8,128)(2,1)} %param.8) | copy-start | bytes 786436
  136.7 52.3 %all-to-all-start.1 = ((bf16[16,32,2048]{2,1,0:T(8,128)(2,1)}), bf16[16,32,2048]{2,1,0:T(8,128)(2,1)}, u32[]{:S(2)}, u32[]{:S(2)}) async-start(bf16[16,32,2048]{2,1,0:T(8,128)(2,1)} %bitcast.111), calls=%async_computation.1 | async-start | bytes 4194304 | tf_op jit(solution)/shard_map/all_to_all | solution.py:94
Sparse Core Ops, SparseCore 0:
  9.8 41.8 all-gather.4
  53.8 45.0 all-gather.6
where the time goes:
time: 199 us
  waiting for transfers between devices  74.3 us (37%)
  blocking collectives  39 us (20%)
  matrix products  32.9 us (17%)
  other arithmetic  18.4 us (9%)
  between operations  13.6 us (7%)
  starting transfers between devices  11.8 us (6%)
  local copies, waits for them, and re-layouts  8.62 us (4%)
    all_to_all x2, waiting for transfers between devices, serve(): lax.all_to_all(produced, 'ep', split_axis=0, concat_axis=0, tiled=True)  63.7 us
    all_gather x2, blocking collectives, serve(): all_ids = lax.all_gather(local_ids, 'ep', axis=0, tiled=True)  39 us
    dot_general x2, matrix products, expert_rows(): jnp.dot(hidden_state, down_mat, preferred_element_type=jnp.float32)  16.7 us
    all_to_all x2, starting transfers between devices, serve(): lax.all_to_all(produced, 'ep', split_axis=0, concat_axis=0, tiled=True)  11.8 us
    all_gather x2, waiting for transfers between devices, serve(): all_rows = lax.all_gather(local_rows, 'ep', axis=0, tiled=True)  9.88 us
    reduce_or x2, other arithmetic, serve(): jnp.any(place[:, :, None] == slot_ids[None, None, :], axis=1)  7.21 us
    dot_general x2, matrix products, serve(): jnp.dot(chooser, rows_here, preferred_element_type=jnp.float32)  6.16 us
    dot_general x2, matrix products, expert_rows(): jnp.dot(block_of_rows, up_matrix, preferred_element_type=jnp.float32)  5.99 us
  transfers between devices with their start and end apart: 4, of which 3 were waited for; matrix products, arithmetic and copies ran while one was open for 26% of the time, Pallas kernels for 0%

commit v1 on v0

v1 whole, which is shorter than its diff:
```python
import jax
import jax.numpy as jnp
from jax import lax
from jax.sharding import PartitionSpec as P


def normalize(rows_in, norm_gain):
    values = rows_in.astype(jnp.float32)
    power = jnp.mean(values * values, axis=-1, keepdims=True)
    return (values * lax.rsqrt(power + 1e-06) * norm_gain).astype(jnp.bfloat16)


def local(
    hidden_in,
    expert_ids,
    route_share,
    norm_gain,
    gate_weight,
    up_weight,
    down_weight,
    exponent_table,
):
    owners = lax.axis_size("ep")
    batches, dev_rows, fanout = expert_ids.shape
    model_width = hidden_in.shape[2]
    groups = exponent_table.shape[2]
    scale_group = gate_weight.shape[2] // groups
    scale_factors = jnp.repeat(jnp.exp2(exponent_table[0].astype(jnp.float32)), scale_group, axis=1)
    gate_matrix = gate_weight[0]
    up_matrix = up_weight[0]
    down_mat = down_weight[0]

    extra = -(-owners // 128) * 128
    columns = jnp.arange(extra, dtype=jnp.int32)
    shares = route_share.astype(jnp.float32) / 64.0
    dense = jnp.sum(
        jnp.where(expert_ids[..., None] == columns, shares[..., None], 0.0), axis=2
    ).astype(jnp.bfloat16)
    payload = jnp.concatenate([normalize(hidden_in, norm_gain), dense], axis=2)
    mine = (columns == lax.axis_index("ep")).astype(jnp.float32)

    gathered = [lax.all_gather(payload[batch], "ep", axis=0, tiled=True) for batch in range(batches)]
    outputs = []
    for batch in range(batches):
        rows = gathered[batch][:, :model_width]
        weight = jnp.sum(gathered[batch][:, model_width:].astype(jnp.float32) * mine, axis=1)
        gate = jnp.dot(rows, gate_matrix, preferred_element_type=jnp.float32) * scale_factors[0]
        up = jnp.dot(rows, up_matrix, preferred_element_type=jnp.float32) * scale_factors[1]
        hidden = (jax.nn.silu(gate) * up * scale_factors[2]).astype(jnp.bfloat16)
        partial = jnp.dot(hidden, down_mat, preferred_element_type=jnp.float32)
        partial = (partial * weight[:, None]).astype(jnp.bfloat16)
        mixed = lax.psum_scatter(partial, "ep", scatter_dimension=0, tiled=True)
        outputs.append(hidden_in[batch].astype(jnp.float32) + mixed.astype(jnp.float32))
    return jnp.stack(outputs).astype(jnp.bfloat16)


def solution(mesh):
    return jax.shard_map(
        local,
        mesh=mesh,
        in_specs=(
            P(None, ("grp", "ep"), None),
            P(None, ("grp", "ep"), None),
            P(None, ("grp", "ep"), None),
            P(),
            P("ep", None, None),
            P("ep", None, None),
            P("ep", None, None),
            P("ep", None, None),
        ),
        out_specs=P(None, ("grp", "ep"), None),
        check_vma=False,
    )
```

time: 199 us -> 242 us (1.22)
  the two profiles are of different devices: /device:TPU:13 before, /device:TPU:0 now
where the time goes in v1:
time: 242 us
  waiting for transfers between devices  192 us (79%)
  matrix products  27.8 us (11%)
  between operations  13.2 us (5%)
  other arithmetic  7.6 us (3%)
    reduce_scatter x2, waiting for transfers between devices, local(): mixed = lax.psum_scatter(partial, 'ep', scatter_dimension=0, tiled=True)  111 us
    all_gather x2, waiting for transfers between devices, local(): lax.all_gather(payload[batch], 'ep', axis=0, tiled=True)  80.5 us
    dot_general x2, matrix products, local(): partial = jnp.dot(hidden, down_mat, preferred_element_type=jnp.float32)  16.9 us
    dot_general x2, matrix products, local(): jnp.dot(rows, up_matrix, preferred_element_type=jnp.float32)  10.9 us
  transfers between devices with their start and end apart: 4, of which 4 were waited for; matrix products, arithmetic and copies ran while one was open for 8% of the time, Pallas kernels for 0%

profile of v1, /device:TPU:0, one launch (start us, length us, event | category | flops | bytes accessed | tf_op | source)
XLA Modules:
  0.0 242.1 jit_solution(10105896699676888315)
XLA Ops:
  6.5 0.0 copy-start
  6.5 0.0 all-gather.7.cloned.1.call-start
  6.5 1.2 fusion.38
  7.8 0.7 convert_multiply_fusion.2
  8.5 0.1 copy.12
  8.6 0.8 copy.11
  9.4 1.1 fusion.40
  10.4 0.2 select_reduce_fusion
  10.7 0.7 pad_maximum_fusion.1
  11.4 0.0 all-gather.7.cloned.1.call-update
  11.4 0.0 all-gather.5.cloned.1.call-start
  11.5 0.7 all-gather.5.cloned.1.call-update
  12.2 0.0 reduce-scatter.5.cloned.1.call-start
  12.2 0.7 multiply_exponential_fusion
  12.9 0.1 broadcast_bitcast_fusion.2
  13.0 0.1 broadcast_bitcast_fusion
  13.1 43.0 %all-gather.7.cloned.1.call-done = bf16[1,512,2176]{2,1,0:T(8,128)(2,1)} async-done(((bf16[1,32,2176]{2,1,0:T(8,128)(2,1)}), bf16[1,512,2176]{2,1,0:T(8,128)(2,1)}) %all-gather.7.cloned.1.call-update) | async-done | bytes 2228240 | tf_op jit(solution)/shard_map/all_gather | solution.py:42
  56.1 5.5 %fusion.2 = f32[512,768]{1,0:T(8,128)} fusion(bf16[1,2048,768]{2,1,0:T(8,128)(2,1)} %param.13, bf16[512,2176]{1,0:T(8,128)(2,1)} %bitcast.50), kind=kOutput, calls=%fused_computation.4 | convolution fusion | flops 1610612736 | bytes 6815744 | tf_op jit(solution)/shard_map/dot_general | solution.py:48
  61.5 37.5 %all-gather.5.cloned.1.call-done = bf16[1,512,2176]{2,1,0:T(8,128)(2,1)} async-done(((bf16[1,32,2176]{2,1,0:T(8,128)(2,1)}), bf16[1,512,2176]{2,1,0:T(8,128)(2,1)}) %all-gather.5.cloned.1.call-update) | async-done | bytes 2228240 | tf_op jit(solution)/shard_map/all_gather | solution.py:42
  99.1 1.2 multiply_reduce_fusion.1
  100.3 0.0 copy-done
  100.3 8.3 %multiply_convert_fusion = bf16[512,2048]{1,0:T(8,128)(2,1)} fusion(bf16[1,768,2048]{2,1,0:T(8,128)(2,1)S(1)} %copy-done, f32[512]{0:T(512)S(1)} %get-tuple-element.6, f32[512,768]{1,0:T(8,128)} %fusion.2, bf16[1,2048,768]{2,1,0:T(8,128)(2,1)} %param.12, bf16[512,2176]{1,0:T(8,128)(2,1)} %bitcast.52, f32[768]{0:T(1024)S(1)} %get-tuple-element.14, ...), kind=kOutput, calls=%fused_computation | convolution fusion | flops 3226861568 | bytes 12069888 | tf_op jit(solution)/shard_map/dot_general | solution.py:50
  108.6 0.0 reduce-scatter.5.cloned.1.call-update
  108.6 0.0 reduce-scatter.3.cloned.1.call-start
  108.7 5.5 %fusion.4 = f32[512,768]{1,0:T(8,128)} fusion(bf16[1,2048,768]{2,1,0:T(8,128)(2,1)} %param.13, bf16[512,2176]{1,0:T(8,128)(2,1)} %bitcast.48), kind=kOutput, calls=%fused_computation.6 | convolution fusion | flops 1610612736 | bytes 6815744 | tf_op jit(solution)/shard_map/dot_general | solution.py:48
  114.1 8.5 %multiply_convert_fusion.1 = bf16[512,2048]{1,0:T(8,128)(2,1)} fusion(bf16[1,768,2048]{2,1,0:T(8,128)(2,1)S(1)} %copy-done, f32[512]{0:T(512)S(1)} %get-tuple-element.5, f32[512,768]{1,0:T(8,128)} %fusion.4, bf16[1,2048,768]{2,1,0:T(8,128)(2,1)} %param.12, bf16[512,2176]{1,0:T(8,128)(2,1)} %bitcast.49, f32[768]{0:T(1024)S(1)} %get-tuple-element.14, ...), kind=kOutput, calls=%fused_computation.1 | convolution fusion | flops 3226861568 | bytes 12069888 | tf_op jit(solution)/shard_map/dot_general | solution.py:50
  122.7 0.0 copy-start.1
  122.7 0.0 reduce-scatter.3.cloned.1.call-update
  122.7 46.5 %reduce-scatter.5.cloned.1.call-done = bf16[32,2048]{1,0:T(8,128)(2,1)} async-done(((bf16[512,2048]{1,0:T(8,128)(2,1)}), bf16[32,2048]{1,0:T(8,128)(2,1)}) %reduce-scatter.5.cloned.1.call-update) | async-done | bytes 131088 | tf_op jit(solution)/shard_map/reduce_scatter | solution.py:52
  169.2 64.6 %reduce-scatter.3.cloned.1.call-done = bf16[32,2048]{1,0:T(8,128)(2,1)} async-done(((bf16[512,2048]{1,0:T(8,128)(2,1)}), bf16[32,2048]{1,0:T(8,128)(2,1)}) %reduce-scatter.3.cloned.1.call-update) | async-done | bytes 131088 | tf_op jit(solution)/shard_map/reduce_scatter | solution.py:52
  233.8 0.0 copy-done.1
  233.9 1.7 fusion.44
  (4 shorter events, 0.0 us)
Async XLA Ops:
  6.5 93.7 %copy-start = (bf16[1,768,2048]{2,1,0:T(8,128)(2,1)S(1)}, bf16[1,768,2048]{2,1,0:T(8,128)(2,1)}, u32[]{:S(2)}) copy-start(bf16[1,768,2048]{2,1,0:T(8,128)(2,1)} %param.14) | copy-start | bytes 9437188
  6.5 49.5 %all-gather.7.cloned.1.call-start = ((), (), s32[]{:S(2)}) async-start(), calls=%async_computation.5 | async-start | bytes 2367488 | tf_op jit(solution)/shard_map/all_gather | solution.py:42
  11.4 87.6 %all-gather.5.cloned.1.call-start = ((), (), s32[]{:S(2)}) async-start(), calls=%async_computation.4 | async-start | bytes 2367488 | tf_op jit(solution)/shard_map/all_gather | solution.py:42
  12.2 157.0 %reduce-scatter.5.cloned.1.call-start = ((), (), s32[]{:S(2)}) async-start(), calls=%async_computation.3 | async-start | bytes 2228224 | tf_op jit(solution)/shard_map/reduce_scatter | solution.py:52
  108.6 125.2 %reduce-scatter.3.cloned.1.call-start = ((), (), s32[]{:S(2)}) async-start(), calls=%async_computation.2 | async-start | bytes 2228224 | tf_op jit(solution)/shard_map/reduce_scatter | solution.py:52
  122.7 111.2 %copy-start.1 = (bf16[2,32,2048]{2,1,0:T(8,128)(2,1)S(1)}, bf16[2,32,2048]{2,1,0:T(8,128)(2,1)}, u32[]{:S(2)}) copy-start(bf16[2,32,2048]{2,1,0:T(8,128)(2,1)} %param.8) | copy-start | bytes 786436
Sparse Core Ops, SparseCore 0:
  11.5 44.4 all-gather.6
  58.4 40.6 all-gather.4
  108.8 60.4 reduce-scatter.4
  173.3 60.5 reduce-scatter.2

commit v2 on v1

--- a/solution.py
+++ b/solution.py
@@ -39,18 +39,52 @@
     payload = jnp.concatenate([normalize(hidden_in, norm_gain), dense], axis=2)
     mine = (columns == lax.axis_index("ep")).astype(jnp.float32)
 
-    gathered = [lax.all_gather(payload[batch], "ep", axis=0, tiled=True) for batch in range(batches)]
+    line = owners // 4
+
+    def along_line(k):
+        return [(i, (i + 4 * k) % owners) for i in range(owners)]
+
+    across_mid = [(i, i ^ 2) for i in range(owners)]
+    across_core = [(i, i ^ 1) for i in range(owners)]
+
+    def gather(rows):
+        pieces = [rows] + [lax.ppermute(rows, "ep", along_line(k)) for k in range(1, line)]
+        here = jnp.concatenate(pieces, axis=0)
+        there = lax.ppermute(here, "ep", across_mid)
+        return [
+            here,
+            there,
+            lax.ppermute(here, "ep", across_core),
+            lax.ppermute(there, "ep", across_core),
+        ]
+
+    def add(a, b):
+        return (a.astype(jnp.float32) + b.astype(jnp.float32)).astype(jnp.bfloat16)
+
+    def scatter(parts):
+        mid_sum = add(parts[1], lax.ppermute(parts[3], "ep", across_core))
+        back = lax.ppermute(mid_sum, "ep", across_mid)
+        total = add(add(parts[0], lax.ppermute(parts[2], "ep", across_core)), back)
+        result = total[:dev_rows].astype(jnp.float32)
+        for k in range(1, line):
+            piece = total[k * dev_rows : (k + 1) * dev_rows]
+            result = result + lax.ppermute(piece, "ep", along_line(line - k)).astype(jnp.float32)
+        return result
+
+    gathered = [gather(payload[batch]) for batch in range(batches)]
     outputs = []
     for batch in range(batches):
-        rows = gathered[batch][:, :model_width]
-        weight = jnp.sum(gathered[batch][:, model_width:].astype(jnp.float32) * mine, axis=1)
+        both = jnp.concatenate(gathered[batch], axis=0)
+        rows = both[:, :model_width]
+        weight = jnp.sum(both[:, model_width:].astype(jnp.float32) * mine, axis=1)
         gate = jnp.dot(rows, gate_matrix, preferred_element_type=jnp.float32) * scale_factors[0]
         up = jnp.dot(rows, up_matrix, preferred_element_type=jnp.float32) * scale_factors[1]
         hidden = (jax.nn.silu(gate) * up * scale_factors[2]).astype(jnp.bfloat16)
         partial = jnp.dot(hidden, down_mat, preferred_element_type=jnp.float32)
         partial = (partial * weight[:, None]).astype(jnp.bfloat16)
-        mixed = lax.psum_scatter(partial, "ep", scatter_dimension=0, tiled=True)
-        outputs.append(hidden_in[batch].astype(jnp.float32) + mixed.astype(jnp.float32))
+        quarter = line * dev_rows
+        mixed = scatter([partial[q * quarter : (q + 1) * quarter] for q in range(4)])
+        outputs.append(hidden_in[batch].astype(jnp.float32) + mixed)
     return jnp.stack(outputs).astype(jnp.bfloat16)
 
 

time: 242 us -> 128 us (0.53)
  waiting for transfers between devices: 192 us -> 37.1 us
  starting transfers between devices: 0.12 us -> 40 us
  local copies, waits for them, and re-layouts: 1.01 us -> 14.6 us
  between operations: 13.2 us -> 0.18 us
  other arithmetic: 7.6 us -> 11.8 us
  matrix products: 27.8 us -> 24.2 us
    reduce_scatter x2 -> x0, waiting for transfers between devices: 111 us -> none  [local(): mixed = lax.psum_scatter(partial, 'ep', scatter_dimension=0, tiled=True)]
    all_gather x2 -> x0, waiting for transfers between devices: 80.5 us -> none  [local(): lax.all_gather(payload[batch], 'ep', axis=0, tiled=True)]
    ppermute x0 -> x24, starting transfers between devices: none -> 40 us  [the longest x6 20.3 us: scatter(): lax.ppermute(piece, 'ep', along_line(line - k)).astype(jnp.float32)]
    ppermute x0 -> x24, waiting for transfers between devices: none -> 37.1 us  [the longest x2 12.5 us: scatter(): back = lax.ppermute(mid_sum, 'ep', across_mid)]
    unnamed x5 -> x23, local copies, waits for them, and re-layouts: 0.79 us -> 9.64 us
    slice x0 -> x4, local copies, waits for them, and re-layouts: none -> 3.84 us  [the longest x2 3.79 us: local(): mixed = scatter([partial[q * quarter:(q + 1) * quarter] for q in range(4)])]
    dot_general x2, matrix products: 10.9 us -> 7.59 us  [local(): jnp.dot(rows, gate_matrix, preferred_element_type=jnp.float32)]
    convert_element_type x0 -> x4, other arithmetic: none -> 2.97 us  [add(): return (a.astype(jnp.float32) + b.astype(jnp.float32)).astype(jnp.bfloat16)]
  transfers between devices with their start and end apart: 4 -> 24, of which waited for: 4 -> 8; matrix products, arithmetic and copies ran while one was open for 8% -> 23% of each run, Pallas kernels for 0% -> 0%
where the time goes in v2:
time: 128 us
  starting transfers between devices  40 us (31%)
  waiting for transfers between devices  37.1 us (29%)
  matrix products  24.2 us (19%)
  local copies, waits for them, and re-layouts  14.6 us (11%)
  other arithmetic  11.8 us (9%)
    ppermute x6, starting transfers between devices, scatter(): lax.ppermute(piece, 'ep', along_line(line - k)).astype(jnp.float32)  20.3 us
    dot_general x2, matrix products, local(): partial = jnp.dot(hidden, down_mat, preferred_element_type=jnp.float32)  16.6 us
    ppermute x2, waiting for transfers between devices, scatter(): back = lax.ppermute(mid_sum, 'ep', across_mid)  12.5 us
    ppermute x6, waiting for transfers between devices, gather(): lax.ppermute(rows, 'ep', along_line(k))  10.6 us
    ppermute x6, starting transfers between devices, gather(): lax.ppermute(rows, 'ep', along_line(k))  10.5 us
    unnamed x23, local copies, waits for them, and re-layouts  9.64 us
    dot_general x2, matrix products, local(): jnp.dot(rows, gate_matrix, preferred_element_type=jnp.float32)  7.59 us
    ppermute x6, waiting for transfers between devices, scatter(): lax.ppermute(piece, 'ep', along_line(line - k)).astype(jnp.float32)  7.36 us
  transfers between devices with their start and end apart: 24, of which 8 were waited for; matrix products, arithmetic and copies ran while one was open for 23% of the time, Pallas kernels for 0%

profile of v2, /device:TPU:0, one launch (start us, length us, event | category | flops | bytes accessed | tf_op | source)
XLA Modules:
  0.0 127.9 jit_solution(849010667922910100)
XLA Ops:
  1.7 1.1 fusion.38
  3.1 1.1 fusion.40
  4.9 3.0 %collective-permute-start = (bf16[32,2176]{1,0:T(8,128)(2,1)S(1)}, bf16[32,2176]{1,0:T(8,128)(2,1)}, u32[]{:S(2)}, u32[]{:S(2)}) collective-permute-start(bf16[32,2176]{1,0:T(8,128)(2,1)S(1)} %get-tuple-element.22), channel_id=1, source_target_pairs={{0,4},{1,5},{2,6},{3,7},{4,8},{5,9},{6,10},{7,11},{8,12},{9,13},{1... | collective-permute-start | bytes 417800 | tf_op jit(solution)/shard_map/ppermute | solution.py:51
  7.9 2.6 %collective-permute-start.1 = (bf16[32,2176]{1,0:T(8,128)(2,1)S(1)}, bf16[32,2176]{1,0:T(8,128)(2,1)}, u32[]{:S(2)}, u32[]{:S(2)}) collective-permute-start(bf16[32,2176]{1,0:T(8,128)(2,1)S(1)} %get-tuple-element.22), channel_id=1, source_target_pairs={{0,8},{1,9},{2,10},{3,11},{4,12},{5,13},{6,14},{7,15},{8,0},{9,1},... | collective-permute-start | bytes 417800 | tf_op jit(solution)/shard_map/ppermute | solution.py:51
  10.5 1.3 %collective-permute-start.2 = (bf16[32,2176]{1,0:T(8,128)(2,1)S(1)}, bf16[32,2176]{1,0:T(8,128)(2,1)}, u32[]{:S(2)}, u32[]{:S(2)}) collective-permute-start(bf16[32,2176]{1,0:T(8,128)(2,1)S(1)} %get-tuple-element.22), channel_id=1, source_target_pairs={{0,12},{1,13},{2,14},{3,15},{4,0},{5,1},{6,2},{7,3},{8,4},{9,5},{1... | collective-permute-start | bytes 417800 | tf_op jit(solution)/shard_map/ppermute | solution.py:51
  14.7 2.5 %collective-permute-start.14 = (bf16[32,2176]{1,0:T(8,128)(2,1)S(1)}, bf16[32,2176]{1,0:T(8,128)(2,1)S(1)}, u32[]{:S(2)}, u32[]{:S(2)}) collective-permute-start(bf16[32,2176]{1,0:T(8,128)(2,1)S(1)} %get-tuple-element.8), channel_id=1, source_target_pairs={{0,12},{1,13},{2,14},{3,15},{4,0},{5,1},{6,2},{7,3},{8,4},{9,5},{1... | collective-permute-start | bytes 417800 | tf_op jit(solution)/shard_map/ppermute | solution.py:51
  17.2 3.5 %collective-permute-done.1 = bf16[32,2176]{1,0:T(8,128)(2,1)} collective-permute-done((bf16[32,2176]{1,0:T(8,128)(2,1)S(1)}, bf16[32,2176]{1,0:T(8,128)(2,1)}, u32[]{:S(2)}, u32[]{:S(2)}) %collective-permute-start.1) | collective-permute-done | bytes 139296 | tf_op jit(solution)/shard_map/ppermute | solution.py:51
  20.7 1.9 %collective-permute-done.2 = bf16[32,2176]{1,0:T(8,128)(2,1)} collective-permute-done((bf16[32,2176]{1,0:T(8,128)(2,1)S(1)}, bf16[32,2176]{1,0:T(8,128)(2,1)}, u32[]{:S(2)}, u32[]{:S(2)}) %collective-permute-start.2) | collective-permute-done | bytes 139296 | tf_op jit(solution)/shard_map/ppermute | solution.py:51
  23.7 3.8 %collective-permute-start.3 = (bf16[128,2176]{1,0:T(8,128)(2,1)S(1)}, bf16[128,2176]{1,0:T(8,128)(2,1)S(1)}, u32[]{:S(2)}, u32[]{:S(2)}) collective-permute-start(bf16[128,2176]{1,0:T(8,128)(2,1)S(1)} %pad_maximum_fusion), channel_id=1, source_target_pairs={{0,2},{1,3},{2,0},{3,1},{4,6},{5,7},{6,4},{7,5},{8,10},{9,11},{10,... | collective-permute-start | bytes 1671176 | tf_op jit(solution)/shard_map/ppermute | solution.py:53
  27.5 4.3 %collective-permute-done.13 = bf16[32,2176]{1,0:T(8,128)(2,1)} collective-permute-done((bf16[32,2176]{1,0:T(8,128)(2,1)S(1)}, bf16[32,2176]{1,0:T(8,128)(2,1)}, u32[]{:S(2)}, u32[]{:S(2)}) %collective-permute-start.13) | collective-permute-done | bytes 139296 | tf_op jit(solution)/shard_map/ppermute | solution.py:51
  32.8 1.6 %collective-permute-start.15 = (bf16[128,2176]{1,0:T(8,128)(2,1)S(1)}, bf16[128,2176]{1,0:T(8,128)(2,1)S(1)}, u32[]{:S(2)}, u32[]{:S(2)}) collective-permute-start(bf16[128,2176]{1,0:T(8,128)(2,1)S(1)} %pad_maximum_fusion.1), channel_id=1, source_target_pairs={{0,2},{1,3},{2,0},{3,1},{4,6},{5,7},{6,4},{7,5},{8,10},{9,11},{10,... | collective-permute-start | bytes 1671176 | tf_op jit(solution)/shard_map/ppermute | solution.py:53
  34.4 1.6 %constant_dynamic-update-slice_fusion.5 = bf16[512,2176]{1,0:T(8,128)(2,1)} fusion(bf16[512,2176]{1,0:T(8,128)(2,1)} %get-tuple-element.21, bf16[32,2176]{1,0:T(8,128)(2,1)} %collective-permute-done), kind=kLoop, calls=%fused_computation.61 | loop fusion | bytes 278528
  36.0 1.6 %constant_dynamic-update-slice_fusion.4 = bf16[512,2176]{1,0:T(8,128)(2,1)} fusion(bf16[512,2176]{1,0:T(8,128)(2,1)} %constant_dynamic-update-slice_fusion.5, bf16[32,2176]{1,0:T(8,128)(2,1)} %collective-permute-done.1), kind=kLoop, calls=%fused_computation.60 | loop fusion | bytes 278528
  37.5 1.6 %constant_dynamic-update-slice_fusion.3 = bf16[512,2176]{1,0:T(8,128)(2,1)} fusion(bf16[512,2176]{1,0:T(8,128)(2,1)} %constant_dynamic-update-slice_fusion.4, bf16[32,2176]{1,0:T(8,128)(2,1)} %collective-permute-done.2), kind=kLoop, calls=%fused_computation.59 | loop fusion | bytes 278528
  41.6 6.6 %collective-permute-done.15 = bf16[128,2176]{1,0:T(8,128)(2,1)S(1)} collective-permute-done((bf16[128,2176]{1,0:T(8,128)(2,1)S(1)}, bf16[128,2176]{1,0:T(8,128)(2,1)S(1)}, u32[]{:S(2)}, u32[]{:S(2)}) %collective-permute-start.15) | collective-permute-done | bytes 557088 | tf_op jit(solution)/shard_map/ppermute | solution.py:53
  51.3 4.6 %fusion.8 = f32[512,768]{1,0:T(8,128)} fusion(bf16[1,2048,768]{2,1,0:T(8,128)(2,1)S(1)} %copy-done.5, bf16[512,2176]{1,0:T(8,128)(2,1)} %constant_dynamic-update-slice_fusion), kind=kOutput, calls=%fused_computation.10 | convolution fusion | flops 1610612736 | bytes 6815744 | tf_op jit(solution)/shard_map/dot_general | solution.py:80
  56.0 3.0 %fusion.6 = f32[512,768]{1,0:T(8,128)} fusion(bf16[1,2048,768]{2,1,0:T(8,128)(2,1)S(1)} %copy-done.5, bf16[512,2176]{1,0:T(8,128)(2,1)S(1)} %constant_dynamic-update-slice_fusion.7), kind=kOutput, calls=%fused_computation.8 | convolution fusion | flops 1610612736 | bytes 6815744 | tf_op jit(solution)/shard_map/dot_general | solution.py:80
  58.9 1.1 multiply_reduce_fusion.1
  60.1 8.3 %multiply_convert_fusion.1 = bf16[512,2048]{1,0:T(8,128)(2,1)} fusion(bf16[1,768,2048]{2,1,0:T(8,128)(2,1)S(1)} %copy-done, f32[512]{0:T(512)S(1)} %get-tuple-element.5, f32[512,768]{1,0:T(8,128)} %fusion.8, bf16[1,2048,768]{2,1,0:T(8,128)(2,1)} %param.13, bf16[512,2176]{1,0:T(8,128)(2,1)} %constant_dynamic-update-slice_fusion, ...), kind=kOutput, calls=%fused_computation.1 | convolution fusion | flops 3226861568 | bytes 12069888 | tf_op jit(solution)/shard_map/dot_general | solution.py:83
  68.4 2.4 %fusion.52 = (bf16[128,2048]{1,0:T(8,128)(2,1)}, bf16[128,2048]{1,0:T(8,128)(2,1)}) fusion(bf16[512,2048]{1,0:T(8,128)(2,1)} %multiply_convert_fusion.1), kind=kLoop, calls=%fused_computation.82 | loop fusion | bytes 2097152 | tf_op jit(solution)/shard_map/slice | solution.py:86
  71.3 8.3 %multiply_convert_fusion = bf16[512,2048]{1,0:T(8,128)(2,1)} fusion(bf16[1,768,2048]{2,1,0:T(8,128)(2,1)S(1)} %copy-done, f32[512]{0:T(512)S(1)} %get-tuple-element.6, f32[512,768]{1,0:T(8,128)} %fusion.6, bf16[1,2048,768]{2,1,0:T(8,128)(2,1)} %param.13, bf16[512,2176]{1,0:T(8,128)(2,1)} %copy-done.4, f32[768]{0:T(1024)S(1)} %get-tuple-element.28, ...), kind=kOutput, calls=%fused_computation | convolution fusion | flops 3226861568 | bytes 12069888 | tf_op jit(solution)/shard_map/dot_general | solution.py:83
  79.6 1.4 %fusion.53 = (bf16[128,2048]{1,0:T(8,128)(2,1)S(1)}, bf16[128,2048]{1,0:T(8,128)(2,1)S(1)}) fusion(bf16[512,2048]{1,0:T(8,128)(2,1)} %multiply_convert_fusion), kind=kLoop, calls=%fused_computation.83 | loop fusion | bytes 2097152 | tf_op jit(solution)/shard_map/slice | solution.py:86
  81.6 1.3 %add_convert_fusion.4 = bf16[128,2048]{1,0:T(8,128)(2,1)S(1)} fusion(bf16[128,2048]{1,0:T(8,128)(2,1)} %collective-permute-done.7, bf16[512,2048]{1,0:T(8,128)(2,1)} %multiply_convert_fusion.1), kind=kLoop, calls=%fused_computation.22 | loop fusion | flops 1048576 | bytes 1572864 | tf_op jit(solution)/shard_map/convert_element_type | solution.py:62
  82.9 1.8 %collective-permute-start.8 = (bf16[128,2048]{1,0:T(8,128)(2,1)S(1)}, bf16[128,2048]{1,0:T(8,128)(2,1)S(1)}, u32[]{:S(2)}, u32[]{:S(2)}) collective-permute-start(bf16[128,2048]{1,0:T(8,128)(2,1)S(1)} %add_convert_fusion.4), channel_id=1, source_target_pairs={{0,2},{1,3},{2,0},{3,1},{4,6},{5,7},{6,4},{7,5},{8,10},{9,11},{10,... | collective-permute-start | bytes 1572872 | tf_op jit(solution)/shard_map/ppermute | solution.py:66
  85.2 12.5 %collective-permute-done.8 = bf16[128,2048]{1,0:T(8,128)(2,1)S(1)} collective-permute-done((bf16[128,2048]{1,0:T(8,128)(2,1)S(1)}, bf16[128,2048]{1,0:T(8,128)(2,1)S(1)}, u32[]{:S(2)}, u32[]{:S(2)}) %collective-permute-start.8) | collective-permute-done | bytes 524320 | tf_op jit(solution)/shard_map/ppermute | solution.py:66
  97.7 1.3 add_convert_fusion.3
  99.1 8.8 %collective-permute-start.11 = (bf16[32,2048]{1,0:T(8,128)(2,1)S(1)}, bf16[32,2048]{1,0:T(8,128)(2,1)S(1)}, u32[]{:S(2)}, u32[]{:S(2)}) collective-permute-start(bf16[32,2048]{1,0:T(8,128)(2,1)S(1)} %get-tuple-element.16), channel_id=1, source_target_pairs={{0,4},{1,5},{2,6},{3,7},{4,8},{5,9},{6,10},{7,11},{8,12},{9,13},{1... | collective-permute-start | bytes 393224 | tf_op jit(solution)/shard_map/ppermute | solution.py:71
  107.9 2.4 %collective-permute-start.9 = (bf16[32,2048]{1,0:T(8,128)(2,1)S(1)}, bf16[32,2048]{1,0:T(8,128)(2,1)S(1)}, u32[]{:S(2)}, u32[]{:S(2)}) collective-permute-start(bf16[32,2048]{1,0:T(8,128)(2,1)S(1)} %get-tuple-element.15), channel_id=1, source_target_pairs={{0,12},{1,13},{2,14},{3,15},{4,0},{5,1},{6,2},{7,3},{8,4},{9,5},{1... | collective-permute-start | bytes 393224 | tf_op jit(solution)/shard_map/ppermute | solution.py:71
  110.6 6.6 %collective-permute-start.23 = (bf16[32,2048]{1,0:T(8,128)(2,1)S(1)}, bf16[32,2048]{1,0:T(8,128)(2,1)S(1)}, u32[]{:S(2)}, u32[]{:S(2)}) collective-permute-start(bf16[32,2048]{1,0:T(8,128)(2,1)S(1)} %get-tuple-element.19), channel_id=1, source_target_pairs={{0,4},{1,5},{2,6},{3,7},{4,8},{5,9},{6,10},{7,11},{8,12},{9,13},{1... | collective-permute-start | bytes 393224 | tf_op jit(solution)/shard_map/ppermute | solution.py:71
  117.2 2.4 %collective-permute-start.21 = (bf16[32,2048]{1,0:T(8,128)(2,1)S(1)}, bf16[32,2048]{1,0:T(8,128)(2,1)S(1)}, u32[]{:S(2)}, u32[]{:S(2)}) collective-permute-start(bf16[32,2048]{1,0:T(8,128)(2,1)S(1)} %get-tuple-element.18), channel_id=1, source_target_pairs={{0,12},{1,13},{2,14},{3,15},{4,0},{5,1},{6,2},{7,3},{8,4},{9,5},{1... | collective-permute-start | bytes 393224 | tf_op jit(solution)/shard_map/ppermute | solution.py:71
  119.6 1.5 %collective-permute-done.23 = bf16[32,2048]{1,0:T(8,128)(2,1)S(1)} collective-permute-done((bf16[32,2048]{1,0:T(8,128)(2,1)S(1)}, bf16[32,2048]{1,0:T(8,128)(2,1)S(1)}, u32[]{:S(2)}, u32[]{:S(2)}) %collective-permute-start.23) | collective-permute-done | bytes 131104 | tf_op jit(solution)/shard_map/ppermute | solution.py:71
  121.2 5.8 %collective-permute-done.22 = bf16[32,2048]{1,0:T(8,128)(2,1)S(1)} collective-permute-done((bf16[32,2048]{1,0:T(8,128)(2,1)S(1)}, bf16[32,2048]{1,0:T(8,128)(2,1)S(1)}, u32[]{:S(2)}, u32[]{:S(2)}) %collective-permute-start.22) | collective-permute-done | bytes 131104 | tf_op jit(solution)/shard_map/ppermute | solution.py:71
  (70 shorter events, 16.0 us)
Async XLA Ops:
  0.0 60.1 %copy-start = (bf16[1,768,2048]{2,1,0:T(8,128)(2,1)S(1)}, bf16[1,768,2048]{2,1,0:T(8,128)(2,1)}, u32[]{:S(2)}) copy-start(bf16[1,768,2048]{2,1,0:T(8,128)(2,1)} %param.14) | copy-start | bytes 9437188
  4.9 9.8 %collective-permute-start = (bf16[32,2176]{1,0:T(8,128)(2,1)S(1)}, bf16[32,2176]{1,0:T(8,128)(2,1)}, u32[]{:S(2)}, u32[]{:S(2)}) collective-permute-start(bf16[32,2176]{1,0:T(8,128)(2,1)S(1)} %get-tuple-element.22), channel_id=1, source_target_pairs={{0,4},{1,5},{2,6},{3,7},{4,8},{5,9},{6,10},{7,11},{8,12},{9,13},{1... | collective-permute-start | bytes 417800 | tf_op jit(solution)/shard_map/ppermute | solution.py:51
  7.9 12.7 %collective-permute-start.1 = (bf16[32,2176]{1,0:T(8,128)(2,1)S(1)}, bf16[32,2176]{1,0:T(8,128)(2,1)}, u32[]{:S(2)}, u32[]{:S(2)}) collective-permute-start(bf16[32,2176]{1,0:T(8,128)(2,1)S(1)} %get-tuple-element.22), channel_id=1, source_target_pairs={{0,8},{1,9},{2,10},{3,11},{4,12},{5,13},{6,14},{7,15},{8,0},{9,1},... | collective-permute-start | bytes 417800 | tf_op jit(solution)/shard_map/ppermute | solution.py:51
  10.5 12.1 %collective-permute-start.2 = (bf16[32,2176]{1,0:T(8,128)(2,1)S(1)}, bf16[32,2176]{1,0:T(8,128)(2,1)}, u32[]{:S(2)}, u32[]{:S(2)}) collective-permute-start(bf16[32,2176]{1,0:T(8,128)(2,1)S(1)} %get-tuple-element.22), channel_id=1, source_target_pairs={{0,12},{1,13},{2,14},{3,15},{4,0},{5,1},{6,2},{7,3},{8,4},{9,5},{1... | collective-permute-start | bytes 417800 | tf_op jit(solution)/shard_map/ppermute | solution.py:51
  11.9 15.6 %collective-permute-start.12 = (bf16[32,2176]{1,0:T(8,128)(2,1)S(1)}, bf16[32,2176]{1,0:T(8,128)(2,1)}, u32[]{:S(2)}, u32[]{:S(2)}) collective-permute-start(bf16[32,2176]{1,0:T(8,128)(2,1)S(1)} %get-tuple-element.8), channel_id=1, source_target_pairs={{0,4},{1,5},{2,6},{3,7},{4,8},{5,9},{6,10},{7,11},{8,12},{9,13},{1... | collective-permute-start | bytes 417800 | tf_op jit(solution)/shard_map/ppermute | solution.py:51
  12.6 19.2 %collective-permute-start.13 = (bf16[32,2176]{1,0:T(8,128)(2,1)S(1)}, bf16[32,2176]{1,0:T(8,128)(2,1)}, u32[]{:S(2)}, u32[]{:S(2)}) collective-permute-start(bf16[32,2176]{1,0:T(8,128)(2,1)S(1)} %get-tuple-element.8), channel_id=1, source_target_pairs={{0,8},{1,9},{2,10},{3,11},{4,12},{5,13},{6,14},{7,15},{8,0},{9,1},... | collective-permute-start | bytes 417800 | tf_op jit(solution)/shard_map/ppermute | solution.py:51
  13.7 25.4 %copy-start.3 = (bf16[512,2176]{1,0:T(8,128)(2,1)S(1)}, bf16[512,2176]{1,0:T(8,128)(2,1)}, u32[]{:S(2)}) copy-start(bf16[512,2176]{1,0:T(8,128)(2,1)} %get-tuple-element.7) | copy-start | bytes 6684676
  14.7 17.1 %collective-permute-start.14 = (bf16[32,2176]{1,0:T(8,128)(2,1)S(1)}, bf16[32,2176]{1,0:T(8,128)(2,1)S(1)}, u32[]{:S(2)}, u32[]{:S(2)}) collective-permute-start(bf16[32,2176]{1,0:T(8,128)(2,1)S(1)} %get-tuple-element.8), channel_id=1, source_target_pairs={{0,12},{1,13},{2,14},{3,15},{4,0},{5,1},{6,2},{7,3},{8,4},{9,5},{1... | collective-permute-start | bytes 417800 | tf_op jit(solution)/shard_map/ppermute | solution.py:51
  23.7 17.3 %collective-permute-start.3 = (bf16[128,2176]{1,0:T(8,128)(2,1)S(1)}, bf16[128,2176]{1,0:T(8,128)(2,1)S(1)}, u32[]{:S(2)}, u32[]{:S(2)}) collective-permute-start(bf16[128,2176]{1,0:T(8,128)(2,1)S(1)} %pad_maximum_fusion), channel_id=1, source_target_pairs={{0,2},{1,3},{2,0},{3,1},{4,6},{5,7},{6,4},{7,5},{8,10},{9,11},{10,... | collective-permute-start | bytes 1671176 | tf_op jit(solution)/shard_map/ppermute | solution.py:53
  27.5 21.5 %collective-permute-start.4 = (bf16[128,2176]{1,0:T(8,128)(2,1)S(1)}, bf16[128,2176]{1,0:T(8,128)(2,1)S(1)}, u32[]{:S(2)}, u32[]{:S(2)}) collective-permute-start(bf16[128,2176]{1,0:T(8,128)(2,1)S(1)} %pad_maximum_fusion), channel_id=1, source_target_pairs={{0,1},{1,0},{2,3},{3,2},{4,5},{5,4},{6,7},{7,6},{8,9},{9,8},{10,11... | collective-permute-start | bytes 1671176 | tf_op jit(solution)/shard_map/ppermute | solution.py:57
  32.8 15.3 %collective-permute-start.15 = (bf16[128,2176]{1,0:T(8,128)(2,1)S(1)}, bf16[128,2176]{1,0:T(8,128)(2,1)S(1)}, u32[]{:S(2)}, u32[]{:S(2)}) collective-permute-start(bf16[128,2176]{1,0:T(8,128)(2,1)S(1)} %pad_maximum_fusion.1), channel_id=1, source_target_pairs={{0,2},{1,3},{2,0},{3,1},{4,6},{5,7},{6,4},{7,5},{8,10},{9,11},{10,... | collective-permute-start | bytes 1671176 | tf_op jit(solution)/shard_map/ppermute | solution.py:53
  34.4 15.5 %collective-permute-start.16 = (bf16[128,2176]{1,0:T(8,128)(2,1)S(1)}, bf16[128,2176]{1,0:T(8,128)(2,1)S(1)}, u32[]{:S(2)}, u32[]{:S(2)}) collective-permute-start(bf16[128,2176]{1,0:T(8,128)(2,1)S(1)} %pad_maximum_fusion.1), channel_id=1, source_target_pairs={{0,1},{1,0},{2,3},{3,2},{4,5},{5,4},{6,7},{7,6},{8,9},{9,8},{10,11... | collective-permute-start | bytes 1671176 | tf_op jit(solution)/shard_map/ppermute | solution.py:57
  41.0 9.0 %collective-permute-start.5 = (bf16[128,2176]{1,0:T(8,128)(2,1)S(1)}, bf16[128,2176]{1,0:T(8,128)(2,1)S(1)}, u32[]{:S(2)}, u32[]{:S(2)}) collective-permute-start(bf16[128,2176]{1,0:T(8,128)(2,1)S(1)} %collective-permute-done.3), channel_id=1, source_target_pairs={{0,1},{1,0},{2,3},{3,2},{4,5},{5,4},{6,7},{7,6},{8,9},{9,8},{10,11... | collective-permute-start | bytes 1671176 | tf_op jit(solution)/shard_map/ppermute | solution.py:58
  48.1 7.7 %collective-permute-start.17 = (bf16[128,2176]{1,0:T(8,128)(2,1)S(1)}, bf16[128,2176]{1,0:T(8,128)(2,1)S(1)}, u32[]{:S(2)}, u32[]{:S(2)}) collective-permute-start(bf16[128,2176]{1,0:T(8,128)(2,1)S(1)} %collective-permute-done.15), channel_id=1, source_target_pairs={{0,1},{1,0},{2,3},{3,2},{4,5},{5,4},{6,7},{7,6},{8,9},{9,8},{10,11... | collective-permute-start | bytes 1671176 | tf_op jit(solution)/shard_map/ppermute | solution.py:58
  49.0 2.3 %copy-start.5 = (bf16[1,2048,768]{2,1,0:T(8,128)(2,1)S(1)}, bf16[1,2048,768]{2,1,0:T(8,128)(2,1)}, u32[]{:S(2)}) copy-start(bf16[1,2048,768]{2,1,0:T(8,128)(2,1)} %param.12) | copy-start | bytes 9437188
  55.9 3.0 %copy-start.4 = (bf16[512,2176]{1,0:T(8,128)(2,1)}, bf16[512,2176]{1,0:T(8,128)(2,1)S(1)}, u32[]{:S(2)}) copy-start(bf16[512,2176]{1,0:T(8,128)(2,1)S(1)} %constant_dynamic-update-slice_fusion.7) | copy-start | bytes 6684676
  70.8 10.8 %collective-permute-start.7 = (bf16[128,2048]{1,0:T(8,128)(2,1)}, bf16[128,2048]{1,0:T(8,128)(2,1)}, u32[]{:S(2)}, u32[]{:S(2)}) collective-permute-start(bf16[128,2048]{1,0:T(8,128)(2,1)} %get-tuple-element.12), channel_id=1, source_target_pairs={{0,1},{1,0},{2,3},{3,2},{4,5},{5,4},{6,7},{7,6},{8,9},{9,8},{10,11... | collective-permute-start | bytes 1572872 | tf_op jit(solution)/shard_map/ppermute | solution.py:65
  79.6 5.2 %copy-start.2 = (bf16[512,2048]{1,0:T(8,128)(2,1)S(1)}, bf16[512,2048]{1,0:T(8,128)(2,1)}, u32[]{:S(2)}) copy-start(bf16[512,2048]{1,0:T(8,128)(2,1)} %multiply_convert_fusion) | copy-start | bytes 6291460
  81.0 3.7 %collective-permute-start.19 = (bf16[128,2048]{1,0:T(8,128)(2,1)S(1)}, bf16[128,2048]{1,0:T(8,128)(2,1)S(1)}, u32[]{:S(2)}, u32[]{:S(2)}) collective-permute-start(bf16[128,2048]{1,0:T(8,128)(2,1)S(1)} %get-tuple-element.14), channel_id=1, source_target_pairs={{0,1},{1,0},{2,3},{3,2},{4,5},{5,4},{6,7},{7,6},{8,9},{9,8},{10,11... | collective-permute-start | bytes 1572872 | tf_op jit(solution)/shard_map/ppermute | solution.py:65
  81.1 4.1 %collective-permute-start.6 = (bf16[128,2048]{1,0:T(8,128)(2,1)}, bf16[128,2048]{1,0:T(8,128)(2,1)S(1)}, u32[]{:S(2)}, u32[]{:S(2)}) collective-permute-start(bf16[128,2048]{1,0:T(8,128)(2,1)} %get-tuple-element.11), channel_id=1, source_target_pairs={{0,1},{1,0},{2,3},{3,2},{4,5},{5,4},{6,7},{7,6},{8,9},{9,8},{10,11... | collective-permute-start | bytes 1572872 | tf_op jit(solution)/shard_map/ppermute | solution.py:67
  82.9 14.8 %collective-permute-start.8 = (bf16[128,2048]{1,0:T(8,128)(2,1)S(1)}, bf16[128,2048]{1,0:T(8,128)(2,1)S(1)}, u32[]{:S(2)}, u32[]{:S(2)}) collective-permute-start(bf16[128,2048]{1,0:T(8,128)(2,1)S(1)} %add_convert_fusion.4), channel_id=1, source_target_pairs={{0,2},{1,3},{2,0},{3,1},{4,6},{5,7},{6,4},{7,5},{8,10},{9,11},{10,... | collective-permute-start | bytes 1572872 | tf_op jit(solution)/shard_map/ppermute | solution.py:66
  84.7 25.6 %collective-permute-start.18 = (bf16[128,2048]{1,0:T(8,128)(2,1)S(1)}, bf16[128,2048]{1,0:T(8,128)(2,1)S(1)}, u32[]{:S(2)}, u32[]{:S(2)}) collective-permute-start(bf16[128,2048]{1,0:T(8,128)(2,1)S(1)} %get-tuple-element.13), channel_id=1, source_target_pairs={{0,1},{1,0},{2,3},{3,2},{4,5},{5,4},{6,7},{7,6},{8,9},{9,8},{10,11... | collective-permute-start | bytes 1572872 | tf_op jit(solution)/shard_map/ppermute | solution.py:67
  84.8 25.5 %collective-permute-start.20 = (bf16[128,2048]{1,0:T(8,128)(2,1)S(1)}, bf16[128,2048]{1,0:T(8,128)(2,1)S(1)}, u32[]{:S(2)}, u32[]{:S(2)}) collective-permute-start(bf16[128,2048]{1,0:T(8,128)(2,1)S(1)} %add_convert_fusion.1), channel_id=1, source_target_pairs={{0,2},{1,3},{2,0},{3,1},{4,6},{5,7},{6,4},{7,5},{8,10},{9,11},{10,... | collective-permute-start | bytes 1572872 | tf_op jit(solution)/shard_map/ppermute | solution.py:66
  99.0 28.0 %copy-start.1 = (bf16[2,32,2048]{2,1,0:T(8,128)(2,1)S(1)}, bf16[2,32,2048]{2,1,0:T(8,128)(2,1)}, u32[]{:S(2)}) copy-start(bf16[2,32,2048]{2,1,0:T(8,128)(2,1)} %param.8) | copy-start | bytes 786436
  99.1 18.1 %collective-permute-start.11 = (bf16[32,2048]{1,0:T(8,128)(2,1)S(1)}, bf16[32,2048]{1,0:T(8,128)(2,1)S(1)}, u32[]{:S(2)}, u32[]{:S(2)}) collective-permute-start(bf16[32,2048]{1,0:T(8,128)(2,1)S(1)} %get-tuple-element.16), channel_id=1, source_target_pairs={{0,4},{1,5},{2,6},{3,7},{4,8},{5,9},{6,10},{7,11},{8,12},{9,13},{1... | collective-permute-start | bytes 393224 | tf_op jit(solution)/shard_map/ppermute | solution.py:71
  107.9 11.8 %collective-permute-start.10 = (bf16[32,2048]{1,0:T(8,128)(2,1)S(1)}, bf16[32,2048]{1,0:T(8,128)(2,1)S(1)}, u32[]{:S(2)}, u32[]{:S(2)}) collective-permute-start(bf16[32,2048]{1,0:T(8,128)(2,1)S(1)} %get-tuple-element.17), channel_id=1, source_target_pairs={{0,8},{1,9},{2,10},{3,11},{4,12},{5,13},{6,14},{7,15},{8,0},{9,1},... | collective-permute-start | bytes 393224 | tf_op jit(solution)/shard_map/ppermute | solution.py:71
  107.9 11.8 %collective-permute-start.9 = (bf16[32,2048]{1,0:T(8,128)(2,1)S(1)}, bf16[32,2048]{1,0:T(8,128)(2,1)S(1)}, u32[]{:S(2)}, u32[]{:S(2)}) collective-permute-start(bf16[32,2048]{1,0:T(8,128)(2,1)S(1)} %get-tuple-element.15), channel_id=1, source_target_pairs={{0,12},{1,13},{2,14},{3,15},{4,0},{5,1},{6,2},{7,3},{8,4},{9,5},{1... | collective-permute-start | bytes 393224 | tf_op jit(solution)/shard_map/ppermute | solution.py:71
  110.6 10.5 %collective-permute-start.23 = (bf16[32,2048]{1,0:T(8,128)(2,1)S(1)}, bf16[32,2048]{1,0:T(8,128)(2,1)S(1)}, u32[]{:S(2)}, u32[]{:S(2)}) collective-permute-start(bf16[32,2048]{1,0:T(8,128)(2,1)S(1)} %get-tuple-element.19), channel_id=1, source_target_pairs={{0,4},{1,5},{2,6},{3,7},{4,8},{5,9},{6,10},{7,11},{8,12},{9,13},{1... | collective-permute-start | bytes 393224 | tf_op jit(solution)/shard_map/ppermute | solution.py:71
  117.2 9.8 %collective-permute-start.22 = (bf16[32,2048]{1,0:T(8,128)(2,1)S(1)}, bf16[32,2048]{1,0:T(8,128)(2,1)S(1)}, u32[]{:S(2)}, u32[]{:S(2)}) collective-permute-start(bf16[32,2048]{1,0:T(8,128)(2,1)S(1)} %get-tuple-element.20), channel_id=1, source_target_pairs={{0,8},{1,9},{2,10},{3,11},{4,12},{5,13},{6,14},{7,15},{8,0},{9,1},... | collective-permute-start | bytes 393224 | tf_op jit(solution)/shard_map/ppermute | solution.py:71
  117.2 9.8 %collective-permute-start.21 = (bf16[32,2048]{1,0:T(8,128)(2,1)S(1)}, bf16[32,2048]{1,0:T(8,128)(2,1)S(1)}, u32[]{:S(2)}, u32[]{:S(2)}) collective-permute-start(bf16[32,2048]{1,0:T(8,128)(2,1)S(1)} %get-tuple-element.18), channel_id=1, source_target_pairs={{0,12},{1,13},{2,14},{3,15},{4,0},{5,1},{6,2},{7,3},{8,4},{9,5},{1... | collective-permute-start | bytes 393224 | tf_op jit(solution)/shard_map/ppermute | solution.py:71

commit v3 on v1

v3 whole, which is shorter than its diff:
```python
import functools

import jax
import jax.numpy as jnp
from jax import lax
from jax.experimental import pallas as pl
from jax.experimental.pallas import tpu as pltpu
from jax.sharding import PartitionSpec as P

LANES = 128
VMEM = pl.BlockSpec(memory_space=pltpu.VMEM)
SMEM = pl.BlockSpec(memory_space=pltpu.SMEM)


def call(kernel, operands, specs, shapes, scratch=(), flops=0, name=None, vmem=8):
    moved = sum(a.size * a.dtype.itemsize for a in operands)
    moved += sum(s.size * s.dtype.itemsize for s in shapes)
    return pl.pallas_call(
        kernel,
        out_shape=shapes,
        in_specs=specs,
        out_specs=[VMEM] * len(shapes),
        scratch_shapes=list(scratch),
        cost_estimate=pl.CostEstimate(flops=flops, bytes_accessed=moved, transcendentals=0),
        compiler_params=pltpu.CompilerParams(vmem_limit_bytes=vmem << 20),
        name=name,
    )(*operands)


def prepare_kernel(hidden_ref, ids_ref, share_ref, gain_ref, *out_refs):
    batches, rows, width = hidden_ref.shape
    fanout = ids_ref.shape[1]
    extra = out_refs[0].shape[1] - width
    for batch in range(batches):
        values = hidden_ref[batch].astype(jnp.float32)
        power = jnp.mean(values * values, axis=-1, keepdims=True)
        normed = values * lax.rsqrt(power + 1e-06) * gain_ref[...]
        out_refs[batch][:, :width] = normed.astype(jnp.bfloat16)
        expert = lax.broadcasted_iota(jnp.int32, (extra, rows), 0)
        dense = jnp.zeros((extra, rows), jnp.float32)
        for k in range(fanout):
            share = share_ref[batch, k : k + 1, :].astype(jnp.float32) * (1.0 / 64.0)
            dense = dense + jnp.where(expert == ids_ref[batch, k : k + 1, :], share, 0.0)
        out_refs[batch][:, width:] = dense.T.astype(jnp.bfloat16)


def ffn_kernel(pieces, owner_ref, scale_ref, gate_ref, up_ref, down_ref, *refs):
    x_refs, out_refs, (x_all, hidden) = refs[:pieces], refs[pieces : 2 * pieces], refs[2 * pieces :]
    width, ff = gate_ref.shape[1:]
    group = ff // scale_ref.shape[1]
    starts = []
    at = 0
    for x_ref in x_refs:
        x_all[at : at + x_ref.shape[0], :] = x_ref[...]
        starts.append(at)
        at += x_ref.shape[0]
    step = 2 * group if ff % (2 * group) == 0 else group
    for f in range(0, ff, step):
        x = x_all[:, :width]
        gate = jnp.dot(x, gate_ref[0, :, f : f + step], preferred_element_type=jnp.float32)
        up = jnp.dot(x, up_ref[0, :, f : f + step], preferred_element_type=jnp.float32)
        for part in range(0, step, group):
            b = (f + part) // group
            g = gate[:, part : part + group] * scale_ref[0, b]
            u = up[:, part : part + group] * scale_ref[1, b]
            h = g / (1.0 + jnp.exp(-g)) * u * scale_ref[2, b]
            hidden[:, f + part : f + part + group] = h.astype(jnp.bfloat16)
    shares = x_all[:, width:].astype(jnp.float32)
    here = lax.broadcasted_iota(jnp.int32, shares.shape, 1) == owner_ref[0]
    weight = jnp.sum(jnp.where(here, shares, 0.0), axis=1, keepdims=True)
    cols = 512 if width % 512 == 0 else LANES
    for n in range(0, width, cols):
        out = jnp.dot(hidden[...], down_ref[0, :, n : n + cols], preferred_element_type=jnp.float32)
        out = (out * weight).astype(jnp.bfloat16)
        for start, out_ref in zip(starts, out_refs):
            out_ref[:, n : n + cols] = out[start : start + out_ref.shape[0], :]


def ffn(xs, owner, scales, weights):
    rows = sum(x.shape[0] for x in xs)
    width, ff = weights[0].shape[1:]
    return call(
        functools.partial(ffn_kernel, len(xs)),
        [owner, scales, *weights, *xs],
        [SMEM, SMEM] + [VMEM] * (3 + len(xs)),
        [jax.ShapeDtypeStruct((x.shape[0], width), jnp.bfloat16) for x in xs],
        [pltpu.VMEM((rows, xs[0].shape[1]), jnp.bfloat16), pltpu.VMEM((rows, ff), jnp.bfloat16)],
        flops=6 * rows * width * ff,
        name="ffn",
        vmem=16,
    )


def join_kernel(*refs):
    at = 0
    for ref in refs[:-1]:
        refs[-1][at : at + ref.shape[0], :] = ref[...]
        at += ref.shape[0]


def join(pieces):
    rows = sum(p.shape[0] for p in pieces)
    shape = jax.ShapeDtypeStruct((rows, pieces[0].shape[1]), pieces[0].dtype)
    return call(join_kernel, pieces, [VMEM] * len(pieces), [shape], name="join")[0]


def add_kernel(terms, *refs):
    at = 0
    for out_ref in refs[terms:]:
        rows = slice(at, at + out_ref.shape[0])
        total = refs[0][rows, :].astype(jnp.float32)
        for ref in refs[1:terms]:
            total = total + ref[rows, :].astype(jnp.float32)
        out_ref[...] = total.astype(out_ref.dtype)
        at += out_ref.shape[0]


def add(terms, cuts=1):
    rows, width = terms[0].shape
    shape = jax.ShapeDtypeStruct((rows // cuts, width), terms[0].dtype)
    return call(
        functools.partial(add_kernel, len(terms)), terms, [VMEM] * len(terms), [shape] * cuts, name="add"
    )


def finish_kernel(terms, hidden_ref, *refs):
    out_ref = refs[-1]
    for batch in range(hidden_ref.shape[0]):
        total = hidden_ref[batch].astype(jnp.float32)
        mine = refs[batch * terms : (batch + 1) * terms]
        mixed = mine[0][...].astype(jnp.float32)
        for ref in mine[1:]:
            mixed = mixed + ref[...].astype(jnp.float32)
        out_ref[batch] = (total + mixed).astype(out_ref.dtype)


def finish(hidden_in, terms):
    flat = [t for batch in terms for t in batch]
    return call(
        functools.partial(finish_kernel, len(terms[0])),
        [hidden_in, *flat],
        [VMEM] * (1 + len(flat)),
        [jax.ShapeDtypeStruct(hidden_in.shape, hidden_in.dtype)],
        name="finish",
    )[0]


def local(
    hidden_in,
    expert_ids,
    route_share,
    norm_gain,
    gate_weight,
    up_weight,
    down_weight,
    exponent_table,
):
    owners = lax.axis_size("ep")
    batches, dev_rows, fanout = expert_ids.shape
    model_width = hidden_in.shape[2]
    extra = -(-owners // LANES) * LANES
    weights = (gate_weight, up_weight, down_weight)
    scales = jnp.exp2(exponent_table[0].astype(jnp.float32))
    owner = lax.axis_index("ep").astype(jnp.int32).reshape(1)

    line = owners // 4

    def along_line(rows, k):
        return lax.ppermute(rows, "ep", [(i, (i + 4 * k) % owners) for i in range(owners)])

    def to_mid(rows):
        return lax.ppermute(rows, "ep", [(i, i ^ 2) for i in range(owners)])

    def to_core(rows):
        return lax.ppermute(rows, "ep", [(i, i ^ 1) for i in range(owners)])

    payload = call(
        prepare_kernel,
        [
            hidden_in,
            expert_ids.transpose(0, 2, 1),
            route_share.transpose(0, 2, 1),
            norm_gain.reshape(1, model_width),
        ],
        [VMEM] * 4,
        [jax.ShapeDtypeStruct((dev_rows, model_width + extra), jnp.bfloat16)] * batches,
        name="prepare",
    )

    terms = []
    pieces = None
    for rows in payload:
        if pieces is not None:
            rows, *pieces = lax.optimization_barrier((rows, *pieces))
        pieces = [rows] + [along_line(rows, k) for k in range(1, line)]
        here = join(pieces)
        there = to_mid(here)
        out_here, out_here_core = ffn([here, to_core(here)], owner, scales, weights)
        out_there, out_there_core = ffn([there, to_core(there)], owner, scales, weights)
        back = to_mid(add([out_there, to_core(out_there_core)])[0])
        total = add([out_here, to_core(out_here_core), back], line)
        terms.append([total[0]] + [along_line(total[k], line - k) for k in range(1, line)])
    return finish(hidden_in, terms)


def solution(mesh):
    return jax.shard_map(
        local,
        mesh=mesh,
        in_specs=(
            P(None, ("grp", "ep"), None),
            P(None, ("grp", "ep"), None),
            P(None, ("grp", "ep"), None),
            P(),
            P("ep", None, None),
            P("ep", None, None),
            P("ep", None, None),
            P("ep", None, None),
        ),
        out_specs=P(None, ("grp", "ep"), None),
        check_vma=False,
    )
```

time: 242 us -> 109 us (0.45)
  waiting for transfers between devices: 192 us -> 52 us
  starting transfers between devices: 0.12 us -> 31.3 us
  matrix products: 27.8 us -> 0 us
  Pallas kernels: 0 us -> 15.4 us
  between operations: 13.2 us -> 0.15 us
  local copies, waits for them, and re-layouts: 1.01 us -> 8.72 us
  other arithmetic: 7.6 us -> 0.69 us
    reduce_scatter x2 -> x0, waiting for transfers between devices: 111 us -> none  [local(): mixed = lax.psum_scatter(partial, 'ep', scatter_dimension=0, tiled=True)]
    all_gather x2 -> x0, waiting for transfers between devices: 80.5 us -> none  [local(): lax.all_gather(payload[batch], 'ep', axis=0, tiled=True)]
    ppermute x0 -> x24, waiting for transfers between devices: none -> 52 us  [the longest x12 29.8 us: along_line(): lax.ppermute(rows, 'ep', [(i, (i + 4 * k) % owners) for i in range(owners)])]
    ppermute x0 -> x24, starting transfers between devices: none -> 31.3 us  [the longest x12 25.2 us: along_line(): lax.ppermute(rows, 'ep', [(i, (i + 4 * k) % owners) for i in range(owners)])]
    dot_general x4 -> x0, matrix products: 27.8 us -> none  [the longest x2 16.9 us: local(): partial = jnp.dot(hidden, down_mat, preferred_element_type=jnp.float32)]
    pallas_call x0 -> x12, Pallas kernels: none -> 15.4 us  [call(): pl.pallas_call(kernel, out_shape=shapes, in_specs=specs, out_specs=[VMEM]...]
    unnamed x5 -> x19, local copies, waits for them, and re-layouts: 0.79 us -> 8.72 us
    reduce_sum x3 -> x0, other arithmetic: 2.63 us -> none  [the longest x1 1.23 us: normalize(): power = jnp.mean(values * values, axis=-1, keepdims=True)]
  transfers between devices with their start and end apart: 4 -> 24, of which waited for: 4 -> 9; matrix products, arithmetic and copies ran while one was open for 8% -> 1% of each run, Pallas kernels for 0% -> 13%
where the time goes in v3:
time: 109 us; the launch traced here: 108 us
  waiting for transfers between devices  52 us (48%)
  starting transfers between devices  31.3 us (29%)
  Pallas kernels  15.4 us (14%)
  local copies, waits for them, and re-layouts  8.72 us (8%)
    ppermute x12, waiting for transfers between devices, along_line(): lax.ppermute(rows, 'ep', [(i, (i + 4 * k) % owners) for i in range(owners)])  29.8 us
    ppermute x12, starting transfers between devices, along_line(): lax.ppermute(rows, 'ep', [(i, (i + 4 * k) % owners) for i in range(owners)])  25.2 us
    ppermute x4, waiting for transfers between devices, to_mid(): return lax.ppermute(rows, 'ep', [(i, i ^ 2) for i in range(owners)])  22.1 us
    pallas_call x12, Pallas kernels, call(): pl.pallas_call(kernel, out_shape=shapes, in_specs=specs, out_specs=[VMEM]...  15.4 us
    unnamed x19, local copies, waits for them, and re-layouts  8.72 us
    ppermute x4, starting transfers between devices, to_mid(): return lax.ppermute(rows, 'ep', [(i, i ^ 2) for i in range(owners)])  4.31 us
  transfers between devices with their start and end apart: 24, of which 9 were waited for; matrix products, arithmetic and copies ran while one was open for 1% of the time, Pallas kernels for 13%

profile of v3, /device:TPU:0, one launch (start us, length us, event | category | flops | bytes accessed | tf_op | source)
XLA Modules:
  0.0 108.3 jit_solution(5154339404939729588)
XLA Ops:
  0.0 0.9 copy-done.4
  3.3 5.1 %collective-permute-start.2 = (bf16[32,2176]{1,0:T(8,128)(2,1)S(1)}, bf16[32,2176]{1,0:T(8,128)(2,1)S(1)}, u32[]{:S(2)}, u32[]{:S(2)}) collective-permute-start(bf16[32,2176]{1,0:T(8,128)(2,1)S(1)} %get-tuple-element.24.refs_0_), channel_id=1, source_target_pairs={{0,12},{1,13},{2,14},{3,15},{4,0},{5,1},{6,2},{7,3},{8,4},{9,5},{1... | collective-permute-start | bytes 417800 | tf_op jit(solution)/shard_map/ppermute | solution.py:169
  8.4 1.0 collective-permute-start
  9.4 3.1 %collective-permute-done.2.refs_3_ = bf16[32,2176]{1,0:T(8,128)(2,1)S(1)} collective-permute-done((bf16[32,2176]{1,0:T(8,128)(2,1)S(1)}, bf16[32,2176]{1,0:T(8,128)(2,1)S(1)}, u32[]{:S(2)}, u32[]{:S(2)}) %collective-permute-start.2) | collective-permute-done | bytes 139296 | tf_op jit(solution)/shard_map/ppermute | solution.py:169
  12.5 7.7 %collective-permute-done.1.refs_2_ = bf16[32,2176]{1,0:T(8,128)(2,1)S(1)} collective-permute-done((bf16[32,2176]{1,0:T(8,128)(2,1)S(1)}, bf16[32,2176]{1,0:T(8,128)(2,1)S(1)}, u32[]{:S(2)}, u32[]{:S(2)}) %collective-permute-start.1) | collective-permute-done | bytes 139296 | tf_op jit(solution)/shard_map/ppermute | solution.py:169
  20.3 1.6 %collective-permute-start.5 = (bf16[128,2176]{1,0:T(8,128)(2,1)S(1)}, bf16[128,2176]{1,0:T(8,128)(2,1)S(1)}, u32[]{:S(2)}, u32[]{:S(2)}) collective-permute-start(bf16[128,2176]{1,0:T(8,128)(2,1)S(1)} %join.2.refs_0_), channel_id=1, source_target_pairs={{0,2},{1,3},{2,0},{3,1},{4,6},{5,7},{6,4},{7,5},{8,10},{9,11},{10,... | collective-permute-start | bytes 1671176 | tf_op jit(solution)/shard_map/ppermute | solution.py:172
  21.8 1.5 %collective-permute-start.14 = (bf16[32,2176]{1,0:T(8,128)(2,1)S(1)}, bf16[32,2176]{1,0:T(8,128)(2,1)S(1)}, u32[]{:S(2)}, u32[]{:S(2)}) collective-permute-start(bf16[32,2176]{1,0:T(8,128)(2,1)S(1)} %get-tuple-element.34.refs_0_), channel_id=1, source_target_pairs={{0,12},{1,13},{2,14},{3,15},{4,0},{5,1},{6,2},{7,3},{8,4},{9,5},{1... | collective-permute-start | bytes 417800 | tf_op jit(solution)/shard_map/ppermute | solution.py:169
  23.4 1.2 %collective-permute-start.13 = (bf16[32,2176]{1,0:T(8,128)(2,1)S(1)}, bf16[32,2176]{1,0:T(8,128)(2,1)S(1)}, u32[]{:S(2)}, u32[]{:S(2)}) collective-permute-start(bf16[32,2176]{1,0:T(8,128)(2,1)S(1)} %get-tuple-element.34.refs_0_), channel_id=1, source_target_pairs={{0,8},{1,9},{2,10},{3,11},{4,12},{5,13},{6,14},{7,15},{8,0},{9,1},... | collective-permute-start | bytes 417800 | tf_op jit(solution)/shard_map/ppermute | solution.py:169
  24.6 2.0 %collective-permute-start.12 = (bf16[32,2176]{1,0:T(8,128)(2,1)S(1)}, bf16[32,2176]{1,0:T(8,128)(2,1)S(1)}, u32[]{:S(2)}, u32[]{:S(2)}) collective-permute-start(bf16[32,2176]{1,0:T(8,128)(2,1)S(1)} %get-tuple-element.34.refs_0_), channel_id=1, source_target_pairs={{0,4},{1,5},{2,6},{3,7},{4,8},{5,9},{6,10},{7,11},{8,12},{9,13},{1... | collective-permute-start | bytes 417800 | tf_op jit(solution)/shard_map/ppermute | solution.py:169
  26.6 1.1 %collective-permute-done.14.refs_3_ = bf16[32,2176]{1,0:T(8,128)(2,1)S(1)} collective-permute-done((bf16[32,2176]{1,0:T(8,128)(2,1)S(1)}, bf16[32,2176]{1,0:T(8,128)(2,1)S(1)}, u32[]{:S(2)}, u32[]{:S(2)}) %collective-permute-start.14) | collective-permute-done | bytes 139296 | tf_op jit(solution)/shard_map/ppermute | solution.py:169
  27.7 8.6 %collective-permute-done.13.refs_2_ = bf16[32,2176]{1,0:T(8,128)(2,1)S(1)} collective-permute-done((bf16[32,2176]{1,0:T(8,128)(2,1)S(1)}, bf16[32,2176]{1,0:T(8,128)(2,1)S(1)}, u32[]{:S(2)}, u32[]{:S(2)}) %collective-permute-start.13) | collective-permute-done | bytes 139296 | tf_op jit(solution)/shard_map/ppermute | solution.py:169
  36.9 10.0 %collective-permute-done.17.refs_0_ = bf16[128,2176]{1,0:T(8,128)(2,1)S(1)} collective-permute-done((bf16[128,2176]{1,0:T(8,128)(2,1)S(1)}, bf16[128,2176]{1,0:T(8,128)(2,1)S(1)}, u32[]{:S(2)}, u32[]{:S(2)}) %collective-permute-start.17) | collective-permute-done | bytes 557088 | tf_op jit(solution)/shard_map/ppermute | solution.py:172
  48.2 1.9 %copy-done = bf16[1,2048,768]{2,1,0:T(8,128)(2,1)S(1)} copy-done((bf16[1,2048,768]{2,1,0:T(8,128)(2,1)S(1)}, bf16[1,2048,768]{2,1,0:T(8,128)(2,1)}, u32[]{:S(2)}) %copy-start) | copy-done | bytes 3145752
  50.1 1.9 %copy-done.2 = bf16[1,2048,768]{2,1,0:T(8,128)(2,1)S(1)} copy-done((bf16[1,2048,768]{2,1,0:T(8,128)(2,1)S(1)}, bf16[1,2048,768]{2,1,0:T(8,128)(2,1)}, u32[]{:S(2)}) %copy-start.2) | copy-done | bytes 3145752
  52.0 1.9 %copy-done.3 = bf16[1,768,2048]{2,1,0:T(8,128)(2,1)S(1)} copy-done((bf16[1,768,2048]{2,1,0:T(8,128)(2,1)S(1)}, bf16[1,768,2048]{2,1,0:T(8,128)(2,1)}, u32[]{:S(2)}) %copy-start.3) | copy-done | bytes 3145752
  53.9 3.8 %ffn.5 = (bf16[128,2048]{1,0:T(8,128)(2,1)S(1)}, bf16[128,2048]{1,0:T(8,128)(2,1)S(1)}) custom-call(s32[1]{0:T(128)} %bitcast.owner_ref, f32[3,6]{1,0:T(4,128)S(1)} %bitcast.7, bf16[1,2048,768]{2,1,0:T(8,128)(2,1)S(1)} %copy-done, bf16[1,2048,768]{2,1,0:T(8,128)(2,1)S(1)} %copy-done.2, bf16[1,768,2048]{2,1,0:T(8,128)(2,1)S(1)} %copy-done.3, ...), custom_call_target="tpu_custom_call" | custom-call | flops 2415919104 | bytes 11599948 | tf_op jit(solution)/shard_map/ffn/pallas_call | solution.py:18
  58.3 3.3 %ffn.7 = (bf16[128,2048]{1,0:T(8,128)(2,1)S(1)}, bf16[128,2048]{1,0:T(8,128)(2,1)S(1)}) custom-call(s32[1]{0:T(128)} %bitcast.owner_ref, f32[3,6]{1,0:T(4,128)S(1)} %bitcast.8, bf16[1,2048,768]{2,1,0:T(8,128)(2,1)S(1)} %copy-done, bf16[1,2048,768]{2,1,0:T(8,128)(2,1)S(1)} %copy-done.2, bf16[1,768,2048]{2,1,0:T(8,128)(2,1)S(1)} %copy-done.3, ...), custom_call_target="tpu_custom_call" | custom-call | flops 2415919104 | bytes 11599948 | tf_op jit(solution)/shard_map/ffn/pallas_call | solution.py:18
  61.6 3.3 %ffn.4 = (bf16[128,2048]{1,0:T(8,128)(2,1)S(1)}, bf16[128,2048]{1,0:T(8,128)(2,1)S(1)}) custom-call(s32[1]{0:T(128)} %bitcast.owner_ref, f32[3,6]{1,0:T(4,128)S(1)} %bitcast.9, bf16[1,2048,768]{2,1,0:T(8,128)(2,1)S(1)} %copy-done.1, bf16[1,2048,768]{2,1,0:T(8,128)(2,1)S(1)} %copy-done.2, bf16[1,768,2048]{2,1,0:T(8,128)(2,1)S(1)} %copy-done.3, ...), custom_call_target="tpu_custom_call" | custom-call | flops 2415919104 | bytes 11599948 | tf_op jit(solution)/shard_map/ffn/pallas_call | solution.py:18
  65.6 0.8 collective-permute-start.8
  66.4 3.3 %ffn.6 = (bf16[128,2048]{1,0:T(8,128)(2,1)S(1)}, bf16[128,2048]{1,0:T(8,128)(2,1)S(1)}) custom-call(s32[1]{0:T(128)} %bitcast.owner_ref, f32[3,6]{1,0:T(4,128)S(1)} %bitcast.10, bf16[1,2048,768]{2,1,0:T(8,128)(2,1)S(1)} %copy-done.1, bf16[1,2048,768]{2,1,0:T(8,128)(2,1)S(1)} %copy-done.2, bf16[1,768,2048]{2,1,0:T(8,128)(2,1)S(1)} %copy-done.3, ...), custom_call_target="tpu_custom_call" | custom-call | flops 2415919104 | bytes 11599948 | tf_op jit(solution)/shard_map/ffn/pallas_call | solution.py:18
  69.9 1.4 %collective-permute-start.20 = (bf16[128,2048]{1,0:T(8,128)(2,1)S(1)}, bf16[128,2048]{1,0:T(8,128)(2,1)S(1)}, u32[]{:S(2)}, u32[]{:S(2)}) collective-permute-start(bf16[128,2048]{1,0:T(8,128)(2,1)S(1)} %add.6), channel_id=1, source_target_pairs={{0,2},{1,3},{2,0},{3,1},{4,6},{5,7},{6,4},{7,5},{8,10},{9,11},{10,... | collective-permute-start | bytes 1572872 | tf_op jit(solution)/shard_map/ppermute | solution.py:172
  71.3 9.2 %collective-permute-done.8.refs_2_ = bf16[128,2048]{1,0:T(8,128)(2,1)S(1)} collective-permute-done((bf16[128,2048]{1,0:T(8,128)(2,1)S(1)}, bf16[128,2048]{1,0:T(8,128)(2,1)S(1)}, u32[]{:S(2)}, u32[]{:S(2)}) %collective-permute-start.8) | collective-permute-done | bytes 524320 | tf_op jit(solution)/shard_map/ppermute | solution.py:172
  80.7 3.1 %collective-permute-start.9 = (bf16[32,2048]{1,0:T(8,128)(2,1)S(1)}, bf16[32,2048]{1,0:T(8,128)(2,1)S(1)}, u32[]{:S(2)}, u32[]{:S(2)}) collective-permute-start(bf16[32,2048]{1,0:T(8,128)(2,1)S(1)} %get-tuple-element.30), channel_id=1, source_target_pairs={{0,12},{1,13},{2,14},{3,15},{4,0},{5,1},{6,2},{7,3},{8,4},{9,5},{1... | collective-permute-start | bytes 393224 | tf_op jit(solution)/shard_map/ppermute | solution.py:169
  83.7 2.2 %collective-permute-start.10 = (bf16[32,2048]{1,0:T(8,128)(2,1)S(1)}, bf16[32,2048]{1,0:T(8,128)(2,1)S(1)}, u32[]{:S(2)}, u32[]{:S(2)}) collective-permute-start(bf16[32,2048]{1,0:T(8,128)(2,1)S(1)} %get-tuple-element.31), channel_id=1, source_target_pairs={{0,8},{1,9},{2,10},{3,11},{4,12},{5,13},{6,14},{7,15},{8,0},{9,1},... | collective-permute-start | bytes 393224 | tf_op jit(solution)/shard_map/ppermute | solution.py:169
  85.9 1.9 %collective-permute-start.11 = (bf16[32,2048]{1,0:T(8,128)(2,1)S(1)}, bf16[32,2048]{1,0:T(8,128)(2,1)S(1)}, u32[]{:S(2)}, u32[]{:S(2)}) collective-permute-start(bf16[32,2048]{1,0:T(8,128)(2,1)S(1)} %get-tuple-element.32), channel_id=1, source_target_pairs={{0,4},{1,5},{2,6},{3,7},{4,8},{5,9},{6,10},{7,11},{8,12},{9,13},{1... | collective-permute-start | bytes 393224 | tf_op jit(solution)/shard_map/ppermute | solution.py:169
  87.8 3.0 %collective-permute-done.20.refs_2_ = bf16[128,2048]{1,0:T(8,128)(2,1)S(1)} collective-permute-done((bf16[128,2048]{1,0:T(8,128)(2,1)S(1)}, bf16[128,2048]{1,0:T(8,128)(2,1)S(1)}, u32[]{:S(2)}, u32[]{:S(2)}) %collective-permute-start.20) | collective-permute-done | bytes 524320 | tf_op jit(solution)/shard_map/ppermute | solution.py:172
  91.0 3.1 %collective-permute-start.21 = (bf16[32,2048]{1,0:T(8,128)(2,1)S(1)}, bf16[32,2048]{1,0:T(8,128)(2,1)S(1)}, u32[]{:S(2)}, u32[]{:S(2)}) collective-permute-start(bf16[32,2048]{1,0:T(8,128)(2,1)S(1)} %get-tuple-element.40), channel_id=1, source_target_pairs={{0,12},{1,13},{2,14},{3,15},{4,0},{5,1},{6,2},{7,3},{8,4},{9,5},{1... | collective-permute-start | bytes 393224 | tf_op jit(solution)/shard_map/ppermute | solution.py:169
  94.0 2.2 %collective-permute-start.22 = (bf16[32,2048]{1,0:T(8,128)(2,1)S(1)}, bf16[32,2048]{1,0:T(8,128)(2,1)S(1)}, u32[]{:S(2)}, u32[]{:S(2)}) collective-permute-start(bf16[32,2048]{1,0:T(8,128)(2,1)S(1)} %get-tuple-element.41), channel_id=1, source_target_pairs={{0,8},{1,9},{2,10},{3,11},{4,12},{5,13},{6,14},{7,15},{8,0},{9,1},... | collective-permute-start | bytes 393224 | tf_op jit(solution)/shard_map/ppermute | solution.py:169
  96.2 1.9 %collective-permute-start.23 = (bf16[32,2048]{1,0:T(8,128)(2,1)S(1)}, bf16[32,2048]{1,0:T(8,128)(2,1)S(1)}, u32[]{:S(2)}, u32[]{:S(2)}) collective-permute-start(bf16[32,2048]{1,0:T(8,128)(2,1)S(1)} %get-tuple-element.42), channel_id=1, source_target_pairs={{0,4},{1,5},{2,6},{3,7},{4,8},{5,9},{6,10},{7,11},{8,12},{9,13},{1... | collective-permute-start | bytes 393224 | tf_op jit(solution)/shard_map/ppermute | solution.py:169
  98.1 1.4 %collective-permute-done.21.refs_5_ = bf16[32,2048]{1,0:T(8,128)(2,1)S(1)} collective-permute-done((bf16[32,2048]{1,0:T(8,128)(2,1)S(1)}, bf16[32,2048]{1,0:T(8,128)(2,1)S(1)}, u32[]{:S(2)}, u32[]{:S(2)}) %collective-permute-start.21) | collective-permute-done | bytes 131104 | tf_op jit(solution)/shard_map/ppermute | solution.py:169
  99.5 7.9 %collective-permute-done.22.refs_6_ = bf16[32,2048]{1,0:T(8,128)(2,1)S(1)} collective-permute-done((bf16[32,2048]{1,0:T(8,128)(2,1)S(1)}, bf16[32,2048]{1,0:T(8,128)(2,1)S(1)}, u32[]{:S(2)}, u32[]{:S(2)}) %collective-permute-start.22) | collective-permute-done | bytes 131104 | tf_op jit(solution)/shard_map/ppermute | solution.py:169
  107.4 0.9 finish.1
  (48 shorter events, 6.2 us)
Async XLA Ops:
  0.0 0.9 copy-start.4
  1.0 0.7 copy-start.6
  1.6 0.7 copy-start.7
  3.3 9.2 %collective-permute-start.2 = (bf16[32,2176]{1,0:T(8,128)(2,1)S(1)}, bf16[32,2176]{1,0:T(8,128)(2,1)S(1)}, u32[]{:S(2)}, u32[]{:S(2)}) collective-permute-start(bf16[32,2176]{1,0:T(8,128)(2,1)S(1)} %get-tuple-element.24.refs_0_), channel_id=1, source_target_pairs={{0,12},{1,13},{2,14},{3,15},{4,0},{5,1},{6,2},{7,3},{8,4},{9,5},{1... | collective-permute-start | bytes 417800 | tf_op jit(solution)/shard_map/ppermute | solution.py:169
  8.4 11.8 %collective-permute-start.1 = (bf16[32,2176]{1,0:T(8,128)(2,1)S(1)}, bf16[32,2176]{1,0:T(8,128)(2,1)S(1)}, u32[]{:S(2)}, u32[]{:S(2)}) collective-permute-start(bf16[32,2176]{1,0:T(8,128)(2,1)S(1)} %get-tuple-element.24.refs_0_), channel_id=1, source_target_pairs={{0,8},{1,9},{2,10},{3,11},{4,12},{5,13},{6,14},{7,15},{8,0},{9,1},... | collective-permute-start | bytes 417800 | tf_op jit(solution)/shard_map/ppermute | solution.py:169
  8.4 11.8 %collective-permute-start = (bf16[32,2176]{1,0:T(8,128)(2,1)S(1)}, bf16[32,2176]{1,0:T(8,128)(2,1)S(1)}, u32[]{:S(2)}, u32[]{:S(2)}) collective-permute-start(bf16[32,2176]{1,0:T(8,128)(2,1)S(1)} %get-tuple-element.24.refs_0_), channel_id=1, source_target_pairs={{0,4},{1,5},{2,6},{3,7},{4,8},{5,9},{6,10},{7,11},{8,12},{9,13},{1... | collective-permute-start | bytes 417800 | tf_op jit(solution)/shard_map/ppermute | solution.py:169
  20.3 16.7 %collective-permute-start.5 = (bf16[128,2176]{1,0:T(8,128)(2,1)S(1)}, bf16[128,2176]{1,0:T(8,128)(2,1)S(1)}, u32[]{:S(2)}, u32[]{:S(2)}) collective-permute-start(bf16[128,2176]{1,0:T(8,128)(2,1)S(1)} %join.2.refs_0_), channel_id=1, source_target_pairs={{0,2},{1,3},{2,0},{3,1},{4,6},{5,7},{6,4},{7,5},{8,10},{9,11},{10,... | collective-permute-start | bytes 1671176 | tf_op jit(solution)/shard_map/ppermute | solution.py:172
  21.8 5.9 %collective-permute-start.14 = (bf16[32,2176]{1,0:T(8,128)(2,1)S(1)}, bf16[32,2176]{1,0:T(8,128)(2,1)S(1)}, u32[]{:S(2)}, u32[]{:S(2)}) collective-permute-start(bf16[32,2176]{1,0:T(8,128)(2,1)S(1)} %get-tuple-element.34.refs_0_), channel_id=1, source_target_pairs={{0,12},{1,13},{2,14},{3,15},{4,0},{5,1},{6,2},{7,3},{8,4},{9,5},{1... | collective-permute-start | bytes 417800 | tf_op jit(solution)/shard_map/ppermute | solution.py:169
  23.4 12.9 %collective-permute-start.13 = (bf16[32,2176]{1,0:T(8,128)(2,1)S(1)}, bf16[32,2176]{1,0:T(8,128)(2,1)S(1)}, u32[]{:S(2)}, u32[]{:S(2)}) collective-permute-start(bf16[32,2176]{1,0:T(8,128)(2,1)S(1)} %get-tuple-element.34.refs_0_), channel_id=1, source_target_pairs={{0,8},{1,9},{2,10},{3,11},{4,12},{5,13},{6,14},{7,15},{8,0},{9,1},... | collective-permute-start | bytes 417800 | tf_op jit(solution)/shard_map/ppermute | solution.py:169
  24.6 11.7 %collective-permute-start.12 = (bf16[32,2176]{1,0:T(8,128)(2,1)S(1)}, bf16[32,2176]{1,0:T(8,128)(2,1)S(1)}, u32[]{:S(2)}, u32[]{:S(2)}) collective-permute-start(bf16[32,2176]{1,0:T(8,128)(2,1)S(1)} %get-tuple-element.34.refs_0_), channel_id=1, source_target_pairs={{0,4},{1,5},{2,6},{3,7},{4,8},{5,9},{6,10},{7,11},{8,12},{9,13},{1... | collective-permute-start | bytes 417800 | tf_op jit(solution)/shard_map/ppermute | solution.py:169
  36.4 10.6 %collective-permute-start.17 = (bf16[128,2176]{1,0:T(8,128)(2,1)S(1)}, bf16[128,2176]{1,0:T(8,128)(2,1)S(1)}, u32[]{:S(2)}, u32[]{:S(2)}) collective-permute-start(bf16[128,2176]{1,0:T(8,128)(2,1)S(1)} %join.3.refs_0_), channel_id=1, source_target_pairs={{0,2},{1,3},{2,0},{3,1},{4,6},{5,7},{6,4},{7,5},{8,10},{9,11},{10,... | collective-permute-start | bytes 1671176 | tf_op jit(solution)/shard_map/ppermute | solution.py:172
  36.9 11.3 %collective-permute-start.6 = (bf16[128,2176]{1,0:T(8,128)(2,1)S(1)}, bf16[128,2176]{1,0:T(8,128)(2,1)}, u32[]{:S(2)}, u32[]{:S(2)}) collective-permute-start(bf16[128,2176]{1,0:T(8,128)(2,1)S(1)} %collective-permute-done.5.refs_0_), channel_id=1, source_target_pairs={{0,1},{1,0},{2,3},{3,2},{4,5},{5,4},{6,7},{7,6},{8,9},{9,8},{10,11... | collective-permute-start | bytes 1671176 | tf_op jit(solution)/shard_map/ppermute | solution.py:175
  46.9 11.3 %collective-permute-start.18 = (bf16[128,2176]{1,0:T(8,128)(2,1)S(1)}, bf16[128,2176]{1,0:T(8,128)(2,1)S(1)}, u32[]{:S(2)}, u32[]{:S(2)}) collective-permute-start(bf16[128,2176]{1,0:T(8,128)(2,1)S(1)} %collective-permute-done.17.refs_0_), channel_id=1, source_target_pairs={{0,1},{1,0},{2,3},{3,2},{4,5},{5,4},{6,7},{7,6},{8,9},{9,8},{10,11... | collective-permute-start | bytes 1671176 | tf_op jit(solution)/shard_map/ppermute | solution.py:175
  46.9 14.7 %collective-permute-start.3 = (bf16[128,2176]{1,0:T(8,128)(2,1)S(1)}, bf16[128,2176]{1,0:T(8,128)(2,1)S(1)}, u32[]{:S(2)}, u32[]{:S(2)}) collective-permute-start(bf16[128,2176]{1,0:T(8,128)(2,1)S(1)} %join.2.refs_0_), channel_id=1, source_target_pairs={{0,1},{1,0},{2,3},{3,2},{4,5},{5,4},{6,7},{7,6},{8,9},{9,8},{10,11... | collective-permute-start | bytes 1671176 | tf_op jit(solution)/shard_map/ppermute | solution.py:175
  48.1 18.3 %collective-permute-start.15 = (bf16[128,2176]{1,0:T(8,128)(2,1)S(1)}, bf16[128,2176]{1,0:T(8,128)(2,1)S(1)}, u32[]{:S(2)}, u32[]{:S(2)}) collective-permute-start(bf16[128,2176]{1,0:T(8,128)(2,1)S(1)} %join.3.refs_0_), channel_id=1, source_target_pairs={{0,1},{1,0},{2,3},{3,2},{4,5},{5,4},{6,7},{7,6},{8,9},{9,8},{10,11... | collective-permute-start | bytes 1671176 | tf_op jit(solution)/shard_map/ppermute | solution.py:175
  48.2 1.9 %copy-start = (bf16[1,2048,768]{2,1,0:T(8,128)(2,1)S(1)}, bf16[1,2048,768]{2,1,0:T(8,128)(2,1)}, u32[]{:S(2)}) copy-start(bf16[1,2048,768]{2,1,0:T(8,128)(2,1)} %gate_ref.7) | copy-start | bytes 9437188
  50.1 1.9 %copy-start.2 = (bf16[1,2048,768]{2,1,0:T(8,128)(2,1)S(1)}, bf16[1,2048,768]{2,1,0:T(8,128)(2,1)}, u32[]{:S(2)}) copy-start(bf16[1,2048,768]{2,1,0:T(8,128)(2,1)} %up_ref.7) | copy-start | bytes 9437188
  52.0 1.9 %copy-start.3 = (bf16[1,768,2048]{2,1,0:T(8,128)(2,1)S(1)}, bf16[1,768,2048]{2,1,0:T(8,128)(2,1)}, u32[]{:S(2)}) copy-start(bf16[1,768,2048]{2,1,0:T(8,128)(2,1)} %down_ref.7) | copy-start | bytes 9437188
  57.7 4.0 %copy-start.1 = (bf16[1,2048,768]{2,1,0:T(8,128)(2,1)S(1)}, bf16[1,2048,768]{2,1,0:T(8,128)(2,1)}, u32[]{:S(2)}) copy-start(bf16[1,2048,768]{2,1,0:T(8,128)(2,1)} %gate_ref.7) | copy-start | bytes 9437188
  57.7 7.8 %collective-permute-start.7 = (bf16[128,2048]{1,0:T(8,128)(2,1)S(1)}, bf16[128,2048]{1,0:T(8,128)(2,1)S(1)}, u32[]{:S(2)}, u32[]{:S(2)}) collective-permute-start(bf16[128,2048]{1,0:T(8,128)(2,1)S(1)} %get-tuple-element.28), channel_id=1, source_target_pairs={{0,1},{1,0},{2,3},{3,2},{4,5},{5,4},{6,7},{7,6},{8,9},{9,8},{10,11... | collective-permute-start | bytes 1572872 | tf_op jit(solution)/shard_map/ppermute | solution.py:175
  61.5 8.2 %collective-permute-start.19 = (bf16[128,2048]{1,0:T(8,128)(2,1)S(1)}, bf16[128,2048]{1,0:T(8,128)(2,1)S(1)}, u32[]{:S(2)}, u32[]{:S(2)}) collective-permute-start(bf16[128,2048]{1,0:T(8,128)(2,1)S(1)} %get-tuple-element.38), channel_id=1, source_target_pairs={{0,1},{1,0},{2,3},{3,2},{4,5},{5,4},{6,7},{7,6},{8,9},{9,8},{10,11... | collective-permute-start | bytes 1572872 | tf_op jit(solution)/shard_map/ppermute | solution.py:175
  64.9 6.4 %collective-permute-start.4 = (bf16[128,2048]{1,0:T(8,128)(2,1)S(1)}, bf16[128,2048]{1,0:T(8,128)(2,1)S(1)}, u32[]{:S(2)}, u32[]{:S(2)}) collective-permute-start(bf16[128,2048]{1,0:T(8,128)(2,1)S(1)} %get-tuple-element.26), channel_id=1, source_target_pairs={{0,1},{1,0},{2,3},{3,2},{4,5},{5,4},{6,7},{7,6},{8,9},{9,8},{10,11... | collective-permute-start | bytes 1572872 | tf_op jit(solution)/shard_map/ppermute | solution.py:175
  65.6 14.8 %collective-permute-start.8 = (bf16[128,2048]{1,0:T(8,128)(2,1)S(1)}, bf16[128,2048]{1,0:T(8,128)(2,1)S(1)}, u32[]{:S(2)}, u32[]{:S(2)}) collective-permute-start(bf16[128,2048]{1,0:T(8,128)(2,1)S(1)} %add.4), channel_id=1, source_target_pairs={{0,2},{1,3},{2,0},{3,1},{4,6},{5,7},{6,4},{7,5},{8,10},{9,11},{10,... | collective-permute-start | bytes 1572872 | tf_op jit(solution)/shard_map/ppermute | solution.py:172
  69.7 37.7 %copy-start.5 = (bf16[2,32,2048]{2,1,0:T(8,128)(2,1)S(1)}, bf16[2,32,2048]{2,1,0:T(8,128)(2,1)}, u32[]{:S(2)}) copy-start(bf16[2,32,2048]{2,1,0:T(8,128)(2,1)} %hidden_ref.3) | copy-start | bytes 786436
  69.7 18.1 %collective-permute-start.16 = (bf16[128,2048]{1,0:T(8,128)(2,1)S(1)}, bf16[128,2048]{1,0:T(8,128)(2,1)S(1)}, u32[]{:S(2)}, u32[]{:S(2)}) collective-permute-start(bf16[128,2048]{1,0:T(8,128)(2,1)S(1)} %get-tuple-element.36), channel_id=1, source_target_pairs={{0,1},{1,0},{2,3},{3,2},{4,5},{5,4},{6,7},{7,6},{8,9},{9,8},{10,11... | collective-permute-start | bytes 1572872 | tf_op jit(solution)/shard_map/ppermute | solution.py:175
  69.9 20.8 %collective-permute-start.20 = (bf16[128,2048]{1,0:T(8,128)(2,1)S(1)}, bf16[128,2048]{1,0:T(8,128)(2,1)S(1)}, u32[]{:S(2)}, u32[]{:S(2)}) collective-permute-start(bf16[128,2048]{1,0:T(8,128)(2,1)S(1)} %add.6), channel_id=1, source_target_pairs={{0,2},{1,3},{2,0},{3,1},{4,6},{5,7},{6,4},{7,5},{8,10},{9,11},{10,... | collective-permute-start | bytes 1572872 | tf_op jit(solution)/shard_map/ppermute | solution.py:172
  80.7 15.5 %collective-permute-start.9 = (bf16[32,2048]{1,0:T(8,128)(2,1)S(1)}, bf16[32,2048]{1,0:T(8,128)(2,1)S(1)}, u32[]{:S(2)}, u32[]{:S(2)}) collective-permute-start(bf16[32,2048]{1,0:T(8,128)(2,1)S(1)} %get-tuple-element.30), channel_id=1, source_target_pairs={{0,12},{1,13},{2,14},{3,15},{4,0},{5,1},{6,2},{7,3},{8,4},{9,5},{1... | collective-permute-start | bytes 393224 | tf_op jit(solution)/shard_map/ppermute | solution.py:169
  83.7 14.4 %collective-permute-start.10 = (bf16[32,2048]{1,0:T(8,128)(2,1)S(1)}, bf16[32,2048]{1,0:T(8,128)(2,1)S(1)}, u32[]{:S(2)}, u32[]{:S(2)}) collective-permute-start(bf16[32,2048]{1,0:T(8,128)(2,1)S(1)} %get-tuple-element.31), channel_id=1, source_target_pairs={{0,8},{1,9},{2,10},{3,11},{4,12},{5,13},{6,14},{7,15},{8,0},{9,1},... | collective-permute-start | bytes 393224 | tf_op jit(solution)/shard_map/ppermute | solution.py:169
  85.9 12.3 %collective-permute-start.11 = (bf16[32,2048]{1,0:T(8,128)(2,1)S(1)}, bf16[32,2048]{1,0:T(8,128)(2,1)S(1)}, u32[]{:S(2)}, u32[]{:S(2)}) collective-permute-start(bf16[32,2048]{1,0:T(8,128)(2,1)S(1)} %get-tuple-element.32), channel_id=1, source_target_pairs={{0,4},{1,5},{2,6},{3,7},{4,8},{5,9},{6,10},{7,11},{8,12},{9,13},{1... | collective-permute-start | bytes 393224 | tf_op jit(solution)/shard_map/ppermute | solution.py:169
  91.0 8.6 %collective-permute-start.21 = (bf16[32,2048]{1,0:T(8,128)(2,1)S(1)}, bf16[32,2048]{1,0:T(8,128)(2,1)S(1)}, u32[]{:S(2)}, u32[]{:S(2)}) collective-permute-start(bf16[32,2048]{1,0:T(8,128)(2,1)S(1)} %get-tuple-element.40), channel_id=1, source_target_pairs={{0,12},{1,13},{2,14},{3,15},{4,0},{5,1},{6,2},{7,3},{8,4},{9,5},{1... | collective-permute-start | bytes 393224 | tf_op jit(solution)/shard_map/ppermute | solution.py:169
  94.0 13.4 %collective-permute-start.22 = (bf16[32,2048]{1,0:T(8,128)(2,1)S(1)}, bf16[32,2048]{1,0:T(8,128)(2,1)S(1)}, u32[]{:S(2)}, u32[]{:S(2)}) collective-permute-start(bf16[32,2048]{1,0:T(8,128)(2,1)S(1)} %get-tuple-element.41), channel_id=1, source_target_pairs={{0,8},{1,9},{2,10},{3,11},{4,12},{5,13},{6,14},{7,15},{8,0},{9,1},... | collective-permute-start | bytes 393224 | tf_op jit(solution)/shard_map/ppermute | solution.py:169
  96.2 11.2 %collective-permute-start.23 = (bf16[32,2048]{1,0:T(8,128)(2,1)S(1)}, bf16[32,2048]{1,0:T(8,128)(2,1)S(1)}, u32[]{:S(2)}, u32[]{:S(2)}) collective-permute-start(bf16[32,2048]{1,0:T(8,128)(2,1)S(1)} %get-tuple-element.42), channel_id=1, source_target_pairs={{0,4},{1,5},{2,6},{3,7},{4,8},{5,9},{6,10},{7,11},{8,12},{9,13},{1... | collective-permute-start | bytes 393224 | tf_op jit(solution)/shard_map/ppermute | solution.py:169
  (1 other events, 0.7 us)

commit v4 on v3

v4 whole, which is shorter than its diff:
```python
import functools

import jax
import jax.numpy as jnp
from jax import lax
from jax.experimental import pallas as pl
from jax.experimental.pallas import tpu as pltpu
from jax.sharding import PartitionSpec as P

LANES = 128
VMEM = pl.BlockSpec(memory_space=pltpu.VMEM)
SMEM = pl.BlockSpec(memory_space=pltpu.SMEM)
HBM = pl.BlockSpec(memory_space=pltpu.HBM)
PARTS = 2


def call(kernel, operands, specs, shapes, scratch=(), flops=0, name=None, vmem=8):
    moved = sum(a.size * a.dtype.itemsize for a in operands)
    moved += sum(s.size * s.dtype.itemsize for s in shapes)
    return pl.pallas_call(
        kernel,
        out_shape=shapes,
        in_specs=specs,
        out_specs=[VMEM] * len(shapes),
        scratch_shapes=list(scratch),
        cost_estimate=pl.CostEstimate(flops=flops, bytes_accessed=moved, transcendentals=0),
        compiler_params=pltpu.CompilerParams(vmem_limit_bytes=vmem << 20),
        name=name,
    )(*operands)


def after(value, *others):
    return lax.optimization_barrier((value, *others))[0]


def prepare_kernel(hidden_hbm, ids_hbm, share_hbm, gain_hbm, *refs):
    out_refs, (hidden_ref, ids_ref, share_ref, gain_ref, sems) = refs[:-5], refs[-5:]
    sources = (hidden_hbm, ids_hbm, share_hbm, gain_hbm)
    targets = (hidden_ref, ids_ref, share_ref, gain_ref)
    copies = [pltpu.make_async_copy(s, t, sems.at[i]) for i, (s, t) in enumerate(zip(sources, targets))]
    for copy in copies:
        copy.start()
    for copy in copies:
        copy.wait()
    batches, rows, width = hidden_ref.shape
    fanout = ids_ref.shape[1]
    line, part, full = out_refs[0].shape
    extra = full - width
    parts = rows // part
    for batch in range(batches):
        values = hidden_ref[batch].astype(jnp.float32)
        power = jnp.mean(values * values, axis=-1, keepdims=True)
        normed = (values * lax.rsqrt(power + 1e-06) * gain_ref[...]).astype(jnp.bfloat16)
        expert = lax.broadcasted_iota(jnp.int32, (extra, rows), 0)
        dense = jnp.zeros((extra, rows), jnp.float32)
        for k in range(fanout):
            share = share_ref[batch, k : k + 1, :].astype(jnp.float32) * (1.0 / 64.0)
            dense = dense + jnp.where(expert == ids_ref[batch, k : k + 1, :], share, 0.0)
        dense = dense.T.astype(jnp.bfloat16)
        for p in range(parts):
            out_ref = out_refs[batch * parts + p]
            for place in range(line):
                out_ref[place, :, :width] = normed[p * part : (p + 1) * part]
                out_ref[place, :, width:] = dense[p * part : (p + 1) * part]


def load_kernel(*refs):
    count = len(refs) // 2
    copies = [pltpu.make_async_copy(refs[i], refs[count + i], refs[-1].at[i]) for i in range(count)]
    for copy in copies:
        copy.start()
    for copy in copies:
        copy.wait()


def load(weights):
    return call(
        load_kernel,
        weights,
        [HBM] * len(weights),
        [jax.ShapeDtypeStruct(w.shape, w.dtype) for w in weights],
        [pltpu.SemaphoreType.DMA((len(weights),))],
        name="load",
    )


def ffn_kernel(owner_ref, scale_ref, gate_ref, up_ref, down_ref, *refs):
    x_refs, (mine_ref, other_ref, x_all, hidden) = refs[:4], refs[4:]
    width, ff = gate_ref.shape[1:]
    group = ff // scale_ref.shape[1]
    line, part, full = x_refs[0].shape
    rows = line * part
    for i, x_ref in enumerate(x_refs):
        x_all[i * rows : (i + 1) * rows, :] = x_ref[...].reshape(rows, full)
    step = 2 * group if ff % (2 * group) == 0 else group
    for f in range(0, ff, step):
        x = x_all[:, :width]
        gate = jnp.dot(x, gate_ref[0, :, f : f + step], preferred_element_type=jnp.float32)
        up = jnp.dot(x, up_ref[0, :, f : f + step], preferred_element_type=jnp.float32)
        for at in range(0, step, group):
            b = (f + at) // group
            g = gate[:, at : at + group] * scale_ref[0, b]
            u = up[:, at : at + group] * scale_ref[1, b]
            h = g / (1.0 + jnp.exp(-g)) * u * scale_ref[2, b]
            hidden[:, f + at : f + at + group] = h.astype(jnp.bfloat16)
    shares = x_all[:, width:].astype(jnp.float32)
    here = lax.broadcasted_iota(jnp.int32, shares.shape, 1) == owner_ref[0]
    weight = jnp.sum(jnp.where(here, shares, 0.0), axis=1, keepdims=True)
    cols = 512 if width % 512 == 0 else LANES
    for n in range(0, width, cols):
        out = jnp.dot(hidden[...], down_ref[0, :, n : n + cols], preferred_element_type=jnp.float32)
        out = (out * weight).astype(jnp.bfloat16).reshape(4, line, part, cols)
        mine_ref[:, :, :, n : n + cols] = out[:2]
        other_ref[:, :, :, n : n + cols] = out[2:]


def ffn(xs, owner, scales, weights):
    line, part, full = xs[0].shape
    width, ff = weights[0].shape[1:]
    rows = 4 * line * part
    return call(
        ffn_kernel,
        [owner, scales, *weights, *xs],
        [SMEM, SMEM] + [VMEM] * 7,
        [jax.ShapeDtypeStruct((2, line, part, width), jnp.bfloat16)] * 2,
        [pltpu.VMEM((rows, full), jnp.bfloat16), pltpu.VMEM((rows, ff), jnp.bfloat16)],
        flops=6 * rows * width * ff,
        name="ffn",
        vmem=16,
    )


def add_kernel(slot, mine_ref, other_ref, *refs):
    out_ref = refs[-1]
    for place in range(out_ref.shape[0]):
        total = mine_ref[slot, place].astype(jnp.float32) + other_ref[slot, place].astype(jnp.float32)
        for ref in refs[:-1]:
            total = total + ref[place].astype(jnp.float32)
        out_ref[place] = total.astype(out_ref.dtype)


def add(slot, mine, other, *more):
    shape = jax.ShapeDtypeStruct(mine.shape[1:], mine.dtype)
    return call(
        functools.partial(add_kernel, slot),
        [mine, other, *more],
        [VMEM] * (2 + len(more)),
        [shape],
        name="add",
    )[0]


def finish_kernel(hidden_ref, *refs):
    term_refs, out_ref = refs[:-1], refs[-1]
    batches, rows, _ = hidden_ref.shape
    part = term_refs[0].shape[1]
    parts = rows // part
    for batch in range(batches):
        for p in range(parts):
            at = slice(p * part, (p + 1) * part)
            term_ref = term_refs[batch * parts + p]
            mixed = term_ref[0].astype(jnp.float32)
            for place in range(1, term_ref.shape[0]):
                mixed = mixed + term_ref[place].astype(jnp.float32)
            total = hidden_ref[batch, at].astype(jnp.float32) + mixed
            out_ref[batch, at] = total.astype(out_ref.dtype)


def finish(hidden_in, terms):
    return call(
        finish_kernel,
        [hidden_in, *terms],
        [VMEM] * (1 + len(terms)),
        [jax.ShapeDtypeStruct(hidden_in.shape, hidden_in.dtype)],
        name="finish",
    )[0]


def local(
    hidden_in,
    expert_ids,
    route_share,
    norm_gain,
    gate_weight,
    up_weight,
    down_weight,
    exponent_table,
):
    owners = lax.axis_size("ep")
    batches, dev_rows, fanout = expert_ids.shape
    model_width = hidden_in.shape[2]
    extra = -(-owners // LANES) * LANES
    parts = PARTS if dev_rows % (16 * PARTS) == 0 else 1
    part = dev_rows // parts
    scales = jnp.exp2(exponent_table[0].astype(jnp.float32))
    owner = lax.axis_index("ep").astype(jnp.int32).reshape(1)

    line = owners // 4
    lines = [[4 * place + at for place in range(line)] for at in range(4)]

    def over_line(rows):
        return lax.all_to_all(rows, "ep", 0, 0, axis_index_groups=lines, tiled=True)

    def to_mid(rows):
        return lax.ppermute(rows, "ep", [(i, i ^ 2) for i in range(owners)])

    def to_core(rows):
        return lax.ppermute(rows, "ep", [(i, i ^ 1) for i in range(owners)])

    operands = [
        hidden_in,
        expert_ids.transpose(0, 2, 1),
        route_share.transpose(0, 2, 1),
        norm_gain.reshape(1, model_width),
    ]
    payload = call(
        prepare_kernel,
        operands,
        [HBM] * 4,
        [jax.ShapeDtypeStruct((line, part, model_width + extra), jnp.bfloat16)] * (batches * parts),
        [pltpu.VMEM(a.shape, a.dtype) for a in operands] + [pltpu.SemaphoreType.DMA((4,))],
        name="prepare",
    )
    weights = load([gate_weight, up_weight, down_weight])

    count = len(payload)
    here, there, here_core = {}, {}, {}
    mine, other, back = {}, {}, {}
    sent = {}
    terms = {}

    def expert(s):
        order = (sent[s - 1],) if s > 0 else ()
        rows = after(there[s], *order)
        mine[s], out_other = ffn([here[s], rows, here_core[s], to_core(rows)], owner, scales, weights)
        other[s] = to_core(out_other)
        sent[s] = add(1, mine[s], other[s])
        back[s] = to_mid(sent[s])

    def give_back(s):
        last = min(s + 1, count - 1)
        total = add(0, mine[s], other[s], after(back[s], sent[last]))
        terms[s] = over_line(total)

    for t in range(count + 4):
        if t < count:
            order = (here[t - 1],) if t > 0 else (payload[0],)
            here[t] = over_line(after(payload[t], *order))
            if t == 0:
                here[t] = after(here[t], *weights)
            elif t >= 3:
                here[t] = after(here[t], sent[t - 3])
            there[t] = to_mid(here[t])
            here_core[t] = to_core(here[t])
        if 0 <= t - 1 < count:
            expert(t - 1)
        if 0 <= t - 3 < count:
            give_back(t - 3)
    return finish(hidden_in, [terms[s] for s in range(count)])


def solution(mesh):
    return jax.shard_map(
        local,
        mesh=mesh,
        in_specs=(
            P(None, ("grp", "ep"), None),
            P(None, ("grp", "ep"), None),
            P(None, ("grp", "ep"), None),
            P(),
            P("ep", None, None),
            P("ep", None, None),
            P("ep", None, None),
            P("ep", None, None),
        ),
        out_specs=P(None, ("grp", "ep"), None),
        check_vma=False,
    )
```

time: 109 us -> 170 us (1.56)
  local copies, waits for them, and re-layouts: 8.72 us -> 40 us
  Pallas kernels: 15.4 us -> 30.5 us
  starting transfers between devices: 31.3 us -> 46.3 us
  waiting for transfers between devices: 52 us -> 40.4 us
  blocking collectives: 0 us -> 10.6 us
    all_to_all x0 -> x7, starting transfers between devices: none -> 36.4 us  [over_line(): return lax.all_to_all(rows, 'ep', 0, 0, axis_index_groups=lines, tiled=True)]
    unnamed x19 -> x77, local copies, waits for them, and re-layouts: 8.72 us -> 40 us
    ppermute x12 -> x0, waiting for transfers between devices: 29.8 us -> none  [along_line(): lax.ppermute(rows, 'ep', [(i, (i + 4 * k) % owners) for i in range(owners)])]
    ppermute x12 -> x0, starting transfers between devices: 25.2 us -> none  [along_line(): lax.ppermute(rows, 'ep', [(i, (i + 4 * k) % owners) for i in range(owners)])]
    ppermute x4 -> x8, waiting for transfers between devices: 22.1 us -> 37.7 us  [to_mid(): return lax.ppermute(rows, 'ep', [(i, i ^ 2) for i in range(owners)])]
    pallas_call x12 -> x15, Pallas kernels: 15.4 us -> 30.5 us  [call(): pl.pallas_call(kernel, out_shape=shapes, in_specs=specs, out_specs=[VMEM]...]
    all_to_all x0 -> x1, blocking collectives: none -> 10.6 us  [over_line(): return lax.all_to_all(rows, 'ep', 0, 0, axis_index_groups=lines, tiled=True)]
    ppermute x4 -> x8, starting transfers between devices: 4.31 us -> 9.12 us  [to_mid(): return lax.ppermute(rows, 'ep', [(i, i ^ 2) for i in range(owners)])]
  transfers between devices with their start and end apart: 24 -> 27, of which waited for: 9 -> 12; matrix products, arithmetic and copies ran while one was open for 1% -> 0% of each run, Pallas kernels for 13% -> 16%
where the time goes in v4:
time: 170 us; the launch traced here: 168 us
  starting transfers between devices  46.3 us (27%)
  waiting for transfers between devices  40.4 us (24%)
  local copies, waits for them, and re-layouts  40 us (24%)
  Pallas kernels  30.5 us (18%)
  blocking collectives  10.6 us (6%)
    unnamed x77, local copies, waits for them, and re-layouts  40 us
    ppermute x8, waiting for transfers between devices, to_mid(): return lax.ppermute(rows, 'ep', [(i, i ^ 2) for i in range(owners)])  37.7 us
    all_to_all x7, starting transfers between devices, over_line(): return lax.all_to_all(rows, 'ep', 0, 0, axis_index_groups=lines, tiled=True)  36.4 us
    pallas_call x15, Pallas kernels, call(): pl.pallas_call(kernel, out_shape=shapes, in_specs=specs, out_specs=[VMEM]...  30.5 us
    all_to_all x1, blocking collectives, over_line(): return lax.all_to_all(rows, 'ep', 0, 0, axis_index_groups=lines, tiled=True)  10.6 us
    ppermute x8, starting transfers between devices, to_mid(): return lax.ppermute(rows, 'ep', [(i, i ^ 2) for i in range(owners)])  9.12 us
  transfers between devices with their start and end apart: 27, of which 12 were waited for; matrix products, arithmetic and copies ran while one was open for 0% of the time, Pallas kernels for 16%

profile of v4, /device:TPU:0, one launch (start us, length us, event | category | flops | bytes accessed | tf_op | source)
XLA Modules:
  0.0 167.9 jit_solution(9583826446501409651)
XLA Ops:
  5.7 6.3 %all-to-all-start = ((bf16[4,16,2176]{2,1,0:T(8,128)(2,1)}), bf16[4,16,2176]{2,1,0:T(8,128)(2,1)}, u32[]{:S(2)}, u32[]{:S(2)}) async-start(bf16[4,16,2176]{2,1,0:T(8,128)(2,1)} %get-tuple-element.35), calls=%async_computation | async-start | bytes 557056 | tf_op jit(solution)/shard_map/all_to_all | solution.py:202
  12.0 1.9 %copy-done.10 = bf16[1,2048,768]{2,1,0:T(8,128)(2,1)S(1)} copy-done((bf16[1,2048,768]{2,1,0:T(8,128)(2,1)S(1)}, bf16[1,2048,768]{2,1,0:T(8,128)(2,1)}, u32[]{:S(2)}) %copy-start.10) | copy-done | bytes 3145752
  13.9 1.9 %copy-done.11 = bf16[1,2048,768]{2,1,0:T(8,128)(2,1)S(1)} copy-done((bf16[1,2048,768]{2,1,0:T(8,128)(2,1)S(1)}, bf16[1,2048,768]{2,1,0:T(8,128)(2,1)}, u32[]{:S(2)}) %copy-start.11) | copy-done | bytes 3145752
  15.8 1.9 %copy-done.12 = bf16[1,768,2048]{2,1,0:T(8,128)(2,1)S(1)} copy-done((bf16[1,768,2048]{2,1,0:T(8,128)(2,1)S(1)}, bf16[1,768,2048]{2,1,0:T(8,128)(2,1)}, u32[]{:S(2)}) %copy-start.12) | copy-done | bytes 3145752
  23.2 6.9 %collective-permute-done.refs_1_ = bf16[4,16,2176]{2,1,0:T(8,128)(2,1)} collective-permute-done((bf16[4,16,2176]{2,1,0:T(8,128)(2,1)}, bf16[4,16,2176]{2,1,0:T(8,128)(2,1)}, u32[]{:S(2)}, u32[]{:S(2)}) %collective-permute-start) | collective-permute-done | bytes 278560 | tf_op jit(solution)/shard_map/ppermute | solution.py:205
  30.1 4.8 %all-to-all-start.1 = ((bf16[4,16,2176]{2,1,0:T(8,128)(2,1)}), bf16[4,16,2176]{2,1,0:T(8,128)(2,1)S(1)}, u32[]{:S(2)}, u32[]{:S(2)}) async-start(bf16[4,16,2176]{2,1,0:T(8,128)(2,1)} %copy-done.30), calls=%async_computation.1 | async-start | bytes 557056 | tf_op jit(solution)/shard_map/all_to_all | solution.py:202
  34.9 1.9 %copy-done.1 = bf16[1,2048,768]{2,1,0:T(8,128)(2,1)S(1)} copy-done((bf16[1,2048,768]{2,1,0:T(8,128)(2,1)S(1)}, bf16[1,2048,768]{2,1,0:T(8,128)(2,1)}, u32[]{:S(2)}) %copy-start.1) | copy-done | bytes 3145752
  36.8 1.9 %copy-done.6 = bf16[1,768,2048]{2,1,0:T(8,128)(2,1)S(1)} copy-done((bf16[1,768,2048]{2,1,0:T(8,128)(2,1)S(1)}, bf16[1,768,2048]{2,1,0:T(8,128)(2,1)}, u32[]{:S(2)}) %copy-start.6) | copy-done | bytes 3145752
  38.7 4.6 %ffn.4 = (bf16[2,4,16,2048]{3,2,1,0:T(8,128)(2,1)S(1)}, bf16[2,4,16,2048]{3,2,1,0:T(8,128)(2,1)}) custom-call(s32[1]{0:T(128)} %bitcast.owner_ref, f32[3,6]{1,0:T(4,128)S(1)} %bitcast.7, bf16[1,2048,768]{2,1,0:T(8,128)(2,1)S(1)} %get-tuple-element.32.gate_ref, bf16[1,2048,768]{2,1,0:T(8,128)(2,1)S(1)} %copy-done.1, bf16[1,768,2048]{2,1,0:T(8,128)(2,1)S(1)} %copy-done.6, ...), custom_call_target="tpu_custom_call" | custom-call | flops 2415919104 | bytes 11599948 | tf_op jit(solution)/shard_map/ffn/pallas_call | solution.py:20
  49.3 4.1 %collective-permute-done.5.refs_1_ = bf16[4,16,2176]{2,1,0:T(8,128)(2,1)} collective-permute-done((bf16[4,16,2176]{2,1,0:T(8,128)(2,1)S(1)}, bf16[4,16,2176]{2,1,0:T(8,128)(2,1)}, u32[]{:S(2)}, u32[]{:S(2)}) %collective-permute-start.5) | collective-permute-done | bytes 278560 | tf_op jit(solution)/shard_map/ppermute | solution.py:205
  53.4 5.1 %all-to-all-start.3 = ((bf16[4,16,2176]{2,1,0:T(8,128)(2,1)}), bf16[4,16,2176]{2,1,0:T(8,128)(2,1)}, u32[]{:S(2)}, u32[]{:S(2)}) async-start(bf16[4,16,2176]{2,1,0:T(8,128)(2,1)} %copy-done.29), calls=%async_computation.3 | async-start | bytes 557056 | tf_op jit(solution)/shard_map/all_to_all | solution.py:202
  58.5 1.9 %copy-done.2 = bf16[1,2048,768]{2,1,0:T(8,128)(2,1)S(1)} copy-done((bf16[1,2048,768]{2,1,0:T(8,128)(2,1)S(1)}, bf16[1,2048,768]{2,1,0:T(8,128)(2,1)}, u32[]{:S(2)}) %copy-start.2) | copy-done | bytes 3145752
  60.4 1.9 %copy-done.7 = bf16[1,768,2048]{2,1,0:T(8,128)(2,1)S(1)} copy-done((bf16[1,768,2048]{2,1,0:T(8,128)(2,1)S(1)}, bf16[1,768,2048]{2,1,0:T(8,128)(2,1)}, u32[]{:S(2)}) %copy-start.7) | copy-done | bytes 3145752
  62.2 4.6 %ffn.5 = (bf16[2,4,16,2048]{3,2,1,0:T(8,128)(2,1)S(1)}, bf16[2,4,16,2048]{3,2,1,0:T(8,128)(2,1)}) custom-call(s32[1]{0:T(128)} %bitcast.owner_ref, f32[3,6]{1,0:T(4,128)S(1)} %bitcast.8, bf16[1,2048,768]{2,1,0:T(8,128)(2,1)S(1)} %get-tuple-element.32.gate_ref, bf16[1,2048,768]{2,1,0:T(8,128)(2,1)S(1)} %copy-done.2, bf16[1,768,2048]{2,1,0:T(8,128)(2,1)S(1)} %copy-done.7, ...), custom_call_target="tpu_custom_call" | custom-call | flops 2415919104 | bytes 11599948 | tf_op jit(solution)/shard_map/ffn/pallas_call | solution.py:20
  72.8 4.2 %collective-permute-done.10.refs_1_ = bf16[4,16,2176]{2,1,0:T(8,128)(2,1)} collective-permute-done((bf16[4,16,2176]{2,1,0:T(8,128)(2,1)}, bf16[4,16,2176]{2,1,0:T(8,128)(2,1)}, u32[]{:S(2)}, u32[]{:S(2)}) %collective-permute-start.10) | collective-permute-done | bytes 278560 | tf_op jit(solution)/shard_map/ppermute | solution.py:205
  77.1 5.1 %all-to-all-start.5 = ((bf16[4,16,2176]{2,1,0:T(8,128)(2,1)}), bf16[4,16,2176]{2,1,0:T(8,128)(2,1)S(1)}, u32[]{:S(2)}, u32[]{:S(2)}) async-start(bf16[4,16,2176]{2,1,0:T(8,128)(2,1)} %copy-done.28), calls=%async_computation.5 | async-start | bytes 557056 | tf_op jit(solution)/shard_map/all_to_all | solution.py:202
  82.2 1.9 %copy-done.3 = bf16[1,2048,768]{2,1,0:T(8,128)(2,1)S(1)} copy-done((bf16[1,2048,768]{2,1,0:T(8,128)(2,1)S(1)}, bf16[1,2048,768]{2,1,0:T(8,128)(2,1)}, u32[]{:S(2)}) %copy-start.3) | copy-done | bytes 3145752
  84.0 1.9 %copy-done.8 = bf16[1,768,2048]{2,1,0:T(8,128)(2,1)S(1)} copy-done((bf16[1,768,2048]{2,1,0:T(8,128)(2,1)S(1)}, bf16[1,768,2048]{2,1,0:T(8,128)(2,1)}, u32[]{:S(2)}) %copy-start.8) | copy-done | bytes 3145752
  85.9 4.7 %ffn.6 = (bf16[2,4,16,2048]{3,2,1,0:T(8,128)(2,1)S(1)}, bf16[2,4,16,2048]{3,2,1,0:T(8,128)(2,1)}) custom-call(s32[1]{0:T(128)} %bitcast.owner_ref, f32[3,6]{1,0:T(4,128)S(1)} %bitcast.9, bf16[1,2048,768]{2,1,0:T(8,128)(2,1)S(1)} %get-tuple-element.32.gate_ref, bf16[1,2048,768]{2,1,0:T(8,128)(2,1)S(1)} %copy-done.3, bf16[1,768,2048]{2,1,0:T(8,128)(2,1)S(1)} %copy-done.8, ...), custom_call_target="tpu_custom_call" | custom-call | flops 2415919104 | bytes 11599948 | tf_op jit(solution)/shard_map/ffn/pallas_call | solution.py:20
  96.9 4.7 %collective-permute-done.15.refs_1_ = bf16[4,16,2176]{2,1,0:T(8,128)(2,1)} collective-permute-done((bf16[4,16,2176]{2,1,0:T(8,128)(2,1)S(1)}, bf16[4,16,2176]{2,1,0:T(8,128)(2,1)}, u32[]{:S(2)}, u32[]{:S(2)}) %collective-permute-start.15) | collective-permute-done | bytes 278560 | tf_op jit(solution)/shard_map/ppermute | solution.py:205
  101.7 4.4 %collective-permute-done.4.refs_0_ = bf16[4,16,2048]{2,1,0:T(8,128)(2,1)S(1)} collective-permute-done((bf16[4,16,2048]{2,1,0:T(8,128)(2,1)}, bf16[4,16,2048]{2,1,0:T(8,128)(2,1)S(1)}, u32[]{:S(2)}, u32[]{:S(2)}) %collective-permute-start.4) | collective-permute-done | bytes 262176 | tf_op jit(solution)/shard_map/ppermute | solution.py:205
  109.0 5.1 %all-to-all-start.2 = ((bf16[4,16,2048]{2,1,0:T(8,128)(2,1)}), bf16[4,16,2048]{2,1,0:T(8,128)(2,1)}, u32[]{:S(2)}, u32[]{:S(2)}) async-start(bf16[4,16,2048]{2,1,0:T(8,128)(2,1)} %copy-done.27), calls=%async_computation.2 | async-start | bytes 524288 | tf_op jit(solution)/shard_map/all_to_all | solution.py:202
  115.6 1.9 %copy-done.4 = bf16[1,2048,768]{2,1,0:T(8,128)(2,1)S(1)} copy-done((bf16[1,2048,768]{2,1,0:T(8,128)(2,1)S(1)}, bf16[1,2048,768]{2,1,0:T(8,128)(2,1)}, u32[]{:S(2)}) %copy-start.4) | copy-done | bytes 3145752
  117.5 1.9 %copy-done.9 = bf16[1,768,2048]{2,1,0:T(8,128)(2,1)S(1)} copy-done((bf16[1,768,2048]{2,1,0:T(8,128)(2,1)S(1)}, bf16[1,768,2048]{2,1,0:T(8,128)(2,1)}, u32[]{:S(2)}) %copy-start.9) | copy-done | bytes 3145752
  119.4 4.7 %ffn.7 = (bf16[2,4,16,2048]{3,2,1,0:T(8,128)(2,1)S(1)}, bf16[2,4,16,2048]{3,2,1,0:T(8,128)(2,1)}) custom-call(s32[1]{0:T(128)} %bitcast.owner_ref, f32[3,6]{1,0:T(4,128)S(1)} %bitcast.10, bf16[1,2048,768]{2,1,0:T(8,128)(2,1)S(1)} %get-tuple-element.32.gate_ref, bf16[1,2048,768]{2,1,0:T(8,128)(2,1)S(1)} %copy-done.4, bf16[1,768,2048]{2,1,0:T(8,128)(2,1)S(1)} %copy-done.9, ...), custom_call_target="tpu_custom_call" | custom-call | flops 2415919104 | bytes 11599948 | tf_op jit(solution)/shard_map/ffn/pallas_call | solution.py:20
  124.9 1.9 %add.12 = bf16[4,16,2048]{2,1,0:T(8,128)(2,1)} custom-call(bf16[2,4,16,2048]{3,2,1,0:T(8,128)(2,1)S(1)} %copy-done.18, bf16[2,4,16,2048]{3,2,1,0:T(8,128)(2,1)} %collective-permute-done.8.other_ref, bf16[4,16,2048]{2,1,0:T(8,128)(2,1)S(1)} %collective-permute-done.9.refs_0_), custom_call_target="tpu_custom_call" | custom-call | bytes 1572864 | tf_op jit(solution)/shard_map/add/pallas_call | solution.py:20
  126.8 5.2 %all-to-all-start.4 = ((bf16[4,16,2048]{2,1,0:T(8,128)(2,1)}), bf16[4,16,2048]{2,1,0:T(8,128)(2,1)S(1)}, u32[]{:S(2)}, u32[]{:S(2)}) async-start(bf16[4,16,2048]{2,1,0:T(8,128)(2,1)} %add.12), calls=%async_computation.4 | async-start | bytes 524288 | tf_op jit(solution)/shard_map/all_to_all | solution.py:202
  133.7 7.0 %collective-permute-done.14.refs_0_ = bf16[4,16,2048]{2,1,0:T(8,128)(2,1)S(1)} collective-permute-done((bf16[4,16,2048]{2,1,0:T(8,128)(2,1)}, bf16[4,16,2048]{2,1,0:T(8,128)(2,1)S(1)}, u32[]{:S(2)}, u32[]{:S(2)}) %collective-permute-start.14) | collective-permute-done | bytes 262176 | tf_op jit(solution)/shard_map/ppermute | solution.py:205
  140.6 1.8 %add.14 = bf16[4,16,2048]{2,1,0:T(8,128)(2,1)} custom-call(bf16[2,4,16,2048]{3,2,1,0:T(8,128)(2,1)S(1)} %copy-done.21, bf16[2,4,16,2048]{3,2,1,0:T(8,128)(2,1)} %collective-permute-done.13.other_ref, bf16[4,16,2048]{2,1,0:T(8,128)(2,1)S(1)} %collective-permute-done.14.refs_0_), custom_call_target="tpu_custom_call" | custom-call | bytes 1572864 | tf_op jit(solution)/shard_map/add/pallas_call | solution.py:20
  142.5 4.8 %all-to-all-start.6 = ((bf16[4,16,2048]{2,1,0:T(8,128)(2,1)}), bf16[4,16,2048]{2,1,0:T(8,128)(2,1)S(1)}, u32[]{:S(2)}, u32[]{:S(2)}) async-start(bf16[4,16,2048]{2,1,0:T(8,128)(2,1)} %add.14), calls=%async_computation.6 | async-start | bytes 524288 | tf_op jit(solution)/shard_map/all_to_all | solution.py:202
  147.8 6.4 %collective-permute-done.19.refs_0_ = bf16[4,16,2048]{2,1,0:T(8,128)(2,1)S(1)} collective-permute-done((bf16[4,16,2048]{2,1,0:T(8,128)(2,1)S(1)}, bf16[4,16,2048]{2,1,0:T(8,128)(2,1)S(1)}, u32[]{:S(2)}, u32[]{:S(2)}) %collective-permute-start.19) | collective-permute-done | bytes 262176 | tf_op jit(solution)/shard_map/ppermute | solution.py:205
  155.5 10.6 %all_to_all.40.refs_3_ = bf16[4,16,2048]{2,1,0:T(8,128)(2,1)S(1)} all-to-all(bf16[4,16,2048]{2,1,0:T(8,128)(2,1)S(1)} %add.15), channel_id=1, replica_groups={{0,4,8,12},{1,5,9,13},{2,6,10,14},{3,7,11,15},{16,20,24,28},{17,21,25,2..., dimensions={0} | all-to-all | bytes 524288 | tf_op jit(solution)/shard_map/all_to_all | solution.py:202
  (116 shorter events, 39.8 us)
Async XLA Ops:
  5.7 16.0 %all-to-all-start = ((bf16[4,16,2176]{2,1,0:T(8,128)(2,1)}), bf16[4,16,2176]{2,1,0:T(8,128)(2,1)}, u32[]{:S(2)}, u32[]{:S(2)}) async-start(bf16[4,16,2176]{2,1,0:T(8,128)(2,1)} %get-tuple-element.35), calls=%async_computation | async-start | bytes 557056 | tf_op jit(solution)/shard_map/all_to_all | solution.py:202
  17.6 12.4 %copy-start.37 = (s32[1,3,6]{2,0,1:T(1,128)S(1)}, s32[1,3,6]{2,0,1:T(1,128)}, u32[]{:S(2)}) copy-start(s32[1,3,6]{2,0,1:T(1,128)} %param.15) | copy-start | bytes 220
  21.6 8.4 %collective-permute-start = (bf16[4,16,2176]{2,1,0:T(8,128)(2,1)}, bf16[4,16,2176]{2,1,0:T(8,128)(2,1)}, u32[]{:S(2)}, u32[]{:S(2)}) collective-permute-start(bf16[4,16,2176]{2,1,0:T(8,128)(2,1)} %all-to-all-done.refs_0_), channel_id=1, source_target_pairs={{0,2},{1,3},{2,0},{3,1},{4,6},{5,7},{6,4},{7,5},{8,10},{9,11},{10,... | collective-permute-start | bytes 835592 | tf_op jit(solution)/shard_map/ppermute | solution.py:205
  23.1 11.8 %collective-permute-start.1 = (bf16[4,16,2176]{2,1,0:T(8,128)(2,1)}, bf16[4,16,2176]{2,1,0:T(8,128)(2,1)}, u32[]{:S(2)}, u32[]{:S(2)}) collective-permute-start(bf16[4,16,2176]{2,1,0:T(8,128)(2,1)} %all-to-all-done.refs_0_), channel_id=1, source_target_pairs={{0,1},{1,0},{2,3},{3,2},{4,5},{5,4},{6,7},{7,6},{8,9},{9,8},{10,11... | collective-permute-start | bytes 835592 | tf_op jit(solution)/shard_map/ppermute | solution.py:208
  30.1 4.9 %collective-permute-start.2 = (bf16[4,16,2176]{2,1,0:T(8,128)(2,1)}, bf16[4,16,2176]{2,1,0:T(8,128)(2,1)}, u32[]{:S(2)}, u32[]{:S(2)}) collective-permute-start(bf16[4,16,2176]{2,1,0:T(8,128)(2,1)} %collective-permute-done.refs_1_), channel_id=1, source_target_pairs={{0,1},{1,0},{2,3},{3,2},{4,5},{5,4},{6,7},{7,6},{8,9},{9,8},{10,11... | collective-permute-start | bytes 835592 | tf_op jit(solution)/shard_map/ppermute | solution.py:208
  30.1 14.7 %all-to-all-start.1 = ((bf16[4,16,2176]{2,1,0:T(8,128)(2,1)}), bf16[4,16,2176]{2,1,0:T(8,128)(2,1)S(1)}, u32[]{:S(2)}, u32[]{:S(2)}) async-start(bf16[4,16,2176]{2,1,0:T(8,128)(2,1)} %copy-done.30), calls=%async_computation.1 | async-start | bytes 557056 | tf_op jit(solution)/shard_map/all_to_all | solution.py:202
  44.2 2.3 %collective-permute-start.3 = (bf16[2,4,16,2048]{3,2,1,0:T(8,128)(2,1)}, bf16[2,4,16,2048]{3,2,1,0:T(8,128)(2,1)}, u32[]{:S(2)}, u32[]{:S(2)}) collective-permute-start(bf16[2,4,16,2048]{3,2,1,0:T(8,128)(2,1)} %get-tuple-element.38), channel_id=1, source_target_pairs={{0,1},{1,0},{2,3},{3,2},{4,5},{5,4},{6,7},{7,6},{8,9},{9,8},{10,11... | collective-permute-start | bytes 1572872 | tf_op jit(solution)/shard_map/ppermute | solution.py:208
  44.8 8.6 %collective-permute-start.5 = (bf16[4,16,2176]{2,1,0:T(8,128)(2,1)S(1)}, bf16[4,16,2176]{2,1,0:T(8,128)(2,1)}, u32[]{:S(2)}, u32[]{:S(2)}) collective-permute-start(bf16[4,16,2176]{2,1,0:T(8,128)(2,1)S(1)} %all-to-all-done.1.refs_0_), channel_id=1, source_target_pairs={{0,2},{1,3},{2,0},{3,1},{4,6},{5,7},{6,4},{7,5},{8,10},{9,11},{10,... | collective-permute-start | bytes 835592 | tf_op jit(solution)/shard_map/ppermute | solution.py:205
  46.3 12.1 %collective-permute-start.6 = (bf16[4,16,2176]{2,1,0:T(8,128)(2,1)S(1)}, bf16[4,16,2176]{2,1,0:T(8,128)(2,1)}, u32[]{:S(2)}, u32[]{:S(2)}) collective-permute-start(bf16[4,16,2176]{2,1,0:T(8,128)(2,1)S(1)} %all-to-all-done.1.refs_0_), channel_id=1, source_target_pairs={{0,1},{1,0},{2,3},{3,2},{4,5},{5,4},{6,7},{7,6},{8,9},{9,8},{10,11... | collective-permute-start | bytes 835592 | tf_op jit(solution)/shard_map/ppermute | solution.py:208
  53.4 5.1 %collective-permute-start.7 = (bf16[4,16,2176]{2,1,0:T(8,128)(2,1)}, bf16[4,16,2176]{2,1,0:T(8,128)(2,1)}, u32[]{:S(2)}, u32[]{:S(2)}) collective-permute-start(bf16[4,16,2176]{2,1,0:T(8,128)(2,1)} %collective-permute-done.5.refs_1_), channel_id=1, source_target_pairs={{0,1},{1,0},{2,3},{3,2},{4,5},{5,4},{6,7},{7,6},{8,9},{9,8},{10,11... | collective-permute-start | bytes 835592 | tf_op jit(solution)/shard_map/ppermute | solution.py:208
  53.4 15.1 %all-to-all-start.3 = ((bf16[4,16,2176]{2,1,0:T(8,128)(2,1)}), bf16[4,16,2176]{2,1,0:T(8,128)(2,1)}, u32[]{:S(2)}, u32[]{:S(2)}) async-start(bf16[4,16,2176]{2,1,0:T(8,128)(2,1)} %copy-done.29), calls=%async_computation.3 | async-start | bytes 557056 | tf_op jit(solution)/shard_map/all_to_all | solution.py:202
  67.7 2.3 %collective-permute-start.8 = (bf16[2,4,16,2048]{3,2,1,0:T(8,128)(2,1)}, bf16[2,4,16,2048]{3,2,1,0:T(8,128)(2,1)}, u32[]{:S(2)}, u32[]{:S(2)}) collective-permute-start(bf16[2,4,16,2048]{3,2,1,0:T(8,128)(2,1)} %get-tuple-element.43), channel_id=1, source_target_pairs={{0,1},{1,0},{2,3},{3,2},{4,5},{5,4},{6,7},{7,6},{8,9},{9,8},{10,11... | collective-permute-start | bytes 1572872 | tf_op jit(solution)/shard_map/ppermute | solution.py:208
  68.5 8.6 %collective-permute-start.10 = (bf16[4,16,2176]{2,1,0:T(8,128)(2,1)}, bf16[4,16,2176]{2,1,0:T(8,128)(2,1)}, u32[]{:S(2)}, u32[]{:S(2)}) collective-permute-start(bf16[4,16,2176]{2,1,0:T(8,128)(2,1)} %all-to-all-done.3.refs_0_), channel_id=1, source_target_pairs={{0,2},{1,3},{2,0},{3,1},{4,6},{5,7},{6,4},{7,5},{8,10},{9,11},{10,... | collective-permute-start | bytes 835592 | tf_op jit(solution)/shard_map/ppermute | solution.py:205
  70.0 12.2 %collective-permute-start.11 = (bf16[4,16,2176]{2,1,0:T(8,128)(2,1)}, bf16[4,16,2176]{2,1,0:T(8,128)(2,1)}, u32[]{:S(2)}, u32[]{:S(2)}) collective-permute-start(bf16[4,16,2176]{2,1,0:T(8,128)(2,1)} %all-to-all-done.3.refs_0_), channel_id=1, source_target_pairs={{0,1},{1,0},{2,3},{3,2},{4,5},{5,4},{6,7},{7,6},{8,9},{9,8},{10,11... | collective-permute-start | bytes 835592 | tf_op jit(solution)/shard_map/ppermute | solution.py:208
  77.1 5.1 %collective-permute-start.12 = (bf16[4,16,2176]{2,1,0:T(8,128)(2,1)}, bf16[4,16,2176]{2,1,0:T(8,128)(2,1)}, u32[]{:S(2)}, u32[]{:S(2)}) collective-permute-start(bf16[4,16,2176]{2,1,0:T(8,128)(2,1)} %collective-permute-done.10.refs_1_), channel_id=1, source_target_pairs={{0,1},{1,0},{2,3},{3,2},{4,5},{5,4},{6,7},{7,6},{8,9},{9,8},{10,11... | collective-permute-start | bytes 835592 | tf_op jit(solution)/shard_map/ppermute | solution.py:208
  77.1 15.0 %all-to-all-start.5 = ((bf16[4,16,2176]{2,1,0:T(8,128)(2,1)}), bf16[4,16,2176]{2,1,0:T(8,128)(2,1)S(1)}, u32[]{:S(2)}, u32[]{:S(2)}) async-start(bf16[4,16,2176]{2,1,0:T(8,128)(2,1)} %copy-done.28), calls=%async_computation.5 | async-start | bytes 557056 | tf_op jit(solution)/shard_map/all_to_all | solution.py:202
  91.4 2.7 %collective-permute-start.13 = (bf16[2,4,16,2048]{3,2,1,0:T(8,128)(2,1)}, bf16[2,4,16,2048]{3,2,1,0:T(8,128)(2,1)}, u32[]{:S(2)}, u32[]{:S(2)}) collective-permute-start(bf16[2,4,16,2048]{3,2,1,0:T(8,128)(2,1)} %get-tuple-element.49), channel_id=1, source_target_pairs={{0,1},{1,0},{2,3},{3,2},{4,5},{5,4},{6,7},{7,6},{8,9},{9,8},{10,11... | collective-permute-start | bytes 1572872 | tf_op jit(solution)/shard_map/ppermute | solution.py:208
  92.0 9.6 %collective-permute-start.15 = (bf16[4,16,2176]{2,1,0:T(8,128)(2,1)S(1)}, bf16[4,16,2176]{2,1,0:T(8,128)(2,1)}, u32[]{:S(2)}, u32[]{:S(2)}) collective-permute-start(bf16[4,16,2176]{2,1,0:T(8,128)(2,1)S(1)} %all-to-all-done.5.refs_0_), channel_id=1, source_target_pairs={{0,2},{1,3},{2,0},{3,1},{4,6},{5,7},{6,4},{7,5},{8,10},{9,11},{10,... | collective-permute-start | bytes 835592 | tf_op jit(solution)/shard_map/ppermute | solution.py:205
  93.6 12.5 %collective-permute-start.4 = (bf16[4,16,2048]{2,1,0:T(8,128)(2,1)}, bf16[4,16,2048]{2,1,0:T(8,128)(2,1)S(1)}, u32[]{:S(2)}, u32[]{:S(2)}) collective-permute-start(bf16[4,16,2048]{2,1,0:T(8,128)(2,1)} %copy-done.31), channel_id=1, source_target_pairs={{0,2},{1,3},{2,0},{3,1},{4,6},{5,7},{6,4},{7,5},{8,10},{9,11},{10,... | collective-permute-start | bytes 786440 | tf_op jit(solution)/shard_map/ppermute | solution.py:205
  94.1 21.5 %collective-permute-start.16 = (bf16[4,16,2176]{2,1,0:T(8,128)(2,1)S(1)}, bf16[4,16,2176]{2,1,0:T(8,128)(2,1)}, u32[]{:S(2)}, u32[]{:S(2)}) collective-permute-start(bf16[4,16,2176]{2,1,0:T(8,128)(2,1)S(1)} %all-to-all-done.5.refs_0_), channel_id=1, source_target_pairs={{0,1},{1,0},{2,3},{3,2},{4,5},{5,4},{6,7},{7,6},{8,9},{9,8},{10,11... | collective-permute-start | bytes 835592 | tf_op jit(solution)/shard_map/ppermute | solution.py:208
  101.7 13.9 %collective-permute-start.17 = (bf16[4,16,2176]{2,1,0:T(8,128)(2,1)}, bf16[4,16,2176]{2,1,0:T(8,128)(2,1)}, u32[]{:S(2)}, u32[]{:S(2)}) collective-permute-start(bf16[4,16,2176]{2,1,0:T(8,128)(2,1)} %collective-permute-done.15.refs_1_), channel_id=1, source_target_pairs={{0,1},{1,0},{2,3},{3,2},{4,5},{5,4},{6,7},{7,6},{8,9},{9,8},{10,11... | collective-permute-start | bytes 835592 | tf_op jit(solution)/shard_map/ppermute | solution.py:208
  109.0 17.9 %all-to-all-start.2 = ((bf16[4,16,2048]{2,1,0:T(8,128)(2,1)}), bf16[4,16,2048]{2,1,0:T(8,128)(2,1)}, u32[]{:S(2)}, u32[]{:S(2)}) async-start(bf16[4,16,2048]{2,1,0:T(8,128)(2,1)} %copy-done.27), calls=%async_computation.2 | async-start | bytes 524288 | tf_op jit(solution)/shard_map/all_to_all | solution.py:202
  114.1 10.8 %collective-permute-start.9 = (bf16[4,16,2048]{2,1,0:T(8,128)(2,1)}, bf16[4,16,2048]{2,1,0:T(8,128)(2,1)S(1)}, u32[]{:S(2)}, u32[]{:S(2)}) collective-permute-start(bf16[4,16,2048]{2,1,0:T(8,128)(2,1)} %copy-done.32), channel_id=1, source_target_pairs={{0,2},{1,3},{2,0},{3,1},{4,6},{5,7},{6,4},{7,5},{8,10},{9,11},{10,... | collective-permute-start | bytes 786440 | tf_op jit(solution)/shard_map/ppermute | solution.py:205
  119.4 5.5 %copy-start.18 = (bf16[2,4,16,2048]{3,2,1,0:T(8,128)(2,1)S(1)}, bf16[2,4,16,2048]{3,2,1,0:T(8,128)(2,1)}, u32[]{:S(2)}) copy-start(bf16[2,4,16,2048]{3,2,1,0:T(8,128)(2,1)} %copy-done.16) | copy-start | bytes 1572868
  124.9 15.8 %copy-start.21 = (bf16[2,4,16,2048]{3,2,1,0:T(8,128)(2,1)S(1)}, bf16[2,4,16,2048]{3,2,1,0:T(8,128)(2,1)}, u32[]{:S(2)}) copy-start(bf16[2,4,16,2048]{3,2,1,0:T(8,128)(2,1)} %copy-done.19) | copy-start | bytes 1572868
  124.9 29.3 %copy-start.24 = (bf16[2,4,16,2048]{3,2,1,0:T(8,128)(2,1)S(1)}, bf16[2,4,16,2048]{3,2,1,0:T(8,128)(2,1)}, u32[]{:S(2)}) copy-start(bf16[2,4,16,2048]{3,2,1,0:T(8,128)(2,1)} %copy-done.22) | copy-start | bytes 1572868
  124.9 7.7 %collective-permute-start.18 = (bf16[2,4,16,2048]{3,2,1,0:T(8,128)(2,1)}, bf16[2,4,16,2048]{3,2,1,0:T(8,128)(2,1)S(1)}, u32[]{:S(2)}, u32[]{:S(2)}) collective-permute-start(bf16[2,4,16,2048]{3,2,1,0:T(8,128)(2,1)} %get-tuple-element.56), channel_id=1, source_target_pairs={{0,1},{1,0},{2,3},{3,2},{4,5},{5,4},{6,7},{7,6},{8,9},{9,8},{10,11... | collective-permute-start | bytes 1572872 | tf_op jit(solution)/shard_map/ppermute | solution.py:208
  126.8 39.2 %copy-start.26 = (bf16[2,32,2048]{2,1,0:T(8,128)(2,1)S(1)}, bf16[2,32,2048]{2,1,0:T(8,128)(2,1)}, u32[]{:S(2)}) copy-start(bf16[2,32,2048]{2,1,0:T(8,128)(2,1)} %hidden_ref.1) | copy-start | bytes 786436
  126.8 15.6 %all-to-all-start.4 = ((bf16[4,16,2048]{2,1,0:T(8,128)(2,1)}), bf16[4,16,2048]{2,1,0:T(8,128)(2,1)S(1)}, u32[]{:S(2)}, u32[]{:S(2)}) async-start(bf16[4,16,2048]{2,1,0:T(8,128)(2,1)} %add.12), calls=%async_computation.4 | async-start | bytes 524288 | tf_op jit(solution)/shard_map/all_to_all | solution.py:202
  132.1 8.6 %collective-permute-start.14 = (bf16[4,16,2048]{2,1,0:T(8,128)(2,1)}, bf16[4,16,2048]{2,1,0:T(8,128)(2,1)S(1)}, u32[]{:S(2)}, u32[]{:S(2)}) collective-permute-start(bf16[4,16,2048]{2,1,0:T(8,128)(2,1)} %copy-done.33), channel_id=1, source_target_pairs={{0,2},{1,3},{2,0},{3,1},{4,6},{5,7},{6,4},{7,5},{8,10},{9,11},{10,... | collective-permute-start | bytes 786440 | tf_op jit(solution)/shard_map/ppermute | solution.py:205
  142.5 13.0 %all-to-all-start.6 = ((bf16[4,16,2048]{2,1,0:T(8,128)(2,1)}), bf16[4,16,2048]{2,1,0:T(8,128)(2,1)S(1)}, u32[]{:S(2)}, u32[]{:S(2)}) async-start(bf16[4,16,2048]{2,1,0:T(8,128)(2,1)} %add.14), calls=%async_computation.6 | async-start | bytes 524288 | tf_op jit(solution)/shard_map/all_to_all | solution.py:202
  147.3 6.9 %collective-permute-start.19 = (bf16[4,16,2048]{2,1,0:T(8,128)(2,1)S(1)}, bf16[4,16,2048]{2,1,0:T(8,128)(2,1)S(1)}, u32[]{:S(2)}, u32[]{:S(2)}) collective-permute-start(bf16[4,16,2048]{2,1,0:T(8,128)(2,1)S(1)} %add.13), channel_id=1, source_target_pairs={{0,2},{1,3},{2,0},{3,1},{4,6},{5,7},{6,4},{7,5},{8,10},{9,11},{10,... | collective-permute-start | bytes 786440 | tf_op jit(solution)/shard_map/ppermute | solution.py:205
  (33 other events, 40.7 us)

commit v5 on v4

--- a/solution.py
+++ b/solution.py
@@ -11,17 +11,25 @@
 VMEM = pl.BlockSpec(memory_space=pltpu.VMEM)
 SMEM = pl.BlockSpec(memory_space=pltpu.SMEM)
 HBM = pl.BlockSpec(memory_space=pltpu.HBM)
-PARTS = 2
-
-
-def call(kernel, operands, specs, shapes, scratch=(), flops=0, name=None, vmem=8):
+ANY_VMEM = pl.BlockSpec(memory_space=pltpu.VMEM)
+PARTS = 1
+
+
+def call(kernel, operands, specs, shapes, scratch=(), flops=0, name=None, vmem=8, out_spec=VMEM):
     moved = sum(a.size * a.dtype.itemsize for a in operands)
     moved += sum(s.size * s.dtype.itemsize for s in shapes)
+    if out_spec is VMEM:
+        shapes = [pltpu.VMEM(s.shape, s.dtype) for s in shapes]
+    pinned = {id(VMEM): pltpu.VMEM, id(HBM): pltpu.HBM}
+    operands = [
+        pltpu.with_memory_space_constraint(a, pinned[id(spec)]) if id(spec) in pinned else a
+        for a, spec in zip(operands, specs)
+    ]
     return pl.pallas_call(
         kernel,
         out_shape=shapes,
         in_specs=specs,
-        out_specs=[VMEM] * len(shapes),
+        out_specs=[out_spec] * len(shapes),
         scratch_shapes=list(scratch),
         cost_estimate=pl.CostEstimate(flops=flops, bytes_accessed=moved, transcendentals=0),
         compiler_params=pltpu.CompilerParams(vmem_limit_bytes=vmem << 20),
@@ -44,7 +52,7 @@
         copy.wait()
     batches, rows, width = hidden_ref.shape
     fanout = ids_ref.shape[1]
-    line, part, full = out_refs[0].shape
+    part, full = out_refs[0].shape
     extra = full - width
     parts = rows // part
     for batch in range(batches):
@@ -59,9 +67,8 @@
         dense = dense.T.astype(jnp.bfloat16)
         for p in range(parts):
             out_ref = out_refs[batch * parts + p]
-            for place in range(line):
-                out_ref[place, :, :width] = normed[p * part : (p + 1) * part]
-                out_ref[place, :, width:] = dense[p * part : (p + 1) * part]
+            out_ref[:, :width] = normed[p * part : (p + 1) * part]
+            out_ref[:, width:] = dense[p * part : (p + 1) * part]
 
 
 def load_kernel(*refs):
@@ -82,6 +89,16 @@
         [pltpu.SemaphoreType.DMA((len(weights),))],
         name="load",
     )
+
+
+def join_kernel(*refs):
+    for place, ref in enumerate(refs[:-1]):
+        refs[-1][place] = ref[...]
+
+
+def join(pieces):
+    shape = jax.ShapeDtypeStruct((len(pieces), *pieces[0].shape), pieces[0].dtype)
+    return call(join_kernel, pieces, [VMEM] * len(pieces), [shape], name="join")[0]
 
 
 def ffn_kernel(owner_ref, scale_ref, gate_ref, up_ref, down_ref, *refs):
@@ -131,48 +148,59 @@
 
 
 def add_kernel(slot, mine_ref, other_ref, *refs):
-    out_ref = refs[-1]
-    for place in range(out_ref.shape[0]):
+    line = mine_ref.shape[1]
+    if slot:
+        more, outs = (), [refs[0].at[place] for place in range(line)]
+    else:
+        more, outs = refs[:1], refs[1:]
+    for place, out_ref in enumerate(outs):
         total = mine_ref[slot, place].astype(jnp.float32) + other_ref[slot, place].astype(jnp.float32)
-        for ref in refs[:-1]:
+        for ref in more:
             total = total + ref[place].astype(jnp.float32)
-        out_ref[place] = total.astype(out_ref.dtype)
-
-
-def add(slot, mine, other, *more):
+        out_ref[...] = total.astype(out_ref.dtype)
+
+
+def add_there(mine, other):
     shape = jax.ShapeDtypeStruct(mine.shape[1:], mine.dtype)
+    return call(functools.partial(add_kernel, 1), [mine, other], [VMEM] * 2, [shape], name="add_there")[0]
+
+
+def add_here(mine, other, back):
+    shape = jax.ShapeDtypeStruct(mine.shape[2:], mine.dtype)
     return call(
-        functools.partial(add_kernel, slot),
-        [mine, other, *more],
-        [VMEM] * (2 + len(more)),
-        [shape],
-        name="add",
-    )[0]
-
-
-def finish_kernel(hidden_ref, *refs):
+        functools.partial(add_kernel, 0),
+        [mine, other, back],
+        [VMEM] * 3,
+        [shape] * mine.shape[1],
+        name="add_here",
+    )
+
+
+def finish_kernel(terms, hidden_ref, *refs):
     term_refs, out_ref = refs[:-1], refs[-1]
     batches, rows, _ = hidden_ref.shape
-    part = term_refs[0].shape[1]
+    part = term_refs[0].shape[0]
     parts = rows // part
     for batch in range(batches):
         for p in range(parts):
             at = slice(p * part, (p + 1) * part)
-            term_ref = term_refs[batch * parts + p]
-            mixed = term_ref[0].astype(jnp.float32)
-            for place in range(1, term_ref.shape[0]):
-                mixed = mixed + term_ref[place].astype(jnp.float32)
+            first = (batch * parts + p) * terms
+            mixed = term_refs[first][...].astype(jnp.float32)
+            for ref in term_refs[first + 1 : first + terms]:
+                mixed = mixed + ref[...].astype(jnp.float32)
             total = hidden_ref[batch, at].astype(jnp.float32) + mixed
             out_ref[batch, at] = total.astype(out_ref.dtype)
 
 
 def finish(hidden_in, terms):
+    flat = [t for mine in terms for t in mine]
     return call(
-        finish_kernel,
-        [hidden_in, *terms],
-        [VMEM] * (1 + len(terms)),
+        functools.partial(finish_kernel, len(terms[0])),
+        [hidden_in, *flat],
+        [ANY_VMEM] + [VMEM] * len(flat),
         [jax.ShapeDtypeStruct(hidden_in.shape, hidden_in.dtype)],
         name="finish",
+        out_spec=ANY_VMEM,
     )[0]
 
 
@@ -196,10 +224,12 @@
     owner = lax.axis_index("ep").astype(jnp.int32).reshape(1)
 
     line = owners // 4
-    lines = [[4 * place + at for place in range(line)] for at in range(4)]
+
+    def along_line(rows, k):
+        return lax.ppermute(rows, "ep", [(i, (i + 4 * k) % owners) for i in range(owners)])
 
     def over_line(rows):
-        return lax.all_to_all(rows, "ep", 0, 0, axis_index_groups=lines, tiled=True)
+        return join([rows] + [along_line(rows, k) for k in range(1, line)])
 
     def to_mid(rows):
         return lax.ppermute(rows, "ep", [(i, i ^ 2) for i in range(owners)])
@@ -217,7 +247,7 @@
         prepare_kernel,
         operands,
         [HBM] * 4,
-        [jax.ShapeDtypeStruct((line, part, model_width + extra), jnp.bfloat16)] * (batches * parts),
+        [jax.ShapeDtypeStruct((part, model_width + extra), jnp.bfloat16)] * (batches * parts),
         [pltpu.VMEM(a.shape, a.dtype) for a in operands] + [pltpu.SemaphoreType.DMA((4,))],
         name="prepare",
     )
@@ -234,13 +264,13 @@
         rows = after(there[s], *order)
         mine[s], out_other = ffn([here[s], rows, here_core[s], to_core(rows)], owner, scales, weights)
         other[s] = to_core(out_other)
-        sent[s] = add(1, mine[s], other[s])
+        sent[s] = add_there(mine[s], other[s])
         back[s] = to_mid(sent[s])
 
     def give_back(s):
         last = min(s + 1, count - 1)
-        total = add(0, mine[s], other[s], after(back[s], sent[last]))
-        terms[s] = over_line(total)
+        total = add_here(mine[s], other[s], after(back[s], sent[last]))
+        terms[s] = [total[0]] + [along_line(total[k], line - k) for k in range(1, line)]
 
     for t in range(count + 4):
         if t < count:

time: 170 us -> 124 us (0.73)
  waiting for transfers between devices: 40.4 us -> 70.8 us
  local copies, waits for them, and re-layouts: 40 us -> 10.7 us
  starting transfers between devices: 46.3 us -> 23.7 us
  Pallas kernels: 30.5 us -> 18 us
  blocking collectives: 10.6 us -> 0 us
    all_to_all x7 -> x0, starting transfers between devices: 36.4 us -> none  [over_line(): return lax.all_to_all(rows, 'ep', 0, 0, axis_index_groups=lines, tiled=True)]
    unnamed x77 -> x17, local copies, waits for them, and re-layouts: 40 us -> 10.7 us
    ppermute x0 -> x12, waiting for transfers between devices: none -> 23 us  [along_line(): lax.ppermute(rows, 'ep', [(i, (i + 4 * k) % owners) for i in range(owners)])]
    ppermute x0 -> x12, starting transfers between devices: none -> 17 us  [along_line(): lax.ppermute(rows, 'ep', [(i, (i + 4 * k) % owners) for i in range(owners)])]
    pallas_call x15 -> x11, Pallas kernels: 30.5 us -> 18 us  [call(): pl.pallas_call(kernel, out_shape=shapes, in_specs=specs, out_specs=[out_s...]
    all_to_all x1 -> x0, blocking collectives: 10.6 us -> none  [over_line(): return lax.all_to_all(rows, 'ep', 0, 0, axis_index_groups=lines, tiled=True)]
    ppermute x8 -> x4, waiting for transfers between devices: 37.7 us -> 42.9 us  [to_mid(): return lax.ppermute(rows, 'ep', [(i, i ^ 2) for i in range(owners)])]
    ppermute x12 -> x6, waiting for transfers between devices: 0.13 us -> 4.87 us  [to_core(): return lax.ppermute(rows, 'ep', [(i, i ^ 1) for i in range(owners)])]
  transfers between devices with their start and end apart: 27 -> 22, of which waited for: 12 -> 12; matrix products, arithmetic and copies ran while one was open for 0% -> 0% of each run, Pallas kernels for 16% -> 4%
where the time goes in v5:
time: 124 us; the launch traced here: 123 us
  waiting for transfers between devices  70.8 us (57%)
  starting transfers between devices  23.7 us (19%)
  Pallas kernels  18 us (15%)
  local copies, waits for them, and re-layouts  10.7 us (9%)
    ppermute x4, waiting for transfers between devices, to_mid(): return lax.ppermute(rows, 'ep', [(i, i ^ 2) for i in range(owners)])  42.9 us
    ppermute x12, waiting for transfers between devices, along_line(): lax.ppermute(rows, 'ep', [(i, (i + 4 * k) % owners) for i in range(owners)])  23 us
    pallas_call x11, Pallas kernels, call(): pl.pallas_call(kernel, out_shape=shapes, in_specs=specs, out_specs=[out_s...  18 us
    ppermute x12, starting transfers between devices, along_line(): lax.ppermute(rows, 'ep', [(i, (i + 4 * k) % owners) for i in range(owners)])  17 us
    unnamed x17, local copies, waits for them, and re-layouts  10.7 us
    ppermute x4, starting transfers between devices, to_mid(): return lax.ppermute(rows, 'ep', [(i, i ^ 2) for i in range(owners)])  6.29 us
    ppermute x6, waiting for transfers between devices, to_core(): return lax.ppermute(rows, 'ep', [(i, i ^ 1) for i in range(owners)])  4.87 us
  transfers between devices with their start and end apart: 22, of which 12 were waited for; matrix products, arithmetic and copies ran while one was open for 0% of the time, Pallas kernels for 4%

profile of v5, /device:TPU:0, one launch (start us, length us, event | category | flops | bytes accessed | tf_op | source)
XLA Modules:
  0.0 123.3 jit_solution(14685367871516385344)
XLA Ops:
  0.0 1.2 prepare.1
  1.2 5.1 %collective-permute-start.2 = (bf16[32,2176]{1,0:T(8,128)(2,1)S(1)}, bf16[32,2176]{1,0:T(8,128)(2,1)S(1)}, u32[]{:S(2)}, u32[]{:S(2)}) collective-permute-start(bf16[32,2176]{1,0:T(8,128)(2,1)S(1)} %get-tuple-element.30.refs_0_), channel_id=1, source_target_pairs={{0,12},{1,13},{2,14},{3,15},{4,0},{5,1},{6,2},{7,3},{8,4},{9,5},{1... | collective-permute-start | bytes 417800 | tf_op jit(solution)/shard_map/ppermute | solution.py:229
  7.4 3.8 %load.1 = (bf16[1,2048,768]{2,1,0:T(8,128)(2,1)S(1)}, bf16[1,2048,768]{2,1,0:T(8,128)(2,1)S(1)}, bf16[1,768,2048]{2,1,0:T(8,128)(2,1)S(1)}) custom-call(bf16[1,2048,768]{2,1,0:T(8,128)(2,1)} %refs_0_.1, bf16[1,2048,768]{2,1,0:T(8,128)(2,1)} %refs_1_.1, bf16[1,768,2048]{2,1,0:T(8,128)(2,1)} %refs_2_.1), custom_call_target="tpu_custom_call" | custom-call | bytes 18874368 | tf_op jit(solution)/shard_map/load/pallas_call | solution.py:28
  11.2 1.6 %copy-done.1 = bf16[1,2048,768]{2,1,0:T(8,128)(2,1)} copy-done((bf16[1,2048,768]{2,1,0:T(8,128)(2,1)}, bf16[1,2048,768]{2,1,0:T(8,128)(2,1)S(1)}, u32[]{:S(2)}) %copy-start.1) | copy-done | bytes 3145752
  12.8 1.7 %copy-done.3 = bf16[1,2048,768]{2,1,0:T(8,128)(2,1)} copy-done((bf16[1,2048,768]{2,1,0:T(8,128)(2,1)}, bf16[1,2048,768]{2,1,0:T(8,128)(2,1)S(1)}, u32[]{:S(2)}) %copy-start.3) | copy-done | bytes 3145752
  14.5 1.7 %copy-done.5 = bf16[1,768,2048]{2,1,0:T(8,128)(2,1)} copy-done((bf16[1,768,2048]{2,1,0:T(8,128)(2,1)}, bf16[1,768,2048]{2,1,0:T(8,128)(2,1)S(1)}, u32[]{:S(2)}) %copy-start.5) | copy-done | bytes 3145752
  16.2 2.0 %collective-permute-done.1.refs_2_ = bf16[32,2176]{1,0:T(8,128)(2,1)S(1)} collective-permute-done((bf16[32,2176]{1,0:T(8,128)(2,1)S(1)}, bf16[32,2176]{1,0:T(8,128)(2,1)S(1)}, u32[]{:S(2)}, u32[]{:S(2)}) %collective-permute-start.1) | collective-permute-done | bytes 139296 | tf_op jit(solution)/shard_map/ppermute | solution.py:229
  18.2 1.6 %collective-permute-start.3 = (bf16[4,32,2176]{2,1,0:T(8,128)(2,1)S(1)}, bf16[4,32,2176]{2,1,0:T(8,128)(2,1)S(1)}, u32[]{:S(2)}, u32[]{:S(2)}) collective-permute-start(bf16[4,32,2176]{2,1,0:T(8,128)(2,1)S(1)} %join.2.refs_0_), channel_id=1, source_target_pairs={{0,2},{1,3},{2,0},{3,1},{4,6},{5,7},{6,4},{7,5},{8,10},{9,11},{10,... | collective-permute-start | bytes 1671176 | tf_op jit(solution)/shard_map/ppermute | solution.py:235
  19.8 12.4 %collective-permute-done.3.refs_1_ = bf16[4,32,2176]{2,1,0:T(8,128)(2,1)S(1)} collective-permute-done((bf16[4,32,2176]{2,1,0:T(8,128)(2,1)S(1)}, bf16[4,32,2176]{2,1,0:T(8,128)(2,1)S(1)}, u32[]{:S(2)}, u32[]{:S(2)}) %collective-permute-start.3) | collective-permute-done | bytes 557088 | tf_op jit(solution)/shard_map/ppermute | solution.py:235
  32.2 1.9 %collective-permute-done.5.refs_3_ = bf16[4,32,2176]{2,1,0:T(8,128)(2,1)S(1)} collective-permute-done((bf16[4,32,2176]{2,1,0:T(8,128)(2,1)S(1)}, bf16[4,32,2176]{2,1,0:T(8,128)(2,1)S(1)}, u32[]{:S(2)}, u32[]{:S(2)}) %collective-permute-start.5) | collective-permute-done | bytes 557088 | tf_op jit(solution)/shard_map/ppermute | solution.py:238
  34.1 1.9 %copy-done.2 = bf16[1,2048,768]{2,1,0:T(8,128)(2,1)S(1)} copy-done((bf16[1,2048,768]{2,1,0:T(8,128)(2,1)S(1)}, bf16[1,2048,768]{2,1,0:T(8,128)(2,1)}, u32[]{:S(2)}) %copy-start.2) | copy-done | bytes 3145752
  36.0 1.9 %copy-done.4 = bf16[1,2048,768]{2,1,0:T(8,128)(2,1)S(1)} copy-done((bf16[1,2048,768]{2,1,0:T(8,128)(2,1)S(1)}, bf16[1,2048,768]{2,1,0:T(8,128)(2,1)}, u32[]{:S(2)}) %copy-start.4) | copy-done | bytes 3145752
  37.9 1.9 %copy-done.6 = bf16[1,768,2048]{2,1,0:T(8,128)(2,1)S(1)} copy-done((bf16[1,768,2048]{2,1,0:T(8,128)(2,1)S(1)}, bf16[1,768,2048]{2,1,0:T(8,128)(2,1)}, u32[]{:S(2)}) %copy-start.6) | copy-done | bytes 3145752
  39.8 5.7 %ffn.2 = (bf16[2,4,32,2048]{3,2,1,0:T(8,128)(2,1)S(1)}, bf16[2,4,32,2048]{3,2,1,0:T(8,128)(2,1)S(1)}) custom-call(s32[1]{0:T(128)} %bitcast.owner_ref, f32[3,6]{1,0:T(4,128)S(1)} %bitcast.7, bf16[1,2048,768]{2,1,0:T(8,128)(2,1)S(1)} %copy-done.2, bf16[1,2048,768]{2,1,0:T(8,128)(2,1)S(1)} %copy-done.4, bf16[1,768,2048]{2,1,0:T(8,128)(2,1)S(1)} %copy-done.6, ...), custom_call_target="tpu_custom_call" | custom-call | flops 4831838208 | bytes 13762636 | tf_op jit(solution)/shard_map/ffn/pallas_call | solution.py:28
  46.5 1.9 %collective-permute-start.9 = (bf16[32,2176]{1,0:T(8,128)(2,1)S(1)}, bf16[32,2176]{1,0:T(8,128)(2,1)S(1)}, u32[]{:S(2)}, u32[]{:S(2)}) collective-permute-start(bf16[32,2176]{1,0:T(8,128)(2,1)S(1)} %get-tuple-element.35.refs_0_), channel_id=1, source_target_pairs={{0,8},{1,9},{2,10},{3,11},{4,12},{5,13},{6,14},{7,15},{8,0},{9,1},... | collective-permute-start | bytes 417800 | tf_op jit(solution)/shard_map/ppermute | solution.py:229
  48.3 2.0 %collective-permute-start.8 = (bf16[32,2176]{1,0:T(8,128)(2,1)S(1)}, bf16[32,2176]{1,0:T(8,128)(2,1)S(1)}, u32[]{:S(2)}, u32[]{:S(2)}) collective-permute-start(bf16[32,2176]{1,0:T(8,128)(2,1)S(1)} %get-tuple-element.35.refs_0_), channel_id=1, source_target_pairs={{0,4},{1,5},{2,6},{3,7},{4,8},{5,9},{6,10},{7,11},{8,12},{9,13},{1... | collective-permute-start | bytes 417800 | tf_op jit(solution)/shard_map/ppermute | solution.py:229
  50.4 1.3 %collective-permute-done.10.refs_3_ = bf16[32,2176]{1,0:T(8,128)(2,1)S(1)} collective-permute-done((bf16[32,2176]{1,0:T(8,128)(2,1)S(1)}, bf16[32,2176]{1,0:T(8,128)(2,1)S(1)}, u32[]{:S(2)}, u32[]{:S(2)}) %collective-permute-start.10) | collective-permute-done | bytes 139296 | tf_op jit(solution)/shard_map/ppermute | solution.py:229
  51.7 9.8 %collective-permute-done.9.refs_2_ = bf16[32,2176]{1,0:T(8,128)(2,1)S(1)} collective-permute-done((bf16[32,2176]{1,0:T(8,128)(2,1)S(1)}, bf16[32,2176]{1,0:T(8,128)(2,1)S(1)}, u32[]{:S(2)}, u32[]{:S(2)}) %collective-permute-start.9) | collective-permute-done | bytes 139296 | tf_op jit(solution)/shard_map/ppermute | solution.py:229
  61.5 1.6 %collective-permute-start.11 = (bf16[4,32,2176]{2,1,0:T(8,128)(2,1)S(1)}, bf16[4,32,2176]{2,1,0:T(8,128)(2,1)S(1)}, u32[]{:S(2)}, u32[]{:S(2)}) collective-permute-start(bf16[4,32,2176]{2,1,0:T(8,128)(2,1)S(1)} %join.3.refs_0_), channel_id=1, source_target_pairs={{0,2},{1,3},{2,0},{3,1},{4,6},{5,7},{6,4},{7,5},{8,10},{9,11},{10,... | collective-permute-start | bytes 1671176 | tf_op jit(solution)/shard_map/ppermute | solution.py:235
  63.2 12.7 %collective-permute-done.11.refs_1_ = bf16[4,32,2176]{2,1,0:T(8,128)(2,1)S(1)} collective-permute-done((bf16[4,32,2176]{2,1,0:T(8,128)(2,1)S(1)}, bf16[4,32,2176]{2,1,0:T(8,128)(2,1)S(1)}, u32[]{:S(2)}, u32[]{:S(2)}) %collective-permute-start.11) | collective-permute-done | bytes 557088 | tf_op jit(solution)/shard_map/ppermute | solution.py:235
  75.9 2.0 %collective-permute-done.13.refs_3_ = bf16[4,32,2176]{2,1,0:T(8,128)(2,1)S(1)} collective-permute-done((bf16[4,32,2176]{2,1,0:T(8,128)(2,1)S(1)}, bf16[4,32,2176]{2,1,0:T(8,128)(2,1)S(1)}, u32[]{:S(2)}, u32[]{:S(2)}) %collective-permute-start.13) | collective-permute-done | bytes 557088 | tf_op jit(solution)/shard_map/ppermute | solution.py:238
  77.9 5.7 %ffn.3 = (bf16[2,4,32,2048]{3,2,1,0:T(8,128)(2,1)S(1)}, bf16[2,4,32,2048]{3,2,1,0:T(8,128)(2,1)S(1)}) custom-call(s32[1]{0:T(128)} %bitcast.owner_ref, f32[3,6]{1,0:T(4,128)S(1)} %bitcast.8, bf16[1,2048,768]{2,1,0:T(8,128)(2,1)S(1)} %copy-done.2, bf16[1,2048,768]{2,1,0:T(8,128)(2,1)S(1)} %copy-done.4, bf16[1,768,2048]{2,1,0:T(8,128)(2,1)S(1)} %copy-done.6, ...), custom_call_target="tpu_custom_call" | custom-call | flops 4831838208 | bytes 13762636 | tf_op jit(solution)/shard_map/ffn/pallas_call | solution.py:28
  83.8 1.5 %collective-permute-start.7 = (bf16[4,32,2048]{2,1,0:T(8,128)(2,1)S(1)}, bf16[4,32,2048]{2,1,0:T(8,128)(2,1)S(1)}, u32[]{:S(2)}, u32[]{:S(2)}) collective-permute-start(bf16[4,32,2048]{2,1,0:T(8,128)(2,1)S(1)} %add_there.2), channel_id=1, source_target_pairs={{0,2},{1,3},{2,0},{3,1},{4,6},{5,7},{6,4},{7,5},{8,10},{9,11},{10,... | collective-permute-start | bytes 1572872 | tf_op jit(solution)/shard_map/ppermute | solution.py:235
  86.5 1.6 %collective-permute-start.18 = (bf16[4,32,2048]{2,1,0:T(8,128)(2,1)S(1)}, bf16[4,32,2048]{2,1,0:T(8,128)(2,1)S(1)}, u32[]{:S(2)}, u32[]{:S(2)}) collective-permute-start(bf16[4,32,2048]{2,1,0:T(8,128)(2,1)S(1)} %add_there.3), channel_id=1, source_target_pairs={{0,2},{1,3},{2,0},{3,1},{4,6},{5,7},{6,4},{7,5},{8,10},{9,11},{10,... | collective-permute-start | bytes 1572872 | tf_op jit(solution)/shard_map/ppermute | solution.py:235
  88.1 10.5 %collective-permute-done.7.refs_0_ = bf16[4,32,2048]{2,1,0:T(8,128)(2,1)S(1)} collective-permute-done((bf16[4,32,2048]{2,1,0:T(8,128)(2,1)S(1)}, bf16[4,32,2048]{2,1,0:T(8,128)(2,1)S(1)}, u32[]{:S(2)}, u32[]{:S(2)}) %collective-permute-start.7) | collective-permute-done | bytes 524320 | tf_op jit(solution)/shard_map/ppermute | solution.py:235
  98.8 1.1 collective-permute-start.16
  99.9 1.9 %collective-permute-start.17 = (bf16[32,2048]{1,0:T(8,128)(2,1)S(1)}, bf16[32,2048]{1,0:T(8,128)(2,1)S(1)}, u32[]{:S(2)}, u32[]{:S(2)}) collective-permute-start(bf16[32,2048]{1,0:T(8,128)(2,1)S(1)} %get-tuple-element.43), channel_id=1, source_target_pairs={{0,4},{1,5},{2,6},{3,7},{4,8},{5,9},{6,10},{7,11},{8,12},{9,13},{1... | collective-permute-start | bytes 393224 | tf_op jit(solution)/shard_map/ppermute | solution.py:229
  101.9 7.4 %collective-permute-done.18.refs_0_ = bf16[4,32,2048]{2,1,0:T(8,128)(2,1)S(1)} collective-permute-done((bf16[4,32,2048]{2,1,0:T(8,128)(2,1)S(1)}, bf16[4,32,2048]{2,1,0:T(8,128)(2,1)S(1)}, u32[]{:S(2)}, u32[]{:S(2)}) %collective-permute-start.18) | collective-permute-done | bytes 524320 | tf_op jit(solution)/shard_map/ppermute | solution.py:235
  109.5 1.1 collective-permute-start.20
  110.6 1.9 %collective-permute-start.21 = (bf16[32,2048]{1,0:T(8,128)(2,1)S(1)}, bf16[32,2048]{1,0:T(8,128)(2,1)S(1)}, u32[]{:S(2)}, u32[]{:S(2)}) collective-permute-start(bf16[32,2048]{1,0:T(8,128)(2,1)S(1)} %get-tuple-element.48), channel_id=1, source_target_pairs={{0,4},{1,5},{2,6},{3,7},{4,8},{5,9},{6,10},{7,11},{8,12},{9,13},{1... | collective-permute-start | bytes 393224 | tf_op jit(solution)/shard_map/ppermute | solution.py:229
  112.6 2.5 %collective-permute-done.19.refs_5_ = bf16[32,2048]{1,0:T(8,128)(2,1)S(1)} collective-permute-done((bf16[32,2048]{1,0:T(8,128)(2,1)S(1)}, bf16[32,2048]{1,0:T(8,128)(2,1)S(1)}, u32[]{:S(2)}, u32[]{:S(2)}) %collective-permute-start.19) | collective-permute-done | bytes 131104 | tf_op jit(solution)/shard_map/ppermute | solution.py:229
  115.1 7.4 %collective-permute-done.20.refs_6_ = bf16[32,2048]{1,0:T(8,128)(2,1)S(1)} collective-permute-done((bf16[32,2048]{1,0:T(8,128)(2,1)S(1)}, bf16[32,2048]{1,0:T(8,128)(2,1)S(1)}, u32[]{:S(2)}, u32[]{:S(2)}) %collective-permute-start.20) | collective-permute-done | bytes 131104 | tf_op jit(solution)/shard_map/ppermute | solution.py:229
  (41 shorter events, 4.9 us)
Async XLA Ops:
  1.2 30.9 %copy-start.7 = (s32[1,3,6]{2,0,1:T(1,128)S(1)}, s32[1,3,6]{2,0,1:T(1,128)}, u32[]{:S(2)}) copy-start(s32[1,3,6]{2,0,1:T(1,128)} %param.15) | copy-start | bytes 220
  1.2 14.9 %collective-permute-start.2 = (bf16[32,2176]{1,0:T(8,128)(2,1)S(1)}, bf16[32,2176]{1,0:T(8,128)(2,1)S(1)}, u32[]{:S(2)}, u32[]{:S(2)}) collective-permute-start(bf16[32,2176]{1,0:T(8,128)(2,1)S(1)} %get-tuple-element.30.refs_0_), channel_id=1, source_target_pairs={{0,12},{1,13},{2,14},{3,15},{4,0},{5,1},{6,2},{7,3},{8,4},{9,5},{1... | collective-permute-start | bytes 417800 | tf_op jit(solution)/shard_map/ppermute | solution.py:229
  6.3 11.8 %collective-permute-start.1 = (bf16[32,2176]{1,0:T(8,128)(2,1)S(1)}, bf16[32,2176]{1,0:T(8,128)(2,1)S(1)}, u32[]{:S(2)}, u32[]{:S(2)}) collective-permute-start(bf16[32,2176]{1,0:T(8,128)(2,1)S(1)} %get-tuple-element.30.refs_0_), channel_id=1, source_target_pairs={{0,8},{1,9},{2,10},{3,11},{4,12},{5,13},{6,14},{7,15},{8,0},{9,1},... | collective-permute-start | bytes 417800 | tf_op jit(solution)/shard_map/ppermute | solution.py:229
  6.3 11.8 %collective-permute-start = (bf16[32,2176]{1,0:T(8,128)(2,1)S(1)}, bf16[32,2176]{1,0:T(8,128)(2,1)S(1)}, u32[]{:S(2)}, u32[]{:S(2)}) collective-permute-start(bf16[32,2176]{1,0:T(8,128)(2,1)S(1)} %get-tuple-element.30.refs_0_), channel_id=1, source_target_pairs={{0,4},{1,5},{2,6},{3,7},{4,8},{5,9},{6,10},{7,11},{8,12},{9,13},{1... | collective-permute-start | bytes 417800 | tf_op jit(solution)/shard_map/ppermute | solution.py:229
  11.1 1.6 %copy-start.1 = (bf16[1,2048,768]{2,1,0:T(8,128)(2,1)}, bf16[1,2048,768]{2,1,0:T(8,128)(2,1)S(1)}, u32[]{:S(2)}) copy-start(bf16[1,2048,768]{2,1,0:T(8,128)(2,1)S(1)} %get-tuple-element.27.gate_ref) | copy-start | bytes 9437188
  12.8 1.7 %copy-start.3 = (bf16[1,2048,768]{2,1,0:T(8,128)(2,1)}, bf16[1,2048,768]{2,1,0:T(8,128)(2,1)S(1)}, u32[]{:S(2)}) copy-start(bf16[1,2048,768]{2,1,0:T(8,128)(2,1)S(1)} %get-tuple-element.28.up_ref) | copy-start | bytes 9437188
  14.5 1.7 %copy-start.5 = (bf16[1,768,2048]{2,1,0:T(8,128)(2,1)}, bf16[1,768,2048]{2,1,0:T(8,128)(2,1)S(1)}, u32[]{:S(2)}) copy-start(bf16[1,768,2048]{2,1,0:T(8,128)(2,1)S(1)} %get-tuple-element.29.down_ref) | copy-start | bytes 9437188
  18.2 13.9 %collective-permute-start.3 = (bf16[4,32,2176]{2,1,0:T(8,128)(2,1)S(1)}, bf16[4,32,2176]{2,1,0:T(8,128)(2,1)S(1)}, u32[]{:S(2)}, u32[]{:S(2)}) collective-permute-start(bf16[4,32,2176]{2,1,0:T(8,128)(2,1)S(1)} %join.2.refs_0_), channel_id=1, source_target_pairs={{0,2},{1,3},{2,0},{3,1},{4,6},{5,7},{6,4},{7,5},{8,10},{9,11},{10,... | collective-permute-start | bytes 1671176 | tf_op jit(solution)/shard_map/ppermute | solution.py:235
  19.8 12.4 %collective-permute-start.4 = (bf16[4,32,2176]{2,1,0:T(8,128)(2,1)S(1)}, bf16[4,32,2176]{2,1,0:T(8,128)(2,1)S(1)}, u32[]{:S(2)}, u32[]{:S(2)}) collective-permute-start(bf16[4,32,2176]{2,1,0:T(8,128)(2,1)S(1)} %join.2.refs_0_), channel_id=1, source_target_pairs={{0,1},{1,0},{2,3},{3,2},{4,5},{5,4},{6,7},{7,6},{8,9},{9,8},{10,11... | collective-permute-start | bytes 1671176 | tf_op jit(solution)/shard_map/ppermute | solution.py:238
  32.2 2.0 %collective-permute-start.5 = (bf16[4,32,2176]{2,1,0:T(8,128)(2,1)S(1)}, bf16[4,32,2176]{2,1,0:T(8,128)(2,1)S(1)}, u32[]{:S(2)}, u32[]{:S(2)}) collective-permute-start(bf16[4,32,2176]{2,1,0:T(8,128)(2,1)S(1)} %collective-permute-done.3.refs_1_), channel_id=1, source_target_pairs={{0,1},{1,0},{2,3},{3,2},{4,5},{5,4},{6,7},{7,6},{8,9},{9,8},{10,11... | collective-permute-start | bytes 1671176 | tf_op jit(solution)/shard_map/ppermute | solution.py:238
  34.1 1.9 %copy-start.2 = (bf16[1,2048,768]{2,1,0:T(8,128)(2,1)S(1)}, bf16[1,2048,768]{2,1,0:T(8,128)(2,1)}, u32[]{:S(2)}) copy-start(bf16[1,2048,768]{2,1,0:T(8,128)(2,1)} %copy-done.1) | copy-start | bytes 9437188
  36.0 1.9 %copy-start.4 = (bf16[1,2048,768]{2,1,0:T(8,128)(2,1)S(1)}, bf16[1,2048,768]{2,1,0:T(8,128)(2,1)}, u32[]{:S(2)}) copy-start(bf16[1,2048,768]{2,1,0:T(8,128)(2,1)} %copy-done.3) | copy-start | bytes 9437188
  37.9 1.9 %copy-start.6 = (bf16[1,768,2048]{2,1,0:T(8,128)(2,1)S(1)}, bf16[1,768,2048]{2,1,0:T(8,128)(2,1)}, u32[]{:S(2)}) copy-start(bf16[1,768,2048]{2,1,0:T(8,128)(2,1)} %copy-done.5) | copy-start | bytes 9437188
  45.5 17.6 %collective-permute-start.6 = (bf16[2,4,32,2048]{3,2,1,0:T(8,128)(2,1)S(1)}, bf16[2,4,32,2048]{3,2,1,0:T(8,128)(2,1)S(1)}, u32[]{:S(2)}, u32[]{:S(2)}) collective-permute-start(bf16[2,4,32,2048]{3,2,1,0:T(8,128)(2,1)S(1)} %get-tuple-element.33), channel_id=1, source_target_pairs={{0,1},{1,0},{2,3},{3,2},{4,5},{5,4},{6,7},{7,6},{8,9},{9,8},{10,11... | collective-permute-start | bytes 3145736 | tf_op jit(solution)/shard_map/ppermute | solution.py:238
  45.7 6.0 %collective-permute-start.10 = (bf16[32,2176]{1,0:T(8,128)(2,1)S(1)}, bf16[32,2176]{1,0:T(8,128)(2,1)S(1)}, u32[]{:S(2)}, u32[]{:S(2)}) collective-permute-start(bf16[32,2176]{1,0:T(8,128)(2,1)S(1)} %get-tuple-element.35.refs_0_), channel_id=1, source_target_pairs={{0,12},{1,13},{2,14},{3,15},{4,0},{5,1},{6,2},{7,3},{8,4},{9,5},{1... | collective-permute-start | bytes 417800 | tf_op jit(solution)/shard_map/ppermute | solution.py:229
  46.5 15.0 %collective-permute-start.9 = (bf16[32,2176]{1,0:T(8,128)(2,1)S(1)}, bf16[32,2176]{1,0:T(8,128)(2,1)S(1)}, u32[]{:S(2)}, u32[]{:S(2)}) collective-permute-start(bf16[32,2176]{1,0:T(8,128)(2,1)S(1)} %get-tuple-element.35.refs_0_), channel_id=1, source_target_pairs={{0,8},{1,9},{2,10},{3,11},{4,12},{5,13},{6,14},{7,15},{8,0},{9,1},... | collective-permute-start | bytes 417800 | tf_op jit(solution)/shard_map/ppermute | solution.py:229
  48.3 13.1 %collective-permute-start.8 = (bf16[32,2176]{1,0:T(8,128)(2,1)S(1)}, bf16[32,2176]{1,0:T(8,128)(2,1)S(1)}, u32[]{:S(2)}, u32[]{:S(2)}) collective-permute-start(bf16[32,2176]{1,0:T(8,128)(2,1)S(1)} %get-tuple-element.35.refs_0_), channel_id=1, source_target_pairs={{0,4},{1,5},{2,6},{3,7},{4,8},{5,9},{6,10},{7,11},{8,12},{9,13},{1... | collective-permute-start | bytes 417800 | tf_op jit(solution)/shard_map/ppermute | solution.py:229
  61.5 14.4 %collective-permute-start.11 = (bf16[4,32,2176]{2,1,0:T(8,128)(2,1)S(1)}, bf16[4,32,2176]{2,1,0:T(8,128)(2,1)S(1)}, u32[]{:S(2)}, u32[]{:S(2)}) collective-permute-start(bf16[4,32,2176]{2,1,0:T(8,128)(2,1)S(1)} %join.3.refs_0_), channel_id=1, source_target_pairs={{0,2},{1,3},{2,0},{3,1},{4,6},{5,7},{6,4},{7,5},{8,10},{9,11},{10,... | collective-permute-start | bytes 1671176 | tf_op jit(solution)/shard_map/ppermute | solution.py:235
  63.1 12.8 %collective-permute-start.12 = (bf16[4,32,2176]{2,1,0:T(8,128)(2,1)S(1)}, bf16[4,32,2176]{2,1,0:T(8,128)(2,1)S(1)}, u32[]{:S(2)}, u32[]{:S(2)}) collective-permute-start(bf16[4,32,2176]{2,1,0:T(8,128)(2,1)S(1)} %join.3.refs_0_), channel_id=1, source_target_pairs={{0,1},{1,0},{2,3},{3,2},{4,5},{5,4},{6,7},{7,6},{8,9},{9,8},{10,11... | collective-permute-start | bytes 1671176 | tf_op jit(solution)/shard_map/ppermute | solution.py:238
  75.9 2.0 %collective-permute-start.13 = (bf16[4,32,2176]{2,1,0:T(8,128)(2,1)S(1)}, bf16[4,32,2176]{2,1,0:T(8,128)(2,1)S(1)}, u32[]{:S(2)}, u32[]{:S(2)}) collective-permute-start(bf16[4,32,2176]{2,1,0:T(8,128)(2,1)S(1)} %collective-permute-done.11.refs_1_), channel_id=1, source_target_pairs={{0,1},{1,0},{2,3},{3,2},{4,5},{5,4},{6,7},{7,6},{8,9},{9,8},{10,11... | collective-permute-start | bytes 1671176 | tf_op jit(solution)/shard_map/ppermute | solution.py:238
  83.6 2.7 %collective-permute-start.14 = (bf16[2,4,32,2048]{3,2,1,0:T(8,128)(2,1)S(1)}, bf16[2,4,32,2048]{3,2,1,0:T(8,128)(2,1)S(1)}, u32[]{:S(2)}, u32[]{:S(2)}) collective-permute-start(bf16[2,4,32,2048]{3,2,1,0:T(8,128)(2,1)S(1)} %get-tuple-element.38), channel_id=1, source_target_pairs={{0,1},{1,0},{2,3},{3,2},{4,5},{5,4},{6,7},{7,6},{8,9},{9,8},{10,11... | collective-permute-start | bytes 3145736 | tf_op jit(solution)/shard_map/ppermute | solution.py:238
  83.8 14.8 %collective-permute-start.7 = (bf16[4,32,2048]{2,1,0:T(8,128)(2,1)S(1)}, bf16[4,32,2048]{2,1,0:T(8,128)(2,1)S(1)}, u32[]{:S(2)}, u32[]{:S(2)}) collective-permute-start(bf16[4,32,2048]{2,1,0:T(8,128)(2,1)S(1)} %add_there.2), channel_id=1, source_target_pairs={{0,2},{1,3},{2,0},{3,1},{4,6},{5,7},{6,4},{7,5},{8,10},{9,11},{10,... | collective-permute-start | bytes 1572872 | tf_op jit(solution)/shard_map/ppermute | solution.py:235
  86.5 36.0 %copy-start = (bf16[2,32,2048]{2,1,0:T(8,128)(2,1)S(1)}, bf16[2,32,2048]{2,1,0:T(8,128)(2,1)}, u32[]{:S(2)}) copy-start(bf16[2,32,2048]{2,1,0:T(8,128)(2,1)} %hidden_ref.1) | copy-start | bytes 786436
  86.5 22.8 %collective-permute-start.18 = (bf16[4,32,2048]{2,1,0:T(8,128)(2,1)S(1)}, bf16[4,32,2048]{2,1,0:T(8,128)(2,1)S(1)}, u32[]{:S(2)}, u32[]{:S(2)}) collective-permute-start(bf16[4,32,2048]{2,1,0:T(8,128)(2,1)S(1)} %add_there.3), channel_id=1, source_target_pairs={{0,2},{1,3},{2,0},{3,1},{4,6},{5,7},{6,4},{7,5},{8,10},{9,11},{10,... | collective-permute-start | bytes 1572872 | tf_op jit(solution)/shard_map/ppermute | solution.py:235
  98.8 11.8 %collective-permute-start.15 = (bf16[32,2048]{1,0:T(8,128)(2,1)S(1)}, bf16[32,2048]{1,0:T(8,128)(2,1)S(1)}, u32[]{:S(2)}, u32[]{:S(2)}) collective-permute-start(bf16[32,2048]{1,0:T(8,128)(2,1)S(1)} %get-tuple-element.41), channel_id=1, source_target_pairs={{0,12},{1,13},{2,14},{3,15},{4,0},{5,1},{6,2},{7,3},{8,4},{9,5},{1... | collective-permute-start | bytes 393224 | tf_op jit(solution)/shard_map/ppermute | solution.py:229
  98.8 13.7 %collective-permute-start.16 = (bf16[32,2048]{1,0:T(8,128)(2,1)S(1)}, bf16[32,2048]{1,0:T(8,128)(2,1)S(1)}, u32[]{:S(2)}, u32[]{:S(2)}) collective-permute-start(bf16[32,2048]{1,0:T(8,128)(2,1)S(1)} %get-tuple-element.42), channel_id=1, source_target_pairs={{0,8},{1,9},{2,10},{3,11},{4,12},{5,13},{6,14},{7,15},{8,0},{9,1},... | collective-permute-start | bytes 393224 | tf_op jit(solution)/shard_map/ppermute | solution.py:229
  99.9 12.6 %collective-permute-start.17 = (bf16[32,2048]{1,0:T(8,128)(2,1)S(1)}, bf16[32,2048]{1,0:T(8,128)(2,1)S(1)}, u32[]{:S(2)}, u32[]{:S(2)}) collective-permute-start(bf16[32,2048]{1,0:T(8,128)(2,1)S(1)} %get-tuple-element.43), channel_id=1, source_target_pairs={{0,4},{1,5},{2,6},{3,7},{4,8},{5,9},{6,10},{7,11},{8,12},{9,13},{1... | collective-permute-start | bytes 393224 | tf_op jit(solution)/shard_map/ppermute | solution.py:229
  109.4 5.6 %collective-permute-start.19 = (bf16[32,2048]{1,0:T(8,128)(2,1)S(1)}, bf16[32,2048]{1,0:T(8,128)(2,1)S(1)}, u32[]{:S(2)}, u32[]{:S(2)}) collective-permute-start(bf16[32,2048]{1,0:T(8,128)(2,1)S(1)} %get-tuple-element.46), channel_id=1, source_target_pairs={{0,12},{1,13},{2,14},{3,15},{4,0},{5,1},{6,2},{7,3},{8,4},{9,5},{1... | collective-permute-start | bytes 393224 | tf_op jit(solution)/shard_map/ppermute | solution.py:229
  109.5 12.9 %collective-permute-start.20 = (bf16[32,2048]{1,0:T(8,128)(2,1)S(1)}, bf16[32,2048]{1,0:T(8,128)(2,1)S(1)}, u32[]{:S(2)}, u32[]{:S(2)}) collective-permute-start(bf16[32,2048]{1,0:T(8,128)(2,1)S(1)} %get-tuple-element.47), channel_id=1, source_target_pairs={{0,8},{1,9},{2,10},{3,11},{4,12},{5,13},{6,14},{7,15},{8,0},{9,1},... | collective-permute-start | bytes 393224 | tf_op jit(solution)/shard_map/ppermute | solution.py:229
  110.6 11.8 %collective-permute-start.21 = (bf16[32,2048]{1,0:T(8,128)(2,1)S(1)}, bf16[32,2048]{1,0:T(8,128)(2,1)S(1)}, u32[]{:S(2)}, u32[]{:S(2)}) collective-permute-start(bf16[32,2048]{1,0:T(8,128)(2,1)S(1)} %get-tuple-element.48), channel_id=1, source_target_pairs={{0,4},{1,5},{2,6},{3,7},{4,8},{5,9},{6,10},{7,11},{8,12},{9,13},{1... | collective-permute-start | bytes 393224 | tf_op jit(solution)/shard_map/ppermute | solution.py:229

commit v6 on v1

v6 whole, which is shorter than its diff:
```python
import functools

import jax
import jax.numpy as jnp
from jax import lax
from jax.experimental import pallas as pl
from jax.experimental.pallas import tpu as pltpu
from jax.sharding import PartitionSpec as P

LANES = 128
VMEM = pl.BlockSpec(memory_space=pltpu.VMEM)
HBM = pl.BlockSpec(memory_space=pltpu.HBM)
SMEM = pl.BlockSpec(memory_space=pltpu.SMEM)
PINNED = {pltpu.VMEM, pltpu.HBM}


def call(kernel, operands, specs, shapes, scratch=(), name=None, vmem=8, pin=True):
    if pin:
        shapes = [pltpu.VMEM(s.shape, s.dtype) for s in shapes]
        operands = [
            pltpu.with_memory_space_constraint(a, spec.memory_space)
            if spec.memory_space in PINNED
            else a
            for a, spec in zip(operands, specs)
        ]
    return pl.pallas_call(
        kernel,
        out_shape=shapes,
        in_specs=specs,
        out_specs=[VMEM] * len(shapes),
        scratch_shapes=list(scratch),
        cost_estimate=pl.CostEstimate(flops=0, bytes_accessed=0, transcendentals=0),
        compiler_params=pltpu.CompilerParams(vmem_limit_bytes=vmem << 20),
        name=name,
    )(*operands)


def after(value, *others):
    return lax.optimization_barrier((value, *others))[0]


def prepare_kernel(hidden_hbm, ids_hbm, share_hbm, gain_hbm, *refs):
    out_refs, (hidden_ref, ids_ref, share_ref, gain_ref, sems) = refs[:-5], refs[-5:]
    sources = (hidden_hbm, ids_hbm, share_hbm, gain_hbm)
    targets = (hidden_ref, ids_ref, share_ref, gain_ref)
    copies = [pltpu.make_async_copy(s, t, sems.at[i]) for i, (s, t) in enumerate(zip(sources, targets))]
    for copy in copies:
        copy.start()
    for copy in copies:
        copy.wait()
    rows, width = hidden_ref.shape[1:]
    fanout = ids_ref.shape[1]
    extra = out_refs[0].shape[2] - width
    for batch, out_ref in enumerate(out_refs):
        values = hidden_ref[batch].astype(jnp.float32)
        power = jnp.mean(values * values, axis=-1, keepdims=True)
        normed = values * lax.rsqrt(power + 1e-06) * gain_ref[...]
        out_ref[0, :, :width] = normed.astype(jnp.bfloat16)
        expert = lax.broadcasted_iota(jnp.int32, (extra, rows), 0)
        dense = jnp.zeros((extra, rows), jnp.float32)
        for k in range(fanout):
            share = share_ref[batch, k : k + 1, :].astype(jnp.float32) * (1.0 / 64.0)
            dense = dense + jnp.where(expert == ids_ref[batch, k : k + 1, :], share, 0.0)
        out_ref[0, :, width:] = dense.T.astype(jnp.bfloat16)


def prepare(hidden_in, expert_ids, route_share, norm_gain, extra):
    batches, rows, width = hidden_in.shape
    operands = [
        hidden_in,
        expert_ids.transpose(0, 2, 1),
        route_share.transpose(0, 2, 1),
        norm_gain.reshape(1, width),
    ]
    return call(
        prepare_kernel,
        operands,
        [HBM] * 4,
        [jax.ShapeDtypeStruct((1, rows, width + extra), jnp.bfloat16)] * batches,
        [pltpu.VMEM(a.shape, a.dtype) for a in operands] + [pltpu.SemaphoreType.DMA((4,))],
        name="prepare",
    )


def join_kernel(*refs):
    at = 0
    for ref in refs[:-1]:
        refs[-1][at : at + ref.shape[0]] = ref[...]
        at += ref.shape[0]


def join(a, b):
    shape = jax.ShapeDtypeStruct((a.shape[0] + b.shape[0], *a.shape[1:]), a.dtype)
    return call(join_kernel, [a, b], [VMEM] * 2, [shape], name="join")[0]


def ffn_kernel(owner_ref, scale_ref, gate_hbm, up_hbm, down_hbm, *refs):
    x_refs, (mine_ref, other_ref, gate_ref, up_ref, down_ref, x_all, hidden, sems) = refs[:4], refs[4:]
    width, ff = gate_ref.shape
    group = ff // scale_ref.shape[1]
    step = 2 * group if ff % (2 * group) == 0 else group
    steps = ff // step
    copies = []
    for i in range(steps):
        cut = slice(i * step, (i + 1) * step)
        copies.append(pltpu.make_async_copy(gate_hbm.at[0, :, cut], gate_ref.at[:, cut], sems.at[2 * i]))
        copies.append(pltpu.make_async_copy(up_hbm.at[0, :, cut], up_ref.at[:, cut], sems.at[2 * i + 1]))
    copies.append(pltpu.make_async_copy(down_hbm.at[0], down_ref, sems.at[2 * steps]))
    for copy in copies:
        copy.start()
    pieces, part, full = x_refs[0].shape
    rows = pieces * part
    for i, x_ref in enumerate(x_refs):
        x_all[i * rows : (i + 1) * rows, :] = x_ref[...].reshape(rows, full)
    for i in range(steps):
        cut = slice(i * step, (i + 1) * step)
        x = x_all[:, :width]
        copies[2 * i].wait()
        gate = jnp.dot(x, gate_ref[:, cut], preferred_element_type=jnp.float32)
        copies[2 * i + 1].wait()
        up = jnp.dot(x, up_ref[:, cut], preferred_element_type=jnp.float32)
        for at in range(0, step, group):
            b = (i * step + at) // group
            g = gate[:, at : at + group] * scale_ref[0, b]
            u = up[:, at : at + group] * scale_ref[1, b]
            h = g / (1.0 + jnp.exp(-g)) * u * scale_ref[2, b]
            hidden[:, i * step + at : i * step + at + group] = h.astype(jnp.bfloat16)
    shares = x_all[:, width:].astype(jnp.float32)
    here = lax.broadcasted_iota(jnp.int32, shares.shape, 1) == owner_ref[0]
    weight = jnp.sum(jnp.where(here, shares, 0.0), axis=1, keepdims=True)
    copies[2 * steps].wait()
    cols = 512 if width % 512 == 0 else LANES
    for n in range(0, width, cols):
        out = jnp.dot(hidden[...], down_ref[:, n : n + cols], preferred_element_type=jnp.float32)
        out = (out * weight).astype(jnp.bfloat16).reshape(4, pieces, part, cols)
        mine_ref[:, :, :, n : n + cols] = out[:2]
        other_ref[:, :, :, n : n + cols] = out[2:]


def ffn(xs, owner, scales, weights):
    pieces, part, full = xs[0].shape
    width, ff = weights[0].shape[1:]
    rows = 4 * pieces * part
    return call(
        ffn_kernel,
        [owner, scales, *weights, *xs],
        [SMEM, SMEM] + [HBM] * 3 + [VMEM] * 4,
        [jax.ShapeDtypeStruct((2, pieces, part, width), jnp.bfloat16)] * 2,
        [
            pltpu.VMEM((width, ff), jnp.bfloat16),
            pltpu.VMEM((width, ff), jnp.bfloat16),
            pltpu.VMEM((ff, width), jnp.bfloat16),
            pltpu.VMEM((rows, full), jnp.bfloat16),
            pltpu.VMEM((rows, ff), jnp.bfloat16),
            pltpu.SemaphoreType.DMA((2 * (ff // LANES) + 1,)),
        ],
        name="ffn",
        vmem=28,
    )


def view(ref, slot):
    return ref if slot is None else ref.at[slot]


def total_kernel(slots, low, *refs):
    out_ref = refs[-1]
    for piece in range(out_ref.shape[0]):
        total = None
        for slot, ref in zip(slots, refs[:-1]):
            term = view(ref, slot)[low + piece].astype(jnp.float32)
            total = term if total is None else total + term
        out_ref[piece] = total.astype(out_ref.dtype)


def total(terms, low, high):
    arrays = [a for a, _ in terms]
    shape = jax.ShapeDtypeStruct((high - low, *arrays[0].shape[-2:]), arrays[0].dtype)
    return call(
        functools.partial(total_kernel, [slot for _, slot in terms], low),
        arrays,
        [VMEM] * len(arrays),
        [shape],
        name="total",
    )[0]


def finish_kernel(slots, hidden_ref, *refs):
    out_ref = refs[-1]
    for batch in range(hidden_ref.shape[0]):
        mixed = None
        for i, slot in enumerate(slots):
            term = view(refs[batch * len(slots) + i], slot)[0].astype(jnp.float32)
            mixed = term if mixed is None else mixed + term
        out_ref[batch] = (hidden_ref[batch].astype(jnp.float32) + mixed).astype(out_ref.dtype)


def finish(hidden_in, terms):
    arrays = [a for batch in terms for a, _ in batch]
    return call(
        functools.partial(finish_kernel, [slot for _, slot in terms[0]]),
        [hidden_in, *arrays],
        [VMEM] * (1 + len(arrays)),
        [jax.ShapeDtypeStruct(hidden_in.shape, hidden_in.dtype)],
        name="finish",
        pin=False,
    )[0]


def local(
    hidden_in,
    expert_ids,
    route_share,
    norm_gain,
    gate_weight,
    up_weight,
    down_weight,
    exponent_table,
):
    owners = lax.axis_size("ep")
    batches = hidden_in.shape[0]
    weights = (gate_weight, up_weight, down_weight)
    scales = jnp.exp2(exponent_table[0].astype(jnp.float32))
    owner = lax.axis_index("ep").astype(jnp.int32).reshape(1)

    line = owners // 4
    half = line // 2

    def mirror(rows, span):
        def partner(i):
            p = i // 4
            return (p // span * span + span - 1 - p % span) * 4 + i % 4

        return lax.ppermute(rows, "ep", [(i, partner(i)) for i in range(owners)])

    def to_mid(rows):
        return lax.ppermute(rows, "ep", [(i, i ^ 2) for i in range(owners)])

    def to_core(rows):
        return lax.ppermute(rows, "ep", [(i, i ^ 1) for i in range(owners)])

    payload = prepare(hidden_in, expert_ids, route_share, norm_gain, -(-owners // LANES) * LANES)

    near, far = [], []
    for batch, rows in enumerate(payload):
        if batch:
            rows = after(rows, near[-1])
        span = line
        while span > 2:
            rows = join(rows, mirror(rows, span))
            if batch:
                rows = after(rows, far[-1])
            span //= 2
        near.append(rows)
        far.append(mirror(rows, 2))

    def expert(rows, there, *others):
        xs = [rows, there, to_core(rows), to_core(there)]
        mine, other = ffn([after(xs[0], *others), *xs[1:]], owner, scales, weights)
        other = to_core(other)
        sent.append(total([(mine, 1), (other, 1)], 0, half))
        back.append(to_mid(sent[-1]))
        return [(mine, 0), (other, 0), (back[-1], None)]

    near_terms, far_terms, sent, back = [], [], [], []
    near_there = [to_mid(rows) for rows in near]
    far_there = [to_mid(rows) for rows in far]
    for batch in range(batches):
        there = near_there[batch]
        if batch + 1 < batches:
            there = after(there, near[batch + 1])
        near_terms.append(expert(near[batch], there, far[-1], *sent[-1:], *back[-2:-1]))
        far_terms.append(expert(far[batch], far_there[batch], *sent[-1:], *back[-2:-1]))

    for batch in range(batches):
        terms = near_terms[batch]
        last = far_terms[batch]
        if batch + 1 < batches:
            last = [*last[:-1], (after(last[-1][0], sent[-1]), None)]
        terms.append((mirror(total(last, 0, half), 2), None))
        span, pieces = 4, half
        while pieces > 1:
            terms.append((mirror(total(terms, pieces // 2, pieces), span), None))
            span, pieces = span * 2, pieces // 2
    return finish(hidden_in, near_terms)


def solution(mesh):
    return jax.shard_map(
        local,
        mesh=mesh,
        in_specs=(
            P(None, ("grp", "ep"), None),
            P(None, ("grp", "ep"), None),
            P(None, ("grp", "ep"), None),
            P(),
            P("ep", None, None),
            P("ep", None, None),
            P("ep", None, None),
            P("ep", None, None),
        ),
        out_specs=P(None, ("grp", "ep"), None),
        check_vma=False,
    )
```

time: 242 us -> 110 us (0.45)
  waiting for transfers between devices: 192 us -> 44 us
  starting transfers between devices: 0.12 us -> 33.7 us
  Pallas kernels: 0 us -> 31.7 us
  matrix products: 27.8 us -> 0 us
  between operations: 13.2 us -> 0.16 us
  other arithmetic: 7.6 us -> 0.69 us
    reduce_scatter x2 -> x0, waiting for transfers between devices: 111 us -> none  [local(): mixed = lax.psum_scatter(partial, 'ep', scatter_dimension=0, tiled=True)]
    all_gather x2 -> x0, waiting for transfers between devices: 80.5 us -> none  [local(): lax.all_gather(payload[batch], 'ep', axis=0, tiled=True)]
    ppermute x0 -> x28, waiting for transfers between devices: none -> 44 us  [the longest x8 21.5 us: to_mid(): return lax.ppermute(rows, 'ep', [(i, i ^ 2) for i in range(owners)])]
    ppermute x0 -> x28, starting transfers between devices: none -> 33.7 us  [the longest x8 22.2 us: mirror(): return lax.ppermute(rows, 'ep', [(i, partner(i)) for i in range(owners)])]
    pallas_call x0 -> x16, Pallas kernels: none -> 31.7 us  [call(): pl.pallas_call(kernel, out_shape=shapes, in_specs=specs, out_specs=[VMEM]...]
    dot_general x4 -> x0, matrix products: 27.8 us -> none  [the longest x2 16.9 us: local(): partial = jnp.dot(hidden, down_mat, preferred_element_type=jnp.float32)]
    reduce_sum x3 -> x0, other arithmetic: 2.63 us -> none  [the longest x1 1.23 us: normalize(): power = jnp.mean(values * values, axis=-1, keepdims=True)]
  transfers between devices with their start and end apart: 4 -> 28, of which waited for: 4 -> 13; matrix products, arithmetic and copies ran while one was open for 8% -> 1% of each run, Pallas kernels for 0% -> 20%
where the time goes in v6:
time: 110 us
  waiting for transfers between devices  44 us (40%)
  starting transfers between devices  33.7 us (31%)
  Pallas kernels  31.7 us (29%)
    pallas_call x16, Pallas kernels, call(): pl.pallas_call(kernel, out_shape=shapes, in_specs=specs, out_specs=[VMEM]...  31.7 us
    ppermute x8, starting transfers between devices, mirror(): return lax.ppermute(rows, 'ep', [(i, partner(i)) for i in range(owners)])  22.2 us
    ppermute x8, waiting for transfers between devices, to_mid(): return lax.ppermute(rows, 'ep', [(i, i ^ 2) for i in range(owners)])  21.5 us
    ppermute x8, waiting for transfers between devices, mirror(): return lax.ppermute(rows, 'ep', [(i, partner(i)) for i in range(owners)])  19.8 us
    ppermute x8, starting transfers between devices, to_mid(): return lax.ppermute(rows, 'ep', [(i, i ^ 2) for i in range(owners)])  9.43 us
    ppermute x12, waiting for transfers between devices, to_core(): return lax.ppermute(rows, 'ep', [(i, i ^ 1) for i in range(owners)])  2.69 us
  transfers between devices with their start and end apart: 28, of which 13 were waited for; matrix products, arithmetic and copies ran while one was open for 1% of the time, Pallas kernels for 20%

profile of v6, /device:TPU:0, one launch (start us, length us, event | category | flops | bytes accessed | tf_op | source)
XLA Modules:
  0.0 110.3 jit_solution(3532792631298837892)
XLA Ops:
  0.0 1.2 %prepare.1 = (bf16[1,32,2176]{2,1,0:T(8,128)(2,1)S(1)}, bf16[1,32,2176]{2,1,0:T(8,128)(2,1)S(1)}) custom-call(bf16[2,32,2048]{2,1,0:T(8,128)(2,1)} %hidden_ref.1, s32[2,8,32]{2,1,0:T(8,128)} %bitcast.11, s32[2,8,32]{2,1,0:T(8,128)} %bitcast.12, f32[1,2048]{1,0:T(1,128)} %bitcast.13), custom_call_target="tpu_custom_call" | custom-call | tf_op jit(solution)/shard_map/prepare/pallas_call | solution.py:26
  1.2 5.1 %collective-permute-start = (bf16[1,32,2176]{2,1,0:T(8,128)(2,1)S(1)}, bf16[1,32,2176]{2,1,0:T(8,128)(2,1)S(1)}, u32[]{:S(2)}, u32[]{:S(2)}) collective-permute-start(bf16[1,32,2176]{2,1,0:T(8,128)(2,1)S(1)} %get-tuple-element.23.refs_0_), channel_id=1, source_target_pairs={{0,12},{1,13},{2,14},{3,15},{4,8},{5,9},{6,10},{7,11},{8,4},{9,5},... | collective-permute-start | bytes 417800 | tf_op jit(solution)/shard_map/ppermute | solution.py:234
  6.3 3.8 %collective-permute-done.refs_1_ = bf16[1,32,2176]{2,1,0:T(8,128)(2,1)S(1)} collective-permute-done((bf16[1,32,2176]{2,1,0:T(8,128)(2,1)S(1)}, bf16[1,32,2176]{2,1,0:T(8,128)(2,1)S(1)}, u32[]{:S(2)}, u32[]{:S(2)}) %collective-permute-start) | collective-permute-done | bytes 139296 | tf_op jit(solution)/shard_map/ppermute | solution.py:234
  10.1 2.7 %collective-permute-start.2 = (bf16[2,32,2176]{2,1,0:T(8,128)(2,1)S(1)}, bf16[2,32,2176]{2,1,0:T(8,128)(2,1)S(1)}, u32[]{:S(2)}, u32[]{:S(2)}) collective-permute-start(bf16[2,32,2176]{2,1,0:T(8,128)(2,1)S(1)} %join.2.refs_0_), channel_id=1, source_target_pairs={{0,4},{1,5},{2,6},{3,7},{4,0},{5,1},{6,2},{7,3},{8,12},{9,13},{10,... | collective-permute-start | bytes 835592 | tf_op jit(solution)/shard_map/ppermute | solution.py:234
  12.8 1.5 %collective-permute-start.4 = (bf16[2,32,2176]{2,1,0:T(8,128)(2,1)S(1)}, bf16[2,32,2176]{2,1,0:T(8,128)(2,1)S(1)}, u32[]{:S(2)}, u32[]{:S(2)}) collective-permute-start(bf16[2,32,2176]{2,1,0:T(8,128)(2,1)S(1)} %join.2.refs_0_), channel_id=1, source_target_pairs={{0,2},{1,3},{2,0},{3,1},{4,6},{5,7},{6,4},{7,5},{8,10},{9,11},{10,... | collective-permute-start | bytes 835592 | tf_op jit(solution)/shard_map/ppermute | solution.py:237
  14.3 2.5 %collective-permute-start.1 = (bf16[1,32,2176]{2,1,0:T(8,128)(2,1)S(1)}, bf16[1,32,2176]{2,1,0:T(8,128)(2,1)S(1)}, u32[]{:S(2)}, u32[]{:S(2)}) collective-permute-start(bf16[1,32,2176]{2,1,0:T(8,128)(2,1)S(1)} %get-tuple-element.25.refs_0_), channel_id=1, source_target_pairs={{0,12},{1,13},{2,14},{3,15},{4,8},{5,9},{6,10},{7,11},{8,4},{9,5},... | collective-permute-start | bytes 417800 | tf_op jit(solution)/shard_map/ppermute | solution.py:234
  16.8 6.0 %collective-permute-done.1.refs_1_ = bf16[1,32,2176]{2,1,0:T(8,128)(2,1)S(1)} collective-permute-done((bf16[1,32,2176]{2,1,0:T(8,128)(2,1)S(1)}, bf16[1,32,2176]{2,1,0:T(8,128)(2,1)S(1)}, u32[]{:S(2)}, u32[]{:S(2)}) %collective-permute-start.1) | collective-permute-done | bytes 139296 | tf_op jit(solution)/shard_map/ppermute | solution.py:234
  23.0 1.4 %collective-permute-start.9 = (bf16[2,32,2176]{2,1,0:T(8,128)(2,1)S(1)}, bf16[2,32,2176]{2,1,0:T(8,128)(2,1)S(1)}, u32[]{:S(2)}, u32[]{:S(2)}) collective-permute-start(bf16[2,32,2176]{2,1,0:T(8,128)(2,1)S(1)} %collective-permute-done.2.refs_0_), channel_id=1, source_target_pairs={{0,2},{1,3},{2,0},{3,1},{4,6},{5,7},{6,4},{7,5},{8,10},{9,11},{10,... | collective-permute-start | bytes 835592 | tf_op jit(solution)/shard_map/ppermute | solution.py:237
  24.4 0.7 multiply_exponential_fusion
  25.0 4.4 %collective-permute-done.3.refs_0_ = bf16[2,32,2176]{2,1,0:T(8,128)(2,1)S(1)} collective-permute-done((bf16[2,32,2176]{2,1,0:T(8,128)(2,1)S(1)}, bf16[2,32,2176]{2,1,0:T(8,128)(2,1)S(1)}, u32[]{:S(2)}, u32[]{:S(2)}) %collective-permute-start.3) | collective-permute-done | bytes 278560 | tf_op jit(solution)/shard_map/ppermute | solution.py:234
  29.4 7.2 %ffn.4 = (bf16[2,2,32,2048]{3,2,1,0:T(8,128)(2,1)S(1)}, bf16[2,2,32,2048]{3,2,1,0:T(8,128)(2,1)S(1)}) custom-call(s32[1]{0:T(128)} %bitcast.owner_ref, f32[3,6]{1,0:T(4,128)S(1)} %bitcast.7, bf16[1,2048,768]{2,1,0:T(8,128)(2,1)} %gate_hbm.7, bf16[1,2048,768]{2,1,0:T(8,128)(2,1)} %up_hbm.7, bf16[1,768,2048]{2,1,0:T(8,128)(2,1)} %down_hbm.7, ...), custom_call_target="tpu_custom_call" | custom-call | tf_op jit(solution)/shard_map/ffn/pallas_call | solution.py:26
  36.8 0.5 collective-permute-start.10
  37.3 1.3 %collective-permute-start.14 = (bf16[2,32,2176]{2,1,0:T(8,128)(2,1)S(1)}, bf16[2,32,2176]{2,1,0:T(8,128)(2,1)S(1)}, u32[]{:S(2)}, u32[]{:S(2)}) collective-permute-start(bf16[2,32,2176]{2,1,0:T(8,128)(2,1)S(1)} %join.3.refs_0_), channel_id=1, source_target_pairs={{0,2},{1,3},{2,0},{3,1},{4,6},{5,7},{6,4},{7,5},{8,10},{9,11},{10,... | collective-permute-start | bytes 835592 | tf_op jit(solution)/shard_map/ppermute | solution.py:237
  39.1 0.4 collective-permute-done.11.refs_3_
  39.5 7.2 %ffn.5 = (bf16[2,2,32,2048]{3,2,1,0:T(8,128)(2,1)S(1)}, bf16[2,2,32,2048]{3,2,1,0:T(8,128)(2,1)S(1)}) custom-call(s32[1]{0:T(128)} %bitcast.owner_ref, f32[3,6]{1,0:T(4,128)S(1)} %bitcast.8, bf16[1,2048,768]{2,1,0:T(8,128)(2,1)} %gate_hbm.7, bf16[1,2048,768]{2,1,0:T(8,128)(2,1)} %up_hbm.7, bf16[1,768,2048]{2,1,0:T(8,128)(2,1)} %down_hbm.7, ...), custom_call_target="tpu_custom_call" | custom-call | tf_op jit(solution)/shard_map/ffn/pallas_call | solution.py:26
  47.4 1.3 %collective-permute-start.8 = (bf16[2,32,2048]{2,1,0:T(8,128)(2,1)S(1)}, bf16[2,32,2048]{2,1,0:T(8,128)(2,1)S(1)}, u32[]{:S(2)}, u32[]{:S(2)}) collective-permute-start(bf16[2,32,2048]{2,1,0:T(8,128)(2,1)S(1)} %total.8), channel_id=1, source_target_pairs={{0,2},{1,3},{2,0},{3,1},{4,6},{5,7},{6,4},{7,5},{8,10},{9,11},{10,... | collective-permute-start | bytes 786440 | tf_op jit(solution)/shard_map/ppermute | solution.py:237
  48.7 0.7 collective-permute-start.18
  49.5 7.0 %collective-permute-done.8.refs_2_ = bf16[2,32,2048]{2,1,0:T(8,128)(2,1)S(1)} collective-permute-done((bf16[2,32,2048]{2,1,0:T(8,128)(2,1)S(1)}, bf16[2,32,2048]{2,1,0:T(8,128)(2,1)S(1)}, u32[]{:S(2)}, u32[]{:S(2)}) %collective-permute-start.8) | collective-permute-done | bytes 262176 | tf_op jit(solution)/shard_map/ppermute | solution.py:237
  56.6 7.2 %ffn.6 = (bf16[2,2,32,2048]{3,2,1,0:T(8,128)(2,1)S(1)}, bf16[2,2,32,2048]{3,2,1,0:T(8,128)(2,1)S(1)}) custom-call(s32[1]{0:T(128)} %bitcast.owner_ref, f32[3,6]{1,0:T(4,128)S(1)} %bitcast.9, bf16[1,2048,768]{2,1,0:T(8,128)(2,1)} %gate_hbm.7, bf16[1,2048,768]{2,1,0:T(8,128)(2,1)} %up_hbm.7, bf16[1,768,2048]{2,1,0:T(8,128)(2,1)} %down_hbm.7, ...), custom_call_target="tpu_custom_call" | custom-call | tf_op jit(solution)/shard_map/ffn/pallas_call | solution.py:26
  63.9 0.5 collective-permute-start.19
  64.5 1.3 %collective-permute-start.13 = (bf16[2,32,2048]{2,1,0:T(8,128)(2,1)S(1)}, bf16[2,32,2048]{2,1,0:T(8,128)(2,1)S(1)}, u32[]{:S(2)}, u32[]{:S(2)}) collective-permute-start(bf16[2,32,2048]{2,1,0:T(8,128)(2,1)S(1)} %total.9), channel_id=1, source_target_pairs={{0,2},{1,3},{2,0},{3,1},{4,6},{5,7},{6,4},{7,5},{8,10},{9,11},{10,... | collective-permute-start | bytes 786440 | tf_op jit(solution)/shard_map/ppermute | solution.py:237
  65.8 7.3 %collective-permute-done.13.refs_2_ = bf16[2,32,2048]{2,1,0:T(8,128)(2,1)S(1)} collective-permute-done((bf16[2,32,2048]{2,1,0:T(8,128)(2,1)S(1)}, bf16[2,32,2048]{2,1,0:T(8,128)(2,1)S(1)}, u32[]{:S(2)}, u32[]{:S(2)}) %collective-permute-start.13) | collective-permute-done | bytes 262176 | tf_op jit(solution)/shard_map/ppermute | solution.py:237
  73.1 7.2 %ffn.7 = (bf16[2,2,32,2048]{3,2,1,0:T(8,128)(2,1)S(1)}, bf16[2,2,32,2048]{3,2,1,0:T(8,128)(2,1)S(1)}) custom-call(s32[1]{0:T(128)} %bitcast.owner_ref, f32[3,6]{1,0:T(4,128)S(1)} %bitcast.10, bf16[1,2048,768]{2,1,0:T(8,128)(2,1)} %gate_hbm.7, bf16[1,2048,768]{2,1,0:T(8,128)(2,1)} %up_hbm.7, bf16[1,768,2048]{2,1,0:T(8,128)(2,1)} %down_hbm.7, ...), custom_call_target="tpu_custom_call" | custom-call | tf_op jit(solution)/shard_map/ffn/pallas_call | solution.py:26
  80.4 1.9 %collective-permute-done.21.refs_1_ = bf16[2,2,32,2048]{3,2,1,0:T(8,128)(2,1)S(1)} collective-permute-done((bf16[2,2,32,2048]{3,2,1,0:T(8,128)(2,1)S(1)}, bf16[2,2,32,2048]{3,2,1,0:T(8,128)(2,1)S(1)}, u32[]{:S(2)}, u32[]{:S(2)}) %collective-permute-start.21) | collective-permute-done | bytes 524320 | tf_op jit(solution)/shard_map/ppermute | solution.py:240
  82.4 1.4 %collective-permute-start.25 = (bf16[2,32,2048]{2,1,0:T(8,128)(2,1)S(1)}, bf16[2,32,2048]{2,1,0:T(8,128)(2,1)S(1)}, u32[]{:S(2)}, u32[]{:S(2)}) collective-permute-start(bf16[2,32,2048]{2,1,0:T(8,128)(2,1)S(1)} %total.11), channel_id=1, source_target_pairs={{0,2},{1,3},{2,0},{3,1},{4,6},{5,7},{6,4},{7,5},{8,10},{9,11},{10,... | collective-permute-start | bytes 786440 | tf_op jit(solution)/shard_map/ppermute | solution.py:237
  84.2 0.6 collective-permute-start.24
  84.8 6.9 %collective-permute-done.25.refs_2_ = bf16[2,32,2048]{2,1,0:T(8,128)(2,1)S(1)} collective-permute-done((bf16[2,32,2048]{2,1,0:T(8,128)(2,1)S(1)}, bf16[2,32,2048]{2,1,0:T(8,128)(2,1)S(1)}, u32[]{:S(2)}, u32[]{:S(2)}) %collective-permute-start.25) | collective-permute-done | bytes 262176 | tf_op jit(solution)/shard_map/ppermute | solution.py:237
  92.1 4.0 %collective-permute-start.23 = (bf16[1,32,2048]{2,1,0:T(8,128)(2,1)S(1)}, bf16[1,32,2048]{2,1,0:T(8,128)(2,1)S(1)}, u32[]{:S(2)}, u32[]{:S(2)}) collective-permute-start(bf16[1,32,2048]{2,1,0:T(8,128)(2,1)S(1)} %total.13), channel_id=1, source_target_pairs={{0,12},{1,13},{2,14},{3,15},{4,8},{5,9},{6,10},{7,11},{8,4},{9,5},... | collective-permute-start | bytes 393224 | tf_op jit(solution)/shard_map/ppermute | solution.py:234
  96.4 2.5 %collective-permute-done.26.refs_3_.refs_8_ = bf16[2,32,2048]{2,1,0:T(8,128)(2,1)S(1)} collective-permute-done((bf16[2,32,2048]{2,1,0:T(8,128)(2,1)S(1)}, bf16[2,32,2048]{2,1,0:T(8,128)(2,1)S(1)}, u32[]{:S(2)}, u32[]{:S(2)}) %collective-permute-start.26) | collective-permute-done | bytes 262176 | tf_op jit(solution)/shard_map/ppermute | solution.py:234
  99.0 7.4 %collective-permute-start.27 = (bf16[1,32,2048]{2,1,0:T(8,128)(2,1)S(1)}, bf16[1,32,2048]{2,1,0:T(8,128)(2,1)S(1)}, u32[]{:S(2)}, u32[]{:S(2)}) collective-permute-start(bf16[1,32,2048]{2,1,0:T(8,128)(2,1)S(1)} %total.15), channel_id=1, source_target_pairs={{0,12},{1,13},{2,14},{3,15},{4,8},{5,9},{6,10},{7,11},{8,4},{9,5},... | collective-permute-start | bytes 393224 | tf_op jit(solution)/shard_map/ppermute | solution.py:234
  106.4 2.9 %collective-permute-done.27.refs_9_ = bf16[1,32,2048]{2,1,0:T(8,128)(2,1)S(1)} collective-permute-done((bf16[1,32,2048]{2,1,0:T(8,128)(2,1)S(1)}, bf16[1,32,2048]{2,1,0:T(8,128)(2,1)S(1)}, u32[]{:S(2)}, u32[]{:S(2)}) %collective-permute-start.27) | collective-permute-done | bytes 131104 | tf_op jit(solution)/shard_map/ppermute | solution.py:234
  109.4 0.9 finish.1
  (44 shorter events, 3.2 us)
Async XLA Ops:
  1.2 8.9 %collective-permute-start = (bf16[1,32,2176]{2,1,0:T(8,128)(2,1)S(1)}, bf16[1,32,2176]{2,1,0:T(8,128)(2,1)S(1)}, u32[]{:S(2)}, u32[]{:S(2)}) collective-permute-start(bf16[1,32,2176]{2,1,0:T(8,128)(2,1)S(1)} %get-tuple-element.23.refs_0_), channel_id=1, source_target_pairs={{0,12},{1,13},{2,14},{3,15},{4,8},{5,9},{6,10},{7,11},{8,4},{9,5},... | collective-permute-start | bytes 417800 | tf_op jit(solution)/shard_map/ppermute | solution.py:234
  10.1 12.7 %collective-permute-start.2 = (bf16[2,32,2176]{2,1,0:T(8,128)(2,1)S(1)}, bf16[2,32,2176]{2,1,0:T(8,128)(2,1)S(1)}, u32[]{:S(2)}, u32[]{:S(2)}) collective-permute-start(bf16[2,32,2176]{2,1,0:T(8,128)(2,1)S(1)} %join.2.refs_0_), channel_id=1, source_target_pairs={{0,4},{1,5},{2,6},{3,7},{4,0},{5,1},{6,2},{7,3},{8,12},{9,13},{10,... | collective-permute-start | bytes 835592 | tf_op jit(solution)/shard_map/ppermute | solution.py:234
  12.8 10.1 %collective-permute-start.4 = (bf16[2,32,2176]{2,1,0:T(8,128)(2,1)S(1)}, bf16[2,32,2176]{2,1,0:T(8,128)(2,1)S(1)}, u32[]{:S(2)}, u32[]{:S(2)}) collective-permute-start(bf16[2,32,2176]{2,1,0:T(8,128)(2,1)S(1)} %join.2.refs_0_), channel_id=1, source_target_pairs={{0,2},{1,3},{2,0},{3,1},{4,6},{5,7},{6,4},{7,5},{8,10},{9,11},{10,... | collective-permute-start | bytes 835592 | tf_op jit(solution)/shard_map/ppermute | solution.py:237
  14.3 8.5 %collective-permute-start.1 = (bf16[1,32,2176]{2,1,0:T(8,128)(2,1)S(1)}, bf16[1,32,2176]{2,1,0:T(8,128)(2,1)S(1)}, u32[]{:S(2)}, u32[]{:S(2)}) collective-permute-start(bf16[1,32,2176]{2,1,0:T(8,128)(2,1)S(1)} %get-tuple-element.25.refs_0_), channel_id=1, source_target_pairs={{0,12},{1,13},{2,14},{3,15},{4,8},{5,9},{6,10},{7,11},{8,4},{9,5},... | collective-permute-start | bytes 417800 | tf_op jit(solution)/shard_map/ppermute | solution.py:234
  16.8 12.6 %collective-permute-start.5 = (bf16[2,32,2176]{2,1,0:T(8,128)(2,1)S(1)}, bf16[2,32,2176]{2,1,0:T(8,128)(2,1)S(1)}, u32[]{:S(2)}, u32[]{:S(2)}) collective-permute-start(bf16[2,32,2176]{2,1,0:T(8,128)(2,1)S(1)} %join.2.refs_0_), channel_id=1, source_target_pairs={{0,1},{1,0},{2,3},{3,2},{4,5},{5,4},{6,7},{7,6},{8,9},{9,8},{10,11... | collective-permute-start | bytes 835592 | tf_op jit(solution)/shard_map/ppermute | solution.py:240
  22.8 6.6 %collective-permute-start.3 = (bf16[2,32,2176]{2,1,0:T(8,128)(2,1)S(1)}, bf16[2,32,2176]{2,1,0:T(8,128)(2,1)S(1)}, u32[]{:S(2)}, u32[]{:S(2)}) collective-permute-start(bf16[2,32,2176]{2,1,0:T(8,128)(2,1)S(1)} %join.3.refs_0_), channel_id=1, source_target_pairs={{0,4},{1,5},{2,6},{3,7},{4,0},{5,1},{6,2},{7,3},{8,12},{9,13},{10,... | collective-permute-start | bytes 835592 | tf_op jit(solution)/shard_map/ppermute | solution.py:234
  22.9 6.5 %collective-permute-start.6 = (bf16[2,32,2176]{2,1,0:T(8,128)(2,1)S(1)}, bf16[2,32,2176]{2,1,0:T(8,128)(2,1)S(1)}, u32[]{:S(2)}, u32[]{:S(2)}) collective-permute-start(bf16[2,32,2176]{2,1,0:T(8,128)(2,1)S(1)} %collective-permute-done.4.refs_1_), channel_id=1, source_target_pairs={{0,1},{1,0},{2,3},{3,2},{4,5},{5,4},{6,7},{7,6},{8,9},{9,8},{10,11... | collective-permute-start | bytes 835592 | tf_op jit(solution)/shard_map/ppermute | solution.py:240
  23.0 14.3 %collective-permute-start.9 = (bf16[2,32,2176]{2,1,0:T(8,128)(2,1)S(1)}, bf16[2,32,2176]{2,1,0:T(8,128)(2,1)S(1)}, u32[]{:S(2)}, u32[]{:S(2)}) collective-permute-start(bf16[2,32,2176]{2,1,0:T(8,128)(2,1)S(1)} %collective-permute-done.2.refs_0_), channel_id=1, source_target_pairs={{0,2},{1,3},{2,0},{3,1},{4,6},{5,7},{6,4},{7,5},{8,10},{9,11},{10,... | collective-permute-start | bytes 835592 | tf_op jit(solution)/shard_map/ppermute | solution.py:237
  36.7 2.0 %collective-permute-start.7 = (bf16[2,2,32,2048]{3,2,1,0:T(8,128)(2,1)S(1)}, bf16[2,2,32,2048]{3,2,1,0:T(8,128)(2,1)S(1)}, u32[]{:S(2)}, u32[]{:S(2)}) collective-permute-start(bf16[2,2,32,2048]{3,2,1,0:T(8,128)(2,1)S(1)} %get-tuple-element.30), channel_id=1, source_target_pairs={{0,1},{1,0},{2,3},{3,2},{4,5},{5,4},{6,7},{7,6},{8,9},{9,8},{10,11... | collective-permute-start | bytes 1572872 | tf_op jit(solution)/shard_map/ppermute | solution.py:240
  36.8 2.3 %collective-permute-start.10 = (bf16[2,32,2176]{2,1,0:T(8,128)(2,1)S(1)}, bf16[2,32,2176]{2,1,0:T(8,128)(2,1)S(1)}, u32[]{:S(2)}, u32[]{:S(2)}) collective-permute-start(bf16[2,32,2176]{2,1,0:T(8,128)(2,1)S(1)} %collective-permute-done.2.refs_0_), channel_id=1, source_target_pairs={{0,1},{1,0},{2,3},{3,2},{4,5},{5,4},{6,7},{7,6},{8,9},{9,8},{10,11... | collective-permute-start | bytes 835592 | tf_op jit(solution)/shard_map/ppermute | solution.py:240
  37.3 2.2 %collective-permute-start.11 = (bf16[2,32,2176]{2,1,0:T(8,128)(2,1)S(1)}, bf16[2,32,2176]{2,1,0:T(8,128)(2,1)S(1)}, u32[]{:S(2)}, u32[]{:S(2)}) collective-permute-start(bf16[2,32,2176]{2,1,0:T(8,128)(2,1)S(1)} %collective-permute-done.9.refs_1_), channel_id=1, source_target_pairs={{0,1},{1,0},{2,3},{3,2},{4,5},{5,4},{6,7},{7,6},{8,9},{9,8},{10,11... | collective-permute-start | bytes 835592 | tf_op jit(solution)/shard_map/ppermute | solution.py:240
  37.3 9.9 %collective-permute-start.14 = (bf16[2,32,2176]{2,1,0:T(8,128)(2,1)S(1)}, bf16[2,32,2176]{2,1,0:T(8,128)(2,1)S(1)}, u32[]{:S(2)}, u32[]{:S(2)}) collective-permute-start(bf16[2,32,2176]{2,1,0:T(8,128)(2,1)S(1)} %join.3.refs_0_), channel_id=1, source_target_pairs={{0,2},{1,3},{2,0},{3,1},{4,6},{5,7},{6,4},{7,5},{8,10},{9,11},{10,... | collective-permute-start | bytes 835592 | tf_op jit(solution)/shard_map/ppermute | solution.py:237
  46.7 2.8 %collective-permute-start.12 = (bf16[2,2,32,2048]{3,2,1,0:T(8,128)(2,1)S(1)}, bf16[2,2,32,2048]{3,2,1,0:T(8,128)(2,1)S(1)}, u32[]{:S(2)}, u32[]{:S(2)}) collective-permute-start(bf16[2,2,32,2048]{3,2,1,0:T(8,128)(2,1)S(1)} %get-tuple-element.33), channel_id=1, source_target_pairs={{0,1},{1,0},{2,3},{3,2},{4,5},{5,4},{6,7},{7,6},{8,9},{9,8},{10,11... | collective-permute-start | bytes 1572872 | tf_op jit(solution)/shard_map/ppermute | solution.py:240
  46.9 9.7 %collective-permute-start.15 = (bf16[2,32,2176]{2,1,0:T(8,128)(2,1)S(1)}, bf16[2,32,2176]{2,1,0:T(8,128)(2,1)S(1)}, u32[]{:S(2)}, u32[]{:S(2)}) collective-permute-start(bf16[2,32,2176]{2,1,0:T(8,128)(2,1)S(1)} %join.3.refs_0_), channel_id=1, source_target_pairs={{0,1},{1,0},{2,3},{3,2},{4,5},{5,4},{6,7},{7,6},{8,9},{9,8},{10,11... | collective-permute-start | bytes 835592 | tf_op jit(solution)/shard_map/ppermute | solution.py:240
  47.3 9.3 %collective-permute-start.16 = (bf16[2,32,2176]{2,1,0:T(8,128)(2,1)S(1)}, bf16[2,32,2176]{2,1,0:T(8,128)(2,1)S(1)}, u32[]{:S(2)}, u32[]{:S(2)}) collective-permute-start(bf16[2,32,2176]{2,1,0:T(8,128)(2,1)S(1)} %collective-permute-done.14.refs_1_), channel_id=1, source_target_pairs={{0,1},{1,0},{2,3},{3,2},{4,5},{5,4},{6,7},{7,6},{8,9},{9,8},{10,11... | collective-permute-start | bytes 835592 | tf_op jit(solution)/shard_map/ppermute | solution.py:240
  47.4 9.1 %collective-permute-start.8 = (bf16[2,32,2048]{2,1,0:T(8,128)(2,1)S(1)}, bf16[2,32,2048]{2,1,0:T(8,128)(2,1)S(1)}, u32[]{:S(2)}, u32[]{:S(2)}) collective-permute-start(bf16[2,32,2048]{2,1,0:T(8,128)(2,1)S(1)} %total.8), channel_id=1, source_target_pairs={{0,2},{1,3},{2,0},{3,1},{4,6},{5,7},{6,4},{7,5},{8,10},{9,11},{10,... | collective-permute-start | bytes 786440 | tf_op jit(solution)/shard_map/ppermute | solution.py:237
  48.7 15.7 %collective-permute-start.18 = (bf16[2,32,2176]{2,1,0:T(8,128)(2,1)S(1)}, bf16[2,32,2176]{2,1,0:T(8,128)(2,1)S(1)}, u32[]{:S(2)}, u32[]{:S(2)}) collective-permute-start(bf16[2,32,2176]{2,1,0:T(8,128)(2,1)S(1)} %collective-permute-done.3.refs_0_), channel_id=1, source_target_pairs={{0,2},{1,3},{2,0},{3,1},{4,6},{5,7},{6,4},{7,5},{8,10},{9,11},{10,... | collective-permute-start | bytes 835592 | tf_op jit(solution)/shard_map/ppermute | solution.py:237
  63.8 2.0 %collective-permute-start.17 = (bf16[2,2,32,2048]{3,2,1,0:T(8,128)(2,1)S(1)}, bf16[2,2,32,2048]{3,2,1,0:T(8,128)(2,1)S(1)}, u32[]{:S(2)}, u32[]{:S(2)}) collective-permute-start(bf16[2,2,32,2048]{3,2,1,0:T(8,128)(2,1)S(1)} %get-tuple-element.36), channel_id=1, source_target_pairs={{0,1},{1,0},{2,3},{3,2},{4,5},{5,4},{6,7},{7,6},{8,9},{9,8},{10,11... | collective-permute-start | bytes 1572872 | tf_op jit(solution)/shard_map/ppermute | solution.py:240
  63.9 9.2 %collective-permute-start.19 = (bf16[2,32,2176]{2,1,0:T(8,128)(2,1)S(1)}, bf16[2,32,2176]{2,1,0:T(8,128)(2,1)S(1)}, u32[]{:S(2)}, u32[]{:S(2)}) collective-permute-start(bf16[2,32,2176]{2,1,0:T(8,128)(2,1)S(1)} %collective-permute-done.3.refs_0_), channel_id=1, source_target_pairs={{0,1},{1,0},{2,3},{3,2},{4,5},{5,4},{6,7},{7,6},{8,9},{9,8},{10,11... | collective-permute-start | bytes 835592 | tf_op jit(solution)/shard_map/ppermute | solution.py:240
  64.4 8.7 %collective-permute-start.20 = (bf16[2,32,2176]{2,1,0:T(8,128)(2,1)S(1)}, bf16[2,32,2176]{2,1,0:T(8,128)(2,1)S(1)}, u32[]{:S(2)}, u32[]{:S(2)}) collective-permute-start(bf16[2,32,2176]{2,1,0:T(8,128)(2,1)S(1)} %collective-permute-done.18.refs_1_), channel_id=1, source_target_pairs={{0,1},{1,0},{2,3},{3,2},{4,5},{5,4},{6,7},{7,6},{8,9},{9,8},{10,11... | collective-permute-start | bytes 835592 | tf_op jit(solution)/shard_map/ppermute | solution.py:240
  64.5 8.7 %collective-permute-start.13 = (bf16[2,32,2048]{2,1,0:T(8,128)(2,1)S(1)}, bf16[2,32,2048]{2,1,0:T(8,128)(2,1)S(1)}, u32[]{:S(2)}, u32[]{:S(2)}) collective-permute-start(bf16[2,32,2048]{2,1,0:T(8,128)(2,1)S(1)} %total.9), channel_id=1, source_target_pairs={{0,2},{1,3},{2,0},{3,1},{4,6},{5,7},{6,4},{7,5},{8,10},{9,11},{10,... | collective-permute-start | bytes 786440 | tf_op jit(solution)/shard_map/ppermute | solution.py:237
  80.4 2.0 %collective-permute-start.21 = (bf16[2,2,32,2048]{3,2,1,0:T(8,128)(2,1)S(1)}, bf16[2,2,32,2048]{3,2,1,0:T(8,128)(2,1)S(1)}, u32[]{:S(2)}, u32[]{:S(2)}) collective-permute-start(bf16[2,2,32,2048]{3,2,1,0:T(8,128)(2,1)S(1)} %get-tuple-element.39), channel_id=1, source_target_pairs={{0,1},{1,0},{2,3},{3,2},{4,5},{5,4},{6,7},{7,6},{8,9},{9,8},{10,11... | collective-permute-start | bytes 1572872 | tf_op jit(solution)/shard_map/ppermute | solution.py:240
  82.4 26.9 %copy-start = (bf16[2,32,2048]{2,1,0:T(8,128)(2,1)S(1)}, bf16[2,32,2048]{2,1,0:T(8,128)(2,1)}, u32[]{:S(2)}) copy-start(bf16[2,32,2048]{2,1,0:T(8,128)(2,1)} %hidden_ref.1) | copy-start | bytes 786436
  82.4 9.2 %collective-permute-start.25 = (bf16[2,32,2048]{2,1,0:T(8,128)(2,1)S(1)}, bf16[2,32,2048]{2,1,0:T(8,128)(2,1)S(1)}, u32[]{:S(2)}, u32[]{:S(2)}) collective-permute-start(bf16[2,32,2048]{2,1,0:T(8,128)(2,1)S(1)} %total.11), channel_id=1, source_target_pairs={{0,2},{1,3},{2,0},{3,1},{4,6},{5,7},{6,4},{7,5},{8,10},{9,11},{10,... | collective-permute-start | bytes 786440 | tf_op jit(solution)/shard_map/ppermute | solution.py:237
  83.9 8.1 %collective-permute-start.22 = (bf16[2,32,2048]{2,1,0:T(8,128)(2,1)S(1)}, bf16[2,32,2048]{2,1,0:T(8,128)(2,1)S(1)}, u32[]{:S(2)}, u32[]{:S(2)}) collective-permute-start(bf16[2,32,2048]{2,1,0:T(8,128)(2,1)S(1)} %total.12), channel_id=1, source_target_pairs={{0,4},{1,5},{2,6},{3,7},{4,0},{5,1},{6,2},{7,3},{8,12},{9,13},{10,... | collective-permute-start | bytes 786440 | tf_op jit(solution)/shard_map/ppermute | solution.py:234
  84.2 12.2 %collective-permute-start.24 = (bf16[2,32,2048]{2,1,0:T(8,128)(2,1)S(1)}, bf16[2,32,2048]{2,1,0:T(8,128)(2,1)S(1)}, u32[]{:S(2)}, u32[]{:S(2)}) collective-permute-start(bf16[2,32,2048]{2,1,0:T(8,128)(2,1)S(1)} %total.10), channel_id=1, source_target_pairs={{0,2},{1,3},{2,0},{3,1},{4,6},{5,7},{6,4},{7,5},{8,10},{9,11},{10,... | collective-permute-start | bytes 786440 | tf_op jit(solution)/shard_map/ppermute | solution.py:237
  91.7 7.2 %collective-permute-start.26 = (bf16[2,32,2048]{2,1,0:T(8,128)(2,1)S(1)}, bf16[2,32,2048]{2,1,0:T(8,128)(2,1)S(1)}, u32[]{:S(2)}, u32[]{:S(2)}) collective-permute-start(bf16[2,32,2048]{2,1,0:T(8,128)(2,1)S(1)} %total.14), channel_id=1, source_target_pairs={{0,4},{1,5},{2,6},{3,7},{4,0},{5,1},{6,2},{7,3},{8,12},{9,13},{10,... | collective-permute-start | bytes 786440 | tf_op jit(solution)/shard_map/ppermute | solution.py:234
  92.1 14.3 %collective-permute-start.23 = (bf16[1,32,2048]{2,1,0:T(8,128)(2,1)S(1)}, bf16[1,32,2048]{2,1,0:T(8,128)(2,1)S(1)}, u32[]{:S(2)}, u32[]{:S(2)}) collective-permute-start(bf16[1,32,2048]{2,1,0:T(8,128)(2,1)S(1)} %total.13), channel_id=1, source_target_pairs={{0,12},{1,13},{2,14},{3,15},{4,8},{5,9},{6,10},{7,11},{8,4},{9,5},... | collective-permute-start | bytes 393224 | tf_op jit(solution)/shard_map/ppermute | solution.py:234
  99.0 10.3 %collective-permute-start.27 = (bf16[1,32,2048]{2,1,0:T(8,128)(2,1)S(1)}, bf16[1,32,2048]{2,1,0:T(8,128)(2,1)S(1)}, u32[]{:S(2)}, u32[]{:S(2)}) collective-permute-start(bf16[1,32,2048]{2,1,0:T(8,128)(2,1)S(1)} %total.15), channel_id=1, source_target_pairs={{0,12},{1,13},{2,14},{3,15},{4,8},{5,9},{6,10},{7,11},{8,4},{9,5},... | collective-permute-start | bytes 393224 | tf_op jit(solution)/shard_map/ppermute | solution.py:234

commit v7 on v6

--- a/solution.py
+++ b/solution.py
@@ -94,90 +94,93 @@
     return call(join_kernel, [a, b], [VMEM] * 2, [shape], name="join")[0]
 
 
-def ffn_kernel(owner_ref, scale_ref, gate_hbm, up_hbm, down_hbm, *refs):
-    x_refs, (mine_ref, other_ref, gate_ref, up_ref, down_ref, x_all, hidden, sems) = refs[:4], refs[4:]
-    width, ff = gate_ref.shape
+def load_kernel(*refs):
+    count = len(refs) // 2
+    copies = [pltpu.make_async_copy(refs[i], refs[count + i], refs[-1].at[i]) for i in range(count)]
+    for copy in copies:
+        copy.start()
+    for copy in copies:
+        copy.wait()
+
+
+def load(weights):
+    return call(
+        load_kernel,
+        weights,
+        [HBM] * len(weights),
+        [jax.ShapeDtypeStruct(w.shape, w.dtype) for w in weights],
+        [pltpu.SemaphoreType.DMA((len(weights),))],
+        name="load",
+    )
+
+
+def ffn_kernel(owner_ref, scale_ref, gate_ref, up_ref, down_ref, *refs):
+    x_refs, (mine_ref, other_ref, x_all, hidden) = refs[:-4], refs[-4:]
+    width, ff = gate_ref.shape[1:]
     group = ff // scale_ref.shape[1]
     step = 2 * group if ff % (2 * group) == 0 else group
-    steps = ff // step
-    copies = []
-    for i in range(steps):
-        cut = slice(i * step, (i + 1) * step)
-        copies.append(pltpu.make_async_copy(gate_hbm.at[0, :, cut], gate_ref.at[:, cut], sems.at[2 * i]))
-        copies.append(pltpu.make_async_copy(up_hbm.at[0, :, cut], up_ref.at[:, cut], sems.at[2 * i + 1]))
-    copies.append(pltpu.make_async_copy(down_hbm.at[0], down_ref, sems.at[2 * steps]))
-    for copy in copies:
-        copy.start()
-    pieces, part, full = x_refs[0].shape
-    rows = pieces * part
-    for i, x_ref in enumerate(x_refs):
-        x_all[i * rows : (i + 1) * rows, :] = x_ref[...].reshape(rows, full)
-    for i in range(steps):
-        cut = slice(i * step, (i + 1) * step)
+    _, pieces, part, _ = mine_ref.shape
+    at = 0
+    for x_ref in x_refs:
+        rows = x_ref.shape[0] * part
+        x_all[at : at + rows, :] = x_ref[...].reshape(rows, x_ref.shape[2])
+        at += rows
+    for f in range(0, ff, step):
         x = x_all[:, :width]
-        copies[2 * i].wait()
-        gate = jnp.dot(x, gate_ref[:, cut], preferred_element_type=jnp.float32)
-        copies[2 * i + 1].wait()
-        up = jnp.dot(x, up_ref[:, cut], preferred_element_type=jnp.float32)
+        gate = jnp.dot(x, gate_ref[0, :, f : f + step], preferred_element_type=jnp.float32)
+        up = jnp.dot(x, up_ref[0, :, f : f + step], preferred_element_type=jnp.float32)
         for at in range(0, step, group):
-            b = (i * step + at) // group
+            b = (f + at) // group
             g = gate[:, at : at + group] * scale_ref[0, b]
             u = up[:, at : at + group] * scale_ref[1, b]
             h = g / (1.0 + jnp.exp(-g)) * u * scale_ref[2, b]
-            hidden[:, i * step + at : i * step + at + group] = h.astype(jnp.bfloat16)
+            hidden[:, f + at : f + at + group] = h.astype(jnp.bfloat16)
     shares = x_all[:, width:].astype(jnp.float32)
     here = lax.broadcasted_iota(jnp.int32, shares.shape, 1) == owner_ref[0]
     weight = jnp.sum(jnp.where(here, shares, 0.0), axis=1, keepdims=True)
-    copies[2 * steps].wait()
     cols = 512 if width % 512 == 0 else LANES
     for n in range(0, width, cols):
-        out = jnp.dot(hidden[...], down_ref[:, n : n + cols], preferred_element_type=jnp.float32)
+        out = jnp.dot(hidden[...], down_ref[0, :, n : n + cols], preferred_element_type=jnp.float32)
         out = (out * weight).astype(jnp.bfloat16).reshape(4, pieces, part, cols)
         mine_ref[:, :, :, n : n + cols] = out[:2]
         other_ref[:, :, :, n : n + cols] = out[2:]
 
 
 def ffn(xs, owner, scales, weights):
-    pieces, part, full = xs[0].shape
+    pieces = sum(x.shape[0] for x in xs) // 4
+    _, part, full = xs[0].shape
     width, ff = weights[0].shape[1:]
     rows = 4 * pieces * part
     return call(
         ffn_kernel,
         [owner, scales, *weights, *xs],
-        [SMEM, SMEM] + [HBM] * 3 + [VMEM] * 4,
+        [SMEM, SMEM] + [VMEM] * (3 + len(xs)),
         [jax.ShapeDtypeStruct((2, pieces, part, width), jnp.bfloat16)] * 2,
-        [
-            pltpu.VMEM((width, ff), jnp.bfloat16),
-            pltpu.VMEM((width, ff), jnp.bfloat16),
-            pltpu.VMEM((ff, width), jnp.bfloat16),
-            pltpu.VMEM((rows, full), jnp.bfloat16),
-            pltpu.VMEM((rows, ff), jnp.bfloat16),
-            pltpu.SemaphoreType.DMA((2 * (ff // LANES) + 1,)),
-        ],
+        [pltpu.VMEM((rows, full), jnp.bfloat16), pltpu.VMEM((rows, ff), jnp.bfloat16)],
         name="ffn",
-        vmem=28,
+        vmem=16,
     )
 
 
-def view(ref, slot):
-    return ref if slot is None else ref.at[slot]
-
-
-def total_kernel(slots, low, *refs):
+def piece_of(ref, slot, piece):
+    return ref[piece] if slot is None else ref[slot, piece]
+
+
+def total_kernel(terms, low, *refs):
     out_ref = refs[-1]
     for piece in range(out_ref.shape[0]):
         total = None
-        for slot, ref in zip(slots, refs[:-1]):
-            term = view(ref, slot)[low + piece].astype(jnp.float32)
+        for (slot, first), ref in zip(terms, refs[:-1]):
+            term = piece_of(ref, slot, low + piece - first).astype(jnp.float32)
             total = term if total is None else total + term
         out_ref[piece] = total.astype(out_ref.dtype)
 
 
 def total(terms, low, high):
-    arrays = [a for a, _ in terms]
+    arrays = [a for a, _, _ in terms]
     shape = jax.ShapeDtypeStruct((high - low, *arrays[0].shape[-2:]), arrays[0].dtype)
     return call(
-        functools.partial(total_kernel, [slot for _, slot in terms], low),
+        functools.partial(total_kernel, [where for _, *where in terms], low),
         arrays,
         [VMEM] * len(arrays),
         [shape],
@@ -185,20 +188,20 @@
     )[0]
 
 
-def finish_kernel(slots, hidden_ref, *refs):
+def finish_kernel(terms, hidden_ref, *refs):
     out_ref = refs[-1]
     for batch in range(hidden_ref.shape[0]):
         mixed = None
-        for i, slot in enumerate(slots):
-            term = view(refs[batch * len(slots) + i], slot)[0].astype(jnp.float32)
+        for i, (slot, first) in enumerate(terms):
+            term = piece_of(refs[batch * len(terms) + i], slot, -first).astype(jnp.float32)
             mixed = term if mixed is None else mixed + term
         out_ref[batch] = (hidden_ref[batch].astype(jnp.float32) + mixed).astype(out_ref.dtype)
 
 
 def finish(hidden_in, terms):
-    arrays = [a for batch in terms for a, _ in batch]
-    return call(
-        functools.partial(finish_kernel, [slot for _, slot in terms[0]]),
+    arrays = [a for batch in terms for a, _, _ in batch]
+    return call(
+        functools.partial(finish_kernel, [where for _, *where in terms[0]]),
         [hidden_in, *arrays],
         [VMEM] * (1 + len(arrays)),
         [jax.ShapeDtypeStruct(hidden_in.shape, hidden_in.dtype)],
@@ -219,7 +222,7 @@
 ):
     owners = lax.axis_size("ep")
     batches = hidden_in.shape[0]
-    weights = (gate_weight, up_weight, down_weight)
+    weights = load([gate_weight, up_weight, down_weight])
     scales = jnp.exp2(exponent_table[0].astype(jnp.float32))
     owner = lax.axis_index("ep").astype(jnp.int32).reshape(1)
 
@@ -247,42 +250,58 @@
             rows = after(rows, near[-1])
         span = line
         while span > 2:
-            rows = join(rows, mirror(rows, span))
+            received = mirror(rows, span)
+            if not batch:
+                received = after(received, *weights)
+            rows = join(rows, received)
             if batch:
                 rows = after(rows, far[-1])
             span //= 2
         near.append(rows)
-        far.append(mirror(rows, 2))
-
-    def expert(rows, there, *others):
-        xs = [rows, there, to_core(rows), to_core(there)]
-        mine, other = ffn([after(xs[0], *others), *xs[1:]], owner, scales, weights)
+        if not batch:
+            near_there = to_mid(rows)
+        far.append(mirror(rows if not batch else after(rows, near_there), 2))
+
+    here, there = [], []
+    for batch in range(batches):
+        if batch == 0:
+            here.append([near[0], far[0]])
+            there.append([near_there, to_mid(far[0])])
+        else:
+            here.append([join(near[batch], far[batch])])
+            there.append([to_mid(here[batch][0])])
+    if batches > 1:
+        there[0][0] = after(there[0][0], near[1])
+
+    terms, sent, back = [], [], []
+    for batch in range(batches):
+        xs = here[batch] + there[batch] + [to_core(rows) for rows in here[batch] + there[batch]]
+        xs[0] = after(xs[0], far[-1], *sent[-1:])
+        mine, other = ffn(xs, owner, scales, weights)
+        if batch + 1 < batches:
+            other = after(other, *there[batch + 1])
+        if batch:
+            other = after(other, back[-1][0])
         other = to_core(other)
-        sent.append(total([(mine, 1), (other, 1)], 0, half))
-        back.append(to_mid(sent[-1]))
-        return [(mine, 0), (other, 0), (back[-1], None)]
-
-    near_terms, far_terms, sent, back = [], [], [], []
-    near_there = [to_mid(rows) for rows in near]
-    far_there = [to_mid(rows) for rows in far]
+        own = [(mine, 1, 0), (other, 1, 0)]
+        if batch + 1 < batches:
+            sent.append(total(own, 0, line))
+            back.append([to_mid(sent[-1])])
+        else:
+            sent.append(total(own, half, line))
+            back.append([to_mid(total(own, 0, half)), to_mid(sent[-1])])
+        terms.append([(mine, 0, 0), (other, 0, 0)])
+
     for batch in range(batches):
-        there = near_there[batch]
-        if batch + 1 < batches:
-            there = after(there, near[batch + 1])
-        near_terms.append(expert(near[batch], there, far[-1], *sent[-1:], *back[-2:-1]))
-        far_terms.append(expert(far[batch], far_there[batch], *sent[-1:], *back[-2:-1]))
-
-    for batch in range(batches):
-        terms = near_terms[batch]
-        last = far_terms[batch]
-        if batch + 1 < batches:
-            last = [*last[:-1], (after(last[-1][0], sent[-1]), None)]
-        terms.append((mirror(total(last, 0, half), 2), None))
+        near_back, far_back = back[batch][0], back[batch][-1]
+        far_sum = total([*terms[batch], (far_back, None, line - far_back.shape[0])], half, line)
+        terms[batch] += [(near_back, None, 0), (mirror(far_sum, 2), None, 0)]
         span, pieces = 4, half
         while pieces > 1:
-            terms.append((mirror(total(terms, pieces // 2, pieces), span), None))
+            part = total(terms[batch], pieces // 2, pieces)
+            terms[batch].append((mirror(part, span), None, 0))
             span, pieces = span * 2, pieces // 2
-    return finish(hidden_in, near_terms)
+    return finish(hidden_in, terms)
 
 
 def solution(mesh):

time: 110 us -> 92.6 us (0.84)
  Pallas kernels: 31.7 us -> 20.3 us
  starting transfers between devices: 33.7 us -> 23.6 us
  local copies, waits for them, and re-layouts: 0.01 us -> 7.11 us
  waiting for transfers between devices: 44 us -> 41.1 us
    pallas_call x16 -> x15, Pallas kernels: 31.7 us -> 20.3 us  [call(): pl.pallas_call(kernel, out_shape=shapes, in_specs=specs, out_specs=[VMEM]...]
    ppermute x8 -> x6, waiting for transfers between devices: 21.5 us -> 12.9 us  [to_mid(): return lax.ppermute(rows, 'ep', [(i, i ^ 2) for i in range(owners)])]
    unnamed x3 -> x13, local copies, waits for them, and re-layouts: 0.01 us -> 7.11 us
    ppermute x8, starting transfers between devices: 22.2 us -> 15.4 us  [mirror(): return lax.ppermute(rows, 'ep', [(i, partner(i)) for i in range(owners)])]
    ppermute x12 -> x8, waiting for transfers between devices: 2.69 us -> 7.74 us  [to_core(): return lax.ppermute(rows, 'ep', [(i, i ^ 1) for i in range(owners)])]
    ppermute x8 -> x6, starting transfers between devices: 9.43 us -> 6.53 us  [to_mid(): return lax.ppermute(rows, 'ep', [(i, i ^ 2) for i in range(owners)])]
  transfers between devices with their start and end apart: 28 -> 22, of which waited for: 13 -> 17; matrix products, arithmetic and copies ran while one was open for 1% -> 0% of each run, Pallas kernels for 20% -> 20%
where the time goes in v7:
time: 92.6 us; the launch traced here: 92.3 us
  waiting for transfers between devices  41.1 us (44%)
  starting transfers between devices  23.6 us (25%)
  Pallas kernels  20.3 us (22%)
  local copies, waits for them, and re-layouts  7.11 us (8%)
    ppermute x8, waiting for transfers between devices, mirror(): return lax.ppermute(rows, 'ep', [(i, partner(i)) for i in range(owners)])  20.4 us
    pallas_call x15, Pallas kernels, call(): pl.pallas_call(kernel, out_shape=shapes, in_specs=specs, out_specs=[VMEM]...  20.3 us
    ppermute x8, starting transfers between devices, mirror(): return lax.ppermute(rows, 'ep', [(i, partner(i)) for i in range(owners)])  15.4 us
    ppermute x6, waiting for transfers between devices, to_mid(): return lax.ppermute(rows, 'ep', [(i, i ^ 2) for i in range(owners)])  12.9 us
    ppermute x8, waiting for transfers between devices, to_core(): return lax.ppermute(rows, 'ep', [(i, i ^ 1) for i in range(owners)])  7.74 us
    unnamed x13, local copies, waits for them, and re-layouts  7.11 us
    ppermute x6, starting transfers between devices, to_mid(): return lax.ppermute(rows, 'ep', [(i, i ^ 2) for i in range(owners)])  6.53 us
  transfers between devices with their start and end apart: 22, of which 17 were waited for; matrix products, arithmetic and copies ran while one was open for 0% of the time, Pallas kernels for 20%

profile of v7, /device:TPU:0, one launch (start us, length us, event | category | flops | bytes accessed | tf_op | source)
XLA Modules:
  0.0 92.3 jit_solution(10715614840989897018)
XLA Ops:
  0.0 1.2 %prepare.1 = (bf16[1,32,2176]{2,1,0:T(8,128)(2,1)S(1)}, bf16[1,32,2176]{2,1,0:T(8,128)(2,1)S(1)}) custom-call(bf16[2,32,2048]{2,1,0:T(8,128)(2,1)} %hidden_ref.1, s32[2,8,32]{2,1,0:T(8,128)} %bitcast.9, s32[2,8,32]{2,1,0:T(8,128)} %bitcast.10, f32[1,2048]{1,0:T(1,128)} %bitcast.11), custom_call_target="tpu_custom_call" | custom-call | tf_op jit(solution)/shard_map/prepare/pallas_call | solution.py:26
  1.2 5.1 %collective-permute-start = (bf16[1,32,2176]{2,1,0:T(8,128)(2,1)S(1)}, bf16[1,32,2176]{2,1,0:T(8,128)(2,1)S(1)}, u32[]{:S(2)}, u32[]{:S(2)}) collective-permute-start(bf16[1,32,2176]{2,1,0:T(8,128)(2,1)S(1)} %get-tuple-element.26.refs_0_), channel_id=1, source_target_pairs={{0,12},{1,13},{2,14},{3,15},{4,8},{5,9},{6,10},{7,11},{8,4},{9,5},... | collective-permute-start | bytes 417800 | tf_op jit(solution)/shard_map/ppermute | solution.py:237
  6.4 3.8 %load.1 = (bf16[1,2048,768]{2,1,0:T(8,128)(2,1)S(1)}, bf16[1,2048,768]{2,1,0:T(8,128)(2,1)S(1)}, bf16[1,768,2048]{2,1,0:T(8,128)(2,1)S(1)}) custom-call(bf16[1,2048,768]{2,1,0:T(8,128)(2,1)} %refs_0_.1, bf16[1,2048,768]{2,1,0:T(8,128)(2,1)} %refs_1_.1, bf16[1,768,2048]{2,1,0:T(8,128)(2,1)} %refs_2_.1), custom_call_target="tpu_custom_call" | custom-call | tf_op jit(solution)/shard_map/load/pallas_call | solution.py:26
  10.2 1.6 %copy-done = bf16[1,2048,768]{2,1,0:T(8,128)(2,1)} copy-done((bf16[1,2048,768]{2,1,0:T(8,128)(2,1)}, bf16[1,2048,768]{2,1,0:T(8,128)(2,1)S(1)}, u32[]{:S(2)}) %copy-start) | copy-done | bytes 3145752
  11.8 1.7 %copy-done.2 = bf16[1,768,2048]{2,1,0:T(8,128)(2,1)} copy-done((bf16[1,768,2048]{2,1,0:T(8,128)(2,1)}, bf16[1,768,2048]{2,1,0:T(8,128)(2,1)S(1)}, u32[]{:S(2)}) %copy-start.2) | copy-done | bytes 3145752
  13.6 1.6 %collective-permute-start.3 = (bf16[2,32,2176]{2,1,0:T(8,128)(2,1)S(1)}, bf16[2,32,2176]{2,1,0:T(8,128)(2,1)}, u32[]{:S(2)}, u32[]{:S(2)}) collective-permute-start(bf16[2,32,2176]{2,1,0:T(8,128)(2,1)S(1)} %join.3.refs_0_), channel_id=1, source_target_pairs={{0,2},{1,3},{2,0},{3,1},{4,6},{5,7},{6,4},{7,5},{8,10},{9,11},{10,... | collective-permute-start | bytes 835592 | tf_op jit(solution)/shard_map/ppermute | solution.py:240
  15.2 1.6 %collective-permute-start.1 = (bf16[1,32,2176]{2,1,0:T(8,128)(2,1)S(1)}, bf16[1,32,2176]{2,1,0:T(8,128)(2,1)S(1)}, u32[]{:S(2)}, u32[]{:S(2)}) collective-permute-start(bf16[1,32,2176]{2,1,0:T(8,128)(2,1)S(1)} %get-tuple-element.29.refs_0_), channel_id=1, source_target_pairs={{0,12},{1,13},{2,14},{3,15},{4,8},{5,9},{6,10},{7,11},{8,4},{9,5},... | collective-permute-start | bytes 417800 | tf_op jit(solution)/shard_map/ppermute | solution.py:237
  16.8 6.9 %collective-permute-done.1.refs_1_ = bf16[1,32,2176]{2,1,0:T(8,128)(2,1)S(1)} collective-permute-done((bf16[1,32,2176]{2,1,0:T(8,128)(2,1)S(1)}, bf16[1,32,2176]{2,1,0:T(8,128)(2,1)S(1)}, u32[]{:S(2)}, u32[]{:S(2)}) %collective-permute-start.1) | collective-permute-done | bytes 139296 | tf_op jit(solution)/shard_map/ppermute | solution.py:237
  23.7 1.2 %collective-permute-done.2.refs_1_ = bf16[2,32,2176]{2,1,0:T(8,128)(2,1)} collective-permute-done((bf16[2,32,2176]{2,1,0:T(8,128)(2,1)S(1)}, bf16[2,32,2176]{2,1,0:T(8,128)(2,1)}, u32[]{:S(2)}, u32[]{:S(2)}) %collective-permute-start.2) | collective-permute-done | bytes 278560 | tf_op jit(solution)/shard_map/ppermute | solution.py:237
  25.0 1.4 %collective-permute-start.5 = (bf16[2,32,2176]{2,1,0:T(8,128)(2,1)}, bf16[2,32,2176]{2,1,0:T(8,128)(2,1)}, u32[]{:S(2)}, u32[]{:S(2)}) collective-permute-start(bf16[2,32,2176]{2,1,0:T(8,128)(2,1)} %collective-permute-done.2.refs_1_), channel_id=1, source_target_pairs={{0,2},{1,3},{2,0},{3,1},{4,6},{5,7},{6,4},{7,5},{8,10},{9,11},{10,... | collective-permute-start | bytes 835592 | tf_op jit(solution)/shard_map/ppermute | solution.py:240
  26.4 5.1 %collective-permute-done.4.refs_1_ = bf16[2,32,2176]{2,1,0:T(8,128)(2,1)S(1)} collective-permute-done((bf16[2,32,2176]{2,1,0:T(8,128)(2,1)S(1)}, bf16[2,32,2176]{2,1,0:T(8,128)(2,1)S(1)}, u32[]{:S(2)}, u32[]{:S(2)}) %collective-permute-start.4) | collective-permute-done | bytes 278560 | tf_op jit(solution)/shard_map/ppermute | solution.py:237
  31.5 0.9 join.5.refs_0_
  32.4 1.4 %collective-permute-start.10 = (bf16[4,32,2176]{2,1,0:T(8,128)(2,1)}, bf16[4,32,2176]{2,1,0:T(8,128)(2,1)}, u32[]{:S(2)}, u32[]{:S(2)}) collective-permute-start(bf16[4,32,2176]{2,1,0:T(8,128)(2,1)} %join.5.refs_0_), channel_id=1, source_target_pairs={{0,2},{1,3},{2,0},{3,1},{4,6},{5,7},{6,4},{7,5},{8,10},{9,11},{10,... | collective-permute-start | bytes 1671176 | tf_op jit(solution)/shard_map/ppermute | solution.py:240
  34.8 1.0 %collective-permute-done.6.refs_4_ = bf16[2,32,2176]{2,1,0:T(8,128)(2,1)} collective-permute-done((bf16[2,32,2176]{2,1,0:T(8,128)(2,1)S(1)}, bf16[2,32,2176]{2,1,0:T(8,128)(2,1)}, u32[]{:S(2)}, u32[]{:S(2)}) %collective-permute-start.6) | collective-permute-done | bytes 278560 | tf_op jit(solution)/shard_map/ppermute | solution.py:243
  36.9 1.9 %copy-done.1 = bf16[1,2048,768]{2,1,0:T(8,128)(2,1)S(1)} copy-done((bf16[1,2048,768]{2,1,0:T(8,128)(2,1)S(1)}, bf16[1,2048,768]{2,1,0:T(8,128)(2,1)}, u32[]{:S(2)}) %copy-start.1) | copy-done | bytes 3145752
  38.8 1.9 %copy-done.3 = bf16[1,768,2048]{2,1,0:T(8,128)(2,1)S(1)} copy-done((bf16[1,768,2048]{2,1,0:T(8,128)(2,1)S(1)}, bf16[1,768,2048]{2,1,0:T(8,128)(2,1)}, u32[]{:S(2)}) %copy-start.3) | copy-done | bytes 3145752
  40.7 6.6 %ffn.2 = (bf16[2,4,32,2048]{3,2,1,0:T(8,128)(2,1)S(1)}, bf16[2,4,32,2048]{3,2,1,0:T(8,128)(2,1)S(1)}) custom-call(s32[1]{0:T(128)} %bitcast.owner_ref, f32[3,6]{1,0:T(4,128)S(1)} %bitcast.7, bf16[1,2048,768]{2,1,0:T(8,128)(2,1)S(1)} %get-tuple-element.23.gate_ref, bf16[1,2048,768]{2,1,0:T(8,128)(2,1)S(1)} %copy-done.1, bf16[1,768,2048]{2,1,0:T(8,128)(2,1)S(1)} %copy-done.3, ...), custom_call_target="tpu_custom_call" | custom-call | tf_op jit(solution)/shard_map/ffn/pallas_call | solution.py:26
  48.0 2.2 %collective-permute-done.11.refs_1_ = bf16[2,4,32,2048]{3,2,1,0:T(8,128)(2,1)S(1)} collective-permute-done((bf16[2,4,32,2048]{3,2,1,0:T(8,128)(2,1)S(1)}, bf16[2,4,32,2048]{3,2,1,0:T(8,128)(2,1)S(1)}, u32[]{:S(2)}, u32[]{:S(2)}) %collective-permute-start.11) | collective-permute-done | bytes 1048608 | tf_op jit(solution)/shard_map/ppermute | solution.py:243
  51.8 6.4 %ffn.3 = (bf16[2,4,32,2048]{3,2,1,0:T(8,128)(2,1)S(1)}, bf16[2,4,32,2048]{3,2,1,0:T(8,128)(2,1)S(1)}) custom-call(s32[1]{0:T(128)} %bitcast.owner_ref, f32[3,6]{1,0:T(4,128)S(1)} %bitcast.8, bf16[1,2048,768]{2,1,0:T(8,128)(2,1)S(1)} %get-tuple-element.23.gate_ref, bf16[1,2048,768]{2,1,0:T(8,128)(2,1)S(1)} %copy-done.1, bf16[1,768,2048]{2,1,0:T(8,128)(2,1)S(1)} %copy-done.3, ...), custom_call_target="tpu_custom_call" | custom-call | tf_op jit(solution)/shard_map/ffn/pallas_call | solution.py:26
  58.2 6.1 %collective-permute-done.12.refs_2_ = bf16[4,32,2048]{2,1,0:T(8,128)(2,1)S(1)} collective-permute-done((bf16[4,32,2048]{2,1,0:T(8,128)(2,1)S(1)}, bf16[4,32,2048]{2,1,0:T(8,128)(2,1)S(1)}, u32[]{:S(2)}, u32[]{:S(2)}) %collective-permute-start.12) | collective-permute-done | bytes 524320 | tf_op jit(solution)/shard_map/ppermute | solution.py:240
  64.3 2.7 %collective-permute-done.17.refs_1_.refs_6_ = bf16[2,4,32,2048]{3,2,1,0:T(8,128)(2,1)S(1)} collective-permute-done((bf16[2,4,32,2048]{3,2,1,0:T(8,128)(2,1)S(1)}, bf16[2,4,32,2048]{3,2,1,0:T(8,128)(2,1)S(1)}, u32[]{:S(2)}, u32[]{:S(2)}) %collective-permute-start.17) | collective-permute-done | bytes 1048608 | tf_op jit(solution)/shard_map/ppermute | solution.py:243
  67.8 2.0 %collective-permute-start.13 = (bf16[2,32,2048]{2,1,0:T(8,128)(2,1)S(1)}, bf16[2,32,2048]{2,1,0:T(8,128)(2,1)S(1)}, u32[]{:S(2)}, u32[]{:S(2)}) collective-permute-start(bf16[2,32,2048]{2,1,0:T(8,128)(2,1)S(1)} %total.8), channel_id=1, source_target_pairs={{0,4},{1,5},{2,6},{3,7},{4,0},{5,1},{6,2},{7,3},{8,12},{9,13},{10,... | collective-permute-start | bytes 786440 | tf_op jit(solution)/shard_map/ppermute | solution.py:237
  69.8 0.8 collective-permute-start.18
  70.7 5.6 %collective-permute-done.19.refs_2_ = bf16[2,32,2048]{2,1,0:T(8,128)(2,1)S(1)} collective-permute-done((bf16[2,32,2048]{2,1,0:T(8,128)(2,1)S(1)}, bf16[2,32,2048]{2,1,0:T(8,128)(2,1)S(1)}, u32[]{:S(2)}, u32[]{:S(2)}) %collective-permute-start.19) | collective-permute-done | bytes 262176 | tf_op jit(solution)/shard_map/ppermute | solution.py:240
  76.4 1.3 %collective-permute-start.20 = (bf16[2,32,2048]{2,1,0:T(8,128)(2,1)S(1)}, bf16[2,32,2048]{2,1,0:T(8,128)(2,1)S(1)}, u32[]{:S(2)}, u32[]{:S(2)}) collective-permute-start(bf16[2,32,2048]{2,1,0:T(8,128)(2,1)S(1)} %total.12), channel_id=1, source_target_pairs={{0,4},{1,5},{2,6},{3,7},{4,0},{5,1},{6,2},{7,3},{8,12},{9,13},{10,... | collective-permute-start | bytes 786440 | tf_op jit(solution)/shard_map/ppermute | solution.py:237
  77.8 2.1 %collective-permute-start.14 = (bf16[1,32,2048]{2,1,0:T(8,128)(2,1)S(1)}, bf16[1,32,2048]{2,1,0:T(8,128)(2,1)S(1)}, u32[]{:S(2)}, u32[]{:S(2)}) collective-permute-start(bf16[1,32,2048]{2,1,0:T(8,128)(2,1)S(1)} %total.9), channel_id=1, source_target_pairs={{0,12},{1,13},{2,14},{3,15},{4,8},{5,9},{6,10},{7,11},{8,4},{9,5},... | collective-permute-start | bytes 393224 | tf_op jit(solution)/shard_map/ppermute | solution.py:237
  79.8 1.2 %collective-permute-done.18.refs_2_.refs_7_ = bf16[2,32,2048]{2,1,0:T(8,128)(2,1)S(1)} collective-permute-done((bf16[2,32,2048]{2,1,0:T(8,128)(2,1)S(1)}, bf16[2,32,2048]{2,1,0:T(8,128)(2,1)S(1)}, u32[]{:S(2)}, u32[]{:S(2)}) %collective-permute-start.18) | collective-permute-done | bytes 262176 | tf_op jit(solution)/shard_map/ppermute | solution.py:240
  81.1 3.4 %collective-permute-done.20.refs_3_.refs_8_ = bf16[2,32,2048]{2,1,0:T(8,128)(2,1)S(1)} collective-permute-done((bf16[2,32,2048]{2,1,0:T(8,128)(2,1)S(1)}, bf16[2,32,2048]{2,1,0:T(8,128)(2,1)S(1)}, u32[]{:S(2)}, u32[]{:S(2)}) %collective-permute-start.20) | collective-permute-done | bytes 262176 | tf_op jit(solution)/shard_map/ppermute | solution.py:237
  84.5 3.1 %collective-permute-start.21 = (bf16[1,32,2048]{2,1,0:T(8,128)(2,1)S(1)}, bf16[1,32,2048]{2,1,0:T(8,128)(2,1)S(1)}, u32[]{:S(2)}, u32[]{:S(2)}) collective-permute-start(bf16[1,32,2048]{2,1,0:T(8,128)(2,1)S(1)} %total.13), channel_id=1, source_target_pairs={{0,12},{1,13},{2,14},{3,15},{4,8},{5,9},{6,10},{7,11},{8,4},{9,5},... | collective-permute-start | bytes 393224 | tf_op jit(solution)/shard_map/ppermute | solution.py:237
  87.6 1.0 %collective-permute-done.14.refs_4_ = bf16[1,32,2048]{2,1,0:T(8,128)(2,1)S(1)} collective-permute-done((bf16[1,32,2048]{2,1,0:T(8,128)(2,1)S(1)}, bf16[1,32,2048]{2,1,0:T(8,128)(2,1)S(1)}, u32[]{:S(2)}, u32[]{:S(2)}) %collective-permute-start.14) | collective-permute-done | bytes 131104 | tf_op jit(solution)/shard_map/ppermute | solution.py:237
  88.7 2.8 %collective-permute-done.21.refs_9_ = bf16[1,32,2048]{2,1,0:T(8,128)(2,1)S(1)} collective-permute-done((bf16[1,32,2048]{2,1,0:T(8,128)(2,1)S(1)}, bf16[1,32,2048]{2,1,0:T(8,128)(2,1)S(1)}, u32[]{:S(2)}, u32[]{:S(2)}) %collective-permute-start.21) | collective-permute-done | bytes 131104 | tf_op jit(solution)/shard_map/ppermute | solution.py:237
  91.4 0.9 finish.1
  (41 shorter events, 5.7 us)
Async XLA Ops:
  1.2 33.6 %copy-start.5 = (s32[1,3,6]{2,0,1:T(1,128)S(1)}, s32[1,3,6]{2,0,1:T(1,128)}, u32[]{:S(2)}) copy-start(s32[1,3,6]{2,0,1:T(1,128)} %param.15) | copy-start | bytes 220
  1.2 12.2 %collective-permute-start = (bf16[1,32,2176]{2,1,0:T(8,128)(2,1)S(1)}, bf16[1,32,2176]{2,1,0:T(8,128)(2,1)S(1)}, u32[]{:S(2)}, u32[]{:S(2)}) collective-permute-start(bf16[1,32,2176]{2,1,0:T(8,128)(2,1)S(1)} %get-tuple-element.26.refs_0_), channel_id=1, source_target_pairs={{0,12},{1,13},{2,14},{3,15},{4,8},{5,9},{6,10},{7,11},{8,4},{9,5},... | collective-permute-start | bytes 417800 | tf_op jit(solution)/shard_map/ppermute | solution.py:237
  10.1 1.6 %copy-start = (bf16[1,2048,768]{2,1,0:T(8,128)(2,1)}, bf16[1,2048,768]{2,1,0:T(8,128)(2,1)S(1)}, u32[]{:S(2)}) copy-start(bf16[1,2048,768]{2,1,0:T(8,128)(2,1)S(1)} %get-tuple-element.24.up_ref) | copy-start | bytes 9437188
  11.8 1.7 %copy-start.2 = (bf16[1,768,2048]{2,1,0:T(8,128)(2,1)}, bf16[1,768,2048]{2,1,0:T(8,128)(2,1)S(1)}, u32[]{:S(2)}) copy-start(bf16[1,768,2048]{2,1,0:T(8,128)(2,1)S(1)} %get-tuple-element.25.down_ref) | copy-start | bytes 9437188
  13.5 11.5 %collective-permute-start.2 = (bf16[2,32,2176]{2,1,0:T(8,128)(2,1)S(1)}, bf16[2,32,2176]{2,1,0:T(8,128)(2,1)}, u32[]{:S(2)}, u32[]{:S(2)}) collective-permute-start(bf16[2,32,2176]{2,1,0:T(8,128)(2,1)S(1)} %join.3.refs_0_), channel_id=1, source_target_pairs={{0,4},{1,5},{2,6},{3,7},{4,0},{5,1},{6,2},{7,3},{8,12},{9,13},{10,... | collective-permute-start | bytes 835592 | tf_op jit(solution)/shard_map/ppermute | solution.py:237
  13.6 11.4 %collective-permute-start.3 = (bf16[2,32,2176]{2,1,0:T(8,128)(2,1)S(1)}, bf16[2,32,2176]{2,1,0:T(8,128)(2,1)}, u32[]{:S(2)}, u32[]{:S(2)}) collective-permute-start(bf16[2,32,2176]{2,1,0:T(8,128)(2,1)S(1)} %join.3.refs_0_), channel_id=1, source_target_pairs={{0,2},{1,3},{2,0},{3,1},{4,6},{5,7},{6,4},{7,5},{8,10},{9,11},{10,... | collective-permute-start | bytes 835592 | tf_op jit(solution)/shard_map/ppermute | solution.py:240
  15.2 8.5 %collective-permute-start.1 = (bf16[1,32,2176]{2,1,0:T(8,128)(2,1)S(1)}, bf16[1,32,2176]{2,1,0:T(8,128)(2,1)S(1)}, u32[]{:S(2)}, u32[]{:S(2)}) collective-permute-start(bf16[1,32,2176]{2,1,0:T(8,128)(2,1)S(1)} %get-tuple-element.29.refs_0_), channel_id=1, source_target_pairs={{0,12},{1,13},{2,14},{3,15},{4,8},{5,9},{6,10},{7,11},{8,4},{9,5},... | collective-permute-start | bytes 417800 | tf_op jit(solution)/shard_map/ppermute | solution.py:237
  25.0 6.5 %collective-permute-start.4 = (bf16[2,32,2176]{2,1,0:T(8,128)(2,1)S(1)}, bf16[2,32,2176]{2,1,0:T(8,128)(2,1)S(1)}, u32[]{:S(2)}, u32[]{:S(2)}) collective-permute-start(bf16[2,32,2176]{2,1,0:T(8,128)(2,1)S(1)} %join.4.refs_0_), channel_id=1, source_target_pairs={{0,4},{1,5},{2,6},{3,7},{4,0},{5,1},{6,2},{7,3},{8,12},{9,13},{10,... | collective-permute-start | bytes 835592 | tf_op jit(solution)/shard_map/ppermute | solution.py:237
  25.0 9.3 %collective-permute-start.5 = (bf16[2,32,2176]{2,1,0:T(8,128)(2,1)}, bf16[2,32,2176]{2,1,0:T(8,128)(2,1)}, u32[]{:S(2)}, u32[]{:S(2)}) collective-permute-start(bf16[2,32,2176]{2,1,0:T(8,128)(2,1)} %collective-permute-done.2.refs_1_), channel_id=1, source_target_pairs={{0,2},{1,3},{2,0},{3,1},{4,6},{5,7},{6,4},{7,5},{8,10},{9,11},{10,... | collective-permute-start | bytes 835592 | tf_op jit(solution)/shard_map/ppermute | solution.py:240
  32.4 14.9 %collective-permute-start.10 = (bf16[4,32,2176]{2,1,0:T(8,128)(2,1)}, bf16[4,32,2176]{2,1,0:T(8,128)(2,1)}, u32[]{:S(2)}, u32[]{:S(2)}) collective-permute-start(bf16[4,32,2176]{2,1,0:T(8,128)(2,1)} %join.5.refs_0_), channel_id=1, source_target_pairs={{0,2},{1,3},{2,0},{3,1},{4,6},{5,7},{6,4},{7,5},{8,10},{9,11},{10,... | collective-permute-start | bytes 1671176 | tf_op jit(solution)/shard_map/ppermute | solution.py:240
  33.8 2.1 %collective-permute-start.6 = (bf16[2,32,2176]{2,1,0:T(8,128)(2,1)S(1)}, bf16[2,32,2176]{2,1,0:T(8,128)(2,1)}, u32[]{:S(2)}, u32[]{:S(2)}) collective-permute-start(bf16[2,32,2176]{2,1,0:T(8,128)(2,1)S(1)} %join.3.refs_0_), channel_id=1, source_target_pairs={{0,1},{1,0},{2,3},{3,2},{4,5},{5,4},{6,7},{7,6},{8,9},{9,8},{10,11... | collective-permute-start | bytes 835592 | tf_op jit(solution)/shard_map/ppermute | solution.py:243
  33.8 2.3 %collective-permute-start.8 = (bf16[2,32,2176]{2,1,0:T(8,128)(2,1)}, bf16[2,32,2176]{2,1,0:T(8,128)(2,1)}, u32[]{:S(2)}, u32[]{:S(2)}) collective-permute-start(bf16[2,32,2176]{2,1,0:T(8,128)(2,1)} %collective-permute-done.3.refs_2_), channel_id=1, source_target_pairs={{0,1},{1,0},{2,3},{3,2},{4,5},{5,4},{6,7},{7,6},{8,9},{9,8},{10,11... | collective-permute-start | bytes 835592 | tf_op jit(solution)/shard_map/ppermute | solution.py:243
  34.3 2.2 %collective-permute-start.7 = (bf16[2,32,2176]{2,1,0:T(8,128)(2,1)}, bf16[2,32,2176]{2,1,0:T(8,128)(2,1)}, u32[]{:S(2)}, u32[]{:S(2)}) collective-permute-start(bf16[2,32,2176]{2,1,0:T(8,128)(2,1)} %collective-permute-done.2.refs_1_), channel_id=1, source_target_pairs={{0,1},{1,0},{2,3},{3,2},{4,5},{5,4},{6,7},{7,6},{8,9},{9,8},{10,11... | collective-permute-start | bytes 835592 | tf_op jit(solution)/shard_map/ppermute | solution.py:243
  34.3 2.6 %collective-permute-start.9 = (bf16[2,32,2176]{2,1,0:T(8,128)(2,1)}, bf16[2,32,2176]{2,1,0:T(8,128)(2,1)}, u32[]{:S(2)}, u32[]{:S(2)}) collective-permute-start(bf16[2,32,2176]{2,1,0:T(8,128)(2,1)} %collective-permute-done.5.refs_3_), channel_id=1, source_target_pairs={{0,1},{1,0},{2,3},{3,2},{4,5},{5,4},{6,7},{7,6},{8,9},{9,8},{10,11... | collective-permute-start | bytes 835592 | tf_op jit(solution)/shard_map/ppermute | solution.py:243
  36.9 1.9 %copy-start.1 = (bf16[1,2048,768]{2,1,0:T(8,128)(2,1)S(1)}, bf16[1,2048,768]{2,1,0:T(8,128)(2,1)}, u32[]{:S(2)}) copy-start(bf16[1,2048,768]{2,1,0:T(8,128)(2,1)} %copy-done) | copy-start | bytes 9437188
  38.8 1.9 %copy-start.3 = (bf16[1,768,2048]{2,1,0:T(8,128)(2,1)S(1)}, bf16[1,768,2048]{2,1,0:T(8,128)(2,1)}, u32[]{:S(2)}) copy-start(bf16[1,768,2048]{2,1,0:T(8,128)(2,1)} %copy-done.2) | copy-start | bytes 9437188
  47.3 2.9 %collective-permute-start.11 = (bf16[2,4,32,2048]{3,2,1,0:T(8,128)(2,1)S(1)}, bf16[2,4,32,2048]{3,2,1,0:T(8,128)(2,1)S(1)}, u32[]{:S(2)}, u32[]{:S(2)}) collective-permute-start(bf16[2,4,32,2048]{3,2,1,0:T(8,128)(2,1)S(1)} %get-tuple-element.36), channel_id=1, source_target_pairs={{0,1},{1,0},{2,3},{3,2},{4,5},{5,4},{6,7},{7,6},{8,9},{9,8},{10,11... | collective-permute-start | bytes 3145736 | tf_op jit(solution)/shard_map/ppermute | solution.py:243
  47.5 3.5 %collective-permute-start.15 = (bf16[4,32,2176]{2,1,0:T(8,128)(2,1)}, bf16[4,32,2176]{2,1,0:T(8,128)(2,1)S(1)}, u32[]{:S(2)}, u32[]{:S(2)}) collective-permute-start(bf16[4,32,2176]{2,1,0:T(8,128)(2,1)} %join.5.refs_0_), channel_id=1, source_target_pairs={{0,1},{1,0},{2,3},{3,2},{4,5},{5,4},{6,7},{7,6},{8,9},{9,8},{10,11... | collective-permute-start | bytes 1671176 | tf_op jit(solution)/shard_map/ppermute | solution.py:243
  47.8 4.0 %collective-permute-start.16 = (bf16[4,32,2176]{2,1,0:T(8,128)(2,1)}, bf16[4,32,2176]{2,1,0:T(8,128)(2,1)S(1)}, u32[]{:S(2)}, u32[]{:S(2)}) collective-permute-start(bf16[4,32,2176]{2,1,0:T(8,128)(2,1)} %collective-permute-done.10.refs_1_), channel_id=1, source_target_pairs={{0,1},{1,0},{2,3},{3,2},{4,5},{5,4},{6,7},{7,6},{8,9},{9,8},{10,11... | collective-permute-start | bytes 1671176 | tf_op jit(solution)/shard_map/ppermute | solution.py:243
  50.3 14.0 %collective-permute-start.12 = (bf16[4,32,2048]{2,1,0:T(8,128)(2,1)S(1)}, bf16[4,32,2048]{2,1,0:T(8,128)(2,1)S(1)}, u32[]{:S(2)}, u32[]{:S(2)}) collective-permute-start(bf16[4,32,2048]{2,1,0:T(8,128)(2,1)S(1)} %total.7), channel_id=1, source_target_pairs={{0,2},{1,3},{2,0},{3,1},{4,6},{5,7},{6,4},{7,5},{8,10},{9,11},{10,... | collective-permute-start | bytes 1572872 | tf_op jit(solution)/shard_map/ppermute | solution.py:240
  64.3 2.7 %collective-permute-start.17 = (bf16[2,4,32,2048]{3,2,1,0:T(8,128)(2,1)S(1)}, bf16[2,4,32,2048]{3,2,1,0:T(8,128)(2,1)S(1)}, u32[]{:S(2)}, u32[]{:S(2)}) collective-permute-start(bf16[2,4,32,2048]{3,2,1,0:T(8,128)(2,1)S(1)} %get-tuple-element.40), channel_id=1, source_target_pairs={{0,1},{1,0},{2,3},{3,2},{4,5},{5,4},{6,7},{7,6},{8,9},{9,8},{10,11... | collective-permute-start | bytes 3145736 | tf_op jit(solution)/shard_map/ppermute | solution.py:243
  67.0 9.2 %collective-permute-start.19 = (bf16[2,32,2048]{2,1,0:T(8,128)(2,1)S(1)}, bf16[2,32,2048]{2,1,0:T(8,128)(2,1)S(1)}, u32[]{:S(2)}, u32[]{:S(2)}) collective-permute-start(bf16[2,32,2048]{2,1,0:T(8,128)(2,1)S(1)} %total.11), channel_id=1, source_target_pairs={{0,2},{1,3},{2,0},{3,1},{4,6},{5,7},{6,4},{7,5},{8,10},{9,11},{10,... | collective-permute-start | bytes 786440 | tf_op jit(solution)/shard_map/ppermute | solution.py:240
  67.8 9.9 %collective-permute-start.13 = (bf16[2,32,2048]{2,1,0:T(8,128)(2,1)S(1)}, bf16[2,32,2048]{2,1,0:T(8,128)(2,1)S(1)}, u32[]{:S(2)}, u32[]{:S(2)}) collective-permute-start(bf16[2,32,2048]{2,1,0:T(8,128)(2,1)S(1)} %total.8), channel_id=1, source_target_pairs={{0,4},{1,5},{2,6},{3,7},{4,0},{5,1},{6,2},{7,3},{8,12},{9,13},{10,... | collective-permute-start | bytes 786440 | tf_op jit(solution)/shard_map/ppermute | solution.py:237
  69.8 11.2 %collective-permute-start.18 = (bf16[2,32,2048]{2,1,0:T(8,128)(2,1)S(1)}, bf16[2,32,2048]{2,1,0:T(8,128)(2,1)S(1)}, u32[]{:S(2)}, u32[]{:S(2)}) collective-permute-start(bf16[2,32,2048]{2,1,0:T(8,128)(2,1)S(1)} %total.10), channel_id=1, source_target_pairs={{0,2},{1,3},{2,0},{3,1},{4,6},{5,7},{6,4},{7,5},{8,10},{9,11},{10,... | collective-permute-start | bytes 786440 | tf_op jit(solution)/shard_map/ppermute | solution.py:240
  76.3 15.1 %copy-start.4 = (bf16[2,32,2048]{2,1,0:T(8,128)(2,1)S(1)}, bf16[2,32,2048]{2,1,0:T(8,128)(2,1)}, u32[]{:S(2)}) copy-start(bf16[2,32,2048]{2,1,0:T(8,128)(2,1)} %hidden_ref.1) | copy-start | bytes 786436
  76.4 8.1 %collective-permute-start.20 = (bf16[2,32,2048]{2,1,0:T(8,128)(2,1)S(1)}, bf16[2,32,2048]{2,1,0:T(8,128)(2,1)S(1)}, u32[]{:S(2)}, u32[]{:S(2)}) collective-permute-start(bf16[2,32,2048]{2,1,0:T(8,128)(2,1)S(1)} %total.12), channel_id=1, source_target_pairs={{0,4},{1,5},{2,6},{3,7},{4,0},{5,1},{6,2},{7,3},{8,12},{9,13},{10,... | collective-permute-start | bytes 786440 | tf_op jit(solution)/shard_map/ppermute | solution.py:237
  77.8 10.9 %collective-permute-start.14 = (bf16[1,32,2048]{2,1,0:T(8,128)(2,1)S(1)}, bf16[1,32,2048]{2,1,0:T(8,128)(2,1)S(1)}, u32[]{:S(2)}, u32[]{:S(2)}) collective-permute-start(bf16[1,32,2048]{2,1,0:T(8,128)(2,1)S(1)} %total.9), channel_id=1, source_target_pairs={{0,12},{1,13},{2,14},{3,15},{4,8},{5,9},{6,10},{7,11},{8,4},{9,5},... | collective-permute-start | bytes 393224 | tf_op jit(solution)/shard_map/ppermute | solution.py:237
  84.5 6.9 %collective-permute-start.21 = (bf16[1,32,2048]{2,1,0:T(8,128)(2,1)S(1)}, bf16[1,32,2048]{2,1,0:T(8,128)(2,1)S(1)}, u32[]{:S(2)}, u32[]{:S(2)}) collective-permute-start(bf16[1,32,2048]{2,1,0:T(8,128)(2,1)S(1)} %total.13), channel_id=1, source_target_pairs={{0,12},{1,13},{2,14},{3,15},{4,8},{5,9},{6,10},{7,11},{8,4},{9,5},... | collective-permute-start | bytes 393224 | tf_op jit(solution)/shard_map/ppermute | solution.py:237

commit v8 on v7

--- a/solution.py
+++ b/solution.py
@@ -222,7 +222,6 @@
 ):
     owners = lax.axis_size("ep")
     batches = hidden_in.shape[0]
-    weights = load([gate_weight, up_weight, down_weight])
     scales = jnp.exp2(exponent_table[0].astype(jnp.float32))
     owner = lax.axis_index("ep").astype(jnp.int32).reshape(1)
 
@@ -244,39 +243,38 @@
 
     payload = prepare(hidden_in, expert_ids, route_share, norm_gain, -(-owners // LANES) * LANES)
 
-    near, far = [], []
+    own_there = [to_mid(rows) for rows in payload]
+    near, far, there = [], [], []
     for batch, rows in enumerate(payload):
         if batch:
             rows = after(rows, near[-1])
+        there.append([own_there[batch]])
         span = line
         while span > 2:
             received = mirror(rows, span)
             if not batch:
-                received = after(received, *weights)
+                received = after(received, *own_there)
+            there[batch].append(to_mid(received))
             rows = join(rows, received)
             if batch:
                 rows = after(rows, far[-1])
             span //= 2
         near.append(rows)
-        if not batch:
-            near_there = to_mid(rows)
-        far.append(mirror(rows if not batch else after(rows, near_there), 2))
-
-    here, there = [], []
+        far.append(mirror(rows if not batch else after(rows, *there[batch - 1]), 2))
+    weights = load([after(w, near[-1]) for w in (gate_weight, up_weight, down_weight)])
+    far[-1] = after(far[-1], *weights)
+    ahead = there[-1][-1]
     for batch in range(batches):
-        if batch == 0:
-            here.append([near[0], far[0]])
-            there.append([near_there, to_mid(far[0])])
-        else:
-            here.append([join(near[batch], far[batch])])
-            there.append([to_mid(here[batch][0])])
-    if batches > 1:
-        there[0][0] = after(there[0][0], near[1])
+        rows = far[batch]
+        if batch + 1 < batches:
+            rows = after(rows, near[batch + 1])
+        there[batch].append(to_mid(rows))
 
     terms, sent, back = [], [], []
     for batch in range(batches):
-        xs = here[batch] + there[batch] + [to_core(rows) for rows in here[batch] + there[batch]]
-        xs[0] = after(xs[0], far[-1], *sent[-1:])
+        xs = [near[batch], far[batch], *there[batch]]
+        xs += [to_core(rows) for rows in xs]
+        xs[0] = after(xs[0], far[-1], ahead, *sent[-1:])
         mine, other = ffn(xs, owner, scales, weights)
         if batch + 1 < batches:
             other = after(other, *there[batch + 1])

time: 92.6 us -> 98.4 us (1.063)
  starting transfers between devices: 23.6 us -> 34.2 us
  waiting for transfers between devices: 41.1 us -> 32.2 us
  local copies, waits for them, and re-layouts: 7.11 us -> 10.5 us
    ppermute x8, waiting for transfers between devices: 20.4 us -> 12.1 us  [mirror(): return lax.ppermute(rows, 'ep', [(i, partner(i)) for i in range(owners)])]
    ppermute x8, starting transfers between devices: 15.4 us -> 21.1 us  [mirror(): return lax.ppermute(rows, 'ep', [(i, partner(i)) for i in range(owners)])]
    ppermute x6 -> x9, starting transfers between devices: 6.53 us -> 11 us  [to_mid(): return lax.ppermute(rows, 'ep', [(i, i ^ 2) for i in range(owners)])]
    unnamed x13 -> x25, local copies, waits for them, and re-layouts: 7.11 us -> 10.5 us
    ppermute x6 -> x9, waiting for transfers between devices: 12.9 us -> 11.2 us  [to_mid(): return lax.ppermute(rows, 'ep', [(i, i ^ 2) for i in range(owners)])]
    ppermute x8 -> x12, waiting for transfers between devices: 7.74 us -> 8.87 us  [to_core(): return lax.ppermute(rows, 'ep', [(i, i ^ 1) for i in range(owners)])]
    pallas_call x15 -> x14, Pallas kernels: 20.3 us -> 21 us  [call(): pl.pallas_call(kernel, out_shape=shapes, in_specs=specs, out_specs=[VMEM]...]
    ppermute x8 -> x12, starting transfers between devices: 1.73 us -> 2.12 us  [to_core(): return lax.ppermute(rows, 'ep', [(i, i ^ 1) for i in range(owners)])]
  transfers between devices with their start and end apart: 22 -> 29, of which waited for: 17 -> 14; matrix products, arithmetic and copies ran while one was open for 0% -> 0% of each run, Pallas kernels for 20% -> 18%
where the time goes in v8:
time: 98.4 us; the launch traced here: 98.1 us
  starting transfers between devices  34.2 us (35%)
  waiting for transfers between devices  32.2 us (33%)
  Pallas kernels  21 us (21%)
  local copies, waits for them, and re-layouts  10.5 us (11%)
    ppermute x8, starting transfers between devices, mirror(): return lax.ppermute(rows, 'ep', [(i, partner(i)) for i in range(owners)])  21.1 us
    pallas_call x14, Pallas kernels, call(): pl.pallas_call(kernel, out_shape=shapes, in_specs=specs, out_specs=[VMEM]...  21 us
    ppermute x8, waiting for transfers between devices, mirror(): return lax.ppermute(rows, 'ep', [(i, partner(i)) for i in range(owners)])  12.1 us
    ppermute x9, waiting for transfers between devices, to_mid(): return lax.ppermute(rows, 'ep', [(i, i ^ 2) for i in range(owners)])  11.2 us
    ppermute x9, starting transfers between devices, to_mid(): return lax.ppermute(rows, 'ep', [(i, i ^ 2) for i in range(owners)])  11 us
    unnamed x25, local copies, waits for them, and re-layouts  10.5 us
    ppermute x12, waiting for transfers between devices, to_core(): return lax.ppermute(rows, 'ep', [(i, i ^ 1) for i in range(owners)])  8.87 us
    ppermute x12, starting transfers between devices, to_core(): return lax.ppermute(rows, 'ep', [(i, i ^ 1) for i in range(owners)])  2.12 us
  transfers between devices with their start and end apart: 29, of which 14 were waited for; matrix products, arithmetic and copies ran while one was open for 0% of the time, Pallas kernels for 18%

profile of v8, /device:TPU:0, one launch (start us, length us, event | category | flops | bytes accessed | tf_op | source)
XLA Modules:
  0.0 98.1 jit_solution(14359865256220337492)
XLA Ops:
  0.0 1.2 %prepare.1 = (bf16[1,32,2176]{2,1,0:T(8,128)(2,1)S(1)}, bf16[1,32,2176]{2,1,0:T(8,128)(2,1)S(1)}) custom-call(bf16[2,32,2048]{2,1,0:T(8,128)(2,1)} %hidden_ref.1, s32[2,8,32]{2,1,0:T(8,128)} %bitcast.9, s32[2,8,32]{2,1,0:T(8,128)} %bitcast.10, f32[1,2048]{1,0:T(1,128)} %bitcast.11), custom_call_target="tpu_custom_call" | custom-call | tf_op jit(solution)/shard_map/prepare/pallas_call | solution.py:26
  1.2 3.0 %collective-permute-start.2 = (bf16[1,32,2176]{2,1,0:T(8,128)(2,1)S(1)}, bf16[1,32,2176]{2,1,0:T(8,128)(2,1)}, u32[]{:S(2)}, u32[]{:S(2)}) collective-permute-start(bf16[1,32,2176]{2,1,0:T(8,128)(2,1)S(1)} %get-tuple-element.30.refs_0_), channel_id=1, source_target_pairs={{0,2},{1,3},{2,0},{3,1},{4,6},{5,7},{6,4},{7,5},{8,10},{9,11},{10,... | collective-permute-start | bytes 417800 | tf_op jit(solution)/shard_map/ppermute | solution.py:239
  4.3 4.0 %collective-permute-start = (bf16[1,32,2176]{2,1,0:T(8,128)(2,1)S(1)}, bf16[1,32,2176]{2,1,0:T(8,128)(2,1)S(1)}, u32[]{:S(2)}, u32[]{:S(2)}) collective-permute-start(bf16[1,32,2176]{2,1,0:T(8,128)(2,1)S(1)} %get-tuple-element.28.refs_0_), channel_id=1, source_target_pairs={{0,12},{1,13},{2,14},{3,15},{4,8},{5,9},{6,10},{7,11},{8,4},{9,5},... | collective-permute-start | bytes 417800 | tf_op jit(solution)/shard_map/ppermute | solution.py:236
  8.9 2.0 %collective-permute-done.1.refs_2_ = bf16[1,32,2176]{2,1,0:T(8,128)(2,1)S(1)} collective-permute-done((bf16[1,32,2176]{2,1,0:T(8,128)(2,1)S(1)}, bf16[1,32,2176]{2,1,0:T(8,128)(2,1)S(1)}, u32[]{:S(2)}, u32[]{:S(2)}) %collective-permute-start.1) | collective-permute-done | bytes 139296 | tf_op jit(solution)/shard_map/ppermute | solution.py:239
  12.3 2.6 %collective-permute-start.4 = (bf16[2,32,2176]{2,1,0:T(8,128)(2,1)}, bf16[2,32,2176]{2,1,0:T(8,128)(2,1)}, u32[]{:S(2)}, u32[]{:S(2)}) collective-permute-start(bf16[2,32,2176]{2,1,0:T(8,128)(2,1)} %join.2.refs_0_), channel_id=1, source_target_pairs={{0,4},{1,5},{2,6},{3,7},{4,0},{5,1},{6,2},{7,3},{8,12},{9,13},{10,... | collective-permute-start | bytes 835592 | tf_op jit(solution)/shard_map/ppermute | solution.py:236
  14.9 2.7 %collective-permute-start.3 = (bf16[1,32,2176]{2,1,0:T(8,128)(2,1)S(1)}, bf16[1,32,2176]{2,1,0:T(8,128)(2,1)}, u32[]{:S(2)}, u32[]{:S(2)}) collective-permute-start(bf16[1,32,2176]{2,1,0:T(8,128)(2,1)S(1)} %get-tuple-element.30.refs_0_), channel_id=1, source_target_pairs={{0,12},{1,13},{2,14},{3,15},{4,8},{5,9},{6,10},{7,11},{8,4},{9,5},... | collective-permute-start | bytes 417800 | tf_op jit(solution)/shard_map/ppermute | solution.py:236
  17.6 1.5 %collective-permute-start.5 = (bf16[1,32,2176]{2,1,0:T(8,128)(2,1)S(1)}, bf16[1,32,2176]{2,1,0:T(8,128)(2,1)S(1)}, u32[]{:S(2)}, u32[]{:S(2)}) collective-permute-start(bf16[1,32,2176]{2,1,0:T(8,128)(2,1)S(1)} %collective-permute-done.refs_1_), channel_id=1, source_target_pairs={{0,2},{1,3},{2,0},{3,1},{4,6},{5,7},{6,4},{7,5},{8,10},{9,11},{10,... | collective-permute-start | bytes 417800 | tf_op jit(solution)/shard_map/ppermute | solution.py:239
  19.1 5.6 %collective-permute-done.3.refs_1_ = bf16[1,32,2176]{2,1,0:T(8,128)(2,1)} collective-permute-done((bf16[1,32,2176]{2,1,0:T(8,128)(2,1)S(1)}, bf16[1,32,2176]{2,1,0:T(8,128)(2,1)}, u32[]{:S(2)}, u32[]{:S(2)}) %collective-permute-start.3) | collective-permute-done | bytes 139296 | tf_op jit(solution)/shard_map/ppermute | solution.py:236
  24.8 0.9 join.3.refs_0_
  25.8 1.6 %collective-permute-start.8 = (bf16[2,32,2176]{2,1,0:T(8,128)(2,1)}, bf16[2,32,2176]{2,1,0:T(8,128)(2,1)}, u32[]{:S(2)}, u32[]{:S(2)}) collective-permute-start(bf16[2,32,2176]{2,1,0:T(8,128)(2,1)} %collective-permute-done.4.refs_1_), channel_id=1, source_target_pairs={{0,2},{1,3},{2,0},{3,1},{4,6},{5,7},{6,4},{7,5},{8,10},{9,11},{10,... | collective-permute-start | bytes 835592 | tf_op jit(solution)/shard_map/ppermute | solution.py:239
  28.1 3.8 %load.1 = (bf16[1,2048,768]{2,1,0:T(8,128)(2,1)S(1)}, bf16[1,2048,768]{2,1,0:T(8,128)(2,1)S(1)}, bf16[1,768,2048]{2,1,0:T(8,128)(2,1)S(1)}) custom-call(bf16[1,2048,768]{2,1,0:T(8,128)(2,1)} %refs_0_, bf16[1,2048,768]{2,1,0:T(8,128)(2,1)} %refs_1_, bf16[1,768,2048]{2,1,0:T(8,128)(2,1)} %refs_2_), custom_call_target="tpu_custom_call" | custom-call | tf_op jit(solution)/shard_map/load/pallas_call | solution.py:26
  31.9 1.6 %copy-done = bf16[1,2048,768]{2,1,0:T(8,128)(2,1)} copy-done((bf16[1,2048,768]{2,1,0:T(8,128)(2,1)}, bf16[1,2048,768]{2,1,0:T(8,128)(2,1)S(1)}, u32[]{:S(2)}) %copy-start) | copy-done | bytes 3145752
  33.6 1.7 %copy-done.2 = bf16[1,768,2048]{2,1,0:T(8,128)(2,1)} copy-done((bf16[1,768,2048]{2,1,0:T(8,128)(2,1)}, bf16[1,768,2048]{2,1,0:T(8,128)(2,1)S(1)}, u32[]{:S(2)}) %copy-start.2) | copy-done | bytes 3145752
  36.5 1.5 %collective-permute-start.14 = (bf16[2,32,2176]{2,1,0:T(8,128)(2,1)}, bf16[2,32,2176]{2,1,0:T(8,128)(2,1)}, u32[]{:S(2)}, u32[]{:S(2)}) collective-permute-start(bf16[2,32,2176]{2,1,0:T(8,128)(2,1)} %collective-permute-done.6.refs_1_), channel_id=1, source_target_pairs={{0,2},{1,3},{2,0},{3,1},{4,6},{5,7},{6,4},{7,5},{8,10},{9,11},{10,... | collective-permute-start | bytes 835592 | tf_op jit(solution)/shard_map/ppermute | solution.py:239
  38.0 1.5 %collective-permute-done.12.refs_8_ = bf16[1,32,2176]{2,1,0:T(8,128)(2,1)S(1)} collective-permute-done((bf16[1,32,2176]{2,1,0:T(8,128)(2,1)}, bf16[1,32,2176]{2,1,0:T(8,128)(2,1)S(1)}, u32[]{:S(2)}, u32[]{:S(2)}) %collective-permute-start.12) | collective-permute-done | bytes 139296 | tf_op jit(solution)/shard_map/ppermute | solution.py:242
  39.6 1.9 %copy-done.1 = bf16[1,2048,768]{2,1,0:T(8,128)(2,1)S(1)} copy-done((bf16[1,2048,768]{2,1,0:T(8,128)(2,1)S(1)}, bf16[1,2048,768]{2,1,0:T(8,128)(2,1)}, u32[]{:S(2)}) %copy-start.1) | copy-done | bytes 3145752
  41.5 1.9 %copy-done.3 = bf16[1,768,2048]{2,1,0:T(8,128)(2,1)S(1)} copy-done((bf16[1,768,2048]{2,1,0:T(8,128)(2,1)S(1)}, bf16[1,768,2048]{2,1,0:T(8,128)(2,1)}, u32[]{:S(2)}) %copy-start.3) | copy-done | bytes 3145752
  46.1 6.5 %ffn.2 = (bf16[2,4,32,2048]{3,2,1,0:T(8,128)(2,1)S(1)}, bf16[2,4,32,2048]{3,2,1,0:T(8,128)(2,1)S(1)}) custom-call(s32[1]{0:T(128)} %bitcast.owner_ref, f32[3,6]{1,0:T(4,128)S(1)} %bitcast.7, bf16[1,2048,768]{2,1,0:T(8,128)(2,1)S(1)} %get-tuple-element.35.gate_ref, bf16[1,2048,768]{2,1,0:T(8,128)(2,1)S(1)} %copy-done.1, bf16[1,768,2048]{2,1,0:T(8,128)(2,1)S(1)} %copy-done.3, ...), custom_call_target="tpu_custom_call" | custom-call | tf_op jit(solution)/shard_map/ffn/pallas_call | solution.py:26
  52.8 2.5 %collective-permute-done.15.refs_1_ = bf16[2,4,32,2048]{3,2,1,0:T(8,128)(2,1)S(1)} collective-permute-done((bf16[2,4,32,2048]{3,2,1,0:T(8,128)(2,1)S(1)}, bf16[2,4,32,2048]{3,2,1,0:T(8,128)(2,1)S(1)}, u32[]{:S(2)}, u32[]{:S(2)}) %collective-permute-start.15) | collective-permute-done | bytes 1048608 | tf_op jit(solution)/shard_map/ppermute | solution.py:242
  57.9 1.4 %collective-permute-done.22.refs_8_ = bf16[1,32,2176]{2,1,0:T(8,128)(2,1)S(1)} collective-permute-done((bf16[1,32,2176]{2,1,0:T(8,128)(2,1)}, bf16[1,32,2176]{2,1,0:T(8,128)(2,1)S(1)}, u32[]{:S(2)}, u32[]{:S(2)}) %collective-permute-start.22) | collective-permute-done | bytes 139296 | tf_op jit(solution)/shard_map/ppermute | solution.py:242
  59.4 6.3 %ffn.3 = (bf16[2,4,32,2048]{3,2,1,0:T(8,128)(2,1)S(1)}, bf16[2,4,32,2048]{3,2,1,0:T(8,128)(2,1)S(1)}) custom-call(s32[1]{0:T(128)} %bitcast.owner_ref, f32[3,6]{1,0:T(4,128)S(1)} %bitcast.8, bf16[1,2048,768]{2,1,0:T(8,128)(2,1)S(1)} %get-tuple-element.35.gate_ref, bf16[1,2048,768]{2,1,0:T(8,128)(2,1)S(1)} %copy-done.1, bf16[1,768,2048]{2,1,0:T(8,128)(2,1)S(1)} %copy-done.3, ...), custom_call_target="tpu_custom_call" | custom-call | tf_op jit(solution)/shard_map/ffn/pallas_call | solution.py:26
  65.7 3.8 %collective-permute-done.16.refs_2_ = bf16[4,32,2048]{2,1,0:T(8,128)(2,1)S(1)} collective-permute-done((bf16[4,32,2048]{2,1,0:T(8,128)(2,1)S(1)}, bf16[4,32,2048]{2,1,0:T(8,128)(2,1)S(1)}, u32[]{:S(2)}, u32[]{:S(2)}) %collective-permute-start.16) | collective-permute-done | bytes 524320 | tf_op jit(solution)/shard_map/ppermute | solution.py:239
  69.5 2.7 %collective-permute-done.24.refs_1_.refs_6_ = bf16[2,4,32,2048]{3,2,1,0:T(8,128)(2,1)S(1)} collective-permute-done((bf16[2,4,32,2048]{3,2,1,0:T(8,128)(2,1)S(1)}, bf16[2,4,32,2048]{3,2,1,0:T(8,128)(2,1)S(1)}, u32[]{:S(2)}, u32[]{:S(2)}) %collective-permute-start.24) | collective-permute-done | bytes 1048608 | tf_op jit(solution)/shard_map/ppermute | solution.py:242
  72.9 2.0 %collective-permute-start.17 = (bf16[2,32,2048]{2,1,0:T(8,128)(2,1)S(1)}, bf16[2,32,2048]{2,1,0:T(8,128)(2,1)S(1)}, u32[]{:S(2)}, u32[]{:S(2)}) collective-permute-start(bf16[2,32,2048]{2,1,0:T(8,128)(2,1)S(1)} %total.8), channel_id=1, source_target_pairs={{0,4},{1,5},{2,6},{3,7},{4,0},{5,1},{6,2},{7,3},{8,12},{9,13},{10,... | collective-permute-start | bytes 786440 | tf_op jit(solution)/shard_map/ppermute | solution.py:236
  75.0 1.6 %collective-permute-start.25 = (bf16[2,32,2048]{2,1,0:T(8,128)(2,1)S(1)}, bf16[2,32,2048]{2,1,0:T(8,128)(2,1)S(1)}, u32[]{:S(2)}, u32[]{:S(2)}) collective-permute-start(bf16[2,32,2048]{2,1,0:T(8,128)(2,1)S(1)} %total.10), channel_id=1, source_target_pairs={{0,2},{1,3},{2,0},{3,1},{4,6},{5,7},{6,4},{7,5},{8,10},{9,11},{10,... | collective-permute-start | bytes 786440 | tf_op jit(solution)/shard_map/ppermute | solution.py:239
  76.6 4.9 %collective-permute-done.26.refs_2_ = bf16[2,32,2048]{2,1,0:T(8,128)(2,1)S(1)} collective-permute-done((bf16[2,32,2048]{2,1,0:T(8,128)(2,1)S(1)}, bf16[2,32,2048]{2,1,0:T(8,128)(2,1)S(1)}, u32[]{:S(2)}, u32[]{:S(2)}) %collective-permute-start.26) | collective-permute-done | bytes 262176 | tf_op jit(solution)/shard_map/ppermute | solution.py:239
  81.6 2.0 %collective-permute-start.27 = (bf16[2,32,2048]{2,1,0:T(8,128)(2,1)S(1)}, bf16[2,32,2048]{2,1,0:T(8,128)(2,1)S(1)}, u32[]{:S(2)}, u32[]{:S(2)}) collective-permute-start(bf16[2,32,2048]{2,1,0:T(8,128)(2,1)S(1)} %total.12), channel_id=1, source_target_pairs={{0,4},{1,5},{2,6},{3,7},{4,0},{5,1},{6,2},{7,3},{8,12},{9,13},{10,... | collective-permute-start | bytes 786440 | tf_op jit(solution)/shard_map/ppermute | solution.py:236
  83.6 3.3 %collective-permute-start.18 = (bf16[1,32,2048]{2,1,0:T(8,128)(2,1)S(1)}, bf16[1,32,2048]{2,1,0:T(8,128)(2,1)S(1)}, u32[]{:S(2)}, u32[]{:S(2)}) collective-permute-start(bf16[1,32,2048]{2,1,0:T(8,128)(2,1)S(1)} %total.9), channel_id=1, source_target_pairs={{0,12},{1,13},{2,14},{3,15},{4,8},{5,9},{6,10},{7,11},{8,4},{9,5},... | collective-permute-start | bytes 393224 | tf_op jit(solution)/shard_map/ppermute | solution.py:236
  86.9 2.3 %collective-permute-done.27.refs_3_.refs_8_ = bf16[2,32,2048]{2,1,0:T(8,128)(2,1)S(1)} collective-permute-done((bf16[2,32,2048]{2,1,0:T(8,128)(2,1)S(1)}, bf16[2,32,2048]{2,1,0:T(8,128)(2,1)S(1)}, u32[]{:S(2)}, u32[]{:S(2)}) %collective-permute-start.27) | collective-permute-done | bytes 262176 | tf_op jit(solution)/shard_map/ppermute | solution.py:236
  89.3 4.4 %collective-permute-start.28 = (bf16[1,32,2048]{2,1,0:T(8,128)(2,1)S(1)}, bf16[1,32,2048]{2,1,0:T(8,128)(2,1)S(1)}, u32[]{:S(2)}, u32[]{:S(2)}) collective-permute-start(bf16[1,32,2048]{2,1,0:T(8,128)(2,1)S(1)} %total.13), channel_id=1, source_target_pairs={{0,12},{1,13},{2,14},{3,15},{4,8},{5,9},{6,10},{7,11},{8,4},{9,5},... | collective-permute-start | bytes 393224 | tf_op jit(solution)/shard_map/ppermute | solution.py:236
  93.7 2.0 %collective-permute-done.18.refs_4_ = bf16[1,32,2048]{2,1,0:T(8,128)(2,1)S(1)} collective-permute-done((bf16[1,32,2048]{2,1,0:T(8,128)(2,1)S(1)}, bf16[1,32,2048]{2,1,0:T(8,128)(2,1)S(1)}, u32[]{:S(2)}, u32[]{:S(2)}) %collective-permute-start.18) | collective-permute-done | bytes 131104 | tf_op jit(solution)/shard_map/ppermute | solution.py:236
  95.7 1.5 %collective-permute-done.28.refs_9_ = bf16[1,32,2048]{2,1,0:T(8,128)(2,1)S(1)} collective-permute-done((bf16[1,32,2048]{2,1,0:T(8,128)(2,1)S(1)}, bf16[1,32,2048]{2,1,0:T(8,128)(2,1)S(1)}, u32[]{:S(2)}, u32[]{:S(2)}) %collective-permute-start.28) | collective-permute-done | bytes 131104 | tf_op jit(solution)/shard_map/ppermute | solution.py:236
  (66 shorter events, 11.5 us)
Async XLA Ops:
  1.2 7.6 %collective-permute-start.2 = (bf16[1,32,2176]{2,1,0:T(8,128)(2,1)S(1)}, bf16[1,32,2176]{2,1,0:T(8,128)(2,1)}, u32[]{:S(2)}, u32[]{:S(2)}) collective-permute-start(bf16[1,32,2176]{2,1,0:T(8,128)(2,1)S(1)} %get-tuple-element.30.refs_0_), channel_id=1, source_target_pairs={{0,2},{1,3},{2,0},{3,1},{4,6},{5,7},{6,4},{7,5},{8,10},{9,11},{10,... | collective-permute-start | bytes 417800 | tf_op jit(solution)/shard_map/ppermute | solution.py:239
  4.3 6.7 %collective-permute-start.1 = (bf16[1,32,2176]{2,1,0:T(8,128)(2,1)S(1)}, bf16[1,32,2176]{2,1,0:T(8,128)(2,1)S(1)}, u32[]{:S(2)}, u32[]{:S(2)}) collective-permute-start(bf16[1,32,2176]{2,1,0:T(8,128)(2,1)S(1)} %get-tuple-element.28.refs_0_), channel_id=1, source_target_pairs={{0,2},{1,3},{2,0},{3,1},{4,6},{5,7},{6,4},{7,5},{8,10},{9,11},{10,... | collective-permute-start | bytes 417800 | tf_op jit(solution)/shard_map/ppermute | solution.py:239
  4.3 7.2 %collective-permute-start = (bf16[1,32,2176]{2,1,0:T(8,128)(2,1)S(1)}, bf16[1,32,2176]{2,1,0:T(8,128)(2,1)S(1)}, u32[]{:S(2)}, u32[]{:S(2)}) collective-permute-start(bf16[1,32,2176]{2,1,0:T(8,128)(2,1)S(1)} %get-tuple-element.28.refs_0_), channel_id=1, source_target_pairs={{0,12},{1,13},{2,14},{3,15},{4,8},{5,9},{6,10},{7,11},{8,4},{9,5},... | collective-permute-start | bytes 417800 | tf_op jit(solution)/shard_map/ppermute | solution.py:236
  10.9 21.0 %copy-start.5 = (bf16[1,32,2176]{2,1,0:T(8,128)(2,1)}, bf16[1,32,2176]{2,1,0:T(8,128)(2,1)S(1)}, u32[]{:S(2)}) copy-start(bf16[1,32,2176]{2,1,0:T(8,128)(2,1)S(1)} %collective-permute-done.1.refs_2_) | copy-start | bytes 417796
  12.3 13.4 %collective-permute-start.4 = (bf16[2,32,2176]{2,1,0:T(8,128)(2,1)}, bf16[2,32,2176]{2,1,0:T(8,128)(2,1)}, u32[]{:S(2)}, u32[]{:S(2)}) collective-permute-start(bf16[2,32,2176]{2,1,0:T(8,128)(2,1)} %join.2.refs_0_), channel_id=1, source_target_pairs={{0,4},{1,5},{2,6},{3,7},{4,0},{5,1},{6,2},{7,3},{8,12},{9,13},{10,... | collective-permute-start | bytes 835592 | tf_op jit(solution)/shard_map/ppermute | solution.py:236
  14.9 9.8 %collective-permute-start.3 = (bf16[1,32,2176]{2,1,0:T(8,128)(2,1)S(1)}, bf16[1,32,2176]{2,1,0:T(8,128)(2,1)}, u32[]{:S(2)}, u32[]{:S(2)}) collective-permute-start(bf16[1,32,2176]{2,1,0:T(8,128)(2,1)S(1)} %get-tuple-element.30.refs_0_), channel_id=1, source_target_pairs={{0,12},{1,13},{2,14},{3,15},{4,8},{5,9},{6,10},{7,11},{8,4},{9,5},... | collective-permute-start | bytes 417800 | tf_op jit(solution)/shard_map/ppermute | solution.py:236
  17.6 8.1 %collective-permute-start.5 = (bf16[1,32,2176]{2,1,0:T(8,128)(2,1)S(1)}, bf16[1,32,2176]{2,1,0:T(8,128)(2,1)S(1)}, u32[]{:S(2)}, u32[]{:S(2)}) collective-permute-start(bf16[1,32,2176]{2,1,0:T(8,128)(2,1)S(1)} %collective-permute-done.refs_1_), channel_id=1, source_target_pairs={{0,2},{1,3},{2,0},{3,1},{4,6},{5,7},{6,4},{7,5},{8,10},{9,11},{10,... | collective-permute-start | bytes 417800 | tf_op jit(solution)/shard_map/ppermute | solution.py:239
  25.7 12.3 %copy-start.11 = (s32[1,3,6]{2,0,1:T(1,128)S(1)}, s32[1,3,6]{2,0,1:T(1,128)}, u32[]{:S(2)}) copy-start(s32[1,3,6]{2,0,1:T(1,128)} %param.15) | copy-start | bytes 220
  25.7 9.5 %collective-permute-start.6 = (bf16[2,32,2176]{2,1,0:T(8,128)(2,1)S(1)}, bf16[2,32,2176]{2,1,0:T(8,128)(2,1)}, u32[]{:S(2)}, u32[]{:S(2)}) collective-permute-start(bf16[2,32,2176]{2,1,0:T(8,128)(2,1)S(1)} %join.3.refs_0_), channel_id=1, source_target_pairs={{0,4},{1,5},{2,6},{3,7},{4,0},{5,1},{6,2},{7,3},{8,12},{9,13},{10,... | collective-permute-start | bytes 835592 | tf_op jit(solution)/shard_map/ppermute | solution.py:236
  25.8 9.7 %collective-permute-start.8 = (bf16[2,32,2176]{2,1,0:T(8,128)(2,1)}, bf16[2,32,2176]{2,1,0:T(8,128)(2,1)}, u32[]{:S(2)}, u32[]{:S(2)}) collective-permute-start(bf16[2,32,2176]{2,1,0:T(8,128)(2,1)} %collective-permute-done.4.refs_1_), channel_id=1, source_target_pairs={{0,2},{1,3},{2,0},{3,1},{4,6},{5,7},{6,4},{7,5},{8,10},{9,11},{10,... | collective-permute-start | bytes 835592 | tf_op jit(solution)/shard_map/ppermute | solution.py:239
  27.4 8.4 %collective-permute-start.11 = (bf16[1,32,2176]{2,1,0:T(8,128)(2,1)S(1)}, bf16[1,32,2176]{2,1,0:T(8,128)(2,1)S(1)}, u32[]{:S(2)}, u32[]{:S(2)}) collective-permute-start(bf16[1,32,2176]{2,1,0:T(8,128)(2,1)S(1)} %collective-permute-done.1.refs_2_), channel_id=1, source_target_pairs={{0,1},{1,0},{2,3},{3,2},{4,5},{5,4},{6,7},{7,6},{8,9},{9,8},{10,11... | collective-permute-start | bytes 417800 | tf_op jit(solution)/shard_map/ppermute | solution.py:242
  27.4 10.6 %collective-permute-start.7 = (bf16[1,32,2176]{2,1,0:T(8,128)(2,1)}, bf16[1,32,2176]{2,1,0:T(8,128)(2,1)}, u32[]{:S(2)}, u32[]{:S(2)}) collective-permute-start(bf16[1,32,2176]{2,1,0:T(8,128)(2,1)} %collective-permute-done.3.refs_1_), channel_id=1, source_target_pairs={{0,2},{1,3},{2,0},{3,1},{4,6},{5,7},{6,4},{7,5},{8,10},{9,11},{10,... | collective-permute-start | bytes 417800 | tf_op jit(solution)/shard_map/ppermute | solution.py:239
  27.9 11.6 %collective-permute-start.9 = (bf16[2,32,2176]{2,1,0:T(8,128)(2,1)}, bf16[2,32,2176]{2,1,0:T(8,128)(2,1)}, u32[]{:S(2)}, u32[]{:S(2)}) collective-permute-start(bf16[2,32,2176]{2,1,0:T(8,128)(2,1)} %join.2.refs_0_), channel_id=1, source_target_pairs={{0,1},{1,0},{2,3},{3,2},{4,5},{5,4},{6,7},{7,6},{8,9},{9,8},{10,11... | collective-permute-start | bytes 835592 | tf_op jit(solution)/shard_map/ppermute | solution.py:242
  35.3 4.3 %collective-permute-start.10 = (bf16[2,32,2176]{2,1,0:T(8,128)(2,1)}, bf16[2,32,2176]{2,1,0:T(8,128)(2,1)}, u32[]{:S(2)}, u32[]{:S(2)}) collective-permute-start(bf16[2,32,2176]{2,1,0:T(8,128)(2,1)} %collective-permute-done.4.refs_1_), channel_id=1, source_target_pairs={{0,1},{1,0},{2,3},{3,2},{4,5},{5,4},{6,7},{7,6},{8,9},{9,8},{10,11... | collective-permute-start | bytes 835592 | tf_op jit(solution)/shard_map/ppermute | solution.py:242
  35.6 4.0 %collective-permute-start.13 = (bf16[2,32,2176]{2,1,0:T(8,128)(2,1)}, bf16[2,32,2176]{2,1,0:T(8,128)(2,1)}, u32[]{:S(2)}, u32[]{:S(2)}) collective-permute-start(bf16[2,32,2176]{2,1,0:T(8,128)(2,1)} %collective-permute-done.8.refs_4_), channel_id=1, source_target_pairs={{0,1},{1,0},{2,3},{3,2},{4,5},{5,4},{6,7},{7,6},{8,9},{9,8},{10,11... | collective-permute-start | bytes 835592 | tf_op jit(solution)/shard_map/ppermute | solution.py:242
  36.5 16.1 %collective-permute-start.14 = (bf16[2,32,2176]{2,1,0:T(8,128)(2,1)}, bf16[2,32,2176]{2,1,0:T(8,128)(2,1)}, u32[]{:S(2)}, u32[]{:S(2)}) collective-permute-start(bf16[2,32,2176]{2,1,0:T(8,128)(2,1)} %collective-permute-done.6.refs_1_), channel_id=1, source_target_pairs={{0,2},{1,3},{2,0},{3,1},{4,6},{5,7},{6,4},{7,5},{8,10},{9,11},{10,... | collective-permute-start | bytes 835592 | tf_op jit(solution)/shard_map/ppermute | solution.py:239
  38.0 1.6 %collective-permute-start.12 = (bf16[1,32,2176]{2,1,0:T(8,128)(2,1)}, bf16[1,32,2176]{2,1,0:T(8,128)(2,1)S(1)}, u32[]{:S(2)}, u32[]{:S(2)}) collective-permute-start(bf16[1,32,2176]{2,1,0:T(8,128)(2,1)} %copy-done.7), channel_id=1, source_target_pairs={{0,1},{1,0},{2,3},{3,2},{4,5},{5,4},{6,7},{7,6},{8,9},{9,8},{10,11... | collective-permute-start | bytes 417800 | tf_op jit(solution)/shard_map/ppermute | solution.py:242
  52.6 2.7 %collective-permute-start.15 = (bf16[2,4,32,2048]{3,2,1,0:T(8,128)(2,1)S(1)}, bf16[2,4,32,2048]{3,2,1,0:T(8,128)(2,1)S(1)}, u32[]{:S(2)}, u32[]{:S(2)}) collective-permute-start(bf16[2,4,32,2048]{3,2,1,0:T(8,128)(2,1)S(1)} %get-tuple-element.44), channel_id=1, source_target_pairs={{0,1},{1,0},{2,3},{3,2},{4,5},{5,4},{6,7},{7,6},{8,9},{9,8},{10,11... | collective-permute-start | bytes 3145736 | tf_op jit(solution)/shard_map/ppermute | solution.py:242
  55.5 14.0 %collective-permute-start.16 = (bf16[4,32,2048]{2,1,0:T(8,128)(2,1)S(1)}, bf16[4,32,2048]{2,1,0:T(8,128)(2,1)S(1)}, u32[]{:S(2)}, u32[]{:S(2)}) collective-permute-start(bf16[4,32,2048]{2,1,0:T(8,128)(2,1)S(1)} %total.7), channel_id=1, source_target_pairs={{0,2},{1,3},{2,0},{3,1},{4,6},{5,7},{6,4},{7,5},{8,10},{9,11},{10,... | collective-permute-start | bytes 1572872 | tf_op jit(solution)/shard_map/ppermute | solution.py:239
  56.0 1.7 %collective-permute-start.21 = (bf16[1,32,2176]{2,1,0:T(8,128)(2,1)}, bf16[1,32,2176]{2,1,0:T(8,128)(2,1)S(1)}, u32[]{:S(2)}, u32[]{:S(2)}) collective-permute-start(bf16[1,32,2176]{2,1,0:T(8,128)(2,1)} %collective-permute-done.2.refs_2_), channel_id=1, source_target_pairs={{0,1},{1,0},{2,3},{3,2},{4,5},{5,4},{6,7},{7,6},{8,9},{9,8},{10,11... | collective-permute-start | bytes 417800 | tf_op jit(solution)/shard_map/ppermute | solution.py:242
  56.0 3.3 %collective-permute-start.19 = (bf16[2,32,2176]{2,1,0:T(8,128)(2,1)S(1)}, bf16[2,32,2176]{2,1,0:T(8,128)(2,1)S(1)}, u32[]{:S(2)}, u32[]{:S(2)}) collective-permute-start(bf16[2,32,2176]{2,1,0:T(8,128)(2,1)S(1)} %join.3.refs_0_), channel_id=1, source_target_pairs={{0,1},{1,0},{2,3},{3,2},{4,5},{5,4},{6,7},{7,6},{8,9},{9,8},{10,11... | collective-permute-start | bytes 835592 | tf_op jit(solution)/shard_map/ppermute | solution.py:242
  56.5 2.8 %collective-permute-start.20 = (bf16[2,32,2176]{2,1,0:T(8,128)(2,1)}, bf16[2,32,2176]{2,1,0:T(8,128)(2,1)S(1)}, u32[]{:S(2)}, u32[]{:S(2)}) collective-permute-start(bf16[2,32,2176]{2,1,0:T(8,128)(2,1)} %collective-permute-done.6.refs_1_), channel_id=1, source_target_pairs={{0,1},{1,0},{2,3},{3,2},{4,5},{5,4},{6,7},{7,6},{8,9},{9,8},{10,11... | collective-permute-start | bytes 835592 | tf_op jit(solution)/shard_map/ppermute | solution.py:242
  56.5 2.8 %collective-permute-start.23 = (bf16[2,32,2176]{2,1,0:T(8,128)(2,1)}, bf16[2,32,2176]{2,1,0:T(8,128)(2,1)S(1)}, u32[]{:S(2)}, u32[]{:S(2)}) collective-permute-start(bf16[2,32,2176]{2,1,0:T(8,128)(2,1)} %collective-permute-done.14.refs_4_), channel_id=1, source_target_pairs={{0,1},{1,0},{2,3},{3,2},{4,5},{5,4},{6,7},{7,6},{8,9},{9,8},{10,11... | collective-permute-start | bytes 835592 | tf_op jit(solution)/shard_map/ppermute | solution.py:242
  57.8 1.6 %collective-permute-start.22 = (bf16[1,32,2176]{2,1,0:T(8,128)(2,1)}, bf16[1,32,2176]{2,1,0:T(8,128)(2,1)S(1)}, u32[]{:S(2)}, u32[]{:S(2)}) collective-permute-start(bf16[1,32,2176]{2,1,0:T(8,128)(2,1)} %collective-permute-done.7.refs_3_), channel_id=1, source_target_pairs={{0,1},{1,0},{2,3},{3,2},{4,5},{5,4},{6,7},{7,6},{8,9},{9,8},{10,11... | collective-permute-start | bytes 417800 | tf_op jit(solution)/shard_map/ppermute | solution.py:242
  69.5 2.7 %collective-permute-start.24 = (bf16[2,4,32,2048]{3,2,1,0:T(8,128)(2,1)S(1)}, bf16[2,4,32,2048]{3,2,1,0:T(8,128)(2,1)S(1)}, u32[]{:S(2)}, u32[]{:S(2)}) collective-permute-start(bf16[2,4,32,2048]{3,2,1,0:T(8,128)(2,1)S(1)} %get-tuple-element.48), channel_id=1, source_target_pairs={{0,1},{1,0},{2,3},{3,2},{4,5},{5,4},{6,7},{7,6},{8,9},{9,8},{10,11... | collective-permute-start | bytes 3145736 | tf_op jit(solution)/shard_map/ppermute | solution.py:242
  72.2 9.2 %collective-permute-start.26 = (bf16[2,32,2048]{2,1,0:T(8,128)(2,1)S(1)}, bf16[2,32,2048]{2,1,0:T(8,128)(2,1)S(1)}, u32[]{:S(2)}, u32[]{:S(2)}) collective-permute-start(bf16[2,32,2048]{2,1,0:T(8,128)(2,1)S(1)} %total.11), channel_id=1, source_target_pairs={{0,2},{1,3},{2,0},{3,1},{4,6},{5,7},{6,4},{7,5},{8,10},{9,11},{10,... | collective-permute-start | bytes 786440 | tf_op jit(solution)/shard_map/ppermute | solution.py:239
  72.9 10.7 %collective-permute-start.17 = (bf16[2,32,2048]{2,1,0:T(8,128)(2,1)S(1)}, bf16[2,32,2048]{2,1,0:T(8,128)(2,1)S(1)}, u32[]{:S(2)}, u32[]{:S(2)}) collective-permute-start(bf16[2,32,2048]{2,1,0:T(8,128)(2,1)S(1)} %total.8), channel_id=1, source_target_pairs={{0,4},{1,5},{2,6},{3,7},{4,0},{5,1},{6,2},{7,3},{8,12},{9,13},{10,... | collective-permute-start | bytes 786440 | tf_op jit(solution)/shard_map/ppermute | solution.py:236
  75.0 12.0 %collective-permute-start.25 = (bf16[2,32,2048]{2,1,0:T(8,128)(2,1)S(1)}, bf16[2,32,2048]{2,1,0:T(8,128)(2,1)S(1)}, u32[]{:S(2)}, u32[]{:S(2)}) collective-permute-start(bf16[2,32,2048]{2,1,0:T(8,128)(2,1)S(1)} %total.10), channel_id=1, source_target_pairs={{0,2},{1,3},{2,0},{3,1},{4,6},{5,7},{6,4},{7,5},{8,10},{9,11},{10,... | collective-permute-start | bytes 786440 | tf_op jit(solution)/shard_map/ppermute | solution.py:239
  81.5 15.7 %copy-start.4 = (bf16[2,32,2048]{2,1,0:T(8,128)(2,1)S(1)}, bf16[2,32,2048]{2,1,0:T(8,128)(2,1)}, u32[]{:S(2)}) copy-start(bf16[2,32,2048]{2,1,0:T(8,128)(2,1)} %hidden_ref.1) | copy-start | bytes 786436
  81.6 7.7 %collective-permute-start.27 = (bf16[2,32,2048]{2,1,0:T(8,128)(2,1)S(1)}, bf16[2,32,2048]{2,1,0:T(8,128)(2,1)S(1)}, u32[]{:S(2)}, u32[]{:S(2)}) collective-permute-start(bf16[2,32,2048]{2,1,0:T(8,128)(2,1)S(1)} %total.12), channel_id=1, source_target_pairs={{0,4},{1,5},{2,6},{3,7},{4,0},{5,1},{6,2},{7,3},{8,12},{9,13},{10,... | collective-permute-start | bytes 786440 | tf_op jit(solution)/shard_map/ppermute | solution.py:236
  83.6 12.1 %collective-permute-start.18 = (bf16[1,32,2048]{2,1,0:T(8,128)(2,1)S(1)}, bf16[1,32,2048]{2,1,0:T(8,128)(2,1)S(1)}, u32[]{:S(2)}, u32[]{:S(2)}) collective-permute-start(bf16[1,32,2048]{2,1,0:T(8,128)(2,1)S(1)} %total.9), channel_id=1, source_target_pairs={{0,12},{1,13},{2,14},{3,15},{4,8},{5,9},{6,10},{7,11},{8,4},{9,5},... | collective-permute-start | bytes 393224 | tf_op jit(solution)/shard_map/ppermute | solution.py:236
  89.3 7.9 %collective-permute-start.28 = (bf16[1,32,2048]{2,1,0:T(8,128)(2,1)S(1)}, bf16[1,32,2048]{2,1,0:T(8,128)(2,1)S(1)}, u32[]{:S(2)}, u32[]{:S(2)}) collective-permute-start(bf16[1,32,2048]{2,1,0:T(8,128)(2,1)S(1)} %total.13), channel_id=1, source_target_pairs={{0,12},{1,13},{2,14},{3,15},{4,8},{5,9},{6,10},{7,11},{8,4},{9,5},... | collective-permute-start | bytes 393224 | tf_op jit(solution)/shard_map/ppermute | solution.py:236
  (9 other events, 12.7 us)

commit v9 on v8

--- a/solution.py
+++ b/solution.py
@@ -114,10 +114,10 @@
     )
 
 
-def ffn_kernel(owner_ref, scale_ref, gate_ref, up_ref, down_ref, *refs):
+def ffn_kernel(table_ref, gate_ref, up_ref, down_ref, *refs):
     x_refs, (mine_ref, other_ref, x_all, hidden) = refs[:-4], refs[-4:]
     width, ff = gate_ref.shape[1:]
-    group = ff // scale_ref.shape[1]
+    group = ff // table_ref.shape[2]
     step = 2 * group if ff % (2 * group) == 0 else group
     _, pieces, part, _ = mine_ref.shape
     at = 0
@@ -125,18 +125,22 @@
         rows = x_ref.shape[0] * part
         x_all[at : at + rows, :] = x_ref[...].reshape(rows, x_ref.shape[2])
         at += rows
+
+    def scale(which, b):
+        return jnp.exp2(jnp.full((1, group), table_ref[which, 0, b], jnp.int32).astype(jnp.float32))
+
     for f in range(0, ff, step):
         x = x_all[:, :width]
         gate = jnp.dot(x, gate_ref[0, :, f : f + step], preferred_element_type=jnp.float32)
         up = jnp.dot(x, up_ref[0, :, f : f + step], preferred_element_type=jnp.float32)
         for at in range(0, step, group):
             b = (f + at) // group
-            g = gate[:, at : at + group] * scale_ref[0, b]
-            u = up[:, at : at + group] * scale_ref[1, b]
-            h = g / (1.0 + jnp.exp(-g)) * u * scale_ref[2, b]
+            g = gate[:, at : at + group] * scale(0, b)
+            u = up[:, at : at + group] * scale(1, b)
+            h = g / (1.0 + jnp.exp(-g)) * u * scale(2, b)
             hidden[:, f + at : f + at + group] = h.astype(jnp.bfloat16)
     shares = x_all[:, width:].astype(jnp.float32)
-    here = lax.broadcasted_iota(jnp.int32, shares.shape, 1) == owner_ref[0]
+    here = lax.broadcasted_iota(jnp.int32, shares.shape, 1) == lax.axis_index("ep")
     weight = jnp.sum(jnp.where(here, shares, 0.0), axis=1, keepdims=True)
     cols = 512 if width % 512 == 0 else LANES
     for n in range(0, width, cols):
@@ -146,15 +150,15 @@
         other_ref[:, :, :, n : n + cols] = out[2:]
 
 
-def ffn(xs, owner, scales, weights):
+def ffn(xs, table, weights):
     pieces = sum(x.shape[0] for x in xs) // 4
     _, part, full = xs[0].shape
     width, ff = weights[0].shape[1:]
     rows = 4 * pieces * part
     return call(
         ffn_kernel,
-        [owner, scales, *weights, *xs],
-        [SMEM, SMEM] + [VMEM] * (3 + len(xs)),
+        [table, *weights, *xs],
+        [SMEM] + [VMEM] * (3 + len(xs)),
         [jax.ShapeDtypeStruct((2, pieces, part, width), jnp.bfloat16)] * 2,
         [pltpu.VMEM((rows, full), jnp.bfloat16), pltpu.VMEM((rows, ff), jnp.bfloat16)],
         name="ffn",
@@ -222,8 +226,7 @@
 ):
     owners = lax.axis_size("ep")
     batches = hidden_in.shape[0]
-    scales = jnp.exp2(exponent_table[0].astype(jnp.float32))
-    owner = lax.axis_index("ep").astype(jnp.int32).reshape(1)
+    table = exponent_table.transpose(1, 0, 2)
 
     line = owners // 4
     half = line // 2
@@ -275,7 +278,7 @@
         xs = [near[batch], far[batch], *there[batch]]
         xs += [to_core(rows) for rows in xs]
         xs[0] = after(xs[0], far[-1], ahead, *sent[-1:])
-        mine, other = ffn(xs, owner, scales, weights)
+        mine, other = ffn(xs, table, weights)
         if batch + 1 < batches:
             other = after(other, *there[batch + 1])
         if batch:

time: 98.4 us -> 89.5 us (0.910)
  local copies, waits for them, and re-layouts: 10.5 us -> 0.01 us
  starting transfers between devices: 34.2 us -> 39.3 us
  Pallas kernels: 21 us -> 18 us
    unnamed x25 -> x4, local copies, waits for them, and re-layouts: 10.5 us -> 0.01 us
    ppermute x8, starting transfers between devices: 21.1 us -> 25.4 us  [mirror(): return lax.ppermute(rows, 'ep', [(i, partner(i)) for i in range(owners)])]
    pallas_call x14, Pallas kernels: 21 us -> 18 us  [call(): pl.pallas_call(kernel, out_shape=shapes, in_specs=specs, out_specs=[VMEM]...]
    ppermute x9, waiting for transfers between devices: 11.2 us -> 13.3 us  [to_mid(): return lax.ppermute(rows, 'ep', [(i, i ^ 2) for i in range(owners)])]
    ppermute x8, waiting for transfers between devices: 12.1 us -> 10.5 us  [mirror(): return lax.ppermute(rows, 'ep', [(i, partner(i)) for i in range(owners)])]
    ppermute x9, starting transfers between devices: 11 us -> 12 us  [to_mid(): return lax.ppermute(rows, 'ep', [(i, i ^ 2) for i in range(owners)])]
  transfers between devices with their start and end apart: 29 -> 29, of which waited for: 14 -> 16; matrix products, arithmetic and copies ran while one was open for 0% -> 0% of each run, Pallas kernels for 18% -> 18%
where the time goes in v9:
time: 89.5 us; the launch traced here: 89.3 us
  starting transfers between devices  39.3 us (44%)
  waiting for transfers between devices  31.9 us (36%)
  Pallas kernels  18 us (20%)
    ppermute x8, starting transfers between devices, mirror(): return lax.ppermute(rows, 'ep', [(i, partner(i)) for i in range(owners)])  25.4 us
    pallas_call x14, Pallas kernels, call(): pl.pallas_call(kernel, out_shape=shapes, in_specs=specs, out_specs=[VMEM]...  18 us
    ppermute x9, waiting for transfers between devices, to_mid(): return lax.ppermute(rows, 'ep', [(i, i ^ 2) for i in range(owners)])  13.3 us
    ppermute x9, starting transfers between devices, to_mid(): return lax.ppermute(rows, 'ep', [(i, i ^ 2) for i in range(owners)])  12 us
    ppermute x8, waiting for transfers between devices, mirror(): return lax.ppermute(rows, 'ep', [(i, partner(i)) for i in range(owners)])  10.5 us
    ppermute x12, waiting for transfers between devices, to_core(): return lax.ppermute(rows, 'ep', [(i, i ^ 1) for i in range(owners)])  8.05 us
    ppermute x12, starting transfers between devices, to_core(): return lax.ppermute(rows, 'ep', [(i, i ^ 1) for i in range(owners)])  1.91 us
  transfers between devices with their start and end apart: 29, of which 16 were waited for; matrix products, arithmetic and copies ran while one was open for 0% of the time, Pallas kernels for 18%

profile of v9, /device:TPU:0, one launch (start us, length us, event | category | flops | bytes accessed | tf_op | source)
XLA Modules:
  0.0 89.3 jit_solution(11926443224334804814)
XLA Ops:
  0.0 1.2 %prepare.1 = (bf16[1,32,2176]{2,1,0:T(8,128)(2,1)S(1)}, bf16[1,32,2176]{2,1,0:T(8,128)(2,1)S(1)}) custom-call(bf16[2,32,2048]{2,1,0:T(8,128)(2,1)} %hidden_ref.1, s32[2,8,32]{2,1,0:T(8,128)} %bitcast.6, s32[2,8,32]{2,1,0:T(8,128)} %bitcast.7, f32[1,2048]{1,0:T(1,128)} %bitcast.8), custom_call_target="tpu_custom_call" | custom-call | tf_op jit(solution)/shard_map/prepare/pallas_call | solution.py:26
  1.2 3.0 %collective-permute-start.2 = (bf16[1,32,2176]{2,1,0:T(8,128)(2,1)S(1)}, bf16[1,32,2176]{2,1,0:T(8,128)(2,1)S(1)}, u32[]{:S(2)}, u32[]{:S(2)}) collective-permute-start(bf16[1,32,2176]{2,1,0:T(8,128)(2,1)S(1)} %get-tuple-element.30.refs_0_), channel_id=1, source_target_pairs={{0,2},{1,3},{2,0},{3,1},{4,6},{5,7},{6,4},{7,5},{8,10},{9,11},{10,... | collective-permute-start | bytes 417800 | tf_op jit(solution)/shard_map/ppermute | solution.py:242
  4.3 4.0 %collective-permute-start = (bf16[1,32,2176]{2,1,0:T(8,128)(2,1)S(1)}, bf16[1,32,2176]{2,1,0:T(8,128)(2,1)S(1)}, u32[]{:S(2)}, u32[]{:S(2)}) collective-permute-start(bf16[1,32,2176]{2,1,0:T(8,128)(2,1)S(1)} %get-tuple-element.28.refs_0_), channel_id=1, source_target_pairs={{0,12},{1,13},{2,14},{3,15},{4,8},{5,9},{6,10},{7,11},{8,4},{9,5},... | collective-permute-start | bytes 417800 | tf_op jit(solution)/shard_map/ppermute | solution.py:239
  8.8 2.2 %collective-permute-done.1.refs_2_ = bf16[1,32,2176]{2,1,0:T(8,128)(2,1)S(1)} collective-permute-done((bf16[1,32,2176]{2,1,0:T(8,128)(2,1)S(1)}, bf16[1,32,2176]{2,1,0:T(8,128)(2,1)S(1)}, u32[]{:S(2)}, u32[]{:S(2)}) %collective-permute-start.1) | collective-permute-done | bytes 139296 | tf_op jit(solution)/shard_map/ppermute | solution.py:242
  10.9 0.7 collective-permute-done.refs_1_
  11.6 2.7 %collective-permute-start.4 = (bf16[2,32,2176]{2,1,0:T(8,128)(2,1)S(1)}, bf16[2,32,2176]{2,1,0:T(8,128)(2,1)S(1)}, u32[]{:S(2)}, u32[]{:S(2)}) collective-permute-start(bf16[2,32,2176]{2,1,0:T(8,128)(2,1)S(1)} %join.2.refs_0_), channel_id=1, source_target_pairs={{0,4},{1,5},{2,6},{3,7},{4,0},{5,1},{6,2},{7,3},{8,12},{9,13},{10,... | collective-permute-start | bytes 835592 | tf_op jit(solution)/shard_map/ppermute | solution.py:239
  14.3 2.7 %collective-permute-start.3 = (bf16[1,32,2176]{2,1,0:T(8,128)(2,1)S(1)}, bf16[1,32,2176]{2,1,0:T(8,128)(2,1)S(1)}, u32[]{:S(2)}, u32[]{:S(2)}) collective-permute-start(bf16[1,32,2176]{2,1,0:T(8,128)(2,1)S(1)} %get-tuple-element.30.refs_0_), channel_id=1, source_target_pairs={{0,12},{1,13},{2,14},{3,15},{4,8},{5,9},{6,10},{7,11},{8,4},{9,5},... | collective-permute-start | bytes 417800 | tf_op jit(solution)/shard_map/ppermute | solution.py:239
  16.9 1.5 %collective-permute-start.5 = (bf16[1,32,2176]{2,1,0:T(8,128)(2,1)S(1)}, bf16[1,32,2176]{2,1,0:T(8,128)(2,1)S(1)}, u32[]{:S(2)}, u32[]{:S(2)}) collective-permute-start(bf16[1,32,2176]{2,1,0:T(8,128)(2,1)S(1)} %collective-permute-done.refs_1_), channel_id=1, source_target_pairs={{0,2},{1,3},{2,0},{3,1},{4,6},{5,7},{6,4},{7,5},{8,10},{9,11},{10,... | collective-permute-start | bytes 417800 | tf_op jit(solution)/shard_map/ppermute | solution.py:242
  18.5 5.3 %collective-permute-done.3.refs_1_ = bf16[1,32,2176]{2,1,0:T(8,128)(2,1)S(1)} collective-permute-done((bf16[1,32,2176]{2,1,0:T(8,128)(2,1)S(1)}, bf16[1,32,2176]{2,1,0:T(8,128)(2,1)S(1)}, u32[]{:S(2)}, u32[]{:S(2)}) %collective-permute-start.3) | collective-permute-done | bytes 139296 | tf_op jit(solution)/shard_map/ppermute | solution.py:239
  23.9 1.6 %collective-permute-start.8 = (bf16[2,32,2176]{2,1,0:T(8,128)(2,1)S(1)}, bf16[2,32,2176]{2,1,0:T(8,128)(2,1)S(1)}, u32[]{:S(2)}, u32[]{:S(2)}) collective-permute-start(bf16[2,32,2176]{2,1,0:T(8,128)(2,1)S(1)} %collective-permute-done.4.refs_1_), channel_id=1, source_target_pairs={{0,2},{1,3},{2,0},{3,1},{4,6},{5,7},{6,4},{7,5},{8,10},{9,11},{10,... | collective-permute-start | bytes 835592 | tf_op jit(solution)/shard_map/ppermute | solution.py:242
  26.5 3.8 %load.1 = (bf16[1,2048,768]{2,1,0:T(8,128)(2,1)S(1)}, bf16[1,2048,768]{2,1,0:T(8,128)(2,1)S(1)}, bf16[1,768,2048]{2,1,0:T(8,128)(2,1)S(1)}) custom-call(bf16[1,2048,768]{2,1,0:T(8,128)(2,1)} %refs_0_, bf16[1,2048,768]{2,1,0:T(8,128)(2,1)} %refs_1_, bf16[1,768,2048]{2,1,0:T(8,128)(2,1)} %refs_2_), custom_call_target="tpu_custom_call" | custom-call | tf_op jit(solution)/shard_map/load/pallas_call | solution.py:26
  30.5 1.6 %collective-permute-done.8.refs_4_ = bf16[2,32,2176]{2,1,0:T(8,128)(2,1)S(1)} collective-permute-done((bf16[2,32,2176]{2,1,0:T(8,128)(2,1)S(1)}, bf16[2,32,2176]{2,1,0:T(8,128)(2,1)S(1)}, u32[]{:S(2)}, u32[]{:S(2)}) %collective-permute-start.8) | collective-permute-done | bytes 278560 | tf_op jit(solution)/shard_map/ppermute | solution.py:242
  32.1 1.5 %collective-permute-start.14 = (bf16[2,32,2176]{2,1,0:T(8,128)(2,1)S(1)}, bf16[2,32,2176]{2,1,0:T(8,128)(2,1)S(1)}, u32[]{:S(2)}, u32[]{:S(2)}) collective-permute-start(bf16[2,32,2176]{2,1,0:T(8,128)(2,1)S(1)} %collective-permute-done.6.refs_1_), channel_id=1, source_target_pairs={{0,2},{1,3},{2,0},{3,1},{4,6},{5,7},{6,4},{7,5},{8,10},{9,11},{10,... | collective-permute-start | bytes 835592 | tf_op jit(solution)/shard_map/ppermute | solution.py:242
  33.8 1.1 %collective-permute-done.12.refs_8_ = bf16[1,32,2176]{2,1,0:T(8,128)(2,1)S(1)} collective-permute-done((bf16[1,32,2176]{2,1,0:T(8,128)(2,1)S(1)}, bf16[1,32,2176]{2,1,0:T(8,128)(2,1)S(1)}, u32[]{:S(2)}, u32[]{:S(2)}) %collective-permute-start.12) | collective-permute-done | bytes 139296 | tf_op jit(solution)/shard_map/ppermute | solution.py:245
  35.0 5.7 %ffn.2 = (bf16[2,4,32,2048]{3,2,1,0:T(8,128)(2,1)S(1)}, bf16[2,4,32,2048]{3,2,1,0:T(8,128)(2,1)S(1)}) custom-call(s32[3,1,6]{2,1,0:T(1,128)S(1)} %bitcast.4, bf16[1,2048,768]{2,1,0:T(8,128)(2,1)S(1)} %get-tuple-element.35.gate_ref, bf16[1,2048,768]{2,1,0:T(8,128)(2,1)S(1)} %get-tuple-element.36.up_ref, bf16[1,768,2048]{2,1,0:T(8,128)(2,1)S(1)} %get-tuple-element.37.down_ref, ...), custom_call_target="tpu_custom_call" | custom-call | tf_op jit(solution)/shard_map/ffn/pallas_call | solution.py:26
  41.1 2.7 %collective-permute-done.15.refs_1_ = bf16[2,4,32,2048]{3,2,1,0:T(8,128)(2,1)S(1)} collective-permute-done((bf16[2,4,32,2048]{3,2,1,0:T(8,128)(2,1)S(1)}, bf16[2,4,32,2048]{3,2,1,0:T(8,128)(2,1)S(1)}, u32[]{:S(2)}, u32[]{:S(2)}) %collective-permute-start.15) | collective-permute-done | bytes 1048608 | tf_op jit(solution)/shard_map/ppermute | solution.py:245
  43.9 1.6 %collective-permute-start.16 = (bf16[4,32,2048]{2,1,0:T(8,128)(2,1)S(1)}, bf16[4,32,2048]{2,1,0:T(8,128)(2,1)S(1)}, u32[]{:S(2)}, u32[]{:S(2)}) collective-permute-start(bf16[4,32,2048]{2,1,0:T(8,128)(2,1)S(1)} %total.7), channel_id=1, source_target_pairs={{0,2},{1,3},{2,0},{3,1},{4,6},{5,7},{6,4},{7,5},{8,10},{9,11},{10,... | collective-permute-start | bytes 1572872 | tf_op jit(solution)/shard_map/ppermute | solution.py:242
  45.5 0.5 collective-permute-start.19
  47.0 1.2 %collective-permute-done.22.refs_8_ = bf16[1,32,2176]{2,1,0:T(8,128)(2,1)S(1)} collective-permute-done((bf16[1,32,2176]{2,1,0:T(8,128)(2,1)S(1)}, bf16[1,32,2176]{2,1,0:T(8,128)(2,1)S(1)}, u32[]{:S(2)}, u32[]{:S(2)}) %collective-permute-start.22) | collective-permute-done | bytes 139296 | tf_op jit(solution)/shard_map/ppermute | solution.py:245
  48.3 5.7 %ffn.3 = (bf16[2,4,32,2048]{3,2,1,0:T(8,128)(2,1)S(1)}, bf16[2,4,32,2048]{3,2,1,0:T(8,128)(2,1)S(1)}) custom-call(s32[3,1,6]{2,1,0:T(1,128)S(1)} %bitcast.5, bf16[1,2048,768]{2,1,0:T(8,128)(2,1)S(1)} %get-tuple-element.35.gate_ref, bf16[1,2048,768]{2,1,0:T(8,128)(2,1)S(1)} %get-tuple-element.36.up_ref, bf16[1,768,2048]{2,1,0:T(8,128)(2,1)S(1)} %get-tuple-element.37.down_ref, ...), custom_call_target="tpu_custom_call" | custom-call | tf_op jit(solution)/shard_map/ffn/pallas_call | solution.py:26
  54.0 3.9 %collective-permute-done.16.refs_2_ = bf16[4,32,2048]{2,1,0:T(8,128)(2,1)S(1)} collective-permute-done((bf16[4,32,2048]{2,1,0:T(8,128)(2,1)S(1)}, bf16[4,32,2048]{2,1,0:T(8,128)(2,1)S(1)}, u32[]{:S(2)}, u32[]{:S(2)}) %collective-permute-start.16) | collective-permute-done | bytes 524320 | tf_op jit(solution)/shard_map/ppermute | solution.py:242
  57.9 2.7 %collective-permute-done.24.refs_1_.refs_6_ = bf16[2,4,32,2048]{3,2,1,0:T(8,128)(2,1)S(1)} collective-permute-done((bf16[2,4,32,2048]{3,2,1,0:T(8,128)(2,1)S(1)}, bf16[2,4,32,2048]{3,2,1,0:T(8,128)(2,1)S(1)}, u32[]{:S(2)}, u32[]{:S(2)}) %collective-permute-start.24) | collective-permute-done | bytes 1048608 | tf_op jit(solution)/shard_map/ppermute | solution.py:245
  60.7 1.6 %collective-permute-start.26 = (bf16[2,32,2048]{2,1,0:T(8,128)(2,1)S(1)}, bf16[2,32,2048]{2,1,0:T(8,128)(2,1)S(1)}, u32[]{:S(2)}, u32[]{:S(2)}) collective-permute-start(bf16[2,32,2048]{2,1,0:T(8,128)(2,1)S(1)} %total.11), channel_id=1, source_target_pairs={{0,2},{1,3},{2,0},{3,1},{4,6},{5,7},{6,4},{7,5},{8,10},{9,11},{10,... | collective-permute-start | bytes 786440 | tf_op jit(solution)/shard_map/ppermute | solution.py:242
  62.4 2.0 %collective-permute-start.17 = (bf16[2,32,2048]{2,1,0:T(8,128)(2,1)S(1)}, bf16[2,32,2048]{2,1,0:T(8,128)(2,1)S(1)}, u32[]{:S(2)}, u32[]{:S(2)}) collective-permute-start(bf16[2,32,2048]{2,1,0:T(8,128)(2,1)S(1)} %total.8), channel_id=1, source_target_pairs={{0,4},{1,5},{2,6},{3,7},{4,0},{5,1},{6,2},{7,3},{8,12},{9,13},{10,... | collective-permute-start | bytes 786440 | tf_op jit(solution)/shard_map/ppermute | solution.py:239
  64.4 0.6 collective-permute-start.25
  65.0 4.9 %collective-permute-done.26.refs_2_ = bf16[2,32,2048]{2,1,0:T(8,128)(2,1)S(1)} collective-permute-done((bf16[2,32,2048]{2,1,0:T(8,128)(2,1)S(1)}, bf16[2,32,2048]{2,1,0:T(8,128)(2,1)S(1)}, u32[]{:S(2)}, u32[]{:S(2)}) %collective-permute-start.26) | collective-permute-done | bytes 262176 | tf_op jit(solution)/shard_map/ppermute | solution.py:242
  70.0 2.0 %collective-permute-start.27 = (bf16[2,32,2048]{2,1,0:T(8,128)(2,1)S(1)}, bf16[2,32,2048]{2,1,0:T(8,128)(2,1)S(1)}, u32[]{:S(2)}, u32[]{:S(2)}) collective-permute-start(bf16[2,32,2048]{2,1,0:T(8,128)(2,1)S(1)} %total.12), channel_id=1, source_target_pairs={{0,4},{1,5},{2,6},{3,7},{4,0},{5,1},{6,2},{7,3},{8,12},{9,13},{10,... | collective-permute-start | bytes 786440 | tf_op jit(solution)/shard_map/ppermute | solution.py:239
  72.1 4.2 %collective-permute-start.18 = (bf16[1,32,2048]{2,1,0:T(8,128)(2,1)S(1)}, bf16[1,32,2048]{2,1,0:T(8,128)(2,1)S(1)}, u32[]{:S(2)}, u32[]{:S(2)}) collective-permute-start(bf16[1,32,2048]{2,1,0:T(8,128)(2,1)S(1)} %total.9), channel_id=1, source_target_pairs={{0,12},{1,13},{2,14},{3,15},{4,8},{5,9},{6,10},{7,11},{8,4},{9,5},... | collective-permute-start | bytes 393224 | tf_op jit(solution)/shard_map/ppermute | solution.py:239
  76.3 1.4 %collective-permute-done.27.refs_3_.refs_8_ = bf16[2,32,2048]{2,1,0:T(8,128)(2,1)S(1)} collective-permute-done((bf16[2,32,2048]{2,1,0:T(8,128)(2,1)S(1)}, bf16[2,32,2048]{2,1,0:T(8,128)(2,1)S(1)}, u32[]{:S(2)}, u32[]{:S(2)}) %collective-permute-start.27) | collective-permute-done | bytes 262176 | tf_op jit(solution)/shard_map/ppermute | solution.py:239
  77.7 7.7 %collective-permute-start.28 = (bf16[1,32,2048]{2,1,0:T(8,128)(2,1)S(1)}, bf16[1,32,2048]{2,1,0:T(8,128)(2,1)S(1)}, u32[]{:S(2)}, u32[]{:S(2)}) collective-permute-start(bf16[1,32,2048]{2,1,0:T(8,128)(2,1)S(1)} %total.13), channel_id=1, source_target_pairs={{0,12},{1,13},{2,14},{3,15},{4,8},{5,9},{6,10},{7,11},{8,4},{9,5},... | collective-permute-start | bytes 393224 | tf_op jit(solution)/shard_map/ppermute | solution.py:239
  85.5 2.9 %collective-permute-done.28.refs_9_ = bf16[1,32,2048]{2,1,0:T(8,128)(2,1)S(1)} collective-permute-done((bf16[1,32,2048]{2,1,0:T(8,128)(2,1)S(1)}, bf16[1,32,2048]{2,1,0:T(8,128)(2,1)S(1)}, u32[]{:S(2)}, u32[]{:S(2)}) %collective-permute-start.28) | collective-permute-done | bytes 131104 | tf_op jit(solution)/shard_map/ppermute | solution.py:239
  88.4 0.9 %finish.1 = bf16[2,32,2048]{2,1,0:T(8,128)(2,1)} custom-call(bf16[2,32,2048]{2,1,0:T(8,128)(2,1)S(1)} %copy-done, bf16[2,4,32,2048]{3,2,1,0:T(8,128)(2,1)S(1)} %get-tuple-element.42.refs_0_, bf16[2,4,32,2048]{3,2,1,0:T(8,128)(2,1)S(1)} %collective-permute-done.15.refs_1_, bf16[4,32,2048]{2,1,0:T(8,128)(2,1)S(1)} %collective-permute-done.16.refs_2_, ...), custom_call_target="tpu_custom_call" | custom-call | tf_op jit(solution)/shard_map/finish/pallas_call | solution.py:26
  (44 shorter events, 4.0 us)
Async XLA Ops:
  1.2 7.5 %collective-permute-start.2 = (bf16[1,32,2176]{2,1,0:T(8,128)(2,1)S(1)}, bf16[1,32,2176]{2,1,0:T(8,128)(2,1)S(1)}, u32[]{:S(2)}, u32[]{:S(2)}) collective-permute-start(bf16[1,32,2176]{2,1,0:T(8,128)(2,1)S(1)} %get-tuple-element.30.refs_0_), channel_id=1, source_target_pairs={{0,2},{1,3},{2,0},{3,1},{4,6},{5,7},{6,4},{7,5},{8,10},{9,11},{10,... | collective-permute-start | bytes 417800 | tf_op jit(solution)/shard_map/ppermute | solution.py:242
  4.3 6.7 %collective-permute-start.1 = (bf16[1,32,2176]{2,1,0:T(8,128)(2,1)S(1)}, bf16[1,32,2176]{2,1,0:T(8,128)(2,1)S(1)}, u32[]{:S(2)}, u32[]{:S(2)}) collective-permute-start(bf16[1,32,2176]{2,1,0:T(8,128)(2,1)S(1)} %get-tuple-element.28.refs_0_), channel_id=1, source_target_pairs={{0,2},{1,3},{2,0},{3,1},{4,6},{5,7},{6,4},{7,5},{8,10},{9,11},{10,... | collective-permute-start | bytes 417800 | tf_op jit(solution)/shard_map/ppermute | solution.py:242
  4.3 7.2 %collective-permute-start = (bf16[1,32,2176]{2,1,0:T(8,128)(2,1)S(1)}, bf16[1,32,2176]{2,1,0:T(8,128)(2,1)S(1)}, u32[]{:S(2)}, u32[]{:S(2)}) collective-permute-start(bf16[1,32,2176]{2,1,0:T(8,128)(2,1)S(1)} %get-tuple-element.28.refs_0_), channel_id=1, source_target_pairs={{0,12},{1,13},{2,14},{3,15},{4,8},{5,9},{6,10},{7,11},{8,4},{9,5},... | collective-permute-start | bytes 417800 | tf_op jit(solution)/shard_map/ppermute | solution.py:239
  11.6 12.2 %collective-permute-start.4 = (bf16[2,32,2176]{2,1,0:T(8,128)(2,1)S(1)}, bf16[2,32,2176]{2,1,0:T(8,128)(2,1)S(1)}, u32[]{:S(2)}, u32[]{:S(2)}) collective-permute-start(bf16[2,32,2176]{2,1,0:T(8,128)(2,1)S(1)} %join.2.refs_0_), channel_id=1, source_target_pairs={{0,4},{1,5},{2,6},{3,7},{4,0},{5,1},{6,2},{7,3},{8,12},{9,13},{10,... | collective-permute-start | bytes 835592 | tf_op jit(solution)/shard_map/ppermute | solution.py:239
  14.3 9.5 %collective-permute-start.3 = (bf16[1,32,2176]{2,1,0:T(8,128)(2,1)S(1)}, bf16[1,32,2176]{2,1,0:T(8,128)(2,1)S(1)}, u32[]{:S(2)}, u32[]{:S(2)}) collective-permute-start(bf16[1,32,2176]{2,1,0:T(8,128)(2,1)S(1)} %get-tuple-element.30.refs_0_), channel_id=1, source_target_pairs={{0,12},{1,13},{2,14},{3,15},{4,8},{5,9},{6,10},{7,11},{8,4},{9,5},... | collective-permute-start | bytes 417800 | tf_op jit(solution)/shard_map/ppermute | solution.py:239
  16.9 6.9 %collective-permute-start.5 = (bf16[1,32,2176]{2,1,0:T(8,128)(2,1)S(1)}, bf16[1,32,2176]{2,1,0:T(8,128)(2,1)S(1)}, u32[]{:S(2)}, u32[]{:S(2)}) collective-permute-start(bf16[1,32,2176]{2,1,0:T(8,128)(2,1)S(1)} %collective-permute-done.refs_1_), channel_id=1, source_target_pairs={{0,2},{1,3},{2,0},{3,1},{4,6},{5,7},{6,4},{7,5},{8,10},{9,11},{10,... | collective-permute-start | bytes 417800 | tf_op jit(solution)/shard_map/ppermute | solution.py:242
  23.8 11.1 %copy-start.1 = (s32[1,3,6]{2,0,1:T(1,128)S(1)}, s32[1,3,6]{2,0,1:T(1,128)}, u32[]{:S(2)}) copy-start(s32[1,3,6]{2,0,1:T(1,128)} %param.15) | copy-start | bytes 220
  23.9 6.6 %collective-permute-start.6 = (bf16[2,32,2176]{2,1,0:T(8,128)(2,1)S(1)}, bf16[2,32,2176]{2,1,0:T(8,128)(2,1)S(1)}, u32[]{:S(2)}, u32[]{:S(2)}) collective-permute-start(bf16[2,32,2176]{2,1,0:T(8,128)(2,1)S(1)} %join.3.refs_0_), channel_id=1, source_target_pairs={{0,4},{1,5},{2,6},{3,7},{4,0},{5,1},{6,2},{7,3},{8,12},{9,13},{10,... | collective-permute-start | bytes 835592 | tf_op jit(solution)/shard_map/ppermute | solution.py:239
  23.9 8.1 %collective-permute-start.8 = (bf16[2,32,2176]{2,1,0:T(8,128)(2,1)S(1)}, bf16[2,32,2176]{2,1,0:T(8,128)(2,1)S(1)}, u32[]{:S(2)}, u32[]{:S(2)}) collective-permute-start(bf16[2,32,2176]{2,1,0:T(8,128)(2,1)S(1)} %collective-permute-done.4.refs_1_), channel_id=1, source_target_pairs={{0,2},{1,3},{2,0},{3,1},{4,6},{5,7},{6,4},{7,5},{8,10},{9,11},{10,... | collective-permute-start | bytes 835592 | tf_op jit(solution)/shard_map/ppermute | solution.py:242
  25.5 6.5 %collective-permute-start.11 = (bf16[1,32,2176]{2,1,0:T(8,128)(2,1)S(1)}, bf16[1,32,2176]{2,1,0:T(8,128)(2,1)S(1)}, u32[]{:S(2)}, u32[]{:S(2)}) collective-permute-start(bf16[1,32,2176]{2,1,0:T(8,128)(2,1)S(1)} %collective-permute-done.1.refs_2_), channel_id=1, source_target_pairs={{0,1},{1,0},{2,3},{3,2},{4,5},{5,4},{6,7},{7,6},{8,9},{9,8},{10,11... | collective-permute-start | bytes 417800 | tf_op jit(solution)/shard_map/ppermute | solution.py:245
  25.5 9.4 %collective-permute-start.9 = (bf16[2,32,2176]{2,1,0:T(8,128)(2,1)S(1)}, bf16[2,32,2176]{2,1,0:T(8,128)(2,1)S(1)}, u32[]{:S(2)}, u32[]{:S(2)}) collective-permute-start(bf16[2,32,2176]{2,1,0:T(8,128)(2,1)S(1)} %join.2.refs_0_), channel_id=1, source_target_pairs={{0,1},{1,0},{2,3},{3,2},{4,5},{5,4},{6,7},{7,6},{8,9},{9,8},{10,11... | collective-permute-start | bytes 835592 | tf_op jit(solution)/shard_map/ppermute | solution.py:245
  26.0 7.5 %collective-permute-start.7 = (bf16[1,32,2176]{2,1,0:T(8,128)(2,1)S(1)}, bf16[1,32,2176]{2,1,0:T(8,128)(2,1)S(1)}, u32[]{:S(2)}, u32[]{:S(2)}) collective-permute-start(bf16[1,32,2176]{2,1,0:T(8,128)(2,1)S(1)} %collective-permute-done.3.refs_1_), channel_id=1, source_target_pairs={{0,2},{1,3},{2,0},{3,1},{4,6},{5,7},{6,4},{7,5},{8,10},{9,11},{10,... | collective-permute-start | bytes 417800 | tf_op jit(solution)/shard_map/ppermute | solution.py:242
  30.5 4.5 %collective-permute-start.10 = (bf16[2,32,2176]{2,1,0:T(8,128)(2,1)S(1)}, bf16[2,32,2176]{2,1,0:T(8,128)(2,1)S(1)}, u32[]{:S(2)}, u32[]{:S(2)}) collective-permute-start(bf16[2,32,2176]{2,1,0:T(8,128)(2,1)S(1)} %collective-permute-done.4.refs_1_), channel_id=1, source_target_pairs={{0,1},{1,0},{2,3},{3,2},{4,5},{5,4},{6,7},{7,6},{8,9},{9,8},{10,11... | collective-permute-start | bytes 835592 | tf_op jit(solution)/shard_map/ppermute | solution.py:245
  32.1 2.9 %collective-permute-start.13 = (bf16[2,32,2176]{2,1,0:T(8,128)(2,1)S(1)}, bf16[2,32,2176]{2,1,0:T(8,128)(2,1)S(1)}, u32[]{:S(2)}, u32[]{:S(2)}) collective-permute-start(bf16[2,32,2176]{2,1,0:T(8,128)(2,1)S(1)} %collective-permute-done.8.refs_4_), channel_id=1, source_target_pairs={{0,1},{1,0},{2,3},{3,2},{4,5},{5,4},{6,7},{7,6},{8,9},{9,8},{10,11... | collective-permute-start | bytes 835592 | tf_op jit(solution)/shard_map/ppermute | solution.py:245
  32.1 9.1 %collective-permute-start.14 = (bf16[2,32,2176]{2,1,0:T(8,128)(2,1)S(1)}, bf16[2,32,2176]{2,1,0:T(8,128)(2,1)S(1)}, u32[]{:S(2)}, u32[]{:S(2)}) collective-permute-start(bf16[2,32,2176]{2,1,0:T(8,128)(2,1)S(1)} %collective-permute-done.6.refs_1_), channel_id=1, source_target_pairs={{0,2},{1,3},{2,0},{3,1},{4,6},{5,7},{6,4},{7,5},{8,10},{9,11},{10,... | collective-permute-start | bytes 835592 | tf_op jit(solution)/shard_map/ppermute | solution.py:242
  33.6 1.4 %collective-permute-start.12 = (bf16[1,32,2176]{2,1,0:T(8,128)(2,1)S(1)}, bf16[1,32,2176]{2,1,0:T(8,128)(2,1)S(1)}, u32[]{:S(2)}, u32[]{:S(2)}) collective-permute-start(bf16[1,32,2176]{2,1,0:T(8,128)(2,1)S(1)} %collective-permute-done.5.refs_3_), channel_id=1, source_target_pairs={{0,1},{1,0},{2,3},{3,2},{4,5},{5,4},{6,7},{7,6},{8,9},{9,8},{10,11... | collective-permute-start | bytes 417800 | tf_op jit(solution)/shard_map/ppermute | solution.py:245
  41.1 2.7 %collective-permute-start.15 = (bf16[2,4,32,2048]{3,2,1,0:T(8,128)(2,1)S(1)}, bf16[2,4,32,2048]{3,2,1,0:T(8,128)(2,1)S(1)}, u32[]{:S(2)}, u32[]{:S(2)}) collective-permute-start(bf16[2,4,32,2048]{3,2,1,0:T(8,128)(2,1)S(1)} %get-tuple-element.44), channel_id=1, source_target_pairs={{0,1},{1,0},{2,3},{3,2},{4,5},{5,4},{6,7},{7,6},{8,9},{9,8},{10,11... | collective-permute-start | bytes 3145736 | tf_op jit(solution)/shard_map/ppermute | solution.py:245
  43.9 14.0 %collective-permute-start.16 = (bf16[4,32,2048]{2,1,0:T(8,128)(2,1)S(1)}, bf16[4,32,2048]{2,1,0:T(8,128)(2,1)S(1)}, u32[]{:S(2)}, u32[]{:S(2)}) collective-permute-start(bf16[4,32,2048]{2,1,0:T(8,128)(2,1)S(1)} %total.7), channel_id=1, source_target_pairs={{0,2},{1,3},{2,0},{3,1},{4,6},{5,7},{6,4},{7,5},{8,10},{9,11},{10,... | collective-permute-start | bytes 1572872 | tf_op jit(solution)/shard_map/ppermute | solution.py:242
  45.5 1.4 %collective-permute-start.21 = (bf16[1,32,2176]{2,1,0:T(8,128)(2,1)S(1)}, bf16[1,32,2176]{2,1,0:T(8,128)(2,1)S(1)}, u32[]{:S(2)}, u32[]{:S(2)}) collective-permute-start(bf16[1,32,2176]{2,1,0:T(8,128)(2,1)S(1)} %collective-permute-done.2.refs_2_), channel_id=1, source_target_pairs={{0,1},{1,0},{2,3},{3,2},{4,5},{5,4},{6,7},{7,6},{8,9},{9,8},{10,11... | collective-permute-start | bytes 417800 | tf_op jit(solution)/shard_map/ppermute | solution.py:245
  45.5 2.8 %collective-permute-start.19 = (bf16[2,32,2176]{2,1,0:T(8,128)(2,1)S(1)}, bf16[2,32,2176]{2,1,0:T(8,128)(2,1)S(1)}, u32[]{:S(2)}, u32[]{:S(2)}) collective-permute-start(bf16[2,32,2176]{2,1,0:T(8,128)(2,1)S(1)} %join.3.refs_0_), channel_id=1, source_target_pairs={{0,1},{1,0},{2,3},{3,2},{4,5},{5,4},{6,7},{7,6},{8,9},{9,8},{10,11... | collective-permute-start | bytes 835592 | tf_op jit(solution)/shard_map/ppermute | solution.py:245
  46.0 2.2 %collective-permute-start.20 = (bf16[2,32,2176]{2,1,0:T(8,128)(2,1)S(1)}, bf16[2,32,2176]{2,1,0:T(8,128)(2,1)S(1)}, u32[]{:S(2)}, u32[]{:S(2)}) collective-permute-start(bf16[2,32,2176]{2,1,0:T(8,128)(2,1)S(1)} %collective-permute-done.6.refs_1_), channel_id=1, source_target_pairs={{0,1},{1,0},{2,3},{3,2},{4,5},{5,4},{6,7},{7,6},{8,9},{9,8},{10,11... | collective-permute-start | bytes 835592 | tf_op jit(solution)/shard_map/ppermute | solution.py:245
  46.0 2.2 %collective-permute-start.23 = (bf16[2,32,2176]{2,1,0:T(8,128)(2,1)S(1)}, bf16[2,32,2176]{2,1,0:T(8,128)(2,1)S(1)}, u32[]{:S(2)}, u32[]{:S(2)}) collective-permute-start(bf16[2,32,2176]{2,1,0:T(8,128)(2,1)S(1)} %collective-permute-done.14.refs_4_), channel_id=1, source_target_pairs={{0,1},{1,0},{2,3},{3,2},{4,5},{5,4},{6,7},{7,6},{8,9},{9,8},{10,11... | collective-permute-start | bytes 835592 | tf_op jit(solution)/shard_map/ppermute | solution.py:245
  46.9 1.4 %collective-permute-start.22 = (bf16[1,32,2176]{2,1,0:T(8,128)(2,1)S(1)}, bf16[1,32,2176]{2,1,0:T(8,128)(2,1)S(1)}, u32[]{:S(2)}, u32[]{:S(2)}) collective-permute-start(bf16[1,32,2176]{2,1,0:T(8,128)(2,1)S(1)} %collective-permute-done.7.refs_3_), channel_id=1, source_target_pairs={{0,1},{1,0},{2,3},{3,2},{4,5},{5,4},{6,7},{7,6},{8,9},{9,8},{10,11... | collective-permute-start | bytes 417800 | tf_op jit(solution)/shard_map/ppermute | solution.py:245
  57.9 2.7 %collective-permute-start.24 = (bf16[2,4,32,2048]{3,2,1,0:T(8,128)(2,1)S(1)}, bf16[2,4,32,2048]{3,2,1,0:T(8,128)(2,1)S(1)}, u32[]{:S(2)}, u32[]{:S(2)}) collective-permute-start(bf16[2,4,32,2048]{3,2,1,0:T(8,128)(2,1)S(1)} %get-tuple-element.48), channel_id=1, source_target_pairs={{0,1},{1,0},{2,3},{3,2},{4,5},{5,4},{6,7},{7,6},{8,9},{9,8},{10,11... | collective-permute-start | bytes 3145736 | tf_op jit(solution)/shard_map/ppermute | solution.py:245
  60.7 9.2 %collective-permute-start.26 = (bf16[2,32,2048]{2,1,0:T(8,128)(2,1)S(1)}, bf16[2,32,2048]{2,1,0:T(8,128)(2,1)S(1)}, u32[]{:S(2)}, u32[]{:S(2)}) collective-permute-start(bf16[2,32,2048]{2,1,0:T(8,128)(2,1)S(1)} %total.11), channel_id=1, source_target_pairs={{0,2},{1,3},{2,0},{3,1},{4,6},{5,7},{6,4},{7,5},{8,10},{9,11},{10,... | collective-permute-start | bytes 786440 | tf_op jit(solution)/shard_map/ppermute | solution.py:242
  62.4 9.7 %collective-permute-start.17 = (bf16[2,32,2048]{2,1,0:T(8,128)(2,1)S(1)}, bf16[2,32,2048]{2,1,0:T(8,128)(2,1)S(1)}, u32[]{:S(2)}, u32[]{:S(2)}) collective-permute-start(bf16[2,32,2048]{2,1,0:T(8,128)(2,1)S(1)} %total.8), channel_id=1, source_target_pairs={{0,4},{1,5},{2,6},{3,7},{4,0},{5,1},{6,2},{7,3},{8,12},{9,13},{10,... | collective-permute-start | bytes 786440 | tf_op jit(solution)/shard_map/ppermute | solution.py:239
  64.4 11.9 %collective-permute-start.25 = (bf16[2,32,2048]{2,1,0:T(8,128)(2,1)S(1)}, bf16[2,32,2048]{2,1,0:T(8,128)(2,1)S(1)}, u32[]{:S(2)}, u32[]{:S(2)}) collective-permute-start(bf16[2,32,2048]{2,1,0:T(8,128)(2,1)S(1)} %total.10), channel_id=1, source_target_pairs={{0,2},{1,3},{2,0},{3,1},{4,6},{5,7},{6,4},{7,5},{8,10},{9,11},{10,... | collective-permute-start | bytes 786440 | tf_op jit(solution)/shard_map/ppermute | solution.py:242
  70.0 18.4 %copy-start = (bf16[2,32,2048]{2,1,0:T(8,128)(2,1)S(1)}, bf16[2,32,2048]{2,1,0:T(8,128)(2,1)}, u32[]{:S(2)}) copy-start(bf16[2,32,2048]{2,1,0:T(8,128)(2,1)} %hidden_ref.1) | copy-start | bytes 786436
  70.0 7.7 %collective-permute-start.27 = (bf16[2,32,2048]{2,1,0:T(8,128)(2,1)S(1)}, bf16[2,32,2048]{2,1,0:T(8,128)(2,1)S(1)}, u32[]{:S(2)}, u32[]{:S(2)}) collective-permute-start(bf16[2,32,2048]{2,1,0:T(8,128)(2,1)S(1)} %total.12), channel_id=1, source_target_pairs={{0,4},{1,5},{2,6},{3,7},{4,0},{5,1},{6,2},{7,3},{8,12},{9,13},{10,... | collective-permute-start | bytes 786440 | tf_op jit(solution)/shard_map/ppermute | solution.py:239
  72.1 13.4 %collective-permute-start.18 = (bf16[1,32,2048]{2,1,0:T(8,128)(2,1)S(1)}, bf16[1,32,2048]{2,1,0:T(8,128)(2,1)S(1)}, u32[]{:S(2)}, u32[]{:S(2)}) collective-permute-start(bf16[1,32,2048]{2,1,0:T(8,128)(2,1)S(1)} %total.9), channel_id=1, source_target_pairs={{0,12},{1,13},{2,14},{3,15},{4,8},{5,9},{6,10},{7,11},{8,4},{9,5},... | collective-permute-start | bytes 393224 | tf_op jit(solution)/shard_map/ppermute | solution.py:239
  77.7 10.7 %collective-permute-start.28 = (bf16[1,32,2048]{2,1,0:T(8,128)(2,1)S(1)}, bf16[1,32,2048]{2,1,0:T(8,128)(2,1)S(1)}, u32[]{:S(2)}, u32[]{:S(2)}) collective-permute-start(bf16[1,32,2048]{2,1,0:T(8,128)(2,1)S(1)} %total.13), channel_id=1, source_target_pairs={{0,12},{1,13},{2,14},{3,15},{4,8},{5,9},{6,10},{7,11},{8,4},{9,5},... | collective-permute-start | bytes 393224 | tf_op jit(solution)/shard_map/ppermute | solution.py:239

commit v10 on v9

--- a/solution.py
+++ b/solution.py
@@ -170,26 +170,28 @@
     return ref[piece] if slot is None else ref[slot, piece]
 
 
-def total_kernel(terms, low, *refs):
-    out_ref = refs[-1]
-    for piece in range(out_ref.shape[0]):
-        total = None
-        for (slot, first), ref in zip(terms, refs[:-1]):
-            term = piece_of(ref, slot, low + piece - first).astype(jnp.float32)
-            total = term if total is None else total + term
-        out_ref[piece] = total.astype(out_ref.dtype)
-
-
-def total(terms, low, high):
+def total_kernel(terms, cuts, *refs):
+    ins, outs = refs[: len(terms)], refs[len(terms) :]
+    for (low, high), out_ref in zip(cuts, outs):
+        for piece in range(low, high):
+            total = None
+            for (slot, first), ref in zip(terms, ins):
+                term = piece_of(ref, slot, piece - first).astype(jnp.float32)
+                total = term if total is None else total + term
+            out_ref[piece - low] = total.astype(out_ref.dtype)
+
+
+def total(terms, cuts):
     arrays = [a for a, _, _ in terms]
-    shape = jax.ShapeDtypeStruct((high - low, *arrays[0].shape[-2:]), arrays[0].dtype)
-    return call(
-        functools.partial(total_kernel, [where for _, *where in terms], low),
+    _, _, part, width = arrays[0].shape
+    shapes = [jax.ShapeDtypeStruct((high - low, part, width), arrays[0].dtype) for low, high in cuts]
+    return call(
+        functools.partial(total_kernel, [where for _, *where in terms], cuts),
         arrays,
         [VMEM] * len(arrays),
-        [shape],
+        shapes,
         name="total",
-    )[0]
+    )
 
 
 def finish_kernel(terms, hidden_ref, *refs):
@@ -231,12 +233,14 @@
     line = owners // 4
     half = line // 2
 
+    def along_line(rows, place_of):
+        return lax.ppermute(rows, "ep", [(i, place_of(i // 4) * 4 + i % 4) for i in range(owners)])
+
+    def mirrored(p, span):
+        return p // span * span + span - 1 - p % span
+
     def mirror(rows, span):
-        def partner(i):
-            p = i // 4
-            return (p // span * span + span - 1 - p % span) * 4 + i % 4
-
-        return lax.ppermute(rows, "ep", [(i, partner(i)) for i in range(owners)])
+        return along_line(rows, lambda p: mirrored(p, span))
 
     def to_mid(rows):
         return lax.ppermute(rows, "ep", [(i, i ^ 2) for i in range(owners)])
@@ -244,64 +248,71 @@
     def to_core(rows):
         return lax.ppermute(rows, "ep", [(i, i ^ 1) for i in range(owners)])
 
+    spans = []
+    while line >> len(spans) > 2:
+        spans.append(line >> len(spans))
+
+    def owner_of(p, piece, levels):
+        for level in range(levels, 0, -1):
+            if piece >= 1 << (level - 1):
+                p, piece = mirrored(p, spans[level - 1]), piece - (1 << (level - 1))
+        return p
+
     payload = prepare(hidden_in, expert_ids, route_share, norm_gain, -(-owners // LANES) * LANES)
 
     own_there = [to_mid(rows) for rows in payload]
-    near, far, there = [], [], []
+    near, near_there = [], []
+    weights = None
     for batch, rows in enumerate(payload):
         if batch:
             rows = after(rows, near[-1])
-        there.append([own_there[batch]])
-        span = line
-        while span > 2:
+        near_there.append([own_there[batch]])
+        for span in spans:
             received = mirror(rows, span)
-            if not batch:
-                received = after(received, *own_there)
-            there[batch].append(to_mid(received))
+            received = after(received, *(weights if batch else own_there))
+            near_there[batch].append(to_mid(received))
             rows = join(rows, received)
-            if batch:
-                rows = after(rows, far[-1])
-            span //= 2
         near.append(rows)
-        far.append(mirror(rows if not batch else after(rows, *there[batch - 1]), 2))
-    weights = load([after(w, near[-1]) for w in (gate_weight, up_weight, down_weight)])
-    far[-1] = after(far[-1], *weights)
-    ahead = there[-1][-1]
+        if weights is None:
+            weights = load([after(w, rows) for w in (gate_weight, up_weight, down_weight)])
+    far = [mirror(rows, 2) for rows in near]
+    far_there = [to_mid(rows) for rows in far]
+
+    halves, sent, back = [], [], []
     for batch in range(batches):
-        rows = far[batch]
-        if batch + 1 < batches:
-            rows = after(rows, near[batch + 1])
-        there[batch].append(to_mid(rows))
-
-    terms, sent, back = [], [], []
+        ahead = batch + 1 < batches
+        for at, xs in enumerate(([near[batch], *near_there[batch]], [far[batch], far_there[batch]])):
+            xs = [*xs, *[to_core(x) for x in xs]]
+            first = [near[batch + 1]] if ahead and at == 0 else []
+            xs[0] = after(xs[0], *first, *sent[-1:])
+            mine, other = ffn(xs, table, weights)
+            wait = []
+            if ahead:
+                wait = [far_there[batch + 1]]
+                if at == 0:
+                    wait = [far[batch + 1], far_there[batch], *near_there[batch + 1]]
+            other = to_core(after(other, *wait, *back[-2:-1]))
+            sent.append(total([(mine, 1, 0), (other, 1, 0)], [(0, half)])[0])
+            back.append(to_mid(sent[-1]))
+            halves.append([(mine, 0, 0), (other, 0, 0), (back[-1], None, 0)])
+
+    terms = []
     for batch in range(batches):
-        xs = [near[batch], far[batch], *there[batch]]
-        xs += [to_core(rows) for rows in xs]
-        xs[0] = after(xs[0], far[-1], ahead, *sent[-1:])
-        mine, other = ffn(xs, table, weights)
-        if batch + 1 < batches:
-            other = after(other, *there[batch + 1])
-        if batch:
-            other = after(other, back[-1][0])
-        other = to_core(other)
-        own = [(mine, 1, 0), (other, 1, 0)]
-        if batch + 1 < batches:
-            sent.append(total(own, 0, line))
-            back.append([to_mid(sent[-1])])
-        else:
-            sent.append(total(own, half, line))
-            back.append([to_mid(total(own, 0, half)), to_mid(sent[-1])])
-        terms.append([(mine, 0, 0), (other, 0, 0)])
-
-    for batch in range(batches):
-        near_back, far_back = back[batch][0], back[batch][-1]
-        far_sum = total([*terms[batch], (far_back, None, line - far_back.shape[0])], half, line)
-        terms[batch] += [(near_back, None, 0), (mirror(far_sum, 2), None, 0)]
-        span, pieces = 4, half
-        while pieces > 1:
-            part = total(terms[batch], pieces // 2, pieces)
-            terms[batch].append((mirror(part, span), None, 0))
-            span, pieces = span * 2, pieces // 2
+        near_terms, far_terms = halves[2 * batch], halves[2 * batch + 1]
+        parts = total(near_terms, [(j, j + 1) for j in range(1, half)])
+        returned = [
+            along_line(part, lambda p, j=j: owner_of(p, j, len(spans)))
+            for j, part in enumerate(parts, 1)
+        ]
+        if batch + 1 == batches and terms:
+            last = [a for a, _, _ in terms[-1][3:]] + returned
+            far_terms = [*far_terms[:-1], (after(far_terms[-1][0], *last), None, 0)]
+        parts = total(far_terms, [(j, j + 1) for j in range(half)])
+        returned += [
+            along_line(part, lambda p, j=j: owner_of(mirrored(p, 2), j, len(spans)))
+            for j, part in enumerate(parts)
+        ]
+        terms.append(near_terms + [(part, None, 0) for part in returned])
     return finish(hidden_in, terms)
 
 

time: 89.5 us -> 96.8 us (1.082)
  waiting for transfers between devices: 31.9 us -> 43.7 us
  starting transfers between devices: 39.3 us -> 33.4 us
  Pallas kernels: 18 us -> 19.4 us
    ppermute x8 -> x10, waiting for transfers between devices: 10.5 us -> 23.7 us  [along_line(): lax.ppermute(rows, 'ep', [(i, place_of(i // 4) * 4 + i % 4) for i in rang...]
    ppermute x8 -> x10, starting transfers between devices: 25.4 us -> 16.7 us  [along_line(): lax.ppermute(rows, 'ep', [(i, place_of(i // 4) * 4 + i % 4) for i in rang...]
    ppermute x12 -> x14, waiting for transfers between devices: 8.05 us -> 3.15 us  [to_core(): return lax.ppermute(rows, 'ep', [(i, i ^ 1) for i in range(owners)])]
    ppermute x9 -> x10, waiting for transfers between devices: 13.3 us -> 16.8 us  [to_mid(): return lax.ppermute(rows, 'ep', [(i, i ^ 2) for i in range(owners)])]
    ppermute x9 -> x10, starting transfers between devices: 12 us -> 14 us  [to_mid(): return lax.ppermute(rows, 'ep', [(i, i ^ 2) for i in range(owners)])]
    pallas_call x14 -> x17, Pallas kernels: 18 us -> 19.4 us  [call(): pl.pallas_call(kernel, out_shape=shapes, in_specs=specs, out_specs=[VMEM]...]
    ppermute x12 -> x14, starting transfers between devices: 1.91 us -> 2.69 us  [to_core(): return lax.ppermute(rows, 'ep', [(i, i ^ 1) for i in range(owners)])]
  transfers between devices with their start and end apart: 29 -> 34, of which waited for: 16 -> 22; matrix products, arithmetic and copies ran while one was open for 0% -> 0% of each run, Pallas kernels for 18% -> 18%
where the time goes in v10:
time: 96.8 us; the launch traced here: 96.7 us
  waiting for transfers between devices  43.7 us (45%)
  starting transfers between devices  33.4 us (35%)
  Pallas kernels  19.4 us (20%)
    ppermute x10, waiting for transfers between devices, along_line(): lax.ppermute(rows, 'ep', [(i, place_of(i // 4) * 4 + i % 4) for i in rang...  23.7 us
    pallas_call x17, Pallas kernels, call(): pl.pallas_call(kernel, out_shape=shapes, in_specs=specs, out_specs=[VMEM]...  19.4 us
    ppermute x10, waiting for transfers between devices, to_mid(): return lax.ppermute(rows, 'ep', [(i, i ^ 2) for i in range(owners)])  16.8 us
    ppermute x10, starting transfers between devices, along_line(): lax.ppermute(rows, 'ep', [(i, place_of(i // 4) * 4 + i % 4) for i in rang...  16.7 us
    ppermute x10, starting transfers between devices, to_mid(): return lax.ppermute(rows, 'ep', [(i, i ^ 2) for i in range(owners)])  14 us
    ppermute x14, waiting for transfers between devices, to_core(): return lax.ppermute(rows, 'ep', [(i, i ^ 1) for i in range(owners)])  3.15 us
    ppermute x14, starting transfers between devices, to_core(): return lax.ppermute(rows, 'ep', [(i, i ^ 1) for i in range(owners)])  2.69 us
  transfers between devices with their start and end apart: 34, of which 22 were waited for; matrix products, arithmetic and copies ran while one was open for 0% of the time, Pallas kernels for 18%

profile of v10, /device:TPU:0, one launch (start us, length us, event | category | flops | bytes accessed | tf_op | source)
XLA Modules:
  0.0 96.7 jit_solution(14168765316142529060)
XLA Ops:
  1.2 5.1 %collective-permute-start = (bf16[1,32,2176]{2,1,0:T(8,128)(2,1)S(1)}, bf16[1,32,2176]{2,1,0:T(8,128)(2,1)S(1)}, u32[]{:S(2)}, u32[]{:S(2)}) collective-permute-start(bf16[1,32,2176]{2,1,0:T(8,128)(2,1)S(1)} %get-tuple-element.37.refs_0_), channel_id=1, source_target_pairs={{0,12},{1,13},{2,14},{3,15},{4,8},{5,9},{6,10},{7,11},{8,4},{9,5},... | collective-permute-start | bytes 417800 | tf_op jit(solution)/shard_map/ppermute | solution.py:237
  6.3 1.5 %collective-permute-start.1 = (bf16[1,32,2176]{2,1,0:T(8,128)(2,1)S(1)}, bf16[1,32,2176]{2,1,0:T(8,128)(2,1)S(1)}, u32[]{:S(2)}, u32[]{:S(2)}) collective-permute-start(bf16[1,32,2176]{2,1,0:T(8,128)(2,1)S(1)} %get-tuple-element.37.refs_0_), channel_id=1, source_target_pairs={{0,2},{1,3},{2,0},{3,1},{4,6},{5,7},{6,4},{7,5},{8,10},{9,11},{10,... | collective-permute-start | bytes 417800 | tf_op jit(solution)/shard_map/ppermute | solution.py:246
  8.4 1.8 %collective-permute-done.refs_1_ = bf16[1,32,2176]{2,1,0:T(8,128)(2,1)S(1)} collective-permute-done((bf16[1,32,2176]{2,1,0:T(8,128)(2,1)S(1)}, bf16[1,32,2176]{2,1,0:T(8,128)(2,1)S(1)}, u32[]{:S(2)}, u32[]{:S(2)}) %collective-permute-start) | collective-permute-done | bytes 139296 | tf_op jit(solution)/shard_map/ppermute | solution.py:237
  10.1 2.8 %collective-permute-done.1.refs_1_ = bf16[1,32,2176]{2,1,0:T(8,128)(2,1)S(1)} collective-permute-done((bf16[1,32,2176]{2,1,0:T(8,128)(2,1)S(1)}, bf16[1,32,2176]{2,1,0:T(8,128)(2,1)S(1)}, u32[]{:S(2)}, u32[]{:S(2)}) %collective-permute-start.1) | collective-permute-done | bytes 139296 | tf_op jit(solution)/shard_map/ppermute | solution.py:246
  12.9 1.5 %collective-permute-done.2.refs_1_ = bf16[1,32,2176]{2,1,0:T(8,128)(2,1)S(1)} collective-permute-done((bf16[1,32,2176]{2,1,0:T(8,128)(2,1)S(1)}, bf16[1,32,2176]{2,1,0:T(8,128)(2,1)S(1)}, u32[]{:S(2)}, u32[]{:S(2)}) %collective-permute-start.2) | collective-permute-done | bytes 139296 | tf_op jit(solution)/shard_map/ppermute | solution.py:246
  15.5 1.5 %collective-permute-start.4 = (bf16[1,32,2176]{2,1,0:T(8,128)(2,1)S(1)}, bf16[1,32,2176]{2,1,0:T(8,128)(2,1)S(1)}, u32[]{:S(2)}, u32[]{:S(2)}) collective-permute-start(bf16[1,32,2176]{2,1,0:T(8,128)(2,1)S(1)} %collective-permute-done.refs_1_), channel_id=1, source_target_pairs={{0,2},{1,3},{2,0},{3,1},{4,6},{5,7},{6,4},{7,5},{8,10},{9,11},{10,... | collective-permute-start | bytes 417800 | tf_op jit(solution)/shard_map/ppermute | solution.py:246
  17.0 3.8 %load.1 = (bf16[1,2048,768]{2,1,0:T(8,128)(2,1)S(1)}, bf16[1,2048,768]{2,1,0:T(8,128)(2,1)S(1)}, bf16[1,768,2048]{2,1,0:T(8,128)(2,1)S(1)}) custom-call(bf16[1,2048,768]{2,1,0:T(8,128)(2,1)} %refs_0_, bf16[1,2048,768]{2,1,0:T(8,128)(2,1)} %refs_1_, bf16[1,768,2048]{2,1,0:T(8,128)(2,1)} %refs_2_), custom_call_target="tpu_custom_call" | custom-call | tf_op jit(solution)/shard_map/load/pallas_call | solution.py:26
  21.3 2.5 %collective-permute-done.3.refs_1_ = bf16[1,32,2176]{2,1,0:T(8,128)(2,1)S(1)} collective-permute-done((bf16[1,32,2176]{2,1,0:T(8,128)(2,1)S(1)}, bf16[1,32,2176]{2,1,0:T(8,128)(2,1)S(1)}, u32[]{:S(2)}, u32[]{:S(2)}) %collective-permute-start.3) | collective-permute-done | bytes 139296 | tf_op jit(solution)/shard_map/ppermute | solution.py:237
  23.9 1.5 %collective-permute-done.9.refs_0_ = bf16[2,32,2176]{2,1,0:T(8,128)(2,1)S(1)} collective-permute-done((bf16[2,32,2176]{2,1,0:T(8,128)(2,1)S(1)}, bf16[2,32,2176]{2,1,0:T(8,128)(2,1)S(1)}, u32[]{:S(2)}, u32[]{:S(2)}) %collective-permute-start.9) | collective-permute-done | bytes 278560 | tf_op jit(solution)/shard_map/ppermute | solution.py:237
  25.4 1.8 %collective-permute-start.10 = (bf16[2,32,2176]{2,1,0:T(8,128)(2,1)S(1)}, bf16[2,32,2176]{2,1,0:T(8,128)(2,1)S(1)}, u32[]{:S(2)}, u32[]{:S(2)}) collective-permute-start(bf16[2,32,2176]{2,1,0:T(8,128)(2,1)S(1)} %collective-permute-done.9.refs_0_), channel_id=1, source_target_pairs={{0,2},{1,3},{2,0},{3,1},{4,6},{5,7},{6,4},{7,5},{8,10},{9,11},{10,... | collective-permute-start | bytes 835592 | tf_op jit(solution)/shard_map/ppermute | solution.py:246
  28.6 3.2 %ffn.4 = (bf16[2,2,32,2048]{3,2,1,0:T(8,128)(2,1)S(1)}, bf16[2,2,32,2048]{3,2,1,0:T(8,128)(2,1)S(1)}) custom-call(s32[3,1,6]{2,1,0:T(1,128)S(1)} %bitcast.4, bf16[1,2048,768]{2,1,0:T(8,128)(2,1)S(1)} %get-tuple-element.43.gate_ref, bf16[1,2048,768]{2,1,0:T(8,128)(2,1)S(1)} %get-tuple-element.44.up_ref, bf16[1,768,2048]{2,1,0:T(8,128)(2,1)S(1)} %get-tuple-element.45.down_ref, ...), custom_call_target="tpu_custom_call" | custom-call | tf_op jit(solution)/shard_map/ffn/pallas_call | solution.py:26
  31.8 3.1 %collective-permute-done.11.refs_2_ = bf16[1,32,2176]{2,1,0:T(8,128)(2,1)S(1)} collective-permute-done((bf16[1,32,2176]{2,1,0:T(8,128)(2,1)S(1)}, bf16[1,32,2176]{2,1,0:T(8,128)(2,1)S(1)}, u32[]{:S(2)}, u32[]{:S(2)}) %collective-permute-start.11) | collective-permute-done | bytes 139296 | tf_op jit(solution)/shard_map/ppermute | solution.py:246
  35.5 1.7 %collective-permute-start.17 = (bf16[2,32,2176]{2,1,0:T(8,128)(2,1)S(1)}, bf16[2,32,2176]{2,1,0:T(8,128)(2,1)S(1)}, u32[]{:S(2)}, u32[]{:S(2)}) collective-permute-start(bf16[2,32,2176]{2,1,0:T(8,128)(2,1)S(1)} %collective-permute-done.8.refs_0_), channel_id=1, source_target_pairs={{0,2},{1,3},{2,0},{3,1},{4,6},{5,7},{6,4},{7,5},{8,10},{9,11},{10,... | collective-permute-start | bytes 835592 | tf_op jit(solution)/shard_map/ppermute | solution.py:246
  37.6 3.2 %ffn.5 = (bf16[2,2,32,2048]{3,2,1,0:T(8,128)(2,1)S(1)}, bf16[2,2,32,2048]{3,2,1,0:T(8,128)(2,1)S(1)}) custom-call(s32[3,1,6]{2,1,0:T(1,128)S(1)} %bitcast.5, bf16[1,2048,768]{2,1,0:T(8,128)(2,1)S(1)} %get-tuple-element.43.gate_ref, bf16[1,2048,768]{2,1,0:T(8,128)(2,1)S(1)} %get-tuple-element.44.up_ref, bf16[1,768,2048]{2,1,0:T(8,128)(2,1)S(1)} %get-tuple-element.45.down_ref, ...), custom_call_target="tpu_custom_call" | custom-call | tf_op jit(solution)/shard_map/ffn/pallas_call | solution.py:26
  40.9 3.6 %collective-permute-done.17.refs_1_ = bf16[2,32,2176]{2,1,0:T(8,128)(2,1)S(1)} collective-permute-done((bf16[2,32,2176]{2,1,0:T(8,128)(2,1)S(1)}, bf16[2,32,2176]{2,1,0:T(8,128)(2,1)S(1)}, u32[]{:S(2)}, u32[]{:S(2)}) %collective-permute-start.17) | collective-permute-done | bytes 278560 | tf_op jit(solution)/shard_map/ppermute | solution.py:246
  45.0 1.7 %collective-permute-start.13 = (bf16[2,32,2048]{2,1,0:T(8,128)(2,1)S(1)}, bf16[2,32,2048]{2,1,0:T(8,128)(2,1)S(1)}, u32[]{:S(2)}, u32[]{:S(2)}) collective-permute-start(bf16[2,32,2048]{2,1,0:T(8,128)(2,1)S(1)} %total.8), channel_id=1, source_target_pairs={{0,2},{1,3},{2,0},{3,1},{4,6},{5,7},{6,4},{7,5},{8,10},{9,11},{10,... | collective-permute-start | bytes 786440 | tf_op jit(solution)/shard_map/ppermute | solution.py:246
  48.2 3.2 %ffn.6 = (bf16[2,2,32,2048]{3,2,1,0:T(8,128)(2,1)S(1)}, bf16[2,2,32,2048]{3,2,1,0:T(8,128)(2,1)S(1)}) custom-call(s32[3,1,6]{2,1,0:T(1,128)S(1)} %bitcast.6, bf16[1,2048,768]{2,1,0:T(8,128)(2,1)S(1)} %get-tuple-element.43.gate_ref, bf16[1,2048,768]{2,1,0:T(8,128)(2,1)S(1)} %get-tuple-element.44.up_ref, bf16[1,768,2048]{2,1,0:T(8,128)(2,1)S(1)} %get-tuple-element.45.down_ref, ...), custom_call_target="tpu_custom_call" | custom-call | tf_op jit(solution)/shard_map/ffn/pallas_call | solution.py:26
  51.5 1.8 %collective-permute-done.13.refs_2_ = bf16[2,32,2048]{2,1,0:T(8,128)(2,1)S(1)} collective-permute-done((bf16[2,32,2048]{2,1,0:T(8,128)(2,1)S(1)}, bf16[2,32,2048]{2,1,0:T(8,128)(2,1)S(1)}, u32[]{:S(2)}, u32[]{:S(2)}) %collective-permute-start.13) | collective-permute-done | bytes 262176 | tf_op jit(solution)/shard_map/ppermute | solution.py:246
  53.7 1.7 %collective-permute-start.19 = (bf16[2,32,2048]{2,1,0:T(8,128)(2,1)S(1)}, bf16[2,32,2048]{2,1,0:T(8,128)(2,1)S(1)}, u32[]{:S(2)}, u32[]{:S(2)}) collective-permute-start(bf16[2,32,2048]{2,1,0:T(8,128)(2,1)S(1)} %total.10), channel_id=1, source_target_pairs={{0,2},{1,3},{2,0},{3,1},{4,6},{5,7},{6,4},{7,5},{8,10},{9,11},{10,... | collective-permute-start | bytes 786440 | tf_op jit(solution)/shard_map/ppermute | solution.py:246
  55.9 3.2 %ffn.7 = (bf16[2,2,32,2048]{3,2,1,0:T(8,128)(2,1)S(1)}, bf16[2,2,32,2048]{3,2,1,0:T(8,128)(2,1)S(1)}) custom-call(s32[3,1,6]{2,1,0:T(1,128)S(1)} %bitcast.7, bf16[1,2048,768]{2,1,0:T(8,128)(2,1)S(1)} %get-tuple-element.43.gate_ref, bf16[1,2048,768]{2,1,0:T(8,128)(2,1)S(1)} %get-tuple-element.44.up_ref, bf16[1,768,2048]{2,1,0:T(8,128)(2,1)S(1)} %get-tuple-element.45.down_ref, ...), custom_call_target="tpu_custom_call" | custom-call | tf_op jit(solution)/shard_map/ffn/pallas_call | solution.py:26
  59.2 3.3 %collective-permute-done.19.refs_2_ = bf16[2,32,2048]{2,1,0:T(8,128)(2,1)S(1)} collective-permute-done((bf16[2,32,2048]{2,1,0:T(8,128)(2,1)S(1)}, bf16[2,32,2048]{2,1,0:T(8,128)(2,1)S(1)}, u32[]{:S(2)}, u32[]{:S(2)}) %collective-permute-start.19) | collective-permute-done | bytes 262176 | tf_op jit(solution)/shard_map/ppermute | solution.py:246
  62.5 1.7 %collective-permute-start.26 = (bf16[2,32,2048]{2,1,0:T(8,128)(2,1)S(1)}, bf16[2,32,2048]{2,1,0:T(8,128)(2,1)S(1)}, u32[]{:S(2)}, u32[]{:S(2)}) collective-permute-start(bf16[2,32,2048]{2,1,0:T(8,128)(2,1)S(1)} %total.12), channel_id=1, source_target_pairs={{0,2},{1,3},{2,0},{3,1},{4,6},{5,7},{6,4},{7,5},{8,10},{9,11},{10,... | collective-permute-start | bytes 786440 | tf_op jit(solution)/shard_map/ppermute | solution.py:246
  64.4 1.7 %collective-permute-start.31 = (bf16[2,32,2048]{2,1,0:T(8,128)(2,1)S(1)}, bf16[2,32,2048]{2,1,0:T(8,128)(2,1)S(1)}, u32[]{:S(2)}, u32[]{:S(2)}) collective-permute-start(bf16[2,32,2048]{2,1,0:T(8,128)(2,1)S(1)} %total.14), channel_id=1, source_target_pairs={{0,2},{1,3},{2,0},{3,1},{4,6},{5,7},{6,4},{7,5},{8,10},{9,11},{10,... | collective-permute-start | bytes 786440 | tf_op jit(solution)/shard_map/ppermute | solution.py:246
  66.2 2.2 %collective-permute-start.14 = (bf16[1,32,2048]{2,1,0:T(8,128)(2,1)S(1)}, bf16[1,32,2048]{2,1,0:T(8,128)(2,1)S(1)}, u32[]{:S(2)}, u32[]{:S(2)}) collective-permute-start(bf16[1,32,2048]{2,1,0:T(8,128)(2,1)S(1)} %total.9), channel_id=1, source_target_pairs={{0,12},{1,13},{2,14},{3,15},{4,8},{5,9},{6,10},{7,11},{8,4},{9,5},... | collective-permute-start | bytes 393224 | tf_op jit(solution)/shard_map/ppermute | solution.py:237
  69.6 1.2 %collective-permute-start.21 = (bf16[1,32,2048]{2,1,0:T(8,128)(2,1)S(1)}, bf16[1,32,2048]{2,1,0:T(8,128)(2,1)S(1)}, u32[]{:S(2)}, u32[]{:S(2)}) collective-permute-start(bf16[1,32,2048]{2,1,0:T(8,128)(2,1)S(1)} %get-tuple-element.57), channel_id=1, source_target_pairs={{0,8},{1,9},{2,10},{3,11},{4,12},{5,13},{6,14},{7,15},{8,0},{9,1},... | collective-permute-start | bytes 393224 | tf_op jit(solution)/shard_map/ppermute | solution.py:237
  71.6 2.1 %collective-permute-start.27 = (bf16[1,32,2048]{2,1,0:T(8,128)(2,1)S(1)}, bf16[1,32,2048]{2,1,0:T(8,128)(2,1)S(1)}, u32[]{:S(2)}, u32[]{:S(2)}) collective-permute-start(bf16[1,32,2048]{2,1,0:T(8,128)(2,1)S(1)} %total.13), channel_id=1, source_target_pairs={{0,12},{1,13},{2,14},{3,15},{4,8},{5,9},{6,10},{7,11},{8,4},{9,5},... | collective-permute-start | bytes 393224 | tf_op jit(solution)/shard_map/ppermute | solution.py:237
  74.5 2.7 %collective-permute-done.20.refs_4_ = bf16[1,32,2048]{2,1,0:T(8,128)(2,1)S(1)} collective-permute-done((bf16[1,32,2048]{2,1,0:T(8,128)(2,1)S(1)}, bf16[1,32,2048]{2,1,0:T(8,128)(2,1)S(1)}, u32[]{:S(2)}, u32[]{:S(2)}) %collective-permute-start.20) | collective-permute-done | bytes 131104 | tf_op jit(solution)/shard_map/ppermute | solution.py:237
  77.2 7.2 %collective-permute-done.21.refs_5_ = bf16[1,32,2048]{2,1,0:T(8,128)(2,1)S(1)} collective-permute-done((bf16[1,32,2048]{2,1,0:T(8,128)(2,1)S(1)}, bf16[1,32,2048]{2,1,0:T(8,128)(2,1)S(1)}, u32[]{:S(2)}, u32[]{:S(2)}) %collective-permute-start.21) | collective-permute-done | bytes 131104 | tf_op jit(solution)/shard_map/ppermute | solution.py:237
  84.6 2.6 %collective-permute-start.32 = (bf16[1,32,2048]{2,1,0:T(8,128)(2,1)S(1)}, bf16[1,32,2048]{2,1,0:T(8,128)(2,1)S(1)}, u32[]{:S(2)}, u32[]{:S(2)}) collective-permute-start(bf16[1,32,2048]{2,1,0:T(8,128)(2,1)S(1)} %get-tuple-element.67), channel_id=1, source_target_pairs={{0,4},{1,5},{2,6},{3,7},{4,0},{5,1},{6,2},{7,3},{8,12},{9,13},{10,... | collective-permute-start | bytes 393224 | tf_op jit(solution)/shard_map/ppermute | solution.py:237
  87.2 1.3 %collective-permute-start.33 = (bf16[1,32,2048]{2,1,0:T(8,128)(2,1)S(1)}, bf16[1,32,2048]{2,1,0:T(8,128)(2,1)S(1)}, u32[]{:S(2)}, u32[]{:S(2)}) collective-permute-start(bf16[1,32,2048]{2,1,0:T(8,128)(2,1)S(1)} %get-tuple-element.68), channel_id=1, source_target_pairs={{0,8},{1,9},{2,10},{3,11},{4,12},{5,13},{6,14},{7,15},{8,0},{9,1},... | collective-permute-start | bytes 393224 | tf_op jit(solution)/shard_map/ppermute | solution.py:237
  88.4 3.1 %collective-permute-done.32.refs_10_ = bf16[1,32,2048]{2,1,0:T(8,128)(2,1)S(1)} collective-permute-done((bf16[1,32,2048]{2,1,0:T(8,128)(2,1)S(1)}, bf16[1,32,2048]{2,1,0:T(8,128)(2,1)S(1)}, u32[]{:S(2)}, u32[]{:S(2)}) %collective-permute-start.32) | collective-permute-done | bytes 131104 | tf_op jit(solution)/shard_map/ppermute | solution.py:237
  91.6 4.2 %collective-permute-done.33.refs_11_ = bf16[1,32,2048]{2,1,0:T(8,128)(2,1)S(1)} collective-permute-done((bf16[1,32,2048]{2,1,0:T(8,128)(2,1)S(1)}, bf16[1,32,2048]{2,1,0:T(8,128)(2,1)S(1)}, u32[]{:S(2)}, u32[]{:S(2)}) %collective-permute-start.33) | collective-permute-done | bytes 131104 | tf_op jit(solution)/shard_map/ppermute | solution.py:237
  (57 shorter events, 13.0 us)
Async XLA Ops:
  1.2 8.9 %collective-permute-start = (bf16[1,32,2176]{2,1,0:T(8,128)(2,1)S(1)}, bf16[1,32,2176]{2,1,0:T(8,128)(2,1)S(1)}, u32[]{:S(2)}, u32[]{:S(2)}) collective-permute-start(bf16[1,32,2176]{2,1,0:T(8,128)(2,1)S(1)} %get-tuple-element.37.refs_0_), channel_id=1, source_target_pairs={{0,12},{1,13},{2,14},{3,15},{4,8},{5,9},{6,10},{7,11},{8,4},{9,5},... | collective-permute-start | bytes 417800 | tf_op jit(solution)/shard_map/ppermute | solution.py:237
  6.3 6.6 %collective-permute-start.1 = (bf16[1,32,2176]{2,1,0:T(8,128)(2,1)S(1)}, bf16[1,32,2176]{2,1,0:T(8,128)(2,1)S(1)}, u32[]{:S(2)}, u32[]{:S(2)}) collective-permute-start(bf16[1,32,2176]{2,1,0:T(8,128)(2,1)S(1)} %get-tuple-element.37.refs_0_), channel_id=1, source_target_pairs={{0,2},{1,3},{2,0},{3,1},{4,6},{5,7},{6,4},{7,5},{8,10},{9,11},{10,... | collective-permute-start | bytes 417800 | tf_op jit(solution)/shard_map/ppermute | solution.py:246
  7.9 6.6 %collective-permute-start.2 = (bf16[1,32,2176]{2,1,0:T(8,128)(2,1)S(1)}, bf16[1,32,2176]{2,1,0:T(8,128)(2,1)S(1)}, u32[]{:S(2)}, u32[]{:S(2)}) collective-permute-start(bf16[1,32,2176]{2,1,0:T(8,128)(2,1)S(1)} %get-tuple-element.46.refs_0_), channel_id=1, source_target_pairs={{0,2},{1,3},{2,0},{3,1},{4,6},{5,7},{6,4},{7,5},{8,10},{9,11},{10,... | collective-permute-start | bytes 417800 | tf_op jit(solution)/shard_map/ppermute | solution.py:246
  14.5 10.9 %collective-permute-start.9 = (bf16[2,32,2176]{2,1,0:T(8,128)(2,1)S(1)}, bf16[2,32,2176]{2,1,0:T(8,128)(2,1)S(1)}, u32[]{:S(2)}, u32[]{:S(2)}) collective-permute-start(bf16[2,32,2176]{2,1,0:T(8,128)(2,1)S(1)} %join.2.refs_0_), channel_id=1, source_target_pairs={{0,4},{1,5},{2,6},{3,7},{4,0},{5,1},{6,2},{7,3},{8,12},{9,13},{10,... | collective-permute-start | bytes 835592 | tf_op jit(solution)/shard_map/ppermute | solution.py:237
  14.6 9.2 %collective-permute-start.3 = (bf16[1,32,2176]{2,1,0:T(8,128)(2,1)S(1)}, bf16[1,32,2176]{2,1,0:T(8,128)(2,1)S(1)}, u32[]{:S(2)}, u32[]{:S(2)}) collective-permute-start(bf16[1,32,2176]{2,1,0:T(8,128)(2,1)S(1)} %get-tuple-element.46.refs_0_), channel_id=1, source_target_pairs={{0,12},{1,13},{2,14},{3,15},{4,8},{5,9},{6,10},{7,11},{8,4},{9,5},... | collective-permute-start | bytes 417800 | tf_op jit(solution)/shard_map/ppermute | solution.py:237
  15.5 11.8 %collective-permute-start.4 = (bf16[1,32,2176]{2,1,0:T(8,128)(2,1)S(1)}, bf16[1,32,2176]{2,1,0:T(8,128)(2,1)S(1)}, u32[]{:S(2)}, u32[]{:S(2)}) collective-permute-start(bf16[1,32,2176]{2,1,0:T(8,128)(2,1)S(1)} %collective-permute-done.refs_1_), channel_id=1, source_target_pairs={{0,2},{1,3},{2,0},{3,1},{4,6},{5,7},{6,4},{7,5},{8,10},{9,11},{10,... | collective-permute-start | bytes 417800 | tf_op jit(solution)/shard_map/ppermute | solution.py:246
  17.0 10.5 %collective-permute-start.5 = (bf16[2,32,2176]{2,1,0:T(8,128)(2,1)S(1)}, bf16[2,32,2176]{2,1,0:T(8,128)(2,1)S(1)}, u32[]{:S(2)}, u32[]{:S(2)}) collective-permute-start(bf16[2,32,2176]{2,1,0:T(8,128)(2,1)S(1)} %join.2.refs_0_), channel_id=1, source_target_pairs={{0,1},{1,0},{2,3},{3,2},{4,5},{5,4},{6,7},{7,6},{8,9},{9,8},{10,11... | collective-permute-start | bytes 835592 | tf_op jit(solution)/shard_map/ppermute | solution.py:249
  20.8 6.5 %collective-permute-start.6 = (bf16[1,32,2176]{2,1,0:T(8,128)(2,1)S(1)}, bf16[1,32,2176]{2,1,0:T(8,128)(2,1)S(1)}, u32[]{:S(2)}, u32[]{:S(2)}) collective-permute-start(bf16[1,32,2176]{2,1,0:T(8,128)(2,1)S(1)} %collective-permute-done.1.refs_1_), channel_id=1, source_target_pairs={{0,1},{1,0},{2,3},{3,2},{4,5},{5,4},{6,7},{7,6},{8,9},{9,8},{10,11... | collective-permute-start | bytes 417800 | tf_op jit(solution)/shard_map/ppermute | solution.py:249
  23.8 11.1 %collective-permute-start.8 = (bf16[2,32,2176]{2,1,0:T(8,128)(2,1)S(1)}, bf16[2,32,2176]{2,1,0:T(8,128)(2,1)S(1)}, u32[]{:S(2)}, u32[]{:S(2)}) collective-permute-start(bf16[2,32,2176]{2,1,0:T(8,128)(2,1)S(1)} %join.3.refs_0_), channel_id=1, source_target_pairs={{0,4},{1,5},{2,6},{3,7},{4,0},{5,1},{6,2},{7,3},{8,12},{9,13},{10,... | collective-permute-start | bytes 835592 | tf_op jit(solution)/shard_map/ppermute | solution.py:237
  25.4 9.5 %collective-permute-start.10 = (bf16[2,32,2176]{2,1,0:T(8,128)(2,1)S(1)}, bf16[2,32,2176]{2,1,0:T(8,128)(2,1)S(1)}, u32[]{:S(2)}, u32[]{:S(2)}) collective-permute-start(bf16[2,32,2176]{2,1,0:T(8,128)(2,1)S(1)} %collective-permute-done.9.refs_0_), channel_id=1, source_target_pairs={{0,2},{1,3},{2,0},{3,1},{4,6},{5,7},{6,4},{7,5},{8,10},{9,11},{10,... | collective-permute-start | bytes 835592 | tf_op jit(solution)/shard_map/ppermute | solution.py:246
  27.2 7.7 %collective-permute-start.11 = (bf16[1,32,2176]{2,1,0:T(8,128)(2,1)S(1)}, bf16[1,32,2176]{2,1,0:T(8,128)(2,1)S(1)}, u32[]{:S(2)}, u32[]{:S(2)}) collective-permute-start(bf16[1,32,2176]{2,1,0:T(8,128)(2,1)S(1)} %collective-permute-done.3.refs_1_), channel_id=1, source_target_pairs={{0,2},{1,3},{2,0},{3,1},{4,6},{5,7},{6,4},{7,5},{8,10},{9,11},{10,... | collective-permute-start | bytes 417800 | tf_op jit(solution)/shard_map/ppermute | solution.py:246
  34.9 2.3 %collective-permute-start.12 = (bf16[2,2,32,2048]{3,2,1,0:T(8,128)(2,1)S(1)}, bf16[2,2,32,2048]{3,2,1,0:T(8,128)(2,1)S(1)}, u32[]{:S(2)}, u32[]{:S(2)}) collective-permute-start(bf16[2,2,32,2048]{3,2,1,0:T(8,128)(2,1)S(1)} %get-tuple-element.51), channel_id=1, source_target_pairs={{0,1},{1,0},{2,3},{3,2},{4,5},{5,4},{6,7},{7,6},{8,9},{9,8},{10,11... | collective-permute-start | bytes 1572872 | tf_op jit(solution)/shard_map/ppermute | solution.py:249
  34.9 2.3 %collective-permute-start.15 = (bf16[2,32,2176]{2,1,0:T(8,128)(2,1)S(1)}, bf16[2,32,2176]{2,1,0:T(8,128)(2,1)S(1)}, u32[]{:S(2)}, u32[]{:S(2)}) collective-permute-start(bf16[2,32,2176]{2,1,0:T(8,128)(2,1)S(1)} %collective-permute-done.9.refs_0_), channel_id=1, source_target_pairs={{0,1},{1,0},{2,3},{3,2},{4,5},{5,4},{6,7},{7,6},{8,9},{9,8},{10,11... | collective-permute-start | bytes 835592 | tf_op jit(solution)/shard_map/ppermute | solution.py:249
  35.4 2.2 %collective-permute-start.16 = (bf16[2,32,2176]{2,1,0:T(8,128)(2,1)S(1)}, bf16[2,32,2176]{2,1,0:T(8,128)(2,1)S(1)}, u32[]{:S(2)}, u32[]{:S(2)}) collective-permute-start(bf16[2,32,2176]{2,1,0:T(8,128)(2,1)S(1)} %collective-permute-done.10.refs_1_), channel_id=1, source_target_pairs={{0,1},{1,0},{2,3},{3,2},{4,5},{5,4},{6,7},{7,6},{8,9},{9,8},{10,11... | collective-permute-start | bytes 835592 | tf_op jit(solution)/shard_map/ppermute | solution.py:249
  35.5 9.0 %collective-permute-start.17 = (bf16[2,32,2176]{2,1,0:T(8,128)(2,1)S(1)}, bf16[2,32,2176]{2,1,0:T(8,128)(2,1)S(1)}, u32[]{:S(2)}, u32[]{:S(2)}) collective-permute-start(bf16[2,32,2176]{2,1,0:T(8,128)(2,1)S(1)} %collective-permute-done.8.refs_0_), channel_id=1, source_target_pairs={{0,2},{1,3},{2,0},{3,1},{4,6},{5,7},{6,4},{7,5},{8,10},{9,11},{10,... | collective-permute-start | bytes 835592 | tf_op jit(solution)/shard_map/ppermute | solution.py:246
  44.5 2.7 %collective-permute-start.18 = (bf16[2,2,32,2048]{3,2,1,0:T(8,128)(2,1)S(1)}, bf16[2,2,32,2048]{3,2,1,0:T(8,128)(2,1)S(1)}, u32[]{:S(2)}, u32[]{:S(2)}) collective-permute-start(bf16[2,2,32,2048]{3,2,1,0:T(8,128)(2,1)S(1)} %get-tuple-element.55), channel_id=1, source_target_pairs={{0,1},{1,0},{2,3},{3,2},{4,5},{5,4},{6,7},{7,6},{8,9},{9,8},{10,11... | collective-permute-start | bytes 1572872 | tf_op jit(solution)/shard_map/ppermute | solution.py:249
  44.5 3.5 %collective-permute-start.22 = (bf16[2,32,2176]{2,1,0:T(8,128)(2,1)S(1)}, bf16[2,32,2176]{2,1,0:T(8,128)(2,1)S(1)}, u32[]{:S(2)}, u32[]{:S(2)}) collective-permute-start(bf16[2,32,2176]{2,1,0:T(8,128)(2,1)S(1)} %join.3.refs_0_), channel_id=1, source_target_pairs={{0,1},{1,0},{2,3},{3,2},{4,5},{5,4},{6,7},{7,6},{8,9},{9,8},{10,11... | collective-permute-start | bytes 835592 | tf_op jit(solution)/shard_map/ppermute | solution.py:249
  45.0 8.2 %collective-permute-start.13 = (bf16[2,32,2048]{2,1,0:T(8,128)(2,1)S(1)}, bf16[2,32,2048]{2,1,0:T(8,128)(2,1)S(1)}, u32[]{:S(2)}, u32[]{:S(2)}) collective-permute-start(bf16[2,32,2048]{2,1,0:T(8,128)(2,1)S(1)} %total.8), channel_id=1, source_target_pairs={{0,2},{1,3},{2,0},{3,1},{4,6},{5,7},{6,4},{7,5},{8,10},{9,11},{10,... | collective-permute-start | bytes 786440 | tf_op jit(solution)/shard_map/ppermute | solution.py:246
  46.7 1.6 %collective-permute-start.24 = (bf16[1,32,2176]{2,1,0:T(8,128)(2,1)S(1)}, bf16[1,32,2176]{2,1,0:T(8,128)(2,1)S(1)}, u32[]{:S(2)}, u32[]{:S(2)}) collective-permute-start(bf16[1,32,2176]{2,1,0:T(8,128)(2,1)S(1)} %collective-permute-done.11.refs_2_), channel_id=1, source_target_pairs={{0,1},{1,0},{2,3},{3,2},{4,5},{5,4},{6,7},{7,6},{8,9},{9,8},{10,11... | collective-permute-start | bytes 417800 | tf_op jit(solution)/shard_map/ppermute | solution.py:249
  53.2 2.2 %collective-permute-start.25 = (bf16[2,2,32,2048]{3,2,1,0:T(8,128)(2,1)S(1)}, bf16[2,2,32,2048]{3,2,1,0:T(8,128)(2,1)S(1)}, u32[]{:S(2)}, u32[]{:S(2)}) collective-permute-start(bf16[2,2,32,2048]{3,2,1,0:T(8,128)(2,1)S(1)} %get-tuple-element.61), channel_id=1, source_target_pairs={{0,1},{1,0},{2,3},{3,2},{4,5},{5,4},{6,7},{7,6},{8,9},{9,8},{10,11... | collective-permute-start | bytes 1572872 | tf_op jit(solution)/shard_map/ppermute | solution.py:249
  53.2 2.3 %collective-permute-start.28 = (bf16[2,32,2176]{2,1,0:T(8,128)(2,1)S(1)}, bf16[2,32,2176]{2,1,0:T(8,128)(2,1)S(1)}, u32[]{:S(2)}, u32[]{:S(2)}) collective-permute-start(bf16[2,32,2176]{2,1,0:T(8,128)(2,1)S(1)} %collective-permute-done.8.refs_0_), channel_id=1, source_target_pairs={{0,1},{1,0},{2,3},{3,2},{4,5},{5,4},{6,7},{7,6},{8,9},{9,8},{10,11... | collective-permute-start | bytes 835592 | tf_op jit(solution)/shard_map/ppermute | solution.py:249
  53.7 2.2 %collective-permute-start.29 = (bf16[2,32,2176]{2,1,0:T(8,128)(2,1)S(1)}, bf16[2,32,2176]{2,1,0:T(8,128)(2,1)S(1)}, u32[]{:S(2)}, u32[]{:S(2)}) collective-permute-start(bf16[2,32,2176]{2,1,0:T(8,128)(2,1)S(1)} %collective-permute-done.17.refs_1_), channel_id=1, source_target_pairs={{0,1},{1,0},{2,3},{3,2},{4,5},{5,4},{6,7},{7,6},{8,9},{9,8},{10,11... | collective-permute-start | bytes 835592 | tf_op jit(solution)/shard_map/ppermute | solution.py:249
  53.7 8.7 %collective-permute-start.19 = (bf16[2,32,2048]{2,1,0:T(8,128)(2,1)S(1)}, bf16[2,32,2048]{2,1,0:T(8,128)(2,1)S(1)}, u32[]{:S(2)}, u32[]{:S(2)}) collective-permute-start(bf16[2,32,2048]{2,1,0:T(8,128)(2,1)S(1)} %total.10), channel_id=1, source_target_pairs={{0,2},{1,3},{2,0},{3,1},{4,6},{5,7},{6,4},{7,5},{8,10},{9,11},{10,... | collective-permute-start | bytes 786440 | tf_op jit(solution)/shard_map/ppermute | solution.py:246
  62.5 1.9 %collective-permute-start.30 = (bf16[2,2,32,2048]{3,2,1,0:T(8,128)(2,1)S(1)}, bf16[2,2,32,2048]{3,2,1,0:T(8,128)(2,1)S(1)}, u32[]{:S(2)}, u32[]{:S(2)}) collective-permute-start(bf16[2,2,32,2048]{3,2,1,0:T(8,128)(2,1)S(1)} %get-tuple-element.65), channel_id=1, source_target_pairs={{0,1},{1,0},{2,3},{3,2},{4,5},{5,4},{6,7},{7,6},{8,9},{9,8},{10,11... | collective-permute-start | bytes 1572872 | tf_op jit(solution)/shard_map/ppermute | solution.py:249
  62.5 9.1 %collective-permute-start.26 = (bf16[2,32,2048]{2,1,0:T(8,128)(2,1)S(1)}, bf16[2,32,2048]{2,1,0:T(8,128)(2,1)S(1)}, u32[]{:S(2)}, u32[]{:S(2)}) collective-permute-start(bf16[2,32,2048]{2,1,0:T(8,128)(2,1)S(1)} %total.12), channel_id=1, source_target_pairs={{0,2},{1,3},{2,0},{3,1},{4,6},{5,7},{6,4},{7,5},{8,10},{9,11},{10,... | collective-permute-start | bytes 786440 | tf_op jit(solution)/shard_map/ppermute | solution.py:246
  64.4 20.0 %collective-permute-start.31 = (bf16[2,32,2048]{2,1,0:T(8,128)(2,1)S(1)}, bf16[2,32,2048]{2,1,0:T(8,128)(2,1)S(1)}, u32[]{:S(2)}, u32[]{:S(2)}) collective-permute-start(bf16[2,32,2048]{2,1,0:T(8,128)(2,1)S(1)} %total.14), channel_id=1, source_target_pairs={{0,2},{1,3},{2,0},{3,1},{4,6},{5,7},{6,4},{7,5},{8,10},{9,11},{10,... | collective-permute-start | bytes 786440 | tf_op jit(solution)/shard_map/ppermute | solution.py:246
  66.2 8.2 %collective-permute-start.14 = (bf16[1,32,2048]{2,1,0:T(8,128)(2,1)S(1)}, bf16[1,32,2048]{2,1,0:T(8,128)(2,1)S(1)}, u32[]{:S(2)}, u32[]{:S(2)}) collective-permute-start(bf16[1,32,2048]{2,1,0:T(8,128)(2,1)S(1)} %total.9), channel_id=1, source_target_pairs={{0,12},{1,13},{2,14},{3,15},{4,8},{5,9},{6,10},{7,11},{8,4},{9,5},... | collective-permute-start | bytes 393224 | tf_op jit(solution)/shard_map/ppermute | solution.py:237
  68.5 8.7 %collective-permute-start.20 = (bf16[1,32,2048]{2,1,0:T(8,128)(2,1)S(1)}, bf16[1,32,2048]{2,1,0:T(8,128)(2,1)S(1)}, u32[]{:S(2)}, u32[]{:S(2)}) collective-permute-start(bf16[1,32,2048]{2,1,0:T(8,128)(2,1)S(1)} %get-tuple-element.56), channel_id=1, source_target_pairs={{0,4},{1,5},{2,6},{3,7},{4,0},{5,1},{6,2},{7,3},{8,12},{9,13},{10,... | collective-permute-start | bytes 393224 | tf_op jit(solution)/shard_map/ppermute | solution.py:237
  69.6 14.8 %collective-permute-start.21 = (bf16[1,32,2048]{2,1,0:T(8,128)(2,1)S(1)}, bf16[1,32,2048]{2,1,0:T(8,128)(2,1)S(1)}, u32[]{:S(2)}, u32[]{:S(2)}) collective-permute-start(bf16[1,32,2048]{2,1,0:T(8,128)(2,1)S(1)} %get-tuple-element.57), channel_id=1, source_target_pairs={{0,8},{1,9},{2,10},{3,11},{4,12},{5,13},{6,14},{7,15},{8,0},{9,1},... | collective-permute-start | bytes 393224 | tf_op jit(solution)/shard_map/ppermute | solution.py:237
  71.6 12.8 %collective-permute-start.27 = (bf16[1,32,2048]{2,1,0:T(8,128)(2,1)S(1)}, bf16[1,32,2048]{2,1,0:T(8,128)(2,1)S(1)}, u32[]{:S(2)}, u32[]{:S(2)}) collective-permute-start(bf16[1,32,2048]{2,1,0:T(8,128)(2,1)S(1)} %total.13), channel_id=1, source_target_pairs={{0,12},{1,13},{2,14},{3,15},{4,8},{5,9},{6,10},{7,11},{8,4},{9,5},... | collective-permute-start | bytes 393224 | tf_op jit(solution)/shard_map/ppermute | solution.py:237
  84.6 7.0 %collective-permute-start.32 = (bf16[1,32,2048]{2,1,0:T(8,128)(2,1)S(1)}, bf16[1,32,2048]{2,1,0:T(8,128)(2,1)S(1)}, u32[]{:S(2)}, u32[]{:S(2)}) collective-permute-start(bf16[1,32,2048]{2,1,0:T(8,128)(2,1)S(1)} %get-tuple-element.67), channel_id=1, source_target_pairs={{0,4},{1,5},{2,6},{3,7},{4,0},{5,1},{6,2},{7,3},{8,12},{9,13},{10,... | collective-permute-start | bytes 393224 | tf_op jit(solution)/shard_map/ppermute | solution.py:237
  87.2 8.5 %collective-permute-start.33 = (bf16[1,32,2048]{2,1,0:T(8,128)(2,1)S(1)}, bf16[1,32,2048]{2,1,0:T(8,128)(2,1)S(1)}, u32[]{:S(2)}, u32[]{:S(2)}) collective-permute-start(bf16[1,32,2048]{2,1,0:T(8,128)(2,1)S(1)} %get-tuple-element.68), channel_id=1, source_target_pairs={{0,8},{1,9},{2,10},{3,11},{4,12},{5,13},{6,14},{7,15},{8,0},{9,1},... | collective-permute-start | bytes 393224 | tf_op jit(solution)/shard_map/ppermute | solution.py:237
  (4 other events, 48.2 us)

commit v11 on v9

--- a/solution.py
+++ b/solution.py
@@ -8,6 +8,7 @@
 from jax.sharding import PartitionSpec as P
 
 LANES = 128
+SHARES = 4
 VMEM = pl.BlockSpec(memory_space=pltpu.VMEM)
 HBM = pl.BlockSpec(memory_space=pltpu.HBM)
 SMEM = pl.BlockSpec(memory_space=pltpu.SMEM)
@@ -115,7 +116,8 @@
 
 
 def ffn_kernel(table_ref, gate_ref, up_ref, down_ref, *refs):
-    x_refs, (mine_ref, other_ref, x_all, hidden) = refs[:-4], refs[-4:]
+    x_refs, outs, (x_all, hidden) = refs[: -3 - SHARES], refs[-3 - SHARES : -2], refs[-2:]
+    mine_ref, other_refs = outs[0], outs[1:]
     width, ff = gate_ref.shape[1:]
     group = ff // table_ref.shape[2]
     step = 2 * group if ff % (2 * group) == 0 else group
@@ -147,7 +149,10 @@
         out = jnp.dot(hidden[...], down_ref[0, :, n : n + cols], preferred_element_type=jnp.float32)
         out = (out * weight).astype(jnp.bfloat16).reshape(4, pieces, part, cols)
         mine_ref[:, :, :, n : n + cols] = out[:2]
-        other_ref[:, :, :, n : n + cols] = out[2:]
+        other = out[2:].reshape(2 * pieces, part, cols)
+        for i, other_ref in enumerate(other_refs):
+            at = i * other_ref.shape[0]
+            other_ref[:, :, n : n + cols] = other[at : at + other_ref.shape[0]]
 
 
 def ffn(xs, table, weights):
@@ -159,53 +164,75 @@
         ffn_kernel,
         [table, *weights, *xs],
         [SMEM] + [VMEM] * (3 + len(xs)),
-        [jax.ShapeDtypeStruct((2, pieces, part, width), jnp.bfloat16)] * 2,
+        [jax.ShapeDtypeStruct((2, pieces, part, width), jnp.bfloat16)]
+        + [jax.ShapeDtypeStruct((2 * pieces // SHARES, part, width), jnp.bfloat16)] * SHARES,
         [pltpu.VMEM((rows, full), jnp.bfloat16), pltpu.VMEM((rows, ff), jnp.bfloat16)],
         name="ffn",
         vmem=16,
     )
 
 
-def piece_of(ref, slot, piece):
-    return ref[piece] if slot is None else ref[slot, piece]
-
-
-def total_kernel(terms, low, *refs):
-    out_ref = refs[-1]
-    for piece in range(out_ref.shape[0]):
-        total = None
-        for (slot, first), ref in zip(terms, refs[:-1]):
-            term = piece_of(ref, slot, low + piece - first).astype(jnp.float32)
-            total = term if total is None else total + term
-        out_ref[piece] = total.astype(out_ref.dtype)
-
-
-def total(terms, low, high):
-    arrays = [a for a, _, _ in terms]
-    shape = jax.ShapeDtypeStruct((high - low, *arrays[0].shape[-2:]), arrays[0].dtype)
-    return call(
-        functools.partial(total_kernel, [where for _, *where in terms], low),
+def piece_of(slot, refs, piece):
+    if slot is not None:
+        return refs[0][slot, piece]
+    for ref in refs:
+        if piece < ref.shape[0]:
+            return ref[piece]
+        piece -= ref.shape[0]
+
+
+def sum_of(layout, refs, piece):
+    result, at = None, 0
+    for slot, skip, count in layout:
+        term = piece_of(slot, refs[at : at + count], piece - skip).astype(jnp.float32)
+        result = term if result is None else result + term
+        at += count
+    return result
+
+
+def total_kernel(layout, cuts, *refs):
+    ins, outs = refs[: -len(cuts)], refs[-len(cuts) :]
+    for (low, high), out_ref in zip(cuts, outs):
+        for piece in range(low, high):
+            out_ref[piece - low] = sum_of(layout, ins, piece).astype(out_ref.dtype)
+
+
+def total(terms, cuts):
+    first = cuts[0][0]
+    kept = []
+    for slot, arrays in terms:
+        skip = 0
+        while slot is None and first >= skip + arrays[0].shape[0]:
+            skip, arrays = skip + arrays[0].shape[0], arrays[1:]
+        high = cuts[-1][1] - skip
+        while slot is None and high <= sum(a.shape[0] for a in arrays[:-1]):
+            arrays = arrays[:-1]
+        kept.append((slot, skip, arrays))
+    layout = [(slot, skip, len(arrays)) for slot, skip, arrays in kept]
+    arrays = [a for _, _, arrays in kept for a in arrays]
+    part, width = arrays[0].shape[-2:]
+    return call(
+        functools.partial(total_kernel, layout, cuts),
         arrays,
         [VMEM] * len(arrays),
-        [shape],
+        [jax.ShapeDtypeStruct((high - low, part, width), arrays[0].dtype) for low, high in cuts],
         name="total",
-    )[0]
-
-
-def finish_kernel(terms, hidden_ref, *refs):
+    )
+
+
+def finish_kernel(layout, hidden_ref, *refs):
     out_ref = refs[-1]
+    count = (len(refs) - 1) // hidden_ref.shape[0]
     for batch in range(hidden_ref.shape[0]):
-        mixed = None
-        for i, (slot, first) in enumerate(terms):
-            term = piece_of(refs[batch * len(terms) + i], slot, -first).astype(jnp.float32)
-            mixed = term if mixed is None else mixed + term
+        mixed = sum_of(layout, refs[batch * count : (batch + 1) * count], 0)
         out_ref[batch] = (hidden_ref[batch].astype(jnp.float32) + mixed).astype(out_ref.dtype)
 
 
 def finish(hidden_in, terms):
-    arrays = [a for batch in terms for a, _, _ in batch]
-    return call(
-        functools.partial(finish_kernel, [where for _, *where in terms[0]]),
+    layout = [(slot, 0, 1) for slot, _ in terms[0]]
+    arrays = [arrays[0] for batch in terms for _, arrays in batch]
+    return call(
+        functools.partial(finish_kernel, layout),
         [hidden_in, *arrays],
         [VMEM] * (1 + len(arrays)),
         [jax.ShapeDtypeStruct(hidden_in.shape, hidden_in.dtype)],
@@ -231,12 +258,14 @@
     line = owners // 4
     half = line // 2
 
+    def along_line(rows, place_of):
+        return lax.ppermute(rows, "ep", [(i, place_of(i // 4) * 4 + i % 4) for i in range(owners)])
+
+    def mirrored(p, span):
+        return p // span * span + span - 1 - p % span
+
     def mirror(rows, span):
-        def partner(i):
-            p = i // 4
-            return (p // span * span + span - 1 - p % span) * 4 + i % 4
-
-        return lax.ppermute(rows, "ep", [(i, partner(i)) for i in range(owners)])
+        return along_line(rows, lambda p: mirrored(p, span))
 
     def to_mid(rows):
         return lax.ppermute(rows, "ep", [(i, i ^ 2) for i in range(owners)])
@@ -278,29 +307,28 @@
         xs = [near[batch], far[batch], *there[batch]]
         xs += [to_core(rows) for rows in xs]
         xs[0] = after(xs[0], far[-1], ahead, *sent[-1:])
-        mine, other = ffn(xs, table, weights)
+        mine, *others = ffn(xs, table, weights)
+        wait = there[batch + 1] if batch + 1 < batches else []
+        others = [to_core(after(other, *wait)) for other in others]
+        other_here, other_there = others[: SHARES // 2], others[SHARES // 2 :]
+        own = [(1, [mine]), (None, [after(other_there[0], *other_here), *other_there[1:]])]
         if batch + 1 < batches:
-            other = after(other, *there[batch + 1])
-        if batch:
-            other = after(other, back[-1][0])
-        other = to_core(other)
-        own = [(mine, 1, 0), (other, 1, 0)]
-        if batch + 1 < batches:
-            sent.append(total(own, 0, line))
+            sent += total(own, [(0, line)])
             back.append([to_mid(sent[-1])])
         else:
-            sent.append(total(own, half, line))
-            back.append([to_mid(total(own, 0, half)), to_mid(sent[-1])])
-        terms.append([(mine, 0, 0), (other, 0, 0)])
+            sent += total(own, [(half, line)])
+            back.append([to_mid(total(own, [(0, half)])[0]), to_mid(sent[-1])])
+        terms.append([(0, [mine]), (None, other_here), (None, back[-1])])
 
     for batch in range(batches):
-        near_back, far_back = back[batch][0], back[batch][-1]
-        far_sum = total([*terms[batch], (far_back, None, line - far_back.shape[0])], half, line)
-        terms[batch] += [(near_back, None, 0), (mirror(far_sum, 2), None, 0)]
+        if batch + 1 < batches:
+            terms[batch][-1] = (None, [after(back[batch][0], sent[-1])])
+        far_sum = total(terms[batch], [(half, line)])[0]
+        terms[batch].append((None, [mirror(far_sum, 2)]))
         span, pieces = 4, half
         while pieces > 1:
-            part = total(terms[batch], pieces // 2, pieces)
-            terms[batch].append((mirror(part, span), None, 0))
+            part = total(terms[batch], [(pieces // 2, pieces)])[0]
+            terms[batch].append((None, [mirror(part, span)]))
             span, pieces = span * 2, pieces // 2
     return finish(hidden_in, terms)
 

time: 89.5 us -> 85.2 us (0.952)
  waiting for transfers between devices: 31.9 us -> 26.2 us
  starting transfers between devices: 39.3 us -> 40.7 us
    ppermute x12 -> x18, waiting for transfers between devices: 8.05 us -> 4.49 us  [to_core(): return lax.ppermute(rows, 'ep', [(i, i ^ 1) for i in range(owners)])]
    ppermute x9, waiting for transfers between devices: 13.3 us -> 11.2 us  [to_mid(): return lax.ppermute(rows, 'ep', [(i, i ^ 2) for i in range(owners)])]
    ppermute x12 -> x18, starting transfers between devices: 1.91 us -> 3.4 us  [to_core(): return lax.ppermute(rows, 'ep', [(i, i ^ 1) for i in range(owners)])]
  transfers between devices with their start and end apart: 29 -> 35, of which waited for: 16 -> 20; matrix products, arithmetic and copies ran while one was open for 0% -> 0% of each run, Pallas kernels for 18% -> 19%
where the time goes in v11:
time: 85.2 us; the launch traced here: 85 us
  starting transfers between devices  40.7 us (48%)
  waiting for transfers between devices  26.2 us (31%)
  Pallas kernels  18 us (21%)
    ppermute x8, starting transfers between devices, along_line(): lax.ppermute(rows, 'ep', [(i, place_of(i // 4) * 4 + i % 4) for i in rang...  25.4 us
    pallas_call x14, Pallas kernels, call(): pl.pallas_call(kernel, out_shape=shapes, in_specs=specs, out_specs=[VMEM]...  18 us
    ppermute x9, starting transfers between devices, to_mid(): return lax.ppermute(rows, 'ep', [(i, i ^ 2) for i in range(owners)])  11.9 us
    ppermute x9, waiting for transfers between devices, to_mid(): return lax.ppermute(rows, 'ep', [(i, i ^ 2) for i in range(owners)])  11.2 us
    ppermute x8, waiting for transfers between devices, along_line(): lax.ppermute(rows, 'ep', [(i, place_of(i // 4) * 4 + i % 4) for i in rang...  10.5 us
    ppermute x18, waiting for transfers between devices, to_core(): return lax.ppermute(rows, 'ep', [(i, i ^ 1) for i in range(owners)])  4.49 us
    ppermute x18, starting transfers between devices, to_core(): return lax.ppermute(rows, 'ep', [(i, i ^ 1) for i in range(owners)])  3.4 us
  transfers between devices with their start and end apart: 35, of which 20 were waited for; matrix products, arithmetic and copies ran while one was open for 0% of the time, Pallas kernels for 19%

profile of v11, /device:TPU:0, one launch (start us, length us, event | category | flops | bytes accessed | tf_op | source)
XLA Modules:
  0.0 85.0 jit_solution(15584352720693920640)
XLA Ops:
  0.0 1.2 %prepare.1 = (bf16[1,32,2176]{2,1,0:T(8,128)(2,1)S(1)}, bf16[1,32,2176]{2,1,0:T(8,128)(2,1)S(1)}) custom-call(bf16[2,32,2048]{2,1,0:T(8,128)(2,1)} %hidden_ref.1, s32[2,8,32]{2,1,0:T(8,128)} %bitcast.6, s32[2,8,32]{2,1,0:T(8,128)} %bitcast.7, f32[1,2048]{1,0:T(1,128)} %bitcast.8), custom_call_target="tpu_custom_call" | custom-call | tf_op jit(solution)/shard_map/prepare/pallas_call | solution.py:27
  1.2 3.0 %collective-permute-start.2 = (bf16[1,32,2176]{2,1,0:T(8,128)(2,1)S(1)}, bf16[1,32,2176]{2,1,0:T(8,128)(2,1)S(1)}, u32[]{:S(2)}, u32[]{:S(2)}) collective-permute-start(bf16[1,32,2176]{2,1,0:T(8,128)(2,1)S(1)} %get-tuple-element.41.refs_0_), channel_id=1, source_target_pairs={{0,2},{1,3},{2,0},{3,1},{4,6},{5,7},{6,4},{7,5},{8,10},{9,11},{10,... | collective-permute-start | bytes 417800 | tf_op jit(solution)/shard_map/ppermute | solution.py:271
  4.3 4.0 %collective-permute-start = (bf16[1,32,2176]{2,1,0:T(8,128)(2,1)S(1)}, bf16[1,32,2176]{2,1,0:T(8,128)(2,1)S(1)}, u32[]{:S(2)}, u32[]{:S(2)}) collective-permute-start(bf16[1,32,2176]{2,1,0:T(8,128)(2,1)S(1)} %get-tuple-element.39.refs_0_), channel_id=1, source_target_pairs={{0,12},{1,13},{2,14},{3,15},{4,8},{5,9},{6,10},{7,11},{8,4},{9,5},... | collective-permute-start | bytes 417800 | tf_op jit(solution)/shard_map/ppermute | solution.py:262
  8.8 2.2 %collective-permute-done.1.refs_2_ = bf16[1,32,2176]{2,1,0:T(8,128)(2,1)S(1)} collective-permute-done((bf16[1,32,2176]{2,1,0:T(8,128)(2,1)S(1)}, bf16[1,32,2176]{2,1,0:T(8,128)(2,1)S(1)}, u32[]{:S(2)}, u32[]{:S(2)}) %collective-permute-start.1) | collective-permute-done | bytes 139296 | tf_op jit(solution)/shard_map/ppermute | solution.py:271
  10.9 0.7 collective-permute-done.refs_1_
  11.6 2.7 %collective-permute-start.4 = (bf16[2,32,2176]{2,1,0:T(8,128)(2,1)S(1)}, bf16[2,32,2176]{2,1,0:T(8,128)(2,1)S(1)}, u32[]{:S(2)}, u32[]{:S(2)}) collective-permute-start(bf16[2,32,2176]{2,1,0:T(8,128)(2,1)S(1)} %join.2.refs_0_), channel_id=1, source_target_pairs={{0,4},{1,5},{2,6},{3,7},{4,0},{5,1},{6,2},{7,3},{8,12},{9,13},{10,... | collective-permute-start | bytes 835592 | tf_op jit(solution)/shard_map/ppermute | solution.py:262
  14.3 2.7 %collective-permute-start.3 = (bf16[1,32,2176]{2,1,0:T(8,128)(2,1)S(1)}, bf16[1,32,2176]{2,1,0:T(8,128)(2,1)S(1)}, u32[]{:S(2)}, u32[]{:S(2)}) collective-permute-start(bf16[1,32,2176]{2,1,0:T(8,128)(2,1)S(1)} %get-tuple-element.41.refs_0_), channel_id=1, source_target_pairs={{0,12},{1,13},{2,14},{3,15},{4,8},{5,9},{6,10},{7,11},{8,4},{9,5},... | collective-permute-start | bytes 417800 | tf_op jit(solution)/shard_map/ppermute | solution.py:262
  16.9 1.5 %collective-permute-start.5 = (bf16[1,32,2176]{2,1,0:T(8,128)(2,1)S(1)}, bf16[1,32,2176]{2,1,0:T(8,128)(2,1)S(1)}, u32[]{:S(2)}, u32[]{:S(2)}) collective-permute-start(bf16[1,32,2176]{2,1,0:T(8,128)(2,1)S(1)} %collective-permute-done.refs_1_), channel_id=1, source_target_pairs={{0,2},{1,3},{2,0},{3,1},{4,6},{5,7},{6,4},{7,5},{8,10},{9,11},{10,... | collective-permute-start | bytes 417800 | tf_op jit(solution)/shard_map/ppermute | solution.py:271
  18.5 5.3 %collective-permute-done.3.refs_1_ = bf16[1,32,2176]{2,1,0:T(8,128)(2,1)S(1)} collective-permute-done((bf16[1,32,2176]{2,1,0:T(8,128)(2,1)S(1)}, bf16[1,32,2176]{2,1,0:T(8,128)(2,1)S(1)}, u32[]{:S(2)}, u32[]{:S(2)}) %collective-permute-start.3) | collective-permute-done | bytes 139296 | tf_op jit(solution)/shard_map/ppermute | solution.py:262
  23.9 1.6 %collective-permute-start.8 = (bf16[2,32,2176]{2,1,0:T(8,128)(2,1)S(1)}, bf16[2,32,2176]{2,1,0:T(8,128)(2,1)S(1)}, u32[]{:S(2)}, u32[]{:S(2)}) collective-permute-start(bf16[2,32,2176]{2,1,0:T(8,128)(2,1)S(1)} %collective-permute-done.4.refs_1_), channel_id=1, source_target_pairs={{0,2},{1,3},{2,0},{3,1},{4,6},{5,7},{6,4},{7,5},{8,10},{9,11},{10,... | collective-permute-start | bytes 835592 | tf_op jit(solution)/shard_map/ppermute | solution.py:271
  26.5 3.8 %load.1 = (bf16[1,2048,768]{2,1,0:T(8,128)(2,1)S(1)}, bf16[1,2048,768]{2,1,0:T(8,128)(2,1)S(1)}, bf16[1,768,2048]{2,1,0:T(8,128)(2,1)S(1)}) custom-call(bf16[1,2048,768]{2,1,0:T(8,128)(2,1)} %refs_0_, bf16[1,2048,768]{2,1,0:T(8,128)(2,1)} %refs_1_, bf16[1,768,2048]{2,1,0:T(8,128)(2,1)} %refs_2_), custom_call_target="tpu_custom_call" | custom-call | tf_op jit(solution)/shard_map/load/pallas_call | solution.py:27
  30.5 1.6 %collective-permute-done.8.refs_4_ = bf16[2,32,2176]{2,1,0:T(8,128)(2,1)S(1)} collective-permute-done((bf16[2,32,2176]{2,1,0:T(8,128)(2,1)S(1)}, bf16[2,32,2176]{2,1,0:T(8,128)(2,1)S(1)}, u32[]{:S(2)}, u32[]{:S(2)}) %collective-permute-start.8) | collective-permute-done | bytes 278560 | tf_op jit(solution)/shard_map/ppermute | solution.py:271
  32.1 1.5 %collective-permute-start.14 = (bf16[2,32,2176]{2,1,0:T(8,128)(2,1)S(1)}, bf16[2,32,2176]{2,1,0:T(8,128)(2,1)S(1)}, u32[]{:S(2)}, u32[]{:S(2)}) collective-permute-start(bf16[2,32,2176]{2,1,0:T(8,128)(2,1)S(1)} %collective-permute-done.6.refs_1_), channel_id=1, source_target_pairs={{0,2},{1,3},{2,0},{3,1},{4,6},{5,7},{6,4},{7,5},{8,10},{9,11},{10,... | collective-permute-start | bytes 835592 | tf_op jit(solution)/shard_map/ppermute | solution.py:271
  33.8 1.1 %collective-permute-done.12.refs_8_ = bf16[1,32,2176]{2,1,0:T(8,128)(2,1)S(1)} collective-permute-done((bf16[1,32,2176]{2,1,0:T(8,128)(2,1)S(1)}, bf16[1,32,2176]{2,1,0:T(8,128)(2,1)S(1)}, u32[]{:S(2)}, u32[]{:S(2)}) %collective-permute-start.12) | collective-permute-done | bytes 139296 | tf_op jit(solution)/shard_map/ppermute | solution.py:274
  35.0 5.7 %ffn.2 = (bf16[2,4,32,2048]{3,2,1,0:T(8,128)(2,1)S(1)}, bf16[2,32,2048]{2,1,0:T(8,128)(2,1)S(1)}, bf16[2,32,2048]{2,1,0:T(8,128)(2,1)S(1)}, bf16[2,32,2048]{2,1,0:T(8,128)(2,1)S(1)}, bf16[2,32,2048]{2,1,0:T(8,128)(2,1)S(1)}) custom-call(s32[3,1,6]{2,1,0:T(1,128)S(1)} %bitcast.4, bf16[1,2048,768]{2,1,0:T(8,128)(2,1)S(1)} %get-tuple-element.46.gate_ref, ...), custom_call_target="tpu_custom_call" | custom-call | tf_op jit(solution)/shard_map/ffn/pallas_call | solution.py:27
  41.1 0.5 collective-permute-start.16
  42.2 0.5 collective-permute-done.15.refs_1_
  44.1 1.1 %collective-permute-done.22.refs_7_ = bf16[1,32,2176]{2,1,0:T(8,128)(2,1)S(1)} collective-permute-done((bf16[1,32,2176]{2,1,0:T(8,128)(2,1)S(1)}, bf16[1,32,2176]{2,1,0:T(8,128)(2,1)S(1)}, u32[]{:S(2)}, u32[]{:S(2)}) %collective-permute-start.22) | collective-permute-done | bytes 139296 | tf_op jit(solution)/shard_map/ppermute | solution.py:274
  45.2 1.5 %collective-permute-start.19 = (bf16[4,32,2048]{2,1,0:T(8,128)(2,1)S(1)}, bf16[4,32,2048]{2,1,0:T(8,128)(2,1)S(1)}, u32[]{:S(2)}, u32[]{:S(2)}) collective-permute-start(bf16[4,32,2048]{2,1,0:T(8,128)(2,1)S(1)} %total.7), channel_id=1, source_target_pairs={{0,2},{1,3},{2,0},{3,1},{4,6},{5,7},{6,4},{7,5},{8,10},{9,11},{10,... | collective-permute-start | bytes 1572872 | tf_op jit(solution)/shard_map/ppermute | solution.py:271
  46.7 5.7 %ffn.3 = (bf16[2,4,32,2048]{3,2,1,0:T(8,128)(2,1)S(1)}, bf16[2,32,2048]{2,1,0:T(8,128)(2,1)S(1)}, bf16[2,32,2048]{2,1,0:T(8,128)(2,1)S(1)}, bf16[2,32,2048]{2,1,0:T(8,128)(2,1)S(1)}, bf16[2,32,2048]{2,1,0:T(8,128)(2,1)S(1)}) custom-call(s32[3,1,6]{2,1,0:T(1,128)S(1)} %bitcast.5, bf16[1,2048,768]{2,1,0:T(8,128)(2,1)S(1)} %get-tuple-element.46.gate_ref, ...), custom_call_target="tpu_custom_call" | custom-call | tf_op jit(solution)/shard_map/ffn/pallas_call | solution.py:27
  53.6 0.5 collective-permute-done.25.refs_1_
  54.1 0.6 collective-permute-start.32
  55.3 4.7 %collective-permute-done.19.refs_2_ = bf16[4,32,2048]{2,1,0:T(8,128)(2,1)S(1)} collective-permute-done((bf16[4,32,2048]{2,1,0:T(8,128)(2,1)S(1)}, bf16[4,32,2048]{2,1,0:T(8,128)(2,1)S(1)}, u32[]{:S(2)}, u32[]{:S(2)}) %collective-permute-start.19) | collective-permute-done | bytes 524320 | tf_op jit(solution)/shard_map/ppermute | solution.py:271
  60.1 2.0 %collective-permute-start.26 = (bf16[2,32,2048]{2,1,0:T(8,128)(2,1)S(1)}, bf16[2,32,2048]{2,1,0:T(8,128)(2,1)S(1)}, u32[]{:S(2)}, u32[]{:S(2)}) collective-permute-start(bf16[2,32,2048]{2,1,0:T(8,128)(2,1)S(1)} %total.9), channel_id=1, source_target_pairs={{0,4},{1,5},{2,6},{3,7},{4,0},{5,1},{6,2},{7,3},{8,12},{9,13},{10,... | collective-permute-start | bytes 786440 | tf_op jit(solution)/shard_map/ppermute | solution.py:262
  62.1 1.5 %collective-permute-start.31 = (bf16[2,32,2048]{2,1,0:T(8,128)(2,1)S(1)}, bf16[2,32,2048]{2,1,0:T(8,128)(2,1)S(1)}, u32[]{:S(2)}, u32[]{:S(2)}) collective-permute-start(bf16[2,32,2048]{2,1,0:T(8,128)(2,1)S(1)} %total.11), channel_id=1, source_target_pairs={{0,2},{1,3},{2,0},{3,1},{4,6},{5,7},{6,4},{7,5},{8,10},{9,11},{10,... | collective-permute-start | bytes 786440 | tf_op jit(solution)/shard_map/ppermute | solution.py:271
  63.6 2.0 %collective-permute-done.32.refs_2_ = bf16[2,32,2048]{2,1,0:T(8,128)(2,1)S(1)} collective-permute-done((bf16[2,32,2048]{2,1,0:T(8,128)(2,1)S(1)}, bf16[2,32,2048]{2,1,0:T(8,128)(2,1)S(1)}, u32[]{:S(2)}, u32[]{:S(2)}) %collective-permute-start.32) | collective-permute-done | bytes 262176 | tf_op jit(solution)/shard_map/ppermute | solution.py:271
  65.7 2.0 %collective-permute-start.33 = (bf16[2,32,2048]{2,1,0:T(8,128)(2,1)S(1)}, bf16[2,32,2048]{2,1,0:T(8,128)(2,1)S(1)}, u32[]{:S(2)}, u32[]{:S(2)}) collective-permute-start(bf16[2,32,2048]{2,1,0:T(8,128)(2,1)S(1)} %total.12), channel_id=1, source_target_pairs={{0,4},{1,5},{2,6},{3,7},{4,0},{5,1},{6,2},{7,3},{8,12},{9,13},{10,... | collective-permute-start | bytes 786440 | tf_op jit(solution)/shard_map/ppermute | solution.py:262
  67.8 4.2 %collective-permute-start.27 = (bf16[1,32,2048]{2,1,0:T(8,128)(2,1)S(1)}, bf16[1,32,2048]{2,1,0:T(8,128)(2,1)S(1)}, u32[]{:S(2)}, u32[]{:S(2)}) collective-permute-start(bf16[1,32,2048]{2,1,0:T(8,128)(2,1)S(1)} %total.10), channel_id=1, source_target_pairs={{0,12},{1,13},{2,14},{3,15},{4,8},{5,9},{6,10},{7,11},{8,4},{9,5},... | collective-permute-start | bytes 393224 | tf_op jit(solution)/shard_map/ppermute | solution.py:262
  72.0 1.4 %collective-permute-done.33.refs_3_.refs_8_ = bf16[2,32,2048]{2,1,0:T(8,128)(2,1)S(1)} collective-permute-done((bf16[2,32,2048]{2,1,0:T(8,128)(2,1)S(1)}, bf16[2,32,2048]{2,1,0:T(8,128)(2,1)S(1)}, u32[]{:S(2)}, u32[]{:S(2)}) %collective-permute-start.33) | collective-permute-done | bytes 262176 | tf_op jit(solution)/shard_map/ppermute | solution.py:262
  73.4 7.7 %collective-permute-start.34 = (bf16[1,32,2048]{2,1,0:T(8,128)(2,1)S(1)}, bf16[1,32,2048]{2,1,0:T(8,128)(2,1)S(1)}, u32[]{:S(2)}, u32[]{:S(2)}) collective-permute-start(bf16[1,32,2048]{2,1,0:T(8,128)(2,1)S(1)} %total.13), channel_id=1, source_target_pairs={{0,12},{1,13},{2,14},{3,15},{4,8},{5,9},{6,10},{7,11},{8,4},{9,5},... | collective-permute-start | bytes 393224 | tf_op jit(solution)/shard_map/ppermute | solution.py:262
  81.2 2.9 %collective-permute-done.34.refs_9_ = bf16[1,32,2048]{2,1,0:T(8,128)(2,1)S(1)} collective-permute-done((bf16[1,32,2048]{2,1,0:T(8,128)(2,1)S(1)}, bf16[1,32,2048]{2,1,0:T(8,128)(2,1)S(1)}, u32[]{:S(2)}, u32[]{:S(2)}) %collective-permute-start.34) | collective-permute-done | bytes 131104 | tf_op jit(solution)/shard_map/ppermute | solution.py:262
  84.1 0.9 %finish.1 = bf16[2,32,2048]{2,1,0:T(8,128)(2,1)} custom-call(bf16[2,32,2048]{2,1,0:T(8,128)(2,1)S(1)} %copy-done, bf16[2,4,32,2048]{3,2,1,0:T(8,128)(2,1)S(1)} %get-tuple-element.53.refs_0_, bf16[2,32,2048]{2,1,0:T(8,128)(2,1)S(1)} %collective-permute-done.15.refs_1_, bf16[4,32,2048]{2,1,0:T(8,128)(2,1)S(1)} %collective-permute-done.19.refs_2_, ...), custom_call_target="tpu_custom_call" | custom-call | tf_op jit(solution)/shard_map/finish/pallas_call | solution.py:27
  (56 shorter events, 6.3 us)
Async XLA Ops:
  1.2 7.5 %collective-permute-start.2 = (bf16[1,32,2176]{2,1,0:T(8,128)(2,1)S(1)}, bf16[1,32,2176]{2,1,0:T(8,128)(2,1)S(1)}, u32[]{:S(2)}, u32[]{:S(2)}) collective-permute-start(bf16[1,32,2176]{2,1,0:T(8,128)(2,1)S(1)} %get-tuple-element.41.refs_0_), channel_id=1, source_target_pairs={{0,2},{1,3},{2,0},{3,1},{4,6},{5,7},{6,4},{7,5},{8,10},{9,11},{10,... | collective-permute-start | bytes 417800 | tf_op jit(solution)/shard_map/ppermute | solution.py:271
  4.3 6.7 %collective-permute-start.1 = (bf16[1,32,2176]{2,1,0:T(8,128)(2,1)S(1)}, bf16[1,32,2176]{2,1,0:T(8,128)(2,1)S(1)}, u32[]{:S(2)}, u32[]{:S(2)}) collective-permute-start(bf16[1,32,2176]{2,1,0:T(8,128)(2,1)S(1)} %get-tuple-element.39.refs_0_), channel_id=1, source_target_pairs={{0,2},{1,3},{2,0},{3,1},{4,6},{5,7},{6,4},{7,5},{8,10},{9,11},{10,... | collective-permute-start | bytes 417800 | tf_op jit(solution)/shard_map/ppermute | solution.py:271
  4.3 7.2 %collective-permute-start = (bf16[1,32,2176]{2,1,0:T(8,128)(2,1)S(1)}, bf16[1,32,2176]{2,1,0:T(8,128)(2,1)S(1)}, u32[]{:S(2)}, u32[]{:S(2)}) collective-permute-start(bf16[1,32,2176]{2,1,0:T(8,128)(2,1)S(1)} %get-tuple-element.39.refs_0_), channel_id=1, source_target_pairs={{0,12},{1,13},{2,14},{3,15},{4,8},{5,9},{6,10},{7,11},{8,4},{9,5},... | collective-permute-start | bytes 417800 | tf_op jit(solution)/shard_map/ppermute | solution.py:262
  11.6 12.2 %collective-permute-start.4 = (bf16[2,32,2176]{2,1,0:T(8,128)(2,1)S(1)}, bf16[2,32,2176]{2,1,0:T(8,128)(2,1)S(1)}, u32[]{:S(2)}, u32[]{:S(2)}) collective-permute-start(bf16[2,32,2176]{2,1,0:T(8,128)(2,1)S(1)} %join.2.refs_0_), channel_id=1, source_target_pairs={{0,4},{1,5},{2,6},{3,7},{4,0},{5,1},{6,2},{7,3},{8,12},{9,13},{10,... | collective-permute-start | bytes 835592 | tf_op jit(solution)/shard_map/ppermute | solution.py:262
  14.3 9.5 %collective-permute-start.3 = (bf16[1,32,2176]{2,1,0:T(8,128)(2,1)S(1)}, bf16[1,32,2176]{2,1,0:T(8,128)(2,1)S(1)}, u32[]{:S(2)}, u32[]{:S(2)}) collective-permute-start(bf16[1,32,2176]{2,1,0:T(8,128)(2,1)S(1)} %get-tuple-element.41.refs_0_), channel_id=1, source_target_pairs={{0,12},{1,13},{2,14},{3,15},{4,8},{5,9},{6,10},{7,11},{8,4},{9,5},... | collective-permute-start | bytes 417800 | tf_op jit(solution)/shard_map/ppermute | solution.py:262
  16.9 6.9 %collective-permute-start.5 = (bf16[1,32,2176]{2,1,0:T(8,128)(2,1)S(1)}, bf16[1,32,2176]{2,1,0:T(8,128)(2,1)S(1)}, u32[]{:S(2)}, u32[]{:S(2)}) collective-permute-start(bf16[1,32,2176]{2,1,0:T(8,128)(2,1)S(1)} %collective-permute-done.refs_1_), channel_id=1, source_target_pairs={{0,2},{1,3},{2,0},{3,1},{4,6},{5,7},{6,4},{7,5},{8,10},{9,11},{10,... | collective-permute-start | bytes 417800 | tf_op jit(solution)/shard_map/ppermute | solution.py:271
  23.9 6.6 %collective-permute-start.6 = (bf16[2,32,2176]{2,1,0:T(8,128)(2,1)S(1)}, bf16[2,32,2176]{2,1,0:T(8,128)(2,1)S(1)}, u32[]{:S(2)}, u32[]{:S(2)}) collective-permute-start(bf16[2,32,2176]{2,1,0:T(8,128)(2,1)S(1)} %join.3.refs_0_), channel_id=1, source_target_pairs={{0,4},{1,5},{2,6},{3,7},{4,0},{5,1},{6,2},{7,3},{8,12},{9,13},{10,... | collective-permute-start | bytes 835592 | tf_op jit(solution)/shard_map/ppermute | solution.py:262
  23.9 8.1 %collective-permute-start.8 = (bf16[2,32,2176]{2,1,0:T(8,128)(2,1)S(1)}, bf16[2,32,2176]{2,1,0:T(8,128)(2,1)S(1)}, u32[]{:S(2)}, u32[]{:S(2)}) collective-permute-start(bf16[2,32,2176]{2,1,0:T(8,128)(2,1)S(1)} %collective-permute-done.4.refs_1_), channel_id=1, source_target_pairs={{0,2},{1,3},{2,0},{3,1},{4,6},{5,7},{6,4},{7,5},{8,10},{9,11},{10,... | collective-permute-start | bytes 835592 | tf_op jit(solution)/shard_map/ppermute | solution.py:271
  25.5 6.5 %collective-permute-start.11 = (bf16[1,32,2176]{2,1,0:T(8,128)(2,1)S(1)}, bf16[1,32,2176]{2,1,0:T(8,128)(2,1)S(1)}, u32[]{:S(2)}, u32[]{:S(2)}) collective-permute-start(bf16[1,32,2176]{2,1,0:T(8,128)(2,1)S(1)} %collective-permute-done.1.refs_2_), channel_id=1, source_target_pairs={{0,1},{1,0},{2,3},{3,2},{4,5},{5,4},{6,7},{7,6},{8,9},{9,8},{10,11... | collective-permute-start | bytes 417800 | tf_op jit(solution)/shard_map/ppermute | solution.py:274
  25.5 9.4 %collective-permute-start.9 = (bf16[2,32,2176]{2,1,0:T(8,128)(2,1)S(1)}, bf16[2,32,2176]{2,1,0:T(8,128)(2,1)S(1)}, u32[]{:S(2)}, u32[]{:S(2)}) collective-permute-start(bf16[2,32,2176]{2,1,0:T(8,128)(2,1)S(1)} %join.2.refs_0_), channel_id=1, source_target_pairs={{0,1},{1,0},{2,3},{3,2},{4,5},{5,4},{6,7},{7,6},{8,9},{9,8},{10,11... | collective-permute-start | bytes 835592 | tf_op jit(solution)/shard_map/ppermute | solution.py:274
  26.0 7.5 %collective-permute-start.7 = (bf16[1,32,2176]{2,1,0:T(8,128)(2,1)S(1)}, bf16[1,32,2176]{2,1,0:T(8,128)(2,1)S(1)}, u32[]{:S(2)}, u32[]{:S(2)}) collective-permute-start(bf16[1,32,2176]{2,1,0:T(8,128)(2,1)S(1)} %collective-permute-done.3.refs_1_), channel_id=1, source_target_pairs={{0,2},{1,3},{2,0},{3,1},{4,6},{5,7},{6,4},{7,5},{8,10},{9,11},{10,... | collective-permute-start | bytes 417800 | tf_op jit(solution)/shard_map/ppermute | solution.py:271
  30.5 4.5 %collective-permute-start.10 = (bf16[2,32,2176]{2,1,0:T(8,128)(2,1)S(1)}, bf16[2,32,2176]{2,1,0:T(8,128)(2,1)S(1)}, u32[]{:S(2)}, u32[]{:S(2)}) collective-permute-start(bf16[2,32,2176]{2,1,0:T(8,128)(2,1)S(1)} %collective-permute-done.4.refs_1_), channel_id=1, source_target_pairs={{0,1},{1,0},{2,3},{3,2},{4,5},{5,4},{6,7},{7,6},{8,9},{9,8},{10,11... | collective-permute-start | bytes 835592 | tf_op jit(solution)/shard_map/ppermute | solution.py:274
  32.1 2.9 %collective-permute-start.13 = (bf16[2,32,2176]{2,1,0:T(8,128)(2,1)S(1)}, bf16[2,32,2176]{2,1,0:T(8,128)(2,1)S(1)}, u32[]{:S(2)}, u32[]{:S(2)}) collective-permute-start(bf16[2,32,2176]{2,1,0:T(8,128)(2,1)S(1)} %collective-permute-done.8.refs_4_), channel_id=1, source_target_pairs={{0,1},{1,0},{2,3},{3,2},{4,5},{5,4},{6,7},{7,6},{8,9},{9,8},{10,11... | collective-permute-start | bytes 835592 | tf_op jit(solution)/shard_map/ppermute | solution.py:274
  32.1 9.1 %collective-permute-start.14 = (bf16[2,32,2176]{2,1,0:T(8,128)(2,1)S(1)}, bf16[2,32,2176]{2,1,0:T(8,128)(2,1)S(1)}, u32[]{:S(2)}, u32[]{:S(2)}) collective-permute-start(bf16[2,32,2176]{2,1,0:T(8,128)(2,1)S(1)} %collective-permute-done.6.refs_1_), channel_id=1, source_target_pairs={{0,2},{1,3},{2,0},{3,1},{4,6},{5,7},{6,4},{7,5},{8,10},{9,11},{10,... | collective-permute-start | bytes 835592 | tf_op jit(solution)/shard_map/ppermute | solution.py:271
  41.1 1.9 %collective-permute-start.16 = (bf16[2,32,2048]{2,1,0:T(8,128)(2,1)S(1)}, bf16[2,32,2048]{2,1,0:T(8,128)(2,1)S(1)}, u32[]{:S(2)}, u32[]{:S(2)}) collective-permute-start(bf16[2,32,2048]{2,1,0:T(8,128)(2,1)S(1)} %get-tuple-element.57), channel_id=1, source_target_pairs={{0,1},{1,0},{2,3},{3,2},{4,5},{5,4},{6,7},{7,6},{8,9},{9,8},{10,11... | collective-permute-start | bytes 786440 | tf_op jit(solution)/shard_map/ppermute | solution.py:274
  41.6 1.8 %collective-permute-start.17 = (bf16[2,32,2048]{2,1,0:T(8,128)(2,1)S(1)}, bf16[2,32,2048]{2,1,0:T(8,128)(2,1)S(1)}, u32[]{:S(2)}, u32[]{:S(2)}) collective-permute-start(bf16[2,32,2048]{2,1,0:T(8,128)(2,1)S(1)} %get-tuple-element.59), channel_id=1, source_target_pairs={{0,1},{1,0},{2,3},{3,2},{4,5},{5,4},{6,7},{7,6},{8,9},{9,8},{10,11... | collective-permute-start | bytes 786440 | tf_op jit(solution)/shard_map/ppermute | solution.py:274
  41.6 2.1 %collective-permute-start.18 = (bf16[2,32,2048]{2,1,0:T(8,128)(2,1)S(1)}, bf16[2,32,2048]{2,1,0:T(8,128)(2,1)S(1)}, u32[]{:S(2)}, u32[]{:S(2)}) collective-permute-start(bf16[2,32,2048]{2,1,0:T(8,128)(2,1)S(1)} %get-tuple-element.62), channel_id=1, source_target_pairs={{0,1},{1,0},{2,3},{3,2},{4,5},{5,4},{6,7},{7,6},{8,9},{9,8},{10,11... | collective-permute-start | bytes 786440 | tf_op jit(solution)/shard_map/ppermute | solution.py:274
  42.2 4.6 %collective-permute-start.20 = (bf16[2,32,2176]{2,1,0:T(8,128)(2,1)S(1)}, bf16[2,32,2176]{2,1,0:T(8,128)(2,1)S(1)}, u32[]{:S(2)}, u32[]{:S(2)}) collective-permute-start(bf16[2,32,2176]{2,1,0:T(8,128)(2,1)S(1)} %join.3.refs_0_), channel_id=1, source_target_pairs={{0,1},{1,0},{2,3},{3,2},{4,5},{5,4},{6,7},{7,6},{8,9},{9,8},{10,11... | collective-permute-start | bytes 835592 | tf_op jit(solution)/shard_map/ppermute | solution.py:274
  42.7 4.0 %collective-permute-start.21 = (bf16[2,32,2176]{2,1,0:T(8,128)(2,1)S(1)}, bf16[2,32,2176]{2,1,0:T(8,128)(2,1)S(1)}, u32[]{:S(2)}, u32[]{:S(2)}) collective-permute-start(bf16[2,32,2176]{2,1,0:T(8,128)(2,1)S(1)} %collective-permute-done.6.refs_1_), channel_id=1, source_target_pairs={{0,1},{1,0},{2,3},{3,2},{4,5},{5,4},{6,7},{7,6},{8,9},{9,8},{10,11... | collective-permute-start | bytes 835592 | tf_op jit(solution)/shard_map/ppermute | solution.py:274
  43.0 3.7 %collective-permute-start.24 = (bf16[2,32,2176]{2,1,0:T(8,128)(2,1)S(1)}, bf16[2,32,2176]{2,1,0:T(8,128)(2,1)S(1)}, u32[]{:S(2)}, u32[]{:S(2)}) collective-permute-start(bf16[2,32,2176]{2,1,0:T(8,128)(2,1)S(1)} %collective-permute-done.14.refs_4_), channel_id=1, source_target_pairs={{0,1},{1,0},{2,3},{3,2},{4,5},{5,4},{6,7},{7,6},{8,9},{9,8},{10,11... | collective-permute-start | bytes 835592 | tf_op jit(solution)/shard_map/ppermute | solution.py:274
  43.4 1.8 %collective-permute-start.22 = (bf16[1,32,2176]{2,1,0:T(8,128)(2,1)S(1)}, bf16[1,32,2176]{2,1,0:T(8,128)(2,1)S(1)}, u32[]{:S(2)}, u32[]{:S(2)}) collective-permute-start(bf16[1,32,2176]{2,1,0:T(8,128)(2,1)S(1)} %collective-permute-done.2.refs_2_), channel_id=1, source_target_pairs={{0,1},{1,0},{2,3},{3,2},{4,5},{5,4},{6,7},{7,6},{8,9},{9,8},{10,11... | collective-permute-start | bytes 417800 | tf_op jit(solution)/shard_map/ppermute | solution.py:274
  43.8 2.9 %collective-permute-start.23 = (bf16[1,32,2176]{2,1,0:T(8,128)(2,1)S(1)}, bf16[1,32,2176]{2,1,0:T(8,128)(2,1)S(1)}, u32[]{:S(2)}, u32[]{:S(2)}) collective-permute-start(bf16[1,32,2176]{2,1,0:T(8,128)(2,1)S(1)} %collective-permute-done.7.refs_3_), channel_id=1, source_target_pairs={{0,1},{1,0},{2,3},{3,2},{4,5},{5,4},{6,7},{7,6},{8,9},{9,8},{10,11... | collective-permute-start | bytes 417800 | tf_op jit(solution)/shard_map/ppermute | solution.py:274
  45.2 14.8 %collective-permute-start.19 = (bf16[4,32,2048]{2,1,0:T(8,128)(2,1)S(1)}, bf16[4,32,2048]{2,1,0:T(8,128)(2,1)S(1)}, u32[]{:S(2)}, u32[]{:S(2)}) collective-permute-start(bf16[4,32,2048]{2,1,0:T(8,128)(2,1)S(1)} %total.7), channel_id=1, source_target_pairs={{0,2},{1,3},{2,0},{3,1},{4,6},{5,7},{6,4},{7,5},{8,10},{9,11},{10,... | collective-permute-start | bytes 1572872 | tf_op jit(solution)/shard_map/ppermute | solution.py:271
  52.6 2.2 %collective-permute-start.28 = (bf16[2,32,2048]{2,1,0:T(8,128)(2,1)S(1)}, bf16[2,32,2048]{2,1,0:T(8,128)(2,1)S(1)}, u32[]{:S(2)}, u32[]{:S(2)}) collective-permute-start(bf16[2,32,2048]{2,1,0:T(8,128)(2,1)S(1)} %get-tuple-element.67), channel_id=1, source_target_pairs={{0,1},{1,0},{2,3},{3,2},{4,5},{5,4},{6,7},{7,6},{8,9},{9,8},{10,11... | collective-permute-start | bytes 786440 | tf_op jit(solution)/shard_map/ppermute | solution.py:274
  53.1 1.8 %collective-permute-start.29 = (bf16[2,32,2048]{2,1,0:T(8,128)(2,1)S(1)}, bf16[2,32,2048]{2,1,0:T(8,128)(2,1)S(1)}, u32[]{:S(2)}, u32[]{:S(2)}) collective-permute-start(bf16[2,32,2048]{2,1,0:T(8,128)(2,1)S(1)} %get-tuple-element.68), channel_id=1, source_target_pairs={{0,1},{1,0},{2,3},{3,2},{4,5},{5,4},{6,7},{7,6},{8,9},{9,8},{10,11... | collective-permute-start | bytes 786440 | tf_op jit(solution)/shard_map/ppermute | solution.py:274
  53.1 2.1 %collective-permute-start.30 = (bf16[2,32,2048]{2,1,0:T(8,128)(2,1)S(1)}, bf16[2,32,2048]{2,1,0:T(8,128)(2,1)S(1)}, u32[]{:S(2)}, u32[]{:S(2)}) collective-permute-start(bf16[2,32,2048]{2,1,0:T(8,128)(2,1)S(1)} %get-tuple-element.69), channel_id=1, source_target_pairs={{0,1},{1,0},{2,3},{3,2},{4,5},{5,4},{6,7},{7,6},{8,9},{9,8},{10,11... | collective-permute-start | bytes 786440 | tf_op jit(solution)/shard_map/ppermute | solution.py:274
  54.1 11.4 %collective-permute-start.32 = (bf16[2,32,2048]{2,1,0:T(8,128)(2,1)S(1)}, bf16[2,32,2048]{2,1,0:T(8,128)(2,1)S(1)}, u32[]{:S(2)}, u32[]{:S(2)}) collective-permute-start(bf16[2,32,2048]{2,1,0:T(8,128)(2,1)S(1)} %total.8), channel_id=1, source_target_pairs={{0,2},{1,3},{2,0},{3,1},{4,6},{5,7},{6,4},{7,5},{8,10},{9,11},{10,... | collective-permute-start | bytes 786440 | tf_op jit(solution)/shard_map/ppermute | solution.py:271
  60.1 7.6 %collective-permute-start.26 = (bf16[2,32,2048]{2,1,0:T(8,128)(2,1)S(1)}, bf16[2,32,2048]{2,1,0:T(8,128)(2,1)S(1)}, u32[]{:S(2)}, u32[]{:S(2)}) collective-permute-start(bf16[2,32,2048]{2,1,0:T(8,128)(2,1)S(1)} %total.9), channel_id=1, source_target_pairs={{0,4},{1,5},{2,6},{3,7},{4,0},{5,1},{6,2},{7,3},{8,12},{9,13},{10,... | collective-permute-start | bytes 786440 | tf_op jit(solution)/shard_map/ppermute | solution.py:262
  62.1 9.9 %collective-permute-start.31 = (bf16[2,32,2048]{2,1,0:T(8,128)(2,1)S(1)}, bf16[2,32,2048]{2,1,0:T(8,128)(2,1)S(1)}, u32[]{:S(2)}, u32[]{:S(2)}) collective-permute-start(bf16[2,32,2048]{2,1,0:T(8,128)(2,1)S(1)} %total.11), channel_id=1, source_target_pairs={{0,2},{1,3},{2,0},{3,1},{4,6},{5,7},{6,4},{7,5},{8,10},{9,11},{10,... | collective-permute-start | bytes 786440 | tf_op jit(solution)/shard_map/ppermute | solution.py:271
  65.7 7.7 %collective-permute-start.33 = (bf16[2,32,2048]{2,1,0:T(8,128)(2,1)S(1)}, bf16[2,32,2048]{2,1,0:T(8,128)(2,1)S(1)}, u32[]{:S(2)}, u32[]{:S(2)}) collective-permute-start(bf16[2,32,2048]{2,1,0:T(8,128)(2,1)S(1)} %total.12), channel_id=1, source_target_pairs={{0,4},{1,5},{2,6},{3,7},{4,0},{5,1},{6,2},{7,3},{8,12},{9,13},{10,... | collective-permute-start | bytes 786440 | tf_op jit(solution)/shard_map/ppermute | solution.py:262
  67.8 13.4 %collective-permute-start.27 = (bf16[1,32,2048]{2,1,0:T(8,128)(2,1)S(1)}, bf16[1,32,2048]{2,1,0:T(8,128)(2,1)S(1)}, u32[]{:S(2)}, u32[]{:S(2)}) collective-permute-start(bf16[1,32,2048]{2,1,0:T(8,128)(2,1)S(1)} %total.10), channel_id=1, source_target_pairs={{0,12},{1,13},{2,14},{3,15},{4,8},{5,9},{6,10},{7,11},{8,4},{9,5},... | collective-permute-start | bytes 393224 | tf_op jit(solution)/shard_map/ppermute | solution.py:262
  73.4 10.7 %collective-permute-start.34 = (bf16[1,32,2048]{2,1,0:T(8,128)(2,1)S(1)}, bf16[1,32,2048]{2,1,0:T(8,128)(2,1)S(1)}, u32[]{:S(2)}, u32[]{:S(2)}) collective-permute-start(bf16[1,32,2048]{2,1,0:T(8,128)(2,1)S(1)} %total.13), channel_id=1, source_target_pairs={{0,12},{1,13},{2,14},{3,15},{4,8},{5,9},{6,10},{7,11},{8,4},{9,5},... | collective-permute-start | bytes 393224 | tf_op jit(solution)/shard_map/ppermute | solution.py:262
  (5 other events, 39.7 us)

commit v12 on v11

--- a/solution.py
+++ b/solution.py
@@ -190,6 +190,19 @@
     return result
 
 
+def narrow(terms, low, high):
+    layout, kept = [], []
+    for slot, arrays, *first in terms:
+        skip = -first[0] if first else 0
+        while slot is None and low >= skip + arrays[0].shape[0]:
+            skip, arrays = skip + arrays[0].shape[0], arrays[1:]
+        while slot is None and high <= skip + sum(a.shape[0] for a in arrays[:-1]):
+            arrays = arrays[:-1]
+        layout.append((slot, skip, len(arrays)))
+        kept += arrays
+    return layout, kept
+
+
 def total_kernel(layout, cuts, *refs):
     ins, outs = refs[: -len(cuts)], refs[-len(cuts) :]
     for (low, high), out_ref in zip(cuts, outs):
@@ -198,41 +211,33 @@
 
 
 def total(terms, cuts):
-    first = cuts[0][0]
-    kept = []
-    for slot, arrays in terms:
-        skip = 0
-        while slot is None and first >= skip + arrays[0].shape[0]:
-            skip, arrays = skip + arrays[0].shape[0], arrays[1:]
-        high = cuts[-1][1] - skip
-        while slot is None and high <= sum(a.shape[0] for a in arrays[:-1]):
-            arrays = arrays[:-1]
-        kept.append((slot, skip, arrays))
-    layout = [(slot, skip, len(arrays)) for slot, skip, arrays in kept]
-    arrays = [a for _, _, arrays in kept for a in arrays]
-    part, width = arrays[0].shape[-2:]
+    layout, kept = narrow(terms, cuts[0][0], cuts[-1][1])
+    part, width = kept[0].shape[-2:]
     return call(
         functools.partial(total_kernel, layout, cuts),
-        arrays,
-        [VMEM] * len(arrays),
-        [jax.ShapeDtypeStruct((high - low, part, width), arrays[0].dtype) for low, high in cuts],
+        kept,
+        [VMEM] * len(kept),
+        [jax.ShapeDtypeStruct((high - low, part, width), kept[0].dtype) for low, high in cuts],
         name="total",
     )
 
 
-def finish_kernel(layout, hidden_ref, *refs):
+def finish_kernel(layouts, hidden_ref, *refs):
     out_ref = refs[-1]
     count = (len(refs) - 1) // hidden_ref.shape[0]
     for batch in range(hidden_ref.shape[0]):
-        mixed = sum_of(layout, refs[batch * count : (batch + 1) * count], 0)
+        mixed = sum_of(layouts[batch], refs[batch * count : (batch + 1) * count], 0)
         out_ref[batch] = (hidden_ref[batch].astype(jnp.float32) + mixed).astype(out_ref.dtype)
 
 
 def finish(hidden_in, terms):
-    layout = [(slot, 0, 1) for slot, _ in terms[0]]
-    arrays = [arrays[0] for batch in terms for _, arrays in batch]
-    return call(
-        functools.partial(finish_kernel, layout),
+    layouts, arrays = [], []
+    for batch in terms:
+        layout, kept = narrow(batch, 0, 1)
+        layouts.append(layout)
+        arrays += kept
+    return call(
+        functools.partial(finish_kernel, layouts),
         [hidden_in, *arrays],
         [VMEM] * (1 + len(arrays)),
         [jax.ShapeDtypeStruct(hidden_in.shape, hidden_in.dtype)],
@@ -273,63 +278,78 @@
     def to_core(rows):
         return lax.ppermute(rows, "ep", [(i, i ^ 1) for i in range(owners)])
 
+    spans = []
+    while line >> len(spans) > 2:
+        spans.append(line >> len(spans))
+
+    def owner_of(p, piece):
+        for level in range(len(spans), 0, -1):
+            if piece >= 1 << (level - 1):
+                p, piece = mirrored(p, spans[level - 1]), piece - (1 << (level - 1))
+        return p
+
     payload = prepare(hidden_in, expert_ids, route_share, norm_gain, -(-owners // LANES) * LANES)
 
     own_there = [to_mid(rows) for rows in payload]
-    near, far, there = [], [], []
+    near, near_there, joined, far = [], [], [], []
+    weights = None
     for batch, rows in enumerate(payload):
         if batch:
-            rows = after(rows, near[-1])
-        there.append([own_there[batch]])
-        span = line
-        while span > 2:
+            rows = after(rows, joined[-1])
+        near.append([rows])
+        near_there.append([own_there[batch]])
+        for span in spans:
             received = mirror(rows, span)
-            if not batch:
-                received = after(received, *own_there)
-            there[batch].append(to_mid(received))
+            received = after(received, *([*weights, far[-1]] if batch else own_there))
+            near[batch].append(received)
+            near_there[batch].append(to_mid(received))
             rows = join(rows, received)
-            if batch:
-                rows = after(rows, far[-1])
-            span //= 2
-        near.append(rows)
-        far.append(mirror(rows if not batch else after(rows, *there[batch - 1]), 2))
-    weights = load([after(w, near[-1]) for w in (gate_weight, up_weight, down_weight)])
-    far[-1] = after(far[-1], *weights)
-    ahead = there[-1][-1]
+        joined.append(rows)
+        far.append(mirror(rows, 2))
+        if weights is None:
+            weights = load([after(w, rows) for w in (gate_weight, up_weight, down_weight)])
+    far_there = [to_mid(rows) for rows in far]
+
+    groups = [[(0, 0)]]
     for batch in range(batches):
-        rows = far[batch]
-        if batch + 1 < batches:
-            rows = after(rows, near[batch + 1])
-        there[batch].append(to_mid(rows))
-
-    terms, sent, back = [], [], []
-    for batch in range(batches):
-        xs = [near[batch], far[batch], *there[batch]]
-        xs += [to_core(rows) for rows in xs]
-        xs[0] = after(xs[0], far[-1], ahead, *sent[-1:])
-        mine, *others = ffn(xs, table, weights)
-        wait = there[batch + 1] if batch + 1 < batches else []
+        groups.append([(batch, 1)] + [(batch + 1, 0)] * (batch + 1 < batches))
+    order, wait = joined[1:2], far[1:2] + [x for xs in near_there[1:2] for x in xs]
+    sums, back, arrived = {}, {}, []
+    for group in groups:
+        here = [x for batch, is_far in group for x in ([far[batch]] if is_far else near[batch])]
+        there = [x for batch, is_far in group for x in ([far_there[batch]] if is_far else near_there[batch])]
+        xs = [*here, *there]
+        xs += [to_core(x) for x in xs]
+        mine, *others = ffn([after(xs[0], *order), *xs[1:]], table, weights)
         others = [to_core(after(other, *wait)) for other in others]
         other_here, other_there = others[: SHARES // 2], others[SHARES // 2 :]
         own = [(1, [mine]), (None, [after(other_there[0], *other_here), *other_there[1:]])]
-        if batch + 1 < batches:
-            sent += total(own, [(0, line)])
-            back.append([to_mid(sent[-1])])
-        else:
-            sent += total(own, [(half, line)])
-            back.append([to_mid(total(own, [(0, half)])[0]), to_mid(sent[-1])])
-        terms.append([(0, [mine]), (None, other_here), (None, back[-1])])
-
-    for batch in range(batches):
-        if batch + 1 < batches:
-            terms[batch][-1] = (None, [after(back[batch][0], sent[-1])])
-        far_sum = total(terms[batch], [(half, line)])[0]
-        terms[batch].append((None, [mirror(far_sum, 2)]))
-        span, pieces = 4, half
-        while pieces > 1:
-            part = total(terms[batch], [(pieces // 2, pieces)])[0]
-            terms[batch].append((None, [mirror(part, span)]))
-            span, pieces = span * 2, pieces // 2
+        order, arrived = [], []
+        for i, unit in enumerate(group):
+            cut = (i * half, (i + 1) * half)
+            sent = total(own, [cut])[0]
+            back[unit] = to_mid(sent)
+            order.append(sent)
+            arrived.append(back[unit])
+            sums[unit] = ([(0, [mine]), (None, other_here)], cut[0])
+        batch, is_far = group[-1]
+        wait = [arrived[0], *far_there[batch + 1 : batch + 2]] if not is_far else arrived[:1]
+
+    terms, last = [[] for _ in range(batches)], []
+    for unit in [unit for group in groups for unit in group]:
+        batch, is_far = unit
+        own, first = sums[unit]
+        own = [(slot, arrays, first) for slot, arrays in own] + [(None, [after(back[unit], *last)], 0)]
+        skip = 0 if is_far else 1
+        parts = total(own, [(j, j + 1) for j in range(skip, half)])
+        returned = [
+            along_line(part, lambda p, j=j: owner_of(mirrored(p, 2) if is_far else p, j))
+            for j, part in enumerate(parts, skip)
+        ]
+        if not is_far:
+            terms[batch] += own
+        terms[batch] += [(None, [part], 0) for part in returned]
+        last = returned
     return finish(hidden_in, terms)
 
 

time: 85.2 us -> 93.9 us (1.10)
  waiting for transfers between devices: 26.2 us -> 32.2 us
  starting transfers between devices: 40.7 us -> 42.6 us
    ppermute x8 -> x10, waiting for transfers between devices: 10.5 us -> 14.3 us  [along_line(): lax.ppermute(rows, 'ep', [(i, place_of(i // 4) * 4 + i % 4) for i in rang...]
    ppermute x9 -> x10, waiting for transfers between devices: 11.2 us -> 14.3 us  [to_mid(): return lax.ppermute(rows, 'ep', [(i, i ^ 2) for i in range(owners)])]
    ppermute x18 -> x24, starting transfers between devices: 3.4 us -> 4.58 us  [to_core(): return lax.ppermute(rows, 'ep', [(i, i ^ 1) for i in range(owners)])]
    ppermute x18 -> x24, waiting for transfers between devices: 4.49 us -> 3.6 us  [to_core(): return lax.ppermute(rows, 'ep', [(i, i ^ 1) for i in range(owners)])]
    pallas_call x14 -> x16, Pallas kernels: 18 us -> 18.7 us  [call(): pl.pallas_call(kernel, out_shape=shapes, in_specs=specs, out_specs=[VMEM]...]
    ppermute x9 -> x10, starting transfers between devices: 11.9 us -> 12.6 us  [to_mid(): return lax.ppermute(rows, 'ep', [(i, i ^ 2) for i in range(owners)])]
    ppermute x8 -> x10, starting transfers between devices: 25.4 us -> 25.4 us  [along_line(): lax.ppermute(rows, 'ep', [(i, place_of(i // 4) * 4 + i % 4) for i in rang...]
  transfers between devices with their start and end apart: 35 -> 44, of which waited for: 20 -> 20; matrix products, arithmetic and copies ran while one was open for 0% -> 0% of each run, Pallas kernels for 19% -> 18%
where the time goes in v12:
time: 93.9 us; the launch traced here: 93.7 us
  starting transfers between devices  42.6 us (45%)
  waiting for transfers between devices  32.2 us (34%)
  Pallas kernels  18.7 us (20%)
    ppermute x10, starting transfers between devices, along_line(): lax.ppermute(rows, 'ep', [(i, place_of(i // 4) * 4 + i % 4) for i in rang...  25.4 us
    pallas_call x16, Pallas kernels, call(): pl.pallas_call(kernel, out_shape=shapes, in_specs=specs, out_specs=[VMEM]...  18.7 us
    ppermute x10, waiting for transfers between devices, along_line(): lax.ppermute(rows, 'ep', [(i, place_of(i // 4) * 4 + i % 4) for i in rang...  14.3 us
    ppermute x10, waiting for transfers between devices, to_mid(): return lax.ppermute(rows, 'ep', [(i, i ^ 2) for i in range(owners)])  14.3 us
    ppermute x10, starting transfers between devices, to_mid(): return lax.ppermute(rows, 'ep', [(i, i ^ 2) for i in range(owners)])  12.6 us
    ppermute x24, starting transfers between devices, to_core(): return lax.ppermute(rows, 'ep', [(i, i ^ 1) for i in range(owners)])  4.58 us
    ppermute x24, waiting for transfers between devices, to_core(): return lax.ppermute(rows, 'ep', [(i, i ^ 1) for i in range(owners)])  3.6 us
  transfers between devices with their start and end apart: 44, of which 20 were waited for; matrix products, arithmetic and copies ran while one was open for 0% of the time, Pallas kernels for 18%

profile of v12, /device:TPU:0, one launch (start us, length us, event | category | flops | bytes accessed | tf_op | source)
XLA Modules:
  0.0 93.7 jit_solution(4701022560293573666)
XLA Ops:
  0.0 1.2 %prepare.1 = (bf16[1,32,2176]{2,1,0:T(8,128)(2,1)S(1)}, bf16[1,32,2176]{2,1,0:T(8,128)(2,1)S(1)}) custom-call(bf16[2,32,2048]{2,1,0:T(8,128)(2,1)} %hidden_ref.1, s32[2,8,32]{2,1,0:T(8,128)} %bitcast.7, s32[2,8,32]{2,1,0:T(8,128)} %bitcast.8, f32[1,2048]{1,0:T(1,128)} %bitcast.9), custom_call_target="tpu_custom_call" | custom-call | tf_op jit(solution)/shard_map/prepare/pallas_call | solution.py:27
  1.2 3.0 %collective-permute-start.2 = (bf16[1,32,2176]{2,1,0:T(8,128)(2,1)S(1)}, bf16[1,32,2176]{2,1,0:T(8,128)(2,1)S(1)}, u32[]{:S(2)}, u32[]{:S(2)}) collective-permute-start(bf16[1,32,2176]{2,1,0:T(8,128)(2,1)S(1)} %get-tuple-element.65.refs_0_.refs_1_), channel_id=1, source_target_pairs={{0,2},{1,3},{2,0},{3,1},{4,6},{5,7},{6,4},{7,5},{8,10},{9,11},{10,... | collective-permute-start | bytes 417800 | tf_op jit(solution)/shard_map/ppermute | solution.py:276
  4.3 4.0 %collective-permute-start = (bf16[1,32,2176]{2,1,0:T(8,128)(2,1)S(1)}, bf16[1,32,2176]{2,1,0:T(8,128)(2,1)S(1)}, u32[]{:S(2)}, u32[]{:S(2)}) collective-permute-start(bf16[1,32,2176]{2,1,0:T(8,128)(2,1)S(1)} %get-tuple-element.67.refs_0_), channel_id=1, source_target_pairs={{0,12},{1,13},{2,14},{3,15},{4,8},{5,9},{6,10},{7,11},{8,4},{9,5},... | collective-permute-start | bytes 417800 | tf_op jit(solution)/shard_map/ppermute | solution.py:267
  8.8 2.2 %collective-permute-done.1.refs_2_ = bf16[1,32,2176]{2,1,0:T(8,128)(2,1)S(1)} collective-permute-done((bf16[1,32,2176]{2,1,0:T(8,128)(2,1)S(1)}, bf16[1,32,2176]{2,1,0:T(8,128)(2,1)S(1)}, u32[]{:S(2)}, u32[]{:S(2)}) %collective-permute-start.1) | collective-permute-done | bytes 139296 | tf_op jit(solution)/shard_map/ppermute | solution.py:276
  10.9 0.7 collective-permute-done.refs_1_
  11.6 2.7 %collective-permute-start.4 = (bf16[2,32,2176]{2,1,0:T(8,128)(2,1)S(1)}, bf16[2,32,2176]{2,1,0:T(8,128)(2,1)S(1)}, u32[]{:S(2)}, u32[]{:S(2)}) collective-permute-start(bf16[2,32,2176]{2,1,0:T(8,128)(2,1)S(1)} %join.2), channel_id=1, source_target_pairs={{0,4},{1,5},{2,6},{3,7},{4,0},{5,1},{6,2},{7,3},{8,12},{9,13},{10,... | collective-permute-start | bytes 835592 | tf_op jit(solution)/shard_map/ppermute | solution.py:267
  14.3 2.7 %collective-permute-start.3 = (bf16[1,32,2176]{2,1,0:T(8,128)(2,1)S(1)}, bf16[1,32,2176]{2,1,0:T(8,128)(2,1)S(1)}, u32[]{:S(2)}, u32[]{:S(2)}) collective-permute-start(bf16[1,32,2176]{2,1,0:T(8,128)(2,1)S(1)} %get-tuple-element.65.refs_0_.refs_1_), channel_id=1, source_target_pairs={{0,12},{1,13},{2,14},{3,15},{4,8},{5,9},{6,10},{7,11},{8,4},{9,5},... | collective-permute-start | bytes 417800 | tf_op jit(solution)/shard_map/ppermute | solution.py:267
  17.0 1.5 %collective-permute-start.5 = (bf16[1,32,2176]{2,1,0:T(8,128)(2,1)S(1)}, bf16[1,32,2176]{2,1,0:T(8,128)(2,1)S(1)}, u32[]{:S(2)}, u32[]{:S(2)}) collective-permute-start(bf16[1,32,2176]{2,1,0:T(8,128)(2,1)S(1)} %collective-permute-done.refs_1_), channel_id=1, source_target_pairs={{0,2},{1,3},{2,0},{3,1},{4,6},{5,7},{6,4},{7,5},{8,10},{9,11},{10,... | collective-permute-start | bytes 417800 | tf_op jit(solution)/shard_map/ppermute | solution.py:276
  18.5 3.8 %load.1 = (bf16[1,2048,768]{2,1,0:T(8,128)(2,1)S(1)}, bf16[1,2048,768]{2,1,0:T(8,128)(2,1)S(1)}, bf16[1,768,2048]{2,1,0:T(8,128)(2,1)S(1)}) custom-call(bf16[1,2048,768]{2,1,0:T(8,128)(2,1)} %refs_0_, bf16[1,2048,768]{2,1,0:T(8,128)(2,1)} %refs_1_, bf16[1,768,2048]{2,1,0:T(8,128)(2,1)} %refs_2_), custom_call_target="tpu_custom_call" | custom-call | tf_op jit(solution)/shard_map/load/pallas_call | solution.py:27
  22.6 1.2 %collective-permute-done.3.refs_1_.refs_2_ = bf16[1,32,2176]{2,1,0:T(8,128)(2,1)S(1)} collective-permute-done((bf16[1,32,2176]{2,1,0:T(8,128)(2,1)S(1)}, bf16[1,32,2176]{2,1,0:T(8,128)(2,1)S(1)}, u32[]{:S(2)}, u32[]{:S(2)}) %collective-permute-start.3) | collective-permute-done | bytes 139296 | tf_op jit(solution)/shard_map/ppermute | solution.py:267
  24.0 1.6 %collective-permute-start.18 = (bf16[2,32,2176]{2,1,0:T(8,128)(2,1)S(1)}, bf16[2,32,2176]{2,1,0:T(8,128)(2,1)S(1)}, u32[]{:S(2)}, u32[]{:S(2)}) collective-permute-start(bf16[2,32,2176]{2,1,0:T(8,128)(2,1)S(1)} %collective-permute-done.4.refs_0_), channel_id=1, source_target_pairs={{0,2},{1,3},{2,0},{3,1},{4,6},{5,7},{6,4},{7,5},{8,10},{9,11},{10,... | collective-permute-start | bytes 835592 | tf_op jit(solution)/shard_map/ppermute | solution.py:276
  26.9 3.2 %ffn.3 = (bf16[2,2,32,2048]{3,2,1,0:T(8,128)(2,1)S(1)}, bf16[1,32,2048]{2,1,0:T(8,128)(2,1)S(1)}, bf16[1,32,2048]{2,1,0:T(8,128)(2,1)S(1)}, bf16[1,32,2048]{2,1,0:T(8,128)(2,1)S(1)}, bf16[1,32,2048]{2,1,0:T(8,128)(2,1)S(1)}) custom-call(s32[3,1,6]{2,1,0:T(1,128)S(1)} %bitcast.4, bf16[1,2048,768]{2,1,0:T(8,128)(2,1)S(1)} %get-tuple-element.62.gate_ref, ...), custom_call_target="tpu_custom_call" | custom-call | tf_op jit(solution)/shard_map/ffn/pallas_call | solution.py:27
  30.2 5.9 %collective-permute-done.11.refs_5_ = bf16[1,32,2176]{2,1,0:T(8,128)(2,1)S(1)} collective-permute-done((bf16[1,32,2176]{2,1,0:T(8,128)(2,1)S(1)}, bf16[1,32,2176]{2,1,0:T(8,128)(2,1)S(1)}, u32[]{:S(2)}, u32[]{:S(2)}) %collective-permute-start.11) | collective-permute-done | bytes 139296 | tf_op jit(solution)/shard_map/ppermute | solution.py:276
  38.1 1.5 %collective-permute-start.25 = (bf16[2,32,2176]{2,1,0:T(8,128)(2,1)S(1)}, bf16[2,32,2176]{2,1,0:T(8,128)(2,1)S(1)}, u32[]{:S(2)}, u32[]{:S(2)}) collective-permute-start(bf16[2,32,2176]{2,1,0:T(8,128)(2,1)S(1)} %collective-permute-done.10.refs_0_), channel_id=1, source_target_pairs={{0,2},{1,3},{2,0},{3,1},{4,6},{5,7},{6,4},{7,5},{8,10},{9,11},{10,... | collective-permute-start | bytes 835592 | tf_op jit(solution)/shard_map/ppermute | solution.py:276
  40.3 1.4 %collective-permute-done.24.refs_11_ = bf16[1,32,2176]{2,1,0:T(8,128)(2,1)S(1)} collective-permute-done((bf16[1,32,2176]{2,1,0:T(8,128)(2,1)S(1)}, bf16[1,32,2176]{2,1,0:T(8,128)(2,1)S(1)}, u32[]{:S(2)}, u32[]{:S(2)}) %collective-permute-start.24) | collective-permute-done | bytes 139296 | tf_op jit(solution)/shard_map/ppermute | solution.py:279
  41.6 5.7 %ffn.4 = (bf16[2,4,32,2048]{3,2,1,0:T(8,128)(2,1)S(1)}, bf16[2,32,2048]{2,1,0:T(8,128)(2,1)S(1)}, bf16[2,32,2048]{2,1,0:T(8,128)(2,1)S(1)}, bf16[2,32,2048]{2,1,0:T(8,128)(2,1)S(1)}, bf16[2,32,2048]{2,1,0:T(8,128)(2,1)S(1)}) custom-call(s32[3,1,6]{2,1,0:T(1,128)S(1)} %bitcast.5, bf16[1,2048,768]{2,1,0:T(8,128)(2,1)S(1)} %get-tuple-element.62.gate_ref, ...), custom_call_target="tpu_custom_call" | custom-call | tf_op jit(solution)/shard_map/ffn/pallas_call | solution.py:27
  47.6 5.0 %collective-permute-done.16.refs_2_ = bf16[2,32,2048]{2,1,0:T(8,128)(2,1)S(1)} collective-permute-done((bf16[2,32,2048]{2,1,0:T(8,128)(2,1)S(1)}, bf16[2,32,2048]{2,1,0:T(8,128)(2,1)S(1)}, u32[]{:S(2)}, u32[]{:S(2)}) %collective-permute-start.16) | collective-permute-done | bytes 262176 | tf_op jit(solution)/shard_map/ppermute | solution.py:276
  54.9 1.6 %collective-permute-start.29 = (bf16[2,32,2048]{2,1,0:T(8,128)(2,1)S(1)}, bf16[2,32,2048]{2,1,0:T(8,128)(2,1)S(1)}, u32[]{:S(2)}, u32[]{:S(2)}) collective-permute-start(bf16[2,32,2048]{2,1,0:T(8,128)(2,1)S(1)} %total.10), channel_id=1, source_target_pairs={{0,2},{1,3},{2,0},{3,1},{4,6},{5,7},{6,4},{7,5},{8,10},{9,11},{10,... | collective-permute-start | bytes 786440 | tf_op jit(solution)/shard_map/ppermute | solution.py:276
  56.6 3.1 %collective-permute-start.17 = (bf16[1,32,2048]{2,1,0:T(8,128)(2,1)S(1)}, bf16[1,32,2048]{2,1,0:T(8,128)(2,1)S(1)}, u32[]{:S(2)}, u32[]{:S(2)}) collective-permute-start(bf16[1,32,2048]{2,1,0:T(8,128)(2,1)S(1)} %total.9), channel_id=1, source_target_pairs={{0,12},{1,13},{2,14},{3,15},{4,8},{5,9},{6,10},{7,11},{8,4},{9,5},... | collective-permute-start | bytes 393224 | tf_op jit(solution)/shard_map/ppermute | solution.py:267
  60.2 3.2 %ffn.5 = (bf16[2,2,32,2048]{3,2,1,0:T(8,128)(2,1)S(1)}, bf16[1,32,2048]{2,1,0:T(8,128)(2,1)S(1)}, bf16[1,32,2048]{2,1,0:T(8,128)(2,1)S(1)}, bf16[1,32,2048]{2,1,0:T(8,128)(2,1)S(1)}, bf16[1,32,2048]{2,1,0:T(8,128)(2,1)S(1)}) custom-call(s32[3,1,6]{2,1,0:T(1,128)S(1)} %bitcast.6, bf16[1,2048,768]{2,1,0:T(8,128)(2,1)S(1)} %get-tuple-element.62.gate_ref, ...), custom_call_target="tpu_custom_call" | custom-call | tf_op jit(solution)/shard_map/ffn/pallas_call | solution.py:27
  63.5 0.7 collective-permute-done.29.refs_2_
  65.5 1.9 %collective-permute-start.30 = (bf16[1,32,2048]{2,1,0:T(8,128)(2,1)S(1)}, bf16[1,32,2048]{2,1,0:T(8,128)(2,1)S(1)}, u32[]{:S(2)}, u32[]{:S(2)}) collective-permute-start(bf16[1,32,2048]{2,1,0:T(8,128)(2,1)S(1)} %get-tuple-element.88), channel_id=1, source_target_pairs={{0,4},{1,5},{2,6},{3,7},{4,0},{5,1},{6,2},{7,3},{8,12},{9,13},{10,... | collective-permute-start | bytes 393224 | tf_op jit(solution)/shard_map/ppermute | solution.py:267
  67.4 1.7 %collective-permute-start.31 = (bf16[1,32,2048]{2,1,0:T(8,128)(2,1)S(1)}, bf16[1,32,2048]{2,1,0:T(8,128)(2,1)S(1)}, u32[]{:S(2)}, u32[]{:S(2)}) collective-permute-start(bf16[1,32,2048]{2,1,0:T(8,128)(2,1)S(1)} %get-tuple-element.89), channel_id=1, source_target_pairs={{0,8},{1,9},{2,10},{3,11},{4,12},{5,13},{6,14},{7,15},{8,0},{9,1},... | collective-permute-start | bytes 393224 | tf_op jit(solution)/shard_map/ppermute | solution.py:267
  69.2 1.6 %collective-permute-start.41 = (bf16[2,32,2048]{2,1,0:T(8,128)(2,1)S(1)}, bf16[2,32,2048]{2,1,0:T(8,128)(2,1)S(1)}, u32[]{:S(2)}, u32[]{:S(2)}) collective-permute-start(bf16[2,32,2048]{2,1,0:T(8,128)(2,1)S(1)} %total.14), channel_id=1, source_target_pairs={{0,2},{1,3},{2,0},{3,1},{4,6},{5,7},{6,4},{7,5},{8,10},{9,11},{10,... | collective-permute-start | bytes 786440 | tf_op jit(solution)/shard_map/ppermute | solution.py:276
  70.8 3.1 %collective-permute-done.30.refs_4_ = bf16[1,32,2048]{2,1,0:T(8,128)(2,1)S(1)} collective-permute-done((bf16[1,32,2048]{2,1,0:T(8,128)(2,1)S(1)}, bf16[1,32,2048]{2,1,0:T(8,128)(2,1)S(1)}, u32[]{:S(2)}, u32[]{:S(2)}) %collective-permute-start.30) | collective-permute-done | bytes 131104 | tf_op jit(solution)/shard_map/ppermute | solution.py:267
  74.5 5.0 %collective-permute-start.34 = (bf16[1,32,2048]{2,1,0:T(8,128)(2,1)S(1)}, bf16[1,32,2048]{2,1,0:T(8,128)(2,1)S(1)}, u32[]{:S(2)}, u32[]{:S(2)}) collective-permute-start(bf16[1,32,2048]{2,1,0:T(8,128)(2,1)S(1)} %total.13), channel_id=1, source_target_pairs={{0,12},{1,13},{2,14},{3,15},{4,8},{5,9},{6,10},{7,11},{8,4},{9,5},... | collective-permute-start | bytes 393224 | tf_op jit(solution)/shard_map/ppermute | solution.py:267
  79.5 3.1 %collective-permute-done.34.refs_9_ = bf16[1,32,2048]{2,1,0:T(8,128)(2,1)S(1)} collective-permute-done((bf16[1,32,2048]{2,1,0:T(8,128)(2,1)S(1)}, bf16[1,32,2048]{2,1,0:T(8,128)(2,1)S(1)}, u32[]{:S(2)}, u32[]{:S(2)}) %collective-permute-start.34) | collective-permute-done | bytes 131104 | tf_op jit(solution)/shard_map/ppermute | solution.py:267
  82.7 2.4 %collective-permute-start.42 = (bf16[1,32,2048]{2,1,0:T(8,128)(2,1)S(1)}, bf16[1,32,2048]{2,1,0:T(8,128)(2,1)S(1)}, u32[]{:S(2)}, u32[]{:S(2)}) collective-permute-start(bf16[1,32,2048]{2,1,0:T(8,128)(2,1)S(1)} %get-tuple-element.105), channel_id=1, source_target_pairs={{0,4},{1,5},{2,6},{3,7},{4,0},{5,1},{6,2},{7,3},{8,12},{9,13},{10,... | collective-permute-start | bytes 393224 | tf_op jit(solution)/shard_map/ppermute | solution.py:267
  85.1 1.9 %collective-permute-start.43 = (bf16[1,32,2048]{2,1,0:T(8,128)(2,1)S(1)}, bf16[1,32,2048]{2,1,0:T(8,128)(2,1)S(1)}, u32[]{:S(2)}, u32[]{:S(2)}) collective-permute-start(bf16[1,32,2048]{2,1,0:T(8,128)(2,1)S(1)} %get-tuple-element.106), channel_id=1, source_target_pairs={{0,8},{1,9},{2,10},{3,11},{4,12},{5,13},{6,14},{7,15},{8,0},{9,1},... | collective-permute-start | bytes 393224 | tf_op jit(solution)/shard_map/ppermute | solution.py:267
  87.0 1.5 %collective-permute-done.42.refs_10_ = bf16[1,32,2048]{2,1,0:T(8,128)(2,1)S(1)} collective-permute-done((bf16[1,32,2048]{2,1,0:T(8,128)(2,1)S(1)}, bf16[1,32,2048]{2,1,0:T(8,128)(2,1)S(1)}, u32[]{:S(2)}, u32[]{:S(2)}) %collective-permute-start.42) | collective-permute-done | bytes 131104 | tf_op jit(solution)/shard_map/ppermute | solution.py:267
  88.5 4.3 %collective-permute-done.43.refs_11_ = bf16[1,32,2048]{2,1,0:T(8,128)(2,1)S(1)} collective-permute-done((bf16[1,32,2048]{2,1,0:T(8,128)(2,1)S(1)}, bf16[1,32,2048]{2,1,0:T(8,128)(2,1)S(1)}, u32[]{:S(2)}, u32[]{:S(2)}) %collective-permute-start.43) | collective-permute-done | bytes 131104 | tf_op jit(solution)/shard_map/ppermute | solution.py:267
  92.8 0.9 finish.1
  (76 shorter events, 10.3 us)
Async XLA Ops:
  1.2 7.5 %collective-permute-start.2 = (bf16[1,32,2176]{2,1,0:T(8,128)(2,1)S(1)}, bf16[1,32,2176]{2,1,0:T(8,128)(2,1)S(1)}, u32[]{:S(2)}, u32[]{:S(2)}) collective-permute-start(bf16[1,32,2176]{2,1,0:T(8,128)(2,1)S(1)} %get-tuple-element.65.refs_0_.refs_1_), channel_id=1, source_target_pairs={{0,2},{1,3},{2,0},{3,1},{4,6},{5,7},{6,4},{7,5},{8,10},{9,11},{10,... | collective-permute-start | bytes 417800 | tf_op jit(solution)/shard_map/ppermute | solution.py:276
  4.3 6.7 %collective-permute-start.1 = (bf16[1,32,2176]{2,1,0:T(8,128)(2,1)S(1)}, bf16[1,32,2176]{2,1,0:T(8,128)(2,1)S(1)}, u32[]{:S(2)}, u32[]{:S(2)}) collective-permute-start(bf16[1,32,2176]{2,1,0:T(8,128)(2,1)S(1)} %get-tuple-element.67.refs_0_), channel_id=1, source_target_pairs={{0,2},{1,3},{2,0},{3,1},{4,6},{5,7},{6,4},{7,5},{8,10},{9,11},{10,... | collective-permute-start | bytes 417800 | tf_op jit(solution)/shard_map/ppermute | solution.py:276
  4.3 7.2 %collective-permute-start = (bf16[1,32,2176]{2,1,0:T(8,128)(2,1)S(1)}, bf16[1,32,2176]{2,1,0:T(8,128)(2,1)S(1)}, u32[]{:S(2)}, u32[]{:S(2)}) collective-permute-start(bf16[1,32,2176]{2,1,0:T(8,128)(2,1)S(1)} %get-tuple-element.67.refs_0_), channel_id=1, source_target_pairs={{0,12},{1,13},{2,14},{3,15},{4,8},{5,9},{6,10},{7,11},{8,4},{9,5},... | collective-permute-start | bytes 417800 | tf_op jit(solution)/shard_map/ppermute | solution.py:267
  11.6 12.2 %collective-permute-start.4 = (bf16[2,32,2176]{2,1,0:T(8,128)(2,1)S(1)}, bf16[2,32,2176]{2,1,0:T(8,128)(2,1)S(1)}, u32[]{:S(2)}, u32[]{:S(2)}) collective-permute-start(bf16[2,32,2176]{2,1,0:T(8,128)(2,1)S(1)} %join.2), channel_id=1, source_target_pairs={{0,4},{1,5},{2,6},{3,7},{4,0},{5,1},{6,2},{7,3},{8,12},{9,13},{10,... | collective-permute-start | bytes 835592 | tf_op jit(solution)/shard_map/ppermute | solution.py:267
  14.3 9.5 %collective-permute-start.3 = (bf16[1,32,2176]{2,1,0:T(8,128)(2,1)S(1)}, bf16[1,32,2176]{2,1,0:T(8,128)(2,1)S(1)}, u32[]{:S(2)}, u32[]{:S(2)}) collective-permute-start(bf16[1,32,2176]{2,1,0:T(8,128)(2,1)S(1)} %get-tuple-element.65.refs_0_.refs_1_), channel_id=1, source_target_pairs={{0,12},{1,13},{2,14},{3,15},{4,8},{5,9},{6,10},{7,11},{8,4},{9,5},... | collective-permute-start | bytes 417800 | tf_op jit(solution)/shard_map/ppermute | solution.py:267
  17.0 7.0 %collective-permute-start.6 = (bf16[1,32,2176]{2,1,0:T(8,128)(2,1)S(1)}, bf16[1,32,2176]{2,1,0:T(8,128)(2,1)S(1)}, u32[]{:S(2)}, u32[]{:S(2)}) collective-permute-start(bf16[1,32,2176]{2,1,0:T(8,128)(2,1)S(1)} %get-tuple-element.67.refs_0_), channel_id=1, source_target_pairs={{0,1},{1,0},{2,3},{3,2},{4,5},{5,4},{6,7},{7,6},{8,9},{9,8},{10,11... | collective-permute-start | bytes 417800 | tf_op jit(solution)/shard_map/ppermute | solution.py:279
  17.0 8.6 %collective-permute-start.5 = (bf16[1,32,2176]{2,1,0:T(8,128)(2,1)S(1)}, bf16[1,32,2176]{2,1,0:T(8,128)(2,1)S(1)}, u32[]{:S(2)}, u32[]{:S(2)}) collective-permute-start(bf16[1,32,2176]{2,1,0:T(8,128)(2,1)S(1)} %collective-permute-done.refs_1_), channel_id=1, source_target_pairs={{0,2},{1,3},{2,0},{3,1},{4,6},{5,7},{6,4},{7,5},{8,10},{9,11},{10,... | collective-permute-start | bytes 417800 | tf_op jit(solution)/shard_map/ppermute | solution.py:276
  22.3 3.5 %collective-permute-start.8 = (bf16[1,32,2176]{2,1,0:T(8,128)(2,1)S(1)}, bf16[1,32,2176]{2,1,0:T(8,128)(2,1)S(1)}, u32[]{:S(2)}, u32[]{:S(2)}) collective-permute-start(bf16[1,32,2176]{2,1,0:T(8,128)(2,1)S(1)} %collective-permute-done.1.refs_2_), channel_id=1, source_target_pairs={{0,1},{1,0},{2,3},{3,2},{4,5},{5,4},{6,7},{7,6},{8,9},{9,8},{10,11... | collective-permute-start | bytes 417800 | tf_op jit(solution)/shard_map/ppermute | solution.py:279
  23.8 12.2 %collective-permute-start.10 = (bf16[2,32,2176]{2,1,0:T(8,128)(2,1)S(1)}, bf16[2,32,2176]{2,1,0:T(8,128)(2,1)S(1)}, u32[]{:S(2)}, u32[]{:S(2)}) collective-permute-start(bf16[2,32,2176]{2,1,0:T(8,128)(2,1)S(1)} %join.3), channel_id=1, source_target_pairs={{0,4},{1,5},{2,6},{3,7},{4,0},{5,1},{6,2},{7,3},{8,12},{9,13},{10,... | collective-permute-start | bytes 835592 | tf_op jit(solution)/shard_map/ppermute | solution.py:267
  24.0 13.1 %collective-permute-start.18 = (bf16[2,32,2176]{2,1,0:T(8,128)(2,1)S(1)}, bf16[2,32,2176]{2,1,0:T(8,128)(2,1)S(1)}, u32[]{:S(2)}, u32[]{:S(2)}) collective-permute-start(bf16[2,32,2176]{2,1,0:T(8,128)(2,1)S(1)} %collective-permute-done.4.refs_0_), channel_id=1, source_target_pairs={{0,2},{1,3},{2,0},{3,1},{4,6},{5,7},{6,4},{7,5},{8,10},{9,11},{10,... | collective-permute-start | bytes 835592 | tf_op jit(solution)/shard_map/ppermute | solution.py:276
  25.7 10.3 %collective-permute-start.11 = (bf16[1,32,2176]{2,1,0:T(8,128)(2,1)S(1)}, bf16[1,32,2176]{2,1,0:T(8,128)(2,1)S(1)}, u32[]{:S(2)}, u32[]{:S(2)}) collective-permute-start(bf16[1,32,2176]{2,1,0:T(8,128)(2,1)S(1)} %collective-permute-done.3.refs_1_.refs_2_), channel_id=1, source_target_pairs={{0,2},{1,3},{2,0},{3,1},{4,6},{5,7},{6,4},{7,5},{8,10},{9,11},{10,... | collective-permute-start | bytes 417800 | tf_op jit(solution)/shard_map/ppermute | solution.py:276
  26.2 10.3 %collective-permute-start.23 = (bf16[1,32,2176]{2,1,0:T(8,128)(2,1)S(1)}, bf16[1,32,2176]{2,1,0:T(8,128)(2,1)S(1)}, u32[]{:S(2)}, u32[]{:S(2)}) collective-permute-start(bf16[1,32,2176]{2,1,0:T(8,128)(2,1)S(1)} %collective-permute-done.2.refs_4_), channel_id=1, source_target_pairs={{0,1},{1,0},{2,3},{3,2},{4,5},{5,4},{6,7},{7,6},{8,9},{9,8},{10,11... | collective-permute-start | bytes 417800 | tf_op jit(solution)/shard_map/ppermute | solution.py:279
  37.4 2.9 %collective-permute-start.21 = (bf16[1,32,2176]{2,1,0:T(8,128)(2,1)S(1)}, bf16[1,32,2176]{2,1,0:T(8,128)(2,1)S(1)}, u32[]{:S(2)}, u32[]{:S(2)}) collective-permute-start(bf16[1,32,2176]{2,1,0:T(8,128)(2,1)S(1)} %collective-permute-done.3.refs_1_.refs_2_), channel_id=1, source_target_pairs={{0,1},{1,0},{2,3},{3,2},{4,5},{5,4},{6,7},{7,6},{8,9},{9,8},{10,11... | collective-permute-start | bytes 417800 | tf_op jit(solution)/shard_map/ppermute | solution.py:279
  37.6 2.7 %collective-permute-start.19 = (bf16[2,32,2176]{2,1,0:T(8,128)(2,1)S(1)}, bf16[2,32,2176]{2,1,0:T(8,128)(2,1)S(1)}, u32[]{:S(2)}, u32[]{:S(2)}) collective-permute-start(bf16[2,32,2176]{2,1,0:T(8,128)(2,1)S(1)} %collective-permute-done.4.refs_0_), channel_id=1, source_target_pairs={{0,1},{1,0},{2,3},{3,2},{4,5},{5,4},{6,7},{7,6},{8,9},{9,8},{10,11... | collective-permute-start | bytes 835592 | tf_op jit(solution)/shard_map/ppermute | solution.py:279
  37.9 3.7 %collective-permute-start.22 = (bf16[2,32,2176]{2,1,0:T(8,128)(2,1)S(1)}, bf16[2,32,2176]{2,1,0:T(8,128)(2,1)S(1)}, u32[]{:S(2)}, u32[]{:S(2)}) collective-permute-start(bf16[2,32,2176]{2,1,0:T(8,128)(2,1)S(1)} %collective-permute-done.18.refs_3_), channel_id=1, source_target_pairs={{0,1},{1,0},{2,3},{3,2},{4,5},{5,4},{6,7},{7,6},{8,9},{9,8},{10,11... | collective-permute-start | bytes 835592 | tf_op jit(solution)/shard_map/ppermute | solution.py:279
  38.1 9.5 %collective-permute-start.25 = (bf16[2,32,2176]{2,1,0:T(8,128)(2,1)S(1)}, bf16[2,32,2176]{2,1,0:T(8,128)(2,1)S(1)}, u32[]{:S(2)}, u32[]{:S(2)}) collective-permute-start(bf16[2,32,2176]{2,1,0:T(8,128)(2,1)S(1)} %collective-permute-done.10.refs_0_), channel_id=1, source_target_pairs={{0,2},{1,3},{2,0},{3,1},{4,6},{5,7},{6,4},{7,5},{8,10},{9,11},{10,... | collective-permute-start | bytes 835592 | tf_op jit(solution)/shard_map/ppermute | solution.py:276
  39.7 12.9 %collective-permute-start.16 = (bf16[2,32,2048]{2,1,0:T(8,128)(2,1)S(1)}, bf16[2,32,2048]{2,1,0:T(8,128)(2,1)S(1)}, u32[]{:S(2)}, u32[]{:S(2)}) collective-permute-start(bf16[2,32,2048]{2,1,0:T(8,128)(2,1)S(1)} %total.8), channel_id=1, source_target_pairs={{0,2},{1,3},{2,0},{3,1},{4,6},{5,7},{6,4},{7,5},{8,10},{9,11},{10,... | collective-permute-start | bytes 786440 | tf_op jit(solution)/shard_map/ppermute | solution.py:276
  53.1 7.1 %collective-permute-start.35 = (bf16[2,32,2176]{2,1,0:T(8,128)(2,1)S(1)}, bf16[2,32,2176]{2,1,0:T(8,128)(2,1)S(1)}, u32[]{:S(2)}, u32[]{:S(2)}) collective-permute-start(bf16[2,32,2176]{2,1,0:T(8,128)(2,1)S(1)} %collective-permute-done.10.refs_0_), channel_id=1, source_target_pairs={{0,1},{1,0},{2,3},{3,2},{4,5},{5,4},{6,7},{7,6},{8,9},{9,8},{10,11... | collective-permute-start | bytes 835592 | tf_op jit(solution)/shard_map/ppermute | solution.py:279
  53.6 6.6 %collective-permute-start.36 = (bf16[2,32,2176]{2,1,0:T(8,128)(2,1)S(1)}, bf16[2,32,2176]{2,1,0:T(8,128)(2,1)S(1)}, u32[]{:S(2)}, u32[]{:S(2)}) collective-permute-start(bf16[2,32,2176]{2,1,0:T(8,128)(2,1)S(1)} %collective-permute-done.25.refs_1_), channel_id=1, source_target_pairs={{0,1},{1,0},{2,3},{3,2},{4,5},{5,4},{6,7},{7,6},{8,9},{9,8},{10,11... | collective-permute-start | bytes 835592 | tf_op jit(solution)/shard_map/ppermute | solution.py:279
  54.1 5.5 %collective-permute-start.32 = (bf16[2,32,2048]{2,1,0:T(8,128)(2,1)S(1)}, bf16[2,32,2048]{2,1,0:T(8,128)(2,1)S(1)}, u32[]{:S(2)}, u32[]{:S(2)}) collective-permute-start(bf16[2,32,2048]{2,1,0:T(8,128)(2,1)S(1)} %get-tuple-element.91), channel_id=1, source_target_pairs={{0,1},{1,0},{2,3},{3,2},{4,5},{5,4},{6,7},{7,6},{8,9},{9,8},{10,11... | collective-permute-start | bytes 786440 | tf_op jit(solution)/shard_map/ppermute | solution.py:279
  54.9 9.2 %collective-permute-start.29 = (bf16[2,32,2048]{2,1,0:T(8,128)(2,1)S(1)}, bf16[2,32,2048]{2,1,0:T(8,128)(2,1)S(1)}, u32[]{:S(2)}, u32[]{:S(2)}) collective-permute-start(bf16[2,32,2048]{2,1,0:T(8,128)(2,1)S(1)} %total.10), channel_id=1, source_target_pairs={{0,2},{1,3},{2,0},{3,1},{4,6},{5,7},{6,4},{7,5},{8,10},{9,11},{10,... | collective-permute-start | bytes 786440 | tf_op jit(solution)/shard_map/ppermute | solution.py:276
  56.6 8.1 %collective-permute-start.17 = (bf16[1,32,2048]{2,1,0:T(8,128)(2,1)S(1)}, bf16[1,32,2048]{2,1,0:T(8,128)(2,1)S(1)}, u32[]{:S(2)}, u32[]{:S(2)}) collective-permute-start(bf16[1,32,2048]{2,1,0:T(8,128)(2,1)S(1)} %total.9), channel_id=1, source_target_pairs={{0,12},{1,13},{2,14},{3,15},{4,8},{5,9},{6,10},{7,11},{8,4},{9,5},... | collective-permute-start | bytes 393224 | tf_op jit(solution)/shard_map/ppermute | solution.py:267
  59.7 11.1 %collective-permute-start.33 = (bf16[2,32,2048]{2,1,0:T(8,128)(2,1)S(1)}, bf16[2,32,2048]{2,1,0:T(8,128)(2,1)S(1)}, u32[]{:S(2)}, u32[]{:S(2)}) collective-permute-start(bf16[2,32,2048]{2,1,0:T(8,128)(2,1)S(1)} %total.12), channel_id=1, source_target_pairs={{0,2},{1,3},{2,0},{3,1},{4,6},{5,7},{6,4},{7,5},{8,10},{9,11},{10,... | collective-permute-start | bytes 786440 | tf_op jit(solution)/shard_map/ppermute | solution.py:276
  64.2 3.3 %collective-permute-start.38 = (bf16[1,32,2048]{2,1,0:T(8,128)(2,1)S(1)}, bf16[1,32,2048]{2,1,0:T(8,128)(2,1)S(1)}, u32[]{:S(2)}, u32[]{:S(2)}) collective-permute-start(bf16[1,32,2048]{2,1,0:T(8,128)(2,1)S(1)} %get-tuple-element.98), channel_id=1, source_target_pairs={{0,1},{1,0},{2,3},{3,2},{4,5},{5,4},{6,7},{7,6},{8,9},{9,8},{10,11... | collective-permute-start | bytes 393224 | tf_op jit(solution)/shard_map/ppermute | solution.py:279
  64.7 4.4 %collective-permute-start.37 = (bf16[1,32,2048]{2,1,0:T(8,128)(2,1)S(1)}, bf16[1,32,2048]{2,1,0:T(8,128)(2,1)S(1)}, u32[]{:S(2)}, u32[]{:S(2)}) collective-permute-start(bf16[1,32,2048]{2,1,0:T(8,128)(2,1)S(1)} %get-tuple-element.96), channel_id=1, source_target_pairs={{0,1},{1,0},{2,3},{3,2},{4,5},{5,4},{6,7},{7,6},{8,9},{9,8},{10,11... | collective-permute-start | bytes 393224 | tf_op jit(solution)/shard_map/ppermute | solution.py:279
  64.7 4.4 %collective-permute-start.40 = (bf16[1,32,2048]{2,1,0:T(8,128)(2,1)S(1)}, bf16[1,32,2048]{2,1,0:T(8,128)(2,1)S(1)}, u32[]{:S(2)}, u32[]{:S(2)}) collective-permute-start(bf16[1,32,2048]{2,1,0:T(8,128)(2,1)S(1)} %get-tuple-element.103), channel_id=1, source_target_pairs={{0,1},{1,0},{2,3},{3,2},{4,5},{5,4},{6,7},{7,6},{8,9},{9,8},{10,11... | collective-permute-start | bytes 393224 | tf_op jit(solution)/shard_map/ppermute | solution.py:279
  65.5 8.4 %collective-permute-start.30 = (bf16[1,32,2048]{2,1,0:T(8,128)(2,1)S(1)}, bf16[1,32,2048]{2,1,0:T(8,128)(2,1)S(1)}, u32[]{:S(2)}, u32[]{:S(2)}) collective-permute-start(bf16[1,32,2048]{2,1,0:T(8,128)(2,1)S(1)} %get-tuple-element.88), channel_id=1, source_target_pairs={{0,4},{1,5},{2,6},{3,7},{4,0},{5,1},{6,2},{7,3},{8,12},{9,13},{10,... | collective-permute-start | bytes 393224 | tf_op jit(solution)/shard_map/ppermute | solution.py:267
  67.4 7.0 %collective-permute-start.31 = (bf16[1,32,2048]{2,1,0:T(8,128)(2,1)S(1)}, bf16[1,32,2048]{2,1,0:T(8,128)(2,1)S(1)}, u32[]{:S(2)}, u32[]{:S(2)}) collective-permute-start(bf16[1,32,2048]{2,1,0:T(8,128)(2,1)S(1)} %get-tuple-element.89), channel_id=1, source_target_pairs={{0,8},{1,9},{2,10},{3,11},{4,12},{5,13},{6,14},{7,15},{8,0},{9,1},... | collective-permute-start | bytes 393224 | tf_op jit(solution)/shard_map/ppermute | solution.py:267
  69.2 13.4 %collective-permute-start.41 = (bf16[2,32,2048]{2,1,0:T(8,128)(2,1)S(1)}, bf16[2,32,2048]{2,1,0:T(8,128)(2,1)S(1)}, u32[]{:S(2)}, u32[]{:S(2)}) collective-permute-start(bf16[2,32,2048]{2,1,0:T(8,128)(2,1)S(1)} %total.14), channel_id=1, source_target_pairs={{0,2},{1,3},{2,0},{3,1},{4,6},{5,7},{6,4},{7,5},{8,10},{9,11},{10,... | collective-permute-start | bytes 786440 | tf_op jit(solution)/shard_map/ppermute | solution.py:276
  74.5 8.1 %collective-permute-start.34 = (bf16[1,32,2048]{2,1,0:T(8,128)(2,1)S(1)}, bf16[1,32,2048]{2,1,0:T(8,128)(2,1)S(1)}, u32[]{:S(2)}, u32[]{:S(2)}) collective-permute-start(bf16[1,32,2048]{2,1,0:T(8,128)(2,1)S(1)} %total.13), channel_id=1, source_target_pairs={{0,12},{1,13},{2,14},{3,15},{4,8},{5,9},{6,10},{7,11},{8,4},{9,5},... | collective-permute-start | bytes 393224 | tf_op jit(solution)/shard_map/ppermute | solution.py:267
  82.7 5.8 %collective-permute-start.42 = (bf16[1,32,2048]{2,1,0:T(8,128)(2,1)S(1)}, bf16[1,32,2048]{2,1,0:T(8,128)(2,1)S(1)}, u32[]{:S(2)}, u32[]{:S(2)}) collective-permute-start(bf16[1,32,2048]{2,1,0:T(8,128)(2,1)S(1)} %get-tuple-element.105), channel_id=1, source_target_pairs={{0,4},{1,5},{2,6},{3,7},{4,0},{5,1},{6,2},{7,3},{8,12},{9,13},{10,... | collective-permute-start | bytes 393224 | tf_op jit(solution)/shard_map/ppermute | solution.py:267
  85.1 7.7 %collective-permute-start.43 = (bf16[1,32,2048]{2,1,0:T(8,128)(2,1)S(1)}, bf16[1,32,2048]{2,1,0:T(8,128)(2,1)S(1)}, u32[]{:S(2)}, u32[]{:S(2)}) collective-permute-start(bf16[1,32,2048]{2,1,0:T(8,128)(2,1)S(1)} %get-tuple-element.106), channel_id=1, source_target_pairs={{0,8},{1,9},{2,10},{3,11},{4,12},{5,13},{6,14},{7,15},{8,0},{9,1},... | collective-permute-start | bytes 393224 | tf_op jit(solution)/shard_map/ppermute | solution.py:267
  (14 other events, 64.7 us)

commit v13 on v12

--- a/solution.py
+++ b/solution.py
@@ -90,9 +90,10 @@
         at += ref.shape[0]
 
 
-def join(a, b):
-    shape = jax.ShapeDtypeStruct((a.shape[0] + b.shape[0], *a.shape[1:]), a.dtype)
-    return call(join_kernel, [a, b], [VMEM] * 2, [shape], name="join")[0]
+def join(pieces):
+    shape = (sum(p.shape[0] for p in pieces), *pieces[0].shape[1:])
+    shape = jax.ShapeDtypeStruct(shape, pieces[0].dtype)
+    return call(join_kernel, pieces, [VMEM] * len(pieces), [shape], name="join")[0]
 
 
 def load_kernel(*refs):
@@ -172,31 +173,30 @@
     )
 
 
-def piece_of(slot, refs, piece):
-    if slot is not None:
-        return refs[0][slot, piece]
-    for ref in refs:
-        if piece < ref.shape[0]:
-            return ref[piece]
-        piece -= ref.shape[0]
+def pieces_in(slot, array):
+    return array.shape[0 if slot is None else 1]
 
 
 def sum_of(layout, refs, piece):
     result, at = None, 0
     for slot, skip, count in layout:
-        term = piece_of(slot, refs[at : at + count], piece - skip).astype(jnp.float32)
-        result = term if result is None else result + term
+        i = piece - skip
+        for ref in refs[at : at + count]:
+            if 0 <= i < pieces_in(slot, ref):
+                term = (ref[i] if slot is None else ref[slot, i]).astype(jnp.float32)
+                result = term if result is None else result + term
+            i -= pieces_in(slot, ref)
         at += count
     return result
 
 
 def narrow(terms, low, high):
     layout, kept = [], []
-    for slot, arrays, *first in terms:
-        skip = -first[0] if first else 0
-        while slot is None and low >= skip + arrays[0].shape[0]:
-            skip, arrays = skip + arrays[0].shape[0], arrays[1:]
-        while slot is None and high <= skip + sum(a.shape[0] for a in arrays[:-1]):
+    for slot, arrays in terms:
+        skip = 0
+        while low >= skip + pieces_in(slot, arrays[0]):
+            skip, arrays = skip + pieces_in(slot, arrays[0]), arrays[1:]
+        while high <= skip + sum(pieces_in(slot, a) for a in arrays[:-1]):
             arrays = arrays[:-1]
         layout.append((slot, skip, len(arrays)))
         kept += arrays
@@ -223,11 +223,11 @@
 
 
 def finish_kernel(layouts, hidden_ref, *refs):
-    out_ref = refs[-1]
-    count = (len(refs) - 1) // hidden_ref.shape[0]
-    for batch in range(hidden_ref.shape[0]):
-        mixed = sum_of(layouts[batch], refs[batch * count : (batch + 1) * count], 0)
+    out_ref, at = refs[-1], 0
+    for batch, layout in enumerate(layouts):
+        mixed = sum_of(layout, refs[at:-1], 0)
         out_ref[batch] = (hidden_ref[batch].astype(jnp.float32) + mixed).astype(out_ref.dtype)
+        at += sum(count for _, _, count in layout)
 
 
 def finish(hidden_in, terms):
@@ -283,6 +283,8 @@
         spans.append(line >> len(spans))
 
     def owner_of(p, piece):
+        if piece >= half:
+            p, piece = mirrored(p, 2), piece - half
         for level in range(len(spans), 0, -1):
             if piece >= 1 << (level - 1):
                 p, piece = mirrored(p, spans[level - 1]), piece - (1 << (level - 1))
@@ -290,66 +292,80 @@
 
     payload = prepare(hidden_in, expert_ids, route_share, norm_gain, -(-owners // LANES) * LANES)
 
-    own_there = [to_mid(rows) for rows in payload]
-    near, near_there, joined, far = [], [], [], []
-    weights = None
+    weights = load([gate_weight, up_weight, down_weight])
+    there = [[to_mid(rows)] for rows in payload]
+    near, far, joined = [], [], []
     for batch, rows in enumerate(payload):
         if batch:
             rows = after(rows, joined[-1])
         near.append([rows])
-        near_there.append([own_there[batch]])
         for span in spans:
             received = mirror(rows, span)
-            received = after(received, *([*weights, far[-1]] if batch else own_there))
+            received = after(received, *([far[-1]] if batch else [*weights, *[x for xs in there for x in xs]]))
             near[batch].append(received)
-            near_there[batch].append(to_mid(received))
-            rows = join(rows, received)
+            rows = join([rows, received])
+            if not batch:
+                there[batch].append(to_mid(received))
         joined.append(rows)
-        far.append(mirror(rows, 2))
-        if weights is None:
-            weights = load([after(w, rows) for w in (gate_weight, up_weight, down_weight)])
-    far_there = [to_mid(rows) for rows in far]
-
-    groups = [[(0, 0)]]
+        far.append(mirror(rows if not batch else after(rows, *there[0]), 2))
     for batch in range(batches):
-        groups.append([(batch, 1)] + [(batch + 1, 0)] * (batch + 1 < batches))
-    order, wait = joined[1:2], far[1:2] + [x for xs in near_there[1:2] for x in xs]
-    sums, back, arrived = {}, {}, []
-    for group in groups:
-        here = [x for batch, is_far in group for x in ([far[batch]] if is_far else near[batch])]
-        there = [x for batch, is_far in group for x in ([far_there[batch]] if is_far else near_there[batch])]
-        xs = [*here, *there]
-        xs += [to_core(x) for x in xs]
-        mine, *others = ffn([after(xs[0], *order), *xs[1:]], table, weights)
-        others = [to_core(after(other, *wait)) for other in others]
-        other_here, other_there = others[: SHARES // 2], others[SHARES // 2 :]
-        own = [(1, [mine]), (None, [after(other_there[0], *other_here), *other_there[1:]])]
-        order, arrived = [], []
-        for i, unit in enumerate(group):
-            cut = (i * half, (i + 1) * half)
-            sent = total(own, [cut])[0]
-            back[unit] = to_mid(sent)
-            order.append(sent)
-            arrived.append(back[unit])
-            sums[unit] = ([(0, [mine]), (None, other_here)], cut[0])
-        batch, is_far = group[-1]
-        wait = [arrived[0], *far_there[batch + 1 : batch + 2]] if not is_far else arrived[:1]
-
-    terms, last = [[] for _ in range(batches)], []
-    for unit in [unit for group in groups for unit in group]:
-        batch, is_far = unit
-        own, first = sums[unit]
-        own = [(slot, arrays, first) for slot, arrays in own] + [(None, [after(back[unit], *last)], 0)]
-        skip = 0 if is_far else 1
-        parts = total(own, [(j, j + 1) for j in range(skip, half)])
-        returned = [
-            along_line(part, lambda p, j=j: owner_of(mirrored(p, 2) if is_far else p, j))
-            for j, part in enumerate(parts, skip)
-        ]
-        if not is_far:
-            terms[batch] += own
-        terms[batch] += [(None, [part], 0) for part in returned]
-        last = returned
+        there[batch].append(to_mid(join([*near[batch][1:], far[batch]]) if batch else far[batch]))
+
+    def swap(arrays):
+        return [to_core(x) for x in arrays]
+
+    def sums(calls, slot):
+        other = []
+        for _, shares in calls:
+            count = len(shares) // 2
+            other += shares[slot * count : (slot + 1) * count]
+        return [(slot, [mine for mine, _ in calls]), (None, other)]
+
+    early = [[*near[batch], far[batch], *there[batch][:-1]] for batch in range(batches)]
+    early_core = [swap(xs) if batch else None for batch, xs in enumerate(early)]
+    terms, sent, back = [], [], []
+    for batch in range(batches):
+        order = [x for xs in early_core[batch + 1 : batch + 2] for x in xs]
+        calls = []
+        if batch == 0:
+            xs = [*near[0], *there[0][:-1]]
+            mine, *other = ffn([after(xs[0], *joined[1:2]), *xs[1:], *swap(xs)], table, weights)
+            calls.append((mine, swap(other)))
+            xs = [far[0], after(there[0][-1], mine)]
+            xs += swap(xs)
+            order += calls[0][1]
+        else:
+            late = after(there[batch][-1], sent[-1])
+            xs = [*early[batch], late, *early_core[batch], to_core(late)]
+            order += calls_before[-1][1][: SHARES // 2]
+        mine, *other = ffn([after(xs[0], *order), *xs[1:]], table, weights)
+        calls.append((mine, swap(other)))
+        calls_before = calls
+        out = sums(calls, 1)
+        if batch + 1 < batches:
+            sent += total(out, [(0, line)])
+            back.append([to_mid(sent[-1])])
+        else:
+            sent += total(out, [(half, line)])
+            back.append([to_mid(total(out, [(0, half)])[0]), to_mid(sent[-1])])
+        terms.append([*sums(calls, 0), (None, back[-1])])
+
+    for batch in range(batches):
+        mixed = terms[batch]
+        if batch + 1 < batches:
+            mixed[-1] = (None, [after(back[batch][0], sent[-1])])
+            mixed.append((None, [mirror(total(mixed, [(half, line)])[0], 2)]))
+            span, pieces = 4, half
+            while pieces > 1:
+                mixed.append((None, [mirror(total(mixed, [(pieces // 2, pieces)])[0], span)]))
+                span, pieces = span * 2, pieces // 2
+        else:
+            far_parts = total(mixed, [(j, j + 1) for j in range(half, line)])
+            mixed[-1] = (None, [after(mixed[-1][1][0], *far_parts), *mixed[-1][1][1:]])
+            parts = total(mixed, [(j, j + 1) for j in range(1, half)]) + far_parts
+            mixed += [
+                (None, [along_line(part, lambda p, j=j: owner_of(p, j))]) for j, part in enumerate(parts, 1)
+            ]
     return finish(hidden_in, terms)
 
 

time: 93.9 us -> 85.2 us (0.907)
  the two profiles are of different devices: /device:TPU:0 before, /device:TPU:11 now
where the time goes in v13:
time: 85.2 us; the launch traced here: 85 us
  waiting for transfers between devices  33.4 us (39%)
  starting transfers between devices  32.7 us (38%)
  Pallas kernels  18.8 us (22%)
    pallas_call x16, Pallas kernels, call(): pl.pallas_call(kernel, out_shape=shapes, in_specs=specs, out_specs=[VMEM]...  18.8 us
    ppermute x9, waiting for transfers between devices, along_line(): lax.ppermute(rows, 'ep', [(i, place_of(i // 4) * 4 + i % 4) for i in rang...  16.6 us
    ppermute x23, starting transfers between devices, to_core(): return lax.ppermute(rows, 'ep', [(i, i ^ 1) for i in range(owners)])  14.5 us
    ppermute x9, starting transfers between devices, along_line(): lax.ppermute(rows, 'ep', [(i, place_of(i // 4) * 4 + i % 4) for i in rang...  12.1 us
    ppermute x8, waiting for transfers between devices, to_mid(): return lax.ppermute(rows, 'ep', [(i, i ^ 2) for i in range(owners)])  10.6 us
    ppermute x23, waiting for transfers between devices, to_core(): return lax.ppermute(rows, 'ep', [(i, i ^ 1) for i in range(owners)])  6.17 us
    ppermute x8, starting transfers between devices, to_mid(): return lax.ppermute(rows, 'ep', [(i, i ^ 2) for i in range(owners)])  6.14 us
  transfers between devices with their start and end apart: 40, of which 17 were waited for; matrix products, arithmetic and copies ran while one was open for 0% of the time, Pallas kernels for 20%

profile of v13, /device:TPU:11, one launch (start us, length us, event | category | flops | bytes accessed | tf_op | source)
XLA Modules:
  0.0 85.0 jit_solution(14622693355885255522)
XLA Ops:
  0.0 1.2 %prepare.1 = (bf16[1,32,2176]{2,1,0:T(8,128)(2,1)S(1)}, bf16[1,32,2176]{2,1,0:T(8,128)(2,1)S(1)}) custom-call(bf16[2,32,2048]{2,1,0:T(8,128)(2,1)} %hidden_ref.1, s32[2,8,32]{2,1,0:T(8,128)} %bitcast.7, s32[2,8,32]{2,1,0:T(8,128)} %bitcast.8, f32[1,2048]{1,0:T(1,128)} %bitcast.9), custom_call_target="tpu_custom_call" | custom-call | tf_op jit(solution)/shard_map/prepare/pallas_call | solution.py:27
  1.2 1.3 %collective-permute-start.2 = (bf16[1,32,2176]{2,1,0:T(8,128)(2,1)S(1)}, bf16[1,32,2176]{2,1,0:T(8,128)(2,1)S(1)}, u32[]{:S(2)}, u32[]{:S(2)}) collective-permute-start(bf16[1,32,2176]{2,1,0:T(8,128)(2,1)S(1)} %get-tuple-element.60.refs_0_), channel_id=1, source_target_pairs={{0,2},{1,3},{2,0},{3,1},{4,6},{5,7},{6,4},{7,5},{8,10},{9,11},{10,... | collective-permute-start | bytes 417800 | tf_op jit(solution)/shard_map/ppermute | solution.py:276
  2.8 1.3 %collective-permute-start = (bf16[1,32,2176]{2,1,0:T(8,128)(2,1)S(1)}, bf16[1,32,2176]{2,1,0:T(8,128)(2,1)S(1)}, u32[]{:S(2)}, u32[]{:S(2)}) collective-permute-start(bf16[1,32,2176]{2,1,0:T(8,128)(2,1)S(1)} %get-tuple-element.46.refs_0_), channel_id=1, source_target_pairs={{0,12},{1,13},{2,14},{3,15},{4,8},{5,9},{6,10},{7,11},{8,4},{9,5},... | collective-permute-start | bytes 417800 | tf_op jit(solution)/shard_map/ppermute | solution.py:267
  4.1 3.8 %load.1 = (bf16[1,2048,768]{2,1,0:T(8,128)(2,1)S(1)}, bf16[1,2048,768]{2,1,0:T(8,128)(2,1)S(1)}, bf16[1,768,2048]{2,1,0:T(8,128)(2,1)S(1)}) custom-call(bf16[1,2048,768]{2,1,0:T(8,128)(2,1)} %refs_0_.1, bf16[1,2048,768]{2,1,0:T(8,128)(2,1)} %refs_1_.1, bf16[1,768,2048]{2,1,0:T(8,128)(2,1)} %refs_2_.1), custom_call_target="tpu_custom_call" | custom-call | tf_op jit(solution)/shard_map/load/pallas_call | solution.py:27
  7.9 1.0 %collective-permute-done.1.refs_2_ = bf16[1,32,2176]{2,1,0:T(8,128)(2,1)S(1)} collective-permute-done((bf16[1,32,2176]{2,1,0:T(8,128)(2,1)S(1)}, bf16[1,32,2176]{2,1,0:T(8,128)(2,1)S(1)}, u32[]{:S(2)}, u32[]{:S(2)}) %collective-permute-start.1) | collective-permute-done | bytes 139296 | tf_op jit(solution)/shard_map/ppermute | solution.py:276
  8.8 1.6 %collective-permute-done.refs_1_ = bf16[1,32,2176]{2,1,0:T(8,128)(2,1)S(1)} collective-permute-done((bf16[1,32,2176]{2,1,0:T(8,128)(2,1)S(1)}, bf16[1,32,2176]{2,1,0:T(8,128)(2,1)S(1)}, u32[]{:S(2)}, u32[]{:S(2)}) %collective-permute-start) | collective-permute-done | bytes 139296 | tf_op jit(solution)/shard_map/ppermute | solution.py:267
  10.5 1.0 %collective-permute-start.3 = (bf16[1,32,2176]{2,1,0:T(8,128)(2,1)S(1)}, bf16[1,32,2176]{2,1,0:T(8,128)(2,1)S(1)}, u32[]{:S(2)}, u32[]{:S(2)}) collective-permute-start(bf16[1,32,2176]{2,1,0:T(8,128)(2,1)S(1)} %get-tuple-element.60.refs_0_), channel_id=1, source_target_pairs={{0,12},{1,13},{2,14},{3,15},{4,8},{5,9},{6,10},{7,11},{8,4},{9,5},... | collective-permute-start | bytes 417800 | tf_op jit(solution)/shard_map/ppermute | solution.py:267
  11.5 1.2 %collective-permute-start.5 = (bf16[1,32,2176]{2,1,0:T(8,128)(2,1)S(1)}, bf16[1,32,2176]{2,1,0:T(8,128)(2,1)S(1)}, u32[]{:S(2)}, u32[]{:S(2)}) collective-permute-start(bf16[1,32,2176]{2,1,0:T(8,128)(2,1)S(1)} %collective-permute-done.refs_1_), channel_id=1, source_target_pairs={{0,2},{1,3},{2,0},{3,1},{4,6},{5,7},{6,4},{7,5},{8,10},{9,11},{10,... | collective-permute-start | bytes 417800 | tf_op jit(solution)/shard_map/ppermute | solution.py:276
  12.7 2.9 %collective-permute-start.6 = (bf16[1,32,2176]{2,1,0:T(8,128)(2,1)S(1)}, bf16[1,32,2176]{2,1,0:T(8,128)(2,1)S(1)}, u32[]{:S(2)}, u32[]{:S(2)}) collective-permute-start(bf16[1,32,2176]{2,1,0:T(8,128)(2,1)S(1)} %get-tuple-element.46.refs_0_), channel_id=1, source_target_pairs={{0,1},{1,0},{2,3},{3,2},{4,5},{5,4},{6,7},{7,6},{8,9},{9,8},{10,11... | collective-permute-start | bytes 417800 | tf_op jit(solution)/shard_map/ppermute | solution.py:279
  15.7 1.6 %collective-permute-done.4.refs_0_ = bf16[2,32,2176]{2,1,0:T(8,128)(2,1)S(1)} collective-permute-done((bf16[2,32,2176]{2,1,0:T(8,128)(2,1)S(1)}, bf16[2,32,2176]{2,1,0:T(8,128)(2,1)S(1)}, u32[]{:S(2)}, u32[]{:S(2)}) %collective-permute-start.4) | collective-permute-done | bytes 278560 | tf_op jit(solution)/shard_map/ppermute | solution.py:267
  17.3 2.3 %collective-permute-start.13 = (bf16[2,32,2176]{2,1,0:T(8,128)(2,1)S(1)}, bf16[2,32,2176]{2,1,0:T(8,128)(2,1)S(1)}, u32[]{:S(2)}, u32[]{:S(2)}) collective-permute-start(bf16[2,32,2176]{2,1,0:T(8,128)(2,1)S(1)} %join.4), channel_id=1, source_target_pairs={{0,4},{1,5},{2,6},{3,7},{4,0},{5,1},{6,2},{7,3},{8,12},{9,13},{10,... | collective-permute-start | bytes 835592 | tf_op jit(solution)/shard_map/ppermute | solution.py:267
  19.6 1.2 %collective-permute-start.19 = (bf16[2,32,2176]{2,1,0:T(8,128)(2,1)S(1)}, bf16[2,32,2176]{2,1,0:T(8,128)(2,1)S(1)}, u32[]{:S(2)}, u32[]{:S(2)}) collective-permute-start(bf16[2,32,2176]{2,1,0:T(8,128)(2,1)S(1)} %collective-permute-done.4.refs_0_), channel_id=1, source_target_pairs={{0,2},{1,3},{2,0},{3,1},{4,6},{5,7},{6,4},{7,5},{8,10},{9,11},{10,... | collective-permute-start | bytes 835592 | tf_op jit(solution)/shard_map/ppermute | solution.py:276
  20.8 4.3 %collective-permute-start.7 = (bf16[1,32,2176]{2,1,0:T(8,128)(2,1)S(1)}, bf16[1,32,2176]{2,1,0:T(8,128)(2,1)S(1)}, u32[]{:S(2)}, u32[]{:S(2)}) collective-permute-start(bf16[1,32,2176]{2,1,0:T(8,128)(2,1)S(1)} %collective-permute-done.refs_1_), channel_id=1, source_target_pairs={{0,1},{1,0},{2,3},{3,2},{4,5},{5,4},{6,7},{7,6},{8,9},{9,8},{10,11... | collective-permute-start | bytes 417800 | tf_op jit(solution)/shard_map/ppermute | solution.py:279
  26.5 3.2 %ffn.3 = (bf16[2,2,32,2048]{3,2,1,0:T(8,128)(2,1)S(1)}, bf16[1,32,2048]{2,1,0:T(8,128)(2,1)S(1)}, bf16[1,32,2048]{2,1,0:T(8,128)(2,1)S(1)}, bf16[1,32,2048]{2,1,0:T(8,128)(2,1)S(1)}, bf16[1,32,2048]{2,1,0:T(8,128)(2,1)S(1)}) custom-call(s32[3,1,6]{2,1,0:T(1,128)S(1)} %bitcast.4, bf16[1,2048,768]{2,1,0:T(8,128)(2,1)S(1)} %get-tuple-element.38.gate_ref, ...), custom_call_target="tpu_custom_call" | custom-call | tf_op jit(solution)/shard_map/ffn/pallas_call | solution.py:27
  30.8 0.8 collective-permute-start.14
  32.3 1.6 %collective-permute-done.18.refs_3_ = bf16[1,32,2048]{2,1,0:T(8,128)(2,1)S(1)} collective-permute-done((bf16[1,32,2048]{2,1,0:T(8,128)(2,1)S(1)}, bf16[1,32,2048]{2,1,0:T(8,128)(2,1)S(1)}, u32[]{:S(2)}, u32[]{:S(2)}) %collective-permute-start.18) | collective-permute-done | bytes 131104 | tf_op jit(solution)/shard_map/ppermute | solution.py:279
  34.2 1.0 %collective-permute-done.12.refs_6_ = bf16[1,32,2176]{2,1,0:T(8,128)(2,1)S(1)} collective-permute-done((bf16[1,32,2176]{2,1,0:T(8,128)(2,1)S(1)}, bf16[1,32,2176]{2,1,0:T(8,128)(2,1)S(1)}, u32[]{:S(2)}, u32[]{:S(2)}) %collective-permute-start.12) | collective-permute-done | bytes 139296 | tf_op jit(solution)/shard_map/ppermute | solution.py:279
  35.2 3.2 %ffn.4 = (bf16[2,2,32,2048]{3,2,1,0:T(8,128)(2,1)S(1)}, bf16[1,32,2048]{2,1,0:T(8,128)(2,1)S(1)}, bf16[1,32,2048]{2,1,0:T(8,128)(2,1)S(1)}, bf16[1,32,2048]{2,1,0:T(8,128)(2,1)S(1)}, bf16[1,32,2048]{2,1,0:T(8,128)(2,1)S(1)}) custom-call(s32[3,1,6]{2,1,0:T(1,128)S(1)} %bitcast.5, bf16[1,2048,768]{2,1,0:T(8,128)(2,1)S(1)} %get-tuple-element.38.gate_ref, ...), custom_call_target="tpu_custom_call" | custom-call | tf_op jit(solution)/shard_map/ffn/pallas_call | solution.py:27
  39.0 0.8 collective-permute-done.22.refs_4_
  40.4 1.2 %collective-permute-done.27.refs_4_ = bf16[3,32,2176]{2,1,0:T(8,128)(2,1)S(1)} collective-permute-done((bf16[3,32,2176]{2,1,0:T(8,128)(2,1)S(1)}, bf16[3,32,2176]{2,1,0:T(8,128)(2,1)S(1)}, u32[]{:S(2)}, u32[]{:S(2)}) %collective-permute-start.27) | collective-permute-done | bytes 417824 | tf_op jit(solution)/shard_map/ppermute | solution.py:276
  41.5 1.1 %collective-permute-start.28 = (bf16[3,32,2176]{2,1,0:T(8,128)(2,1)S(1)}, bf16[3,32,2176]{2,1,0:T(8,128)(2,1)S(1)}, u32[]{:S(2)}, u32[]{:S(2)}) collective-permute-start(bf16[3,32,2176]{2,1,0:T(8,128)(2,1)S(1)} %collective-permute-done.27.refs_4_), channel_id=1, source_target_pairs={{0,1},{1,0},{2,3},{3,2},{4,5},{5,4},{6,7},{7,6},{8,9},{9,8},{10,11... | collective-permute-start | bytes 1253384 | tf_op jit(solution)/shard_map/ppermute | solution.py:279
  43.4 0.8 collective-permute-done.25.refs_1_
  44.5 5.7 %ffn.5 = (bf16[2,4,32,2048]{3,2,1,0:T(8,128)(2,1)S(1)}, bf16[2,32,2048]{2,1,0:T(8,128)(2,1)S(1)}, bf16[2,32,2048]{2,1,0:T(8,128)(2,1)S(1)}, bf16[2,32,2048]{2,1,0:T(8,128)(2,1)S(1)}, bf16[2,32,2048]{2,1,0:T(8,128)(2,1)S(1)}) custom-call(s32[3,1,6]{2,1,0:T(1,128)S(1)} %bitcast.6, bf16[1,2048,768]{2,1,0:T(8,128)(2,1)S(1)} %get-tuple-element.38.gate_ref, ...), custom_call_target="tpu_custom_call" | custom-call | tf_op jit(solution)/shard_map/ffn/pallas_call | solution.py:27
  51.9 1.3 %collective-permute-start.36 = (bf16[2,32,2048]{2,1,0:T(8,128)(2,1)S(1)}, bf16[2,32,2048]{2,1,0:T(8,128)(2,1)S(1)}, u32[]{:S(2)}, u32[]{:S(2)}) collective-permute-start(bf16[2,32,2048]{2,1,0:T(8,128)(2,1)S(1)} %total.8), channel_id=1, source_target_pairs={{0,2},{1,3},{2,0},{3,1},{4,6},{5,7},{6,4},{7,5},{8,10},{9,11},{10,... | collective-permute-start | bytes 786440 | tf_op jit(solution)/shard_map/ppermute | solution.py:276
  54.4 1.8 %collective-permute-done.24.refs_3_.refs_2_ = bf16[4,32,2048]{2,1,0:T(8,128)(2,1)S(1)} collective-permute-done((bf16[4,32,2048]{2,1,0:T(8,128)(2,1)S(1)}, bf16[4,32,2048]{2,1,0:T(8,128)(2,1)S(1)}, u32[]{:S(2)}, u32[]{:S(2)}) %collective-permute-start.24) | collective-permute-done | bytes 524320 | tf_op jit(solution)/shard_map/ppermute | solution.py:276
  56.4 5.4 %collective-permute-done.36.refs_2_ = bf16[2,32,2048]{2,1,0:T(8,128)(2,1)S(1)} collective-permute-done((bf16[2,32,2048]{2,1,0:T(8,128)(2,1)S(1)}, bf16[2,32,2048]{2,1,0:T(8,128)(2,1)S(1)}, u32[]{:S(2)}, u32[]{:S(2)}) %collective-permute-start.36) | collective-permute-done | bytes 262176 | tf_op jit(solution)/shard_map/ppermute | solution.py:276
  62.0 4.1 %collective-permute-start.39 = (bf16[1,32,2048]{2,1,0:T(8,128)(2,1)S(1)}, bf16[1,32,2048]{2,1,0:T(8,128)(2,1)S(1)}, u32[]{:S(2)}, u32[]{:S(2)}) collective-permute-start(bf16[1,32,2048]{2,1,0:T(8,128)(2,1)S(1)} %get-tuple-element.69), channel_id=1, source_target_pairs={{0,8},{1,9},{2,10},{3,11},{4,12},{5,13},{6,14},{7,15},{8,0},{9,1},... | collective-permute-start | bytes 393224 | tf_op jit(solution)/shard_map/ppermute | solution.py:267
  66.2 1.3 %collective-permute-done.34.refs_2_.refs_7_ = bf16[2,32,2048]{2,1,0:T(8,128)(2,1)S(1)} collective-permute-done((bf16[2,32,2048]{2,1,0:T(8,128)(2,1)S(1)}, bf16[2,32,2048]{2,1,0:T(8,128)(2,1)S(1)}, u32[]{:S(2)}, u32[]{:S(2)}) %collective-permute-start.34) | collective-permute-done | bytes 262176 | tf_op jit(solution)/shard_map/ppermute | solution.py:276
  67.5 3.0 %collective-permute-start.37 = (bf16[1,32,2048]{2,1,0:T(8,128)(2,1)S(1)}, bf16[1,32,2048]{2,1,0:T(8,128)(2,1)S(1)}, u32[]{:S(2)}, u32[]{:S(2)}) collective-permute-start(bf16[1,32,2048]{2,1,0:T(8,128)(2,1)S(1)} %total.13), channel_id=1, source_target_pairs={{0,12},{1,13},{2,14},{3,15},{4,8},{5,9},{6,10},{7,11},{8,4},{9,5},... | collective-permute-start | bytes 393224 | tf_op jit(solution)/shard_map/ppermute | solution.py:267
  70.7 10.6 %collective-permute-done.37.refs_8_ = bf16[1,32,2048]{2,1,0:T(8,128)(2,1)S(1)} collective-permute-done((bf16[1,32,2048]{2,1,0:T(8,128)(2,1)S(1)}, bf16[1,32,2048]{2,1,0:T(8,128)(2,1)S(1)}, u32[]{:S(2)}, u32[]{:S(2)}) %collective-permute-start.37) | collective-permute-done | bytes 131104 | tf_op jit(solution)/shard_map/ppermute | solution.py:267
  81.3 2.8 %collective-permute-done.31.refs_4_ = bf16[1,32,2048]{2,1,0:T(8,128)(2,1)S(1)} collective-permute-done((bf16[1,32,2048]{2,1,0:T(8,128)(2,1)S(1)}, bf16[1,32,2048]{2,1,0:T(8,128)(2,1)S(1)}, u32[]{:S(2)}, u32[]{:S(2)}) %collective-permute-start.31) | collective-permute-done | bytes 131104 | tf_op jit(solution)/shard_map/ppermute | solution.py:267
  84.1 0.9 %finish.1 = bf16[2,32,2048]{2,1,0:T(8,128)(2,1)} custom-call(bf16[2,32,2048]{2,1,0:T(8,128)(2,1)S(1)} %copy-done, bf16[2,2,32,2048]{3,2,1,0:T(8,128)(2,1)S(1)} %get-tuple-element.47.refs_0_, bf16[1,32,2048]{2,1,0:T(8,128)(2,1)S(1)} %collective-permute-done.10.refs_1_, bf16[4,32,2048]{2,1,0:T(8,128)(2,1)S(1)} %collective-permute-done.24.refs_3_.refs_2_, ...), custom_call_target="tpu_custom_call" | custom-call | tf_op jit(solution)/shard_map/finish/pallas_call | solution.py:27
  (68 shorter events, 9.3 us)
Async XLA Ops:
  1.2 6.6 %collective-permute-start.2 = (bf16[1,32,2176]{2,1,0:T(8,128)(2,1)S(1)}, bf16[1,32,2176]{2,1,0:T(8,128)(2,1)S(1)}, u32[]{:S(2)}, u32[]{:S(2)}) collective-permute-start(bf16[1,32,2176]{2,1,0:T(8,128)(2,1)S(1)} %get-tuple-element.60.refs_0_), channel_id=1, source_target_pairs={{0,2},{1,3},{2,0},{3,1},{4,6},{5,7},{6,4},{7,5},{8,10},{9,11},{10,... | collective-permute-start | bytes 417800 | tf_op jit(solution)/shard_map/ppermute | solution.py:276
  2.5 6.3 %collective-permute-start.1 = (bf16[1,32,2176]{2,1,0:T(8,128)(2,1)S(1)}, bf16[1,32,2176]{2,1,0:T(8,128)(2,1)S(1)}, u32[]{:S(2)}, u32[]{:S(2)}) collective-permute-start(bf16[1,32,2176]{2,1,0:T(8,128)(2,1)S(1)} %get-tuple-element.46.refs_0_), channel_id=1, source_target_pairs={{0,2},{1,3},{2,0},{3,1},{4,6},{5,7},{6,4},{7,5},{8,10},{9,11},{10,... | collective-permute-start | bytes 417800 | tf_op jit(solution)/shard_map/ppermute | solution.py:276
  2.8 7.7 %collective-permute-start = (bf16[1,32,2176]{2,1,0:T(8,128)(2,1)S(1)}, bf16[1,32,2176]{2,1,0:T(8,128)(2,1)S(1)}, u32[]{:S(2)}, u32[]{:S(2)}) collective-permute-start(bf16[1,32,2176]{2,1,0:T(8,128)(2,1)S(1)} %get-tuple-element.46.refs_0_), channel_id=1, source_target_pairs={{0,12},{1,13},{2,14},{3,15},{4,8},{5,9},{6,10},{7,11},{8,4},{9,5},... | collective-permute-start | bytes 417800 | tf_op jit(solution)/shard_map/ppermute | solution.py:267
  10.4 6.8 %collective-permute-start.4 = (bf16[2,32,2176]{2,1,0:T(8,128)(2,1)S(1)}, bf16[2,32,2176]{2,1,0:T(8,128)(2,1)S(1)}, u32[]{:S(2)}, u32[]{:S(2)}) collective-permute-start(bf16[2,32,2176]{2,1,0:T(8,128)(2,1)S(1)} %join.3), channel_id=1, source_target_pairs={{0,4},{1,5},{2,6},{3,7},{4,0},{5,1},{6,2},{7,3},{8,12},{9,13},{10,... | collective-permute-start | bytes 835592 | tf_op jit(solution)/shard_map/ppermute | solution.py:267
  10.5 5.2 %collective-permute-start.3 = (bf16[1,32,2176]{2,1,0:T(8,128)(2,1)S(1)}, bf16[1,32,2176]{2,1,0:T(8,128)(2,1)S(1)}, u32[]{:S(2)}, u32[]{:S(2)}) collective-permute-start(bf16[1,32,2176]{2,1,0:T(8,128)(2,1)S(1)} %get-tuple-element.60.refs_0_), channel_id=1, source_target_pairs={{0,12},{1,13},{2,14},{3,15},{4,8},{5,9},{6,10},{7,11},{8,4},{9,5},... | collective-permute-start | bytes 417800 | tf_op jit(solution)/shard_map/ppermute | solution.py:267
  11.5 5.8 %collective-permute-start.5 = (bf16[1,32,2176]{2,1,0:T(8,128)(2,1)S(1)}, bf16[1,32,2176]{2,1,0:T(8,128)(2,1)S(1)}, u32[]{:S(2)}, u32[]{:S(2)}) collective-permute-start(bf16[1,32,2176]{2,1,0:T(8,128)(2,1)S(1)} %collective-permute-done.refs_1_), channel_id=1, source_target_pairs={{0,2},{1,3},{2,0},{3,1},{4,6},{5,7},{6,4},{7,5},{8,10},{9,11},{10,... | collective-permute-start | bytes 417800 | tf_op jit(solution)/shard_map/ppermute | solution.py:276
  12.7 12.4 %collective-permute-start.6 = (bf16[1,32,2176]{2,1,0:T(8,128)(2,1)S(1)}, bf16[1,32,2176]{2,1,0:T(8,128)(2,1)S(1)}, u32[]{:S(2)}, u32[]{:S(2)}) collective-permute-start(bf16[1,32,2176]{2,1,0:T(8,128)(2,1)S(1)} %get-tuple-element.46.refs_0_), channel_id=1, source_target_pairs={{0,1},{1,0},{2,3},{3,2},{4,5},{5,4},{6,7},{7,6},{8,9},{9,8},{10,11... | collective-permute-start | bytes 417800 | tf_op jit(solution)/shard_map/ppermute | solution.py:279
  15.7 9.4 %collective-permute-start.8 = (bf16[1,32,2176]{2,1,0:T(8,128)(2,1)S(1)}, bf16[1,32,2176]{2,1,0:T(8,128)(2,1)S(1)}, u32[]{:S(2)}, u32[]{:S(2)}) collective-permute-start(bf16[1,32,2176]{2,1,0:T(8,128)(2,1)S(1)} %collective-permute-done.1.refs_2_), channel_id=1, source_target_pairs={{0,1},{1,0},{2,3},{3,2},{4,5},{5,4},{6,7},{7,6},{8,9},{9,8},{10,11... | collective-permute-start | bytes 417800 | tf_op jit(solution)/shard_map/ppermute | solution.py:279
  17.3 13.0 %collective-permute-start.13 = (bf16[2,32,2176]{2,1,0:T(8,128)(2,1)S(1)}, bf16[2,32,2176]{2,1,0:T(8,128)(2,1)S(1)}, u32[]{:S(2)}, u32[]{:S(2)}) collective-permute-start(bf16[2,32,2176]{2,1,0:T(8,128)(2,1)S(1)} %join.4), channel_id=1, source_target_pairs={{0,4},{1,5},{2,6},{3,7},{4,0},{5,1},{6,2},{7,3},{8,12},{9,13},{10,... | collective-permute-start | bytes 835592 | tf_op jit(solution)/shard_map/ppermute | solution.py:267
  19.6 10.9 %collective-permute-start.19 = (bf16[2,32,2176]{2,1,0:T(8,128)(2,1)S(1)}, bf16[2,32,2176]{2,1,0:T(8,128)(2,1)S(1)}, u32[]{:S(2)}, u32[]{:S(2)}) collective-permute-start(bf16[2,32,2176]{2,1,0:T(8,128)(2,1)S(1)} %collective-permute-done.4.refs_0_), channel_id=1, source_target_pairs={{0,2},{1,3},{2,0},{3,1},{4,6},{5,7},{6,4},{7,5},{8,10},{9,11},{10,... | collective-permute-start | bytes 835592 | tf_op jit(solution)/shard_map/ppermute | solution.py:276
  20.8 5.3 %collective-permute-start.7 = (bf16[1,32,2176]{2,1,0:T(8,128)(2,1)S(1)}, bf16[1,32,2176]{2,1,0:T(8,128)(2,1)S(1)}, u32[]{:S(2)}, u32[]{:S(2)}) collective-permute-start(bf16[1,32,2176]{2,1,0:T(8,128)(2,1)S(1)} %collective-permute-done.refs_1_), channel_id=1, source_target_pairs={{0,1},{1,0},{2,3},{3,2},{4,5},{5,4},{6,7},{7,6},{8,9},{9,8},{10,11... | collective-permute-start | bytes 417800 | tf_op jit(solution)/shard_map/ppermute | solution.py:279
  25.1 4.9 %collective-permute-start.15 = (bf16[1,32,2176]{2,1,0:T(8,128)(2,1)S(1)}, bf16[1,32,2176]{2,1,0:T(8,128)(2,1)S(1)}, u32[]{:S(2)}, u32[]{:S(2)}) collective-permute-start(bf16[1,32,2176]{2,1,0:T(8,128)(2,1)S(1)} %collective-permute-done.2.refs_3_), channel_id=1, source_target_pairs={{0,1},{1,0},{2,3},{3,2},{4,5},{5,4},{6,7},{7,6},{8,9},{9,8},{10,11... | collective-permute-start | bytes 417800 | tf_op jit(solution)/shard_map/ppermute | solution.py:279
  26.1 4.7 %collective-permute-start.11 = (bf16[1,32,2176]{2,1,0:T(8,128)(2,1)S(1)}, bf16[1,32,2176]{2,1,0:T(8,128)(2,1)S(1)}, u32[]{:S(2)}, u32[]{:S(2)}) collective-permute-start(bf16[1,32,2176]{2,1,0:T(8,128)(2,1)S(1)} %get-tuple-element.60.refs_0_), channel_id=1, source_target_pairs={{0,1},{1,0},{2,3},{3,2},{4,5},{5,4},{6,7},{7,6},{8,9},{9,8},{10,11... | collective-permute-start | bytes 417800 | tf_op jit(solution)/shard_map/ppermute | solution.py:279
  29.7 1.9 %collective-permute-start.10 = (bf16[1,32,2048]{2,1,0:T(8,128)(2,1)S(1)}, bf16[1,32,2048]{2,1,0:T(8,128)(2,1)S(1)}, u32[]{:S(2)}, u32[]{:S(2)}) collective-permute-start(bf16[1,32,2048]{2,1,0:T(8,128)(2,1)S(1)} %get-tuple-element.48), channel_id=1, source_target_pairs={{0,1},{1,0},{2,3},{3,2},{4,5},{5,4},{6,7},{7,6},{8,9},{9,8},{10,11... | collective-permute-start | bytes 393224 | tf_op jit(solution)/shard_map/ppermute | solution.py:279
  30.0 1.8 %collective-permute-start.16 = (bf16[1,32,2048]{2,1,0:T(8,128)(2,1)S(1)}, bf16[1,32,2048]{2,1,0:T(8,128)(2,1)S(1)}, u32[]{:S(2)}, u32[]{:S(2)}) collective-permute-start(bf16[1,32,2048]{2,1,0:T(8,128)(2,1)S(1)} %get-tuple-element.50), channel_id=1, source_target_pairs={{0,1},{1,0},{2,3},{3,2},{4,5},{5,4},{6,7},{7,6},{8,9},{9,8},{10,11... | collective-permute-start | bytes 393224 | tf_op jit(solution)/shard_map/ppermute | solution.py:279
  30.3 1.9 %collective-permute-start.17 = (bf16[1,32,2048]{2,1,0:T(8,128)(2,1)S(1)}, bf16[1,32,2048]{2,1,0:T(8,128)(2,1)S(1)}, u32[]{:S(2)}, u32[]{:S(2)}) collective-permute-start(bf16[1,32,2048]{2,1,0:T(8,128)(2,1)S(1)} %get-tuple-element.51), channel_id=1, source_target_pairs={{0,1},{1,0},{2,3},{3,2},{4,5},{5,4},{6,7},{7,6},{8,9},{9,8},{10,11... | collective-permute-start | bytes 393224 | tf_op jit(solution)/shard_map/ppermute | solution.py:279
  30.5 11.0 %collective-permute-start.27 = (bf16[3,32,2176]{2,1,0:T(8,128)(2,1)S(1)}, bf16[3,32,2176]{2,1,0:T(8,128)(2,1)S(1)}, u32[]{:S(2)}, u32[]{:S(2)}) collective-permute-start(bf16[3,32,2176]{2,1,0:T(8,128)(2,1)S(1)} %join.5), channel_id=1, source_target_pairs={{0,2},{1,3},{2,0},{3,1},{4,6},{5,7},{6,4},{7,5},{8,10},{9,11},{10,... | collective-permute-start | bytes 1253384 | tf_op jit(solution)/shard_map/ppermute | solution.py:276
  30.8 4.4 %collective-permute-start.14 = (bf16[2,32,2176]{2,1,0:T(8,128)(2,1)S(1)}, bf16[2,32,2176]{2,1,0:T(8,128)(2,1)S(1)}, u32[]{:S(2)}, u32[]{:S(2)}) collective-permute-start(bf16[2,32,2176]{2,1,0:T(8,128)(2,1)S(1)} %collective-permute-done.13.refs_1_.refs_2_), channel_id=1, source_target_pairs={{0,1},{1,0},{2,3},{3,2},{4,5},{5,4},{6,7},{7,6},{8,9},{9,8},{10,11... | collective-permute-start | bytes 835592 | tf_op jit(solution)/shard_map/ppermute | solution.py:279
  31.7 3.5 %collective-permute-start.20 = (bf16[2,32,2176]{2,1,0:T(8,128)(2,1)S(1)}, bf16[2,32,2176]{2,1,0:T(8,128)(2,1)S(1)}, u32[]{:S(2)}, u32[]{:S(2)}) collective-permute-start(bf16[2,32,2176]{2,1,0:T(8,128)(2,1)S(1)} %collective-permute-done.4.refs_0_), channel_id=1, source_target_pairs={{0,1},{1,0},{2,3},{3,2},{4,5},{5,4},{6,7},{7,6},{8,9},{9,8},{10,11... | collective-permute-start | bytes 835592 | tf_op jit(solution)/shard_map/ppermute | solution.py:279
  31.7 3.5 %collective-permute-start.21 = (bf16[2,32,2176]{2,1,0:T(8,128)(2,1)S(1)}, bf16[2,32,2176]{2,1,0:T(8,128)(2,1)S(1)}, u32[]{:S(2)}, u32[]{:S(2)}) collective-permute-start(bf16[2,32,2176]{2,1,0:T(8,128)(2,1)S(1)} %collective-permute-done.19.refs_1_), channel_id=1, source_target_pairs={{0,1},{1,0},{2,3},{3,2},{4,5},{5,4},{6,7},{7,6},{8,9},{9,8},{10,11... | collective-permute-start | bytes 835592 | tf_op jit(solution)/shard_map/ppermute | solution.py:279
  41.5 3.0 %collective-permute-start.28 = (bf16[3,32,2176]{2,1,0:T(8,128)(2,1)S(1)}, bf16[3,32,2176]{2,1,0:T(8,128)(2,1)S(1)}, u32[]{:S(2)}, u32[]{:S(2)}) collective-permute-start(bf16[3,32,2176]{2,1,0:T(8,128)(2,1)S(1)} %collective-permute-done.27.refs_4_), channel_id=1, source_target_pairs={{0,1},{1,0},{2,3},{3,2},{4,5},{5,4},{6,7},{7,6},{8,9},{9,8},{10,11... | collective-permute-start | bytes 1253384 | tf_op jit(solution)/shard_map/ppermute | solution.py:279
  42.7 13.6 %collective-permute-start.24 = (bf16[4,32,2048]{2,1,0:T(8,128)(2,1)S(1)}, bf16[4,32,2048]{2,1,0:T(8,128)(2,1)S(1)}, u32[]{:S(2)}, u32[]{:S(2)}) collective-permute-start(bf16[4,32,2048]{2,1,0:T(8,128)(2,1)S(1)} %total.7), channel_id=1, source_target_pairs={{0,2},{1,3},{2,0},{3,1},{4,6},{5,7},{6,4},{7,5},{8,10},{9,11},{10,... | collective-permute-start | bytes 1572872 | tf_op jit(solution)/shard_map/ppermute | solution.py:276
  50.6 2.6 %collective-permute-start.33 = (bf16[2,32,2048]{2,1,0:T(8,128)(2,1)S(1)}, bf16[2,32,2048]{2,1,0:T(8,128)(2,1)S(1)}, u32[]{:S(2)}, u32[]{:S(2)}) collective-permute-start(bf16[2,32,2048]{2,1,0:T(8,128)(2,1)S(1)} %get-tuple-element.66), channel_id=1, source_target_pairs={{0,1},{1,0},{2,3},{3,2},{4,5},{5,4},{6,7},{7,6},{8,9},{9,8},{10,11... | collective-permute-start | bytes 786440 | tf_op jit(solution)/shard_map/ppermute | solution.py:279
  50.9 5.6 %collective-permute-start.35 = (bf16[2,32,2048]{2,1,0:T(8,128)(2,1)S(1)}, bf16[2,32,2048]{2,1,0:T(8,128)(2,1)S(1)}, u32[]{:S(2)}, u32[]{:S(2)}) collective-permute-start(bf16[2,32,2048]{2,1,0:T(8,128)(2,1)S(1)} %get-tuple-element.67), channel_id=1, source_target_pairs={{0,1},{1,0},{2,3},{3,2},{4,5},{5,4},{6,7},{7,6},{8,9},{9,8},{10,11... | collective-permute-start | bytes 786440 | tf_op jit(solution)/shard_map/ppermute | solution.py:279
  51.9 9.9 %collective-permute-start.36 = (bf16[2,32,2048]{2,1,0:T(8,128)(2,1)S(1)}, bf16[2,32,2048]{2,1,0:T(8,128)(2,1)S(1)}, u32[]{:S(2)}, u32[]{:S(2)}) collective-permute-start(bf16[2,32,2048]{2,1,0:T(8,128)(2,1)S(1)} %total.8), channel_id=1, source_target_pairs={{0,2},{1,3},{2,0},{3,1},{4,6},{5,7},{6,4},{7,5},{8,10},{9,11},{10,... | collective-permute-start | bytes 786440 | tf_op jit(solution)/shard_map/ppermute | solution.py:276
  53.3 14.1 %collective-permute-start.34 = (bf16[2,32,2048]{2,1,0:T(8,128)(2,1)S(1)}, bf16[2,32,2048]{2,1,0:T(8,128)(2,1)S(1)}, u32[]{:S(2)}, u32[]{:S(2)}) collective-permute-start(bf16[2,32,2048]{2,1,0:T(8,128)(2,1)S(1)} %total.11), channel_id=1, source_target_pairs={{0,2},{1,3},{2,0},{3,1},{4,6},{5,7},{6,4},{7,5},{8,10},{9,11},{10,... | collective-permute-start | bytes 786440 | tf_op jit(solution)/shard_map/ppermute | solution.py:276
  53.6 13.8 %collective-permute-start.32 = (bf16[2,32,2048]{2,1,0:T(8,128)(2,1)S(1)}, bf16[2,32,2048]{2,1,0:T(8,128)(2,1)S(1)}, u32[]{:S(2)}, u32[]{:S(2)}) collective-permute-start(bf16[2,32,2048]{2,1,0:T(8,128)(2,1)S(1)} %get-tuple-element.65), channel_id=1, source_target_pairs={{0,1},{1,0},{2,3},{3,2},{4,5},{5,4},{6,7},{7,6},{8,9},{9,8},{10,11... | collective-permute-start | bytes 786440 | tf_op jit(solution)/shard_map/ppermute | solution.py:279
  56.3 14.2 %collective-permute-start.30 = (bf16[2,32,2048]{2,1,0:T(8,128)(2,1)S(1)}, bf16[2,32,2048]{2,1,0:T(8,128)(2,1)S(1)}, u32[]{:S(2)}, u32[]{:S(2)}) collective-permute-start(bf16[2,32,2048]{2,1,0:T(8,128)(2,1)S(1)} %total.9), channel_id=1, source_target_pairs={{0,4},{1,5},{2,6},{3,7},{4,0},{5,1},{6,2},{7,3},{8,12},{9,13},{10,... | collective-permute-start | bytes 786440 | tf_op jit(solution)/shard_map/ppermute | solution.py:267
  61.9 19.4 %collective-permute-start.38 = (bf16[1,32,2048]{2,1,0:T(8,128)(2,1)S(1)}, bf16[1,32,2048]{2,1,0:T(8,128)(2,1)S(1)}, u32[]{:S(2)}, u32[]{:S(2)}) collective-permute-start(bf16[1,32,2048]{2,1,0:T(8,128)(2,1)S(1)} %get-tuple-element.68), channel_id=1, source_target_pairs={{0,4},{1,5},{2,6},{3,7},{4,0},{5,1},{6,2},{7,3},{8,12},{9,13},{10,... | collective-permute-start | bytes 393224 | tf_op jit(solution)/shard_map/ppermute | solution.py:267
  62.0 19.3 %collective-permute-start.39 = (bf16[1,32,2048]{2,1,0:T(8,128)(2,1)S(1)}, bf16[1,32,2048]{2,1,0:T(8,128)(2,1)S(1)}, u32[]{:S(2)}, u32[]{:S(2)}) collective-permute-start(bf16[1,32,2048]{2,1,0:T(8,128)(2,1)S(1)} %get-tuple-element.69), channel_id=1, source_target_pairs={{0,8},{1,9},{2,10},{3,11},{4,12},{5,13},{6,14},{7,15},{8,0},{9,1},... | collective-permute-start | bytes 393224 | tf_op jit(solution)/shard_map/ppermute | solution.py:267
  67.5 13.8 %collective-permute-start.37 = (bf16[1,32,2048]{2,1,0:T(8,128)(2,1)S(1)}, bf16[1,32,2048]{2,1,0:T(8,128)(2,1)S(1)}, u32[]{:S(2)}, u32[]{:S(2)}) collective-permute-start(bf16[1,32,2048]{2,1,0:T(8,128)(2,1)S(1)} %total.13), channel_id=1, source_target_pairs={{0,12},{1,13},{2,14},{3,15},{4,8},{5,9},{6,10},{7,11},{8,4},{9,5},... | collective-permute-start | bytes 393224 | tf_op jit(solution)/shard_map/ppermute | solution.py:267
  70.6 13.5 %collective-permute-start.31 = (bf16[1,32,2048]{2,1,0:T(8,128)(2,1)S(1)}, bf16[1,32,2048]{2,1,0:T(8,128)(2,1)S(1)}, u32[]{:S(2)}, u32[]{:S(2)}) collective-permute-start(bf16[1,32,2048]{2,1,0:T(8,128)(2,1)S(1)} %total.10), channel_id=1, source_target_pairs={{0,12},{1,13},{2,14},{3,15},{4,8},{5,9},{6,10},{7,11},{8,4},{9,5},... | collective-permute-start | bytes 393224 | tf_op jit(solution)/shard_map/ppermute | solution.py:267
  (10 other events, 65.9 us)

commit v14 on v13

--- a/solution.py
+++ b/solution.py
@@ -357,11 +357,12 @@
             mixed.append((None, [mirror(total(mixed, [(half, line)])[0], 2)]))
             span, pieces = 4, half
             while pieces > 1:
-                mixed.append((None, [mirror(total(mixed, [(pieces // 2, pieces)])[0], span)]))
+                part = total(mixed, [(pieces // 2, pieces)])[0]
+                mixed.append((None, [mirror(part, span)]))
                 span, pieces = span * 2, pieces // 2
         else:
             far_parts = total(mixed, [(j, j + 1) for j in range(half, line)])
-            mixed[-1] = (None, [after(mixed[-1][1][0], *far_parts), *mixed[-1][1][1:]])
+            mixed[-1] = (None, [after(mixed[-1][1][0], *far_parts, part), *mixed[-1][1][1:]])
             parts = total(mixed, [(j, j + 1) for j in range(1, half)]) + far_parts
             mixed += [
                 (None, [along_line(part, lambda p, j=j: owner_of(p, j))]) for j, part in enumerate(parts, 1)

time: 85.2 us -> 85.2 us (level)
  starting transfers between devices: 32.7 us -> 34 us
  waiting for transfers between devices: 33.4 us -> 32.1 us
    ppermute x8, waiting for transfers between devices: 10.6 us -> 9.29 us  [to_mid(): return lax.ppermute(rows, 'ep', [(i, i ^ 2) for i in range(owners)])]
    ppermute x23, starting transfers between devices: 14.5 us -> 15.4 us  [to_core(): return lax.ppermute(rows, 'ep', [(i, i ^ 1) for i in range(owners)])]
  transfers between devices with their start and end apart: 40 -> 40, of which waited for: 17 -> 18; matrix products, arithmetic and copies ran while one was open for 0% -> 0% of each run, Pallas kernels for 20% -> 20%
where the time goes in v14:
time: 85.2 us; the launch traced here: 85 us
  starting transfers between devices  34 us (40%)
  waiting for transfers between devices  32.1 us (38%)
  Pallas kernels  18.8 us (22%)
    pallas_call x16, Pallas kernels, call(): pl.pallas_call(kernel, out_shape=shapes, in_specs=specs, out_specs=[VMEM]...  18.8 us
    ppermute x9, waiting for transfers between devices, along_line(): lax.ppermute(rows, 'ep', [(i, place_of(i // 4) * 4 + i % 4) for i in rang...  16.7 us
    ppermute x23, starting transfers between devices, to_core(): return lax.ppermute(rows, 'ep', [(i, i ^ 1) for i in range(owners)])  15.4 us
    ppermute x9, starting transfers between devices, along_line(): lax.ppermute(rows, 'ep', [(i, place_of(i // 4) * 4 + i % 4) for i in rang...  12.1 us
    ppermute x8, waiting for transfers between devices, to_mid(): return lax.ppermute(rows, 'ep', [(i, i ^ 2) for i in range(owners)])  9.29 us
    ppermute x8, starting transfers between devices, to_mid(): return lax.ppermute(rows, 'ep', [(i, i ^ 2) for i in range(owners)])  6.47 us
    ppermute x23, waiting for transfers between devices, to_core(): return lax.ppermute(rows, 'ep', [(i, i ^ 1) for i in range(owners)])  6.17 us
  transfers between devices with their start and end apart: 40, of which 18 were waited for; matrix products, arithmetic and copies ran while one was open for 0% of the time, Pallas kernels for 20%

profile of v14, /device:TPU:11, one launch (start us, length us, event | category | flops | bytes accessed | tf_op | source)
XLA Modules:
  0.0 85.0 jit_solution(12845187709909680602)
XLA Ops:
  0.0 1.2 %prepare.1 = (bf16[1,32,2176]{2,1,0:T(8,128)(2,1)S(1)}, bf16[1,32,2176]{2,1,0:T(8,128)(2,1)S(1)}) custom-call(bf16[2,32,2048]{2,1,0:T(8,128)(2,1)} %hidden_ref.1, s32[2,8,32]{2,1,0:T(8,128)} %bitcast.7, s32[2,8,32]{2,1,0:T(8,128)} %bitcast.8, f32[1,2048]{1,0:T(1,128)} %bitcast.9), custom_call_target="tpu_custom_call" | custom-call | tf_op jit(solution)/shard_map/prepare/pallas_call | solution.py:27
  1.2 1.3 %collective-permute-start.2 = (bf16[1,32,2176]{2,1,0:T(8,128)(2,1)S(1)}, bf16[1,32,2176]{2,1,0:T(8,128)(2,1)S(1)}, u32[]{:S(2)}, u32[]{:S(2)}) collective-permute-start(bf16[1,32,2176]{2,1,0:T(8,128)(2,1)S(1)} %get-tuple-element.60.refs_0_), channel_id=1, source_target_pairs={{0,2},{1,3},{2,0},{3,1},{4,6},{5,7},{6,4},{7,5},{8,10},{9,11},{10,... | collective-permute-start | bytes 417800 | tf_op jit(solution)/shard_map/ppermute | solution.py:276
  2.8 1.3 %collective-permute-start = (bf16[1,32,2176]{2,1,0:T(8,128)(2,1)S(1)}, bf16[1,32,2176]{2,1,0:T(8,128)(2,1)S(1)}, u32[]{:S(2)}, u32[]{:S(2)}) collective-permute-start(bf16[1,32,2176]{2,1,0:T(8,128)(2,1)S(1)} %get-tuple-element.46.refs_0_), channel_id=1, source_target_pairs={{0,12},{1,13},{2,14},{3,15},{4,8},{5,9},{6,10},{7,11},{8,4},{9,5},... | collective-permute-start | bytes 417800 | tf_op jit(solution)/shard_map/ppermute | solution.py:267
  4.1 3.8 %load.1 = (bf16[1,2048,768]{2,1,0:T(8,128)(2,1)S(1)}, bf16[1,2048,768]{2,1,0:T(8,128)(2,1)S(1)}, bf16[1,768,2048]{2,1,0:T(8,128)(2,1)S(1)}) custom-call(bf16[1,2048,768]{2,1,0:T(8,128)(2,1)} %refs_0_.1, bf16[1,2048,768]{2,1,0:T(8,128)(2,1)} %refs_1_.1, bf16[1,768,2048]{2,1,0:T(8,128)(2,1)} %refs_2_.1), custom_call_target="tpu_custom_call" | custom-call | tf_op jit(solution)/shard_map/load/pallas_call | solution.py:27
  7.9 1.0 %collective-permute-done.1.refs_2_ = bf16[1,32,2176]{2,1,0:T(8,128)(2,1)S(1)} collective-permute-done((bf16[1,32,2176]{2,1,0:T(8,128)(2,1)S(1)}, bf16[1,32,2176]{2,1,0:T(8,128)(2,1)S(1)}, u32[]{:S(2)}, u32[]{:S(2)}) %collective-permute-start.1) | collective-permute-done | bytes 139296 | tf_op jit(solution)/shard_map/ppermute | solution.py:276
  8.8 1.6 %collective-permute-done.refs_1_ = bf16[1,32,2176]{2,1,0:T(8,128)(2,1)S(1)} collective-permute-done((bf16[1,32,2176]{2,1,0:T(8,128)(2,1)S(1)}, bf16[1,32,2176]{2,1,0:T(8,128)(2,1)S(1)}, u32[]{:S(2)}, u32[]{:S(2)}) %collective-permute-start) | collective-permute-done | bytes 139296 | tf_op jit(solution)/shard_map/ppermute | solution.py:267
  10.5 1.0 %collective-permute-start.3 = (bf16[1,32,2176]{2,1,0:T(8,128)(2,1)S(1)}, bf16[1,32,2176]{2,1,0:T(8,128)(2,1)S(1)}, u32[]{:S(2)}, u32[]{:S(2)}) collective-permute-start(bf16[1,32,2176]{2,1,0:T(8,128)(2,1)S(1)} %get-tuple-element.60.refs_0_), channel_id=1, source_target_pairs={{0,12},{1,13},{2,14},{3,15},{4,8},{5,9},{6,10},{7,11},{8,4},{9,5},... | collective-permute-start | bytes 417800 | tf_op jit(solution)/shard_map/ppermute | solution.py:267
  11.5 1.2 %collective-permute-start.5 = (bf16[1,32,2176]{2,1,0:T(8,128)(2,1)S(1)}, bf16[1,32,2176]{2,1,0:T(8,128)(2,1)S(1)}, u32[]{:S(2)}, u32[]{:S(2)}) collective-permute-start(bf16[1,32,2176]{2,1,0:T(8,128)(2,1)S(1)} %collective-permute-done.refs_1_), channel_id=1, source_target_pairs={{0,2},{1,3},{2,0},{3,1},{4,6},{5,7},{6,4},{7,5},{8,10},{9,11},{10,... | collective-permute-start | bytes 417800 | tf_op jit(solution)/shard_map/ppermute | solution.py:276
  12.7 2.9 %collective-permute-start.6 = (bf16[1,32,2176]{2,1,0:T(8,128)(2,1)S(1)}, bf16[1,32,2176]{2,1,0:T(8,128)(2,1)S(1)}, u32[]{:S(2)}, u32[]{:S(2)}) collective-permute-start(bf16[1,32,2176]{2,1,0:T(8,128)(2,1)S(1)} %get-tuple-element.46.refs_0_), channel_id=1, source_target_pairs={{0,1},{1,0},{2,3},{3,2},{4,5},{5,4},{6,7},{7,6},{8,9},{9,8},{10,11... | collective-permute-start | bytes 417800 | tf_op jit(solution)/shard_map/ppermute | solution.py:279
  15.7 1.6 %collective-permute-done.4.refs_0_ = bf16[2,32,2176]{2,1,0:T(8,128)(2,1)S(1)} collective-permute-done((bf16[2,32,2176]{2,1,0:T(8,128)(2,1)S(1)}, bf16[2,32,2176]{2,1,0:T(8,128)(2,1)S(1)}, u32[]{:S(2)}, u32[]{:S(2)}) %collective-permute-start.4) | collective-permute-done | bytes 278560 | tf_op jit(solution)/shard_map/ppermute | solution.py:267
  17.3 2.3 %collective-permute-start.13 = (bf16[2,32,2176]{2,1,0:T(8,128)(2,1)S(1)}, bf16[2,32,2176]{2,1,0:T(8,128)(2,1)S(1)}, u32[]{:S(2)}, u32[]{:S(2)}) collective-permute-start(bf16[2,32,2176]{2,1,0:T(8,128)(2,1)S(1)} %join.4), channel_id=1, source_target_pairs={{0,4},{1,5},{2,6},{3,7},{4,0},{5,1},{6,2},{7,3},{8,12},{9,13},{10,... | collective-permute-start | bytes 835592 | tf_op jit(solution)/shard_map/ppermute | solution.py:267
  19.6 1.2 %collective-permute-start.19 = (bf16[2,32,2176]{2,1,0:T(8,128)(2,1)S(1)}, bf16[2,32,2176]{2,1,0:T(8,128)(2,1)S(1)}, u32[]{:S(2)}, u32[]{:S(2)}) collective-permute-start(bf16[2,32,2176]{2,1,0:T(8,128)(2,1)S(1)} %collective-permute-done.4.refs_0_), channel_id=1, source_target_pairs={{0,2},{1,3},{2,0},{3,1},{4,6},{5,7},{6,4},{7,5},{8,10},{9,11},{10,... | collective-permute-start | bytes 835592 | tf_op jit(solution)/shard_map/ppermute | solution.py:276
  20.8 4.3 %collective-permute-start.7 = (bf16[1,32,2176]{2,1,0:T(8,128)(2,1)S(1)}, bf16[1,32,2176]{2,1,0:T(8,128)(2,1)S(1)}, u32[]{:S(2)}, u32[]{:S(2)}) collective-permute-start(bf16[1,32,2176]{2,1,0:T(8,128)(2,1)S(1)} %collective-permute-done.refs_1_), channel_id=1, source_target_pairs={{0,1},{1,0},{2,3},{3,2},{4,5},{5,4},{6,7},{7,6},{8,9},{9,8},{10,11... | collective-permute-start | bytes 417800 | tf_op jit(solution)/shard_map/ppermute | solution.py:279
  26.5 3.2 %ffn.3 = (bf16[2,2,32,2048]{3,2,1,0:T(8,128)(2,1)S(1)}, bf16[1,32,2048]{2,1,0:T(8,128)(2,1)S(1)}, bf16[1,32,2048]{2,1,0:T(8,128)(2,1)S(1)}, bf16[1,32,2048]{2,1,0:T(8,128)(2,1)S(1)}, bf16[1,32,2048]{2,1,0:T(8,128)(2,1)S(1)}) custom-call(s32[3,1,6]{2,1,0:T(1,128)S(1)} %bitcast.4, bf16[1,2048,768]{2,1,0:T(8,128)(2,1)S(1)} %get-tuple-element.38.gate_ref, ...), custom_call_target="tpu_custom_call" | custom-call | tf_op jit(solution)/shard_map/ffn/pallas_call | solution.py:27
  32.3 1.6 %collective-permute-done.18.refs_3_ = bf16[1,32,2048]{2,1,0:T(8,128)(2,1)S(1)} collective-permute-done((bf16[1,32,2048]{2,1,0:T(8,128)(2,1)S(1)}, bf16[1,32,2048]{2,1,0:T(8,128)(2,1)S(1)}, u32[]{:S(2)}, u32[]{:S(2)}) %collective-permute-start.18) | collective-permute-done | bytes 131104 | tf_op jit(solution)/shard_map/ppermute | solution.py:279
  34.2 1.0 %collective-permute-done.12.refs_6_ = bf16[1,32,2176]{2,1,0:T(8,128)(2,1)S(1)} collective-permute-done((bf16[1,32,2176]{2,1,0:T(8,128)(2,1)S(1)}, bf16[1,32,2176]{2,1,0:T(8,128)(2,1)S(1)}, u32[]{:S(2)}, u32[]{:S(2)}) %collective-permute-start.12) | collective-permute-done | bytes 139296 | tf_op jit(solution)/shard_map/ppermute | solution.py:279
  35.2 3.2 %ffn.4 = (bf16[2,2,32,2048]{3,2,1,0:T(8,128)(2,1)S(1)}, bf16[1,32,2048]{2,1,0:T(8,128)(2,1)S(1)}, bf16[1,32,2048]{2,1,0:T(8,128)(2,1)S(1)}, bf16[1,32,2048]{2,1,0:T(8,128)(2,1)S(1)}, bf16[1,32,2048]{2,1,0:T(8,128)(2,1)S(1)}) custom-call(s32[3,1,6]{2,1,0:T(1,128)S(1)} %bitcast.5, bf16[1,2048,768]{2,1,0:T(8,128)(2,1)S(1)} %get-tuple-element.38.gate_ref, ...), custom_call_target="tpu_custom_call" | custom-call | tf_op jit(solution)/shard_map/ffn/pallas_call | solution.py:27
  39.0 0.8 collective-permute-done.22.refs_4_
  40.4 1.2 %collective-permute-done.27.refs_4_ = bf16[3,32,2176]{2,1,0:T(8,128)(2,1)S(1)} collective-permute-done((bf16[3,32,2176]{2,1,0:T(8,128)(2,1)S(1)}, bf16[3,32,2176]{2,1,0:T(8,128)(2,1)S(1)}, u32[]{:S(2)}, u32[]{:S(2)}) %collective-permute-start.27) | collective-permute-done | bytes 417824 | tf_op jit(solution)/shard_map/ppermute | solution.py:276
  41.5 1.1 %collective-permute-start.28 = (bf16[3,32,2176]{2,1,0:T(8,128)(2,1)S(1)}, bf16[3,32,2176]{2,1,0:T(8,128)(2,1)S(1)}, u32[]{:S(2)}, u32[]{:S(2)}) collective-permute-start(bf16[3,32,2176]{2,1,0:T(8,128)(2,1)S(1)} %collective-permute-done.27.refs_4_), channel_id=1, source_target_pairs={{0,1},{1,0},{2,3},{3,2},{4,5},{5,4},{6,7},{7,6},{8,9},{9,8},{10,11... | collective-permute-start | bytes 1253384 | tf_op jit(solution)/shard_map/ppermute | solution.py:279
  44.5 5.7 %ffn.5 = (bf16[2,4,32,2048]{3,2,1,0:T(8,128)(2,1)S(1)}, bf16[2,32,2048]{2,1,0:T(8,128)(2,1)S(1)}, bf16[2,32,2048]{2,1,0:T(8,128)(2,1)S(1)}, bf16[2,32,2048]{2,1,0:T(8,128)(2,1)S(1)}, bf16[2,32,2048]{2,1,0:T(8,128)(2,1)S(1)}) custom-call(s32[3,1,6]{2,1,0:T(1,128)S(1)} %bitcast.6, bf16[1,2048,768]{2,1,0:T(8,128)(2,1)S(1)} %get-tuple-element.38.gate_ref, ...), custom_call_target="tpu_custom_call" | custom-call | tf_op jit(solution)/shard_map/ffn/pallas_call | solution.py:27
  51.9 1.3 %collective-permute-start.36 = (bf16[2,32,2048]{2,1,0:T(8,128)(2,1)S(1)}, bf16[2,32,2048]{2,1,0:T(8,128)(2,1)S(1)}, u32[]{:S(2)}, u32[]{:S(2)}) collective-permute-start(bf16[2,32,2048]{2,1,0:T(8,128)(2,1)S(1)} %total.8), channel_id=1, source_target_pairs={{0,2},{1,3},{2,0},{3,1},{4,6},{5,7},{6,4},{7,5},{8,10},{9,11},{10,... | collective-permute-start | bytes 786440 | tf_op jit(solution)/shard_map/ppermute | solution.py:276
  53.2 3.0 %collective-permute-done.24.refs_3_.refs_2_ = bf16[4,32,2048]{2,1,0:T(8,128)(2,1)S(1)} collective-permute-done((bf16[4,32,2048]{2,1,0:T(8,128)(2,1)S(1)}, bf16[4,32,2048]{2,1,0:T(8,128)(2,1)S(1)}, u32[]{:S(2)}, u32[]{:S(2)}) %collective-permute-start.24) | collective-permute-done | bytes 524320 | tf_op jit(solution)/shard_map/ppermute | solution.py:276
  57.1 1.7 %collective-permute-start.32 = (bf16[2,32,2048]{2,1,0:T(8,128)(2,1)S(1)}, bf16[2,32,2048]{2,1,0:T(8,128)(2,1)S(1)}, u32[]{:S(2)}, u32[]{:S(2)}) collective-permute-start(bf16[2,32,2048]{2,1,0:T(8,128)(2,1)S(1)} %get-tuple-element.65), channel_id=1, source_target_pairs={{0,1},{1,0},{2,3},{3,2},{4,5},{5,4},{6,7},{7,6},{8,9},{9,8},{10,11... | collective-permute-start | bytes 786440 | tf_op jit(solution)/shard_map/ppermute | solution.py:279
  58.9 3.0 %collective-permute-done.36.refs_2_ = bf16[2,32,2048]{2,1,0:T(8,128)(2,1)S(1)} collective-permute-done((bf16[2,32,2048]{2,1,0:T(8,128)(2,1)S(1)}, bf16[2,32,2048]{2,1,0:T(8,128)(2,1)S(1)}, u32[]{:S(2)}, u32[]{:S(2)}) %collective-permute-start.36) | collective-permute-done | bytes 262176 | tf_op jit(solution)/shard_map/ppermute | solution.py:276
  62.0 4.1 %collective-permute-start.39 = (bf16[1,32,2048]{2,1,0:T(8,128)(2,1)S(1)}, bf16[1,32,2048]{2,1,0:T(8,128)(2,1)S(1)}, u32[]{:S(2)}, u32[]{:S(2)}) collective-permute-start(bf16[1,32,2048]{2,1,0:T(8,128)(2,1)S(1)} %get-tuple-element.69), channel_id=1, source_target_pairs={{0,8},{1,9},{2,10},{3,11},{4,12},{5,13},{6,14},{7,15},{8,0},{9,1},... | collective-permute-start | bytes 393224 | tf_op jit(solution)/shard_map/ppermute | solution.py:267
  66.2 1.2 %collective-permute-done.34.refs_2_.refs_7_ = bf16[2,32,2048]{2,1,0:T(8,128)(2,1)S(1)} collective-permute-done((bf16[2,32,2048]{2,1,0:T(8,128)(2,1)S(1)}, bf16[2,32,2048]{2,1,0:T(8,128)(2,1)S(1)}, u32[]{:S(2)}, u32[]{:S(2)}) %collective-permute-start.34) | collective-permute-done | bytes 262176 | tf_op jit(solution)/shard_map/ppermute | solution.py:276
  67.5 3.0 %collective-permute-start.37 = (bf16[1,32,2048]{2,1,0:T(8,128)(2,1)S(1)}, bf16[1,32,2048]{2,1,0:T(8,128)(2,1)S(1)}, u32[]{:S(2)}, u32[]{:S(2)}) collective-permute-start(bf16[1,32,2048]{2,1,0:T(8,128)(2,1)S(1)} %total.13), channel_id=1, source_target_pairs={{0,12},{1,13},{2,14},{3,15},{4,8},{5,9},{6,10},{7,11},{8,4},{9,5},... | collective-permute-start | bytes 393224 | tf_op jit(solution)/shard_map/ppermute | solution.py:267
  70.6 6.8 %collective-permute-done.39.refs_10_ = bf16[1,32,2048]{2,1,0:T(8,128)(2,1)S(1)} collective-permute-done((bf16[1,32,2048]{2,1,0:T(8,128)(2,1)S(1)}, bf16[1,32,2048]{2,1,0:T(8,128)(2,1)S(1)}, u32[]{:S(2)}, u32[]{:S(2)}) %collective-permute-start.39) | collective-permute-done | bytes 131104 | tf_op jit(solution)/shard_map/ppermute | solution.py:267
  77.4 3.9 %collective-permute-done.37.refs_8_ = bf16[1,32,2048]{2,1,0:T(8,128)(2,1)S(1)} collective-permute-done((bf16[1,32,2048]{2,1,0:T(8,128)(2,1)S(1)}, bf16[1,32,2048]{2,1,0:T(8,128)(2,1)S(1)}, u32[]{:S(2)}, u32[]{:S(2)}) %collective-permute-start.37) | collective-permute-done | bytes 131104 | tf_op jit(solution)/shard_map/ppermute | solution.py:267
  81.3 2.8 %collective-permute-done.31.refs_4_ = bf16[1,32,2048]{2,1,0:T(8,128)(2,1)S(1)} collective-permute-done((bf16[1,32,2048]{2,1,0:T(8,128)(2,1)S(1)}, bf16[1,32,2048]{2,1,0:T(8,128)(2,1)S(1)}, u32[]{:S(2)}, u32[]{:S(2)}) %collective-permute-start.31) | collective-permute-done | bytes 131104 | tf_op jit(solution)/shard_map/ppermute | solution.py:267
  84.1 0.9 %finish.1 = bf16[2,32,2048]{2,1,0:T(8,128)(2,1)} custom-call(bf16[2,32,2048]{2,1,0:T(8,128)(2,1)S(1)} %copy-done, bf16[2,2,32,2048]{3,2,1,0:T(8,128)(2,1)S(1)} %get-tuple-element.47.refs_0_, bf16[1,32,2048]{2,1,0:T(8,128)(2,1)S(1)} %collective-permute-done.10.refs_1_, bf16[4,32,2048]{2,1,0:T(8,128)(2,1)S(1)} %collective-permute-done.24.refs_3_.refs_2_, ...), custom_call_target="tpu_custom_call" | custom-call | tf_op jit(solution)/shard_map/finish/pallas_call | solution.py:27
  (68 shorter events, 10.4 us)
Async XLA Ops:
  1.2 6.6 %collective-permute-start.2 = (bf16[1,32,2176]{2,1,0:T(8,128)(2,1)S(1)}, bf16[1,32,2176]{2,1,0:T(8,128)(2,1)S(1)}, u32[]{:S(2)}, u32[]{:S(2)}) collective-permute-start(bf16[1,32,2176]{2,1,0:T(8,128)(2,1)S(1)} %get-tuple-element.60.refs_0_), channel_id=1, source_target_pairs={{0,2},{1,3},{2,0},{3,1},{4,6},{5,7},{6,4},{7,5},{8,10},{9,11},{10,... | collective-permute-start | bytes 417800 | tf_op jit(solution)/shard_map/ppermute | solution.py:276
  2.5 6.3 %collective-permute-start.1 = (bf16[1,32,2176]{2,1,0:T(8,128)(2,1)S(1)}, bf16[1,32,2176]{2,1,0:T(8,128)(2,1)S(1)}, u32[]{:S(2)}, u32[]{:S(2)}) collective-permute-start(bf16[1,32,2176]{2,1,0:T(8,128)(2,1)S(1)} %get-tuple-element.46.refs_0_), channel_id=1, source_target_pairs={{0,2},{1,3},{2,0},{3,1},{4,6},{5,7},{6,4},{7,5},{8,10},{9,11},{10,... | collective-permute-start | bytes 417800 | tf_op jit(solution)/shard_map/ppermute | solution.py:276
  2.8 7.7 %collective-permute-start = (bf16[1,32,2176]{2,1,0:T(8,128)(2,1)S(1)}, bf16[1,32,2176]{2,1,0:T(8,128)(2,1)S(1)}, u32[]{:S(2)}, u32[]{:S(2)}) collective-permute-start(bf16[1,32,2176]{2,1,0:T(8,128)(2,1)S(1)} %get-tuple-element.46.refs_0_), channel_id=1, source_target_pairs={{0,12},{1,13},{2,14},{3,15},{4,8},{5,9},{6,10},{7,11},{8,4},{9,5},... | collective-permute-start | bytes 417800 | tf_op jit(solution)/shard_map/ppermute | solution.py:267
  10.4 6.8 %collective-permute-start.4 = (bf16[2,32,2176]{2,1,0:T(8,128)(2,1)S(1)}, bf16[2,32,2176]{2,1,0:T(8,128)(2,1)S(1)}, u32[]{:S(2)}, u32[]{:S(2)}) collective-permute-start(bf16[2,32,2176]{2,1,0:T(8,128)(2,1)S(1)} %join.3), channel_id=1, source_target_pairs={{0,4},{1,5},{2,6},{3,7},{4,0},{5,1},{6,2},{7,3},{8,12},{9,13},{10,... | collective-permute-start | bytes 835592 | tf_op jit(solution)/shard_map/ppermute | solution.py:267
  10.5 5.2 %collective-permute-start.3 = (bf16[1,32,2176]{2,1,0:T(8,128)(2,1)S(1)}, bf16[1,32,2176]{2,1,0:T(8,128)(2,1)S(1)}, u32[]{:S(2)}, u32[]{:S(2)}) collective-permute-start(bf16[1,32,2176]{2,1,0:T(8,128)(2,1)S(1)} %get-tuple-element.60.refs_0_), channel_id=1, source_target_pairs={{0,12},{1,13},{2,14},{3,15},{4,8},{5,9},{6,10},{7,11},{8,4},{9,5},... | collective-permute-start | bytes 417800 | tf_op jit(solution)/shard_map/ppermute | solution.py:267
  11.5 5.8 %collective-permute-start.5 = (bf16[1,32,2176]{2,1,0:T(8,128)(2,1)S(1)}, bf16[1,32,2176]{2,1,0:T(8,128)(2,1)S(1)}, u32[]{:S(2)}, u32[]{:S(2)}) collective-permute-start(bf16[1,32,2176]{2,1,0:T(8,128)(2,1)S(1)} %collective-permute-done.refs_1_), channel_id=1, source_target_pairs={{0,2},{1,3},{2,0},{3,1},{4,6},{5,7},{6,4},{7,5},{8,10},{9,11},{10,... | collective-permute-start | bytes 417800 | tf_op jit(solution)/shard_map/ppermute | solution.py:276
  12.7 12.4 %collective-permute-start.6 = (bf16[1,32,2176]{2,1,0:T(8,128)(2,1)S(1)}, bf16[1,32,2176]{2,1,0:T(8,128)(2,1)S(1)}, u32[]{:S(2)}, u32[]{:S(2)}) collective-permute-start(bf16[1,32,2176]{2,1,0:T(8,128)(2,1)S(1)} %get-tuple-element.46.refs_0_), channel_id=1, source_target_pairs={{0,1},{1,0},{2,3},{3,2},{4,5},{5,4},{6,7},{7,6},{8,9},{9,8},{10,11... | collective-permute-start | bytes 417800 | tf_op jit(solution)/shard_map/ppermute | solution.py:279
  15.7 9.4 %collective-permute-start.8 = (bf16[1,32,2176]{2,1,0:T(8,128)(2,1)S(1)}, bf16[1,32,2176]{2,1,0:T(8,128)(2,1)S(1)}, u32[]{:S(2)}, u32[]{:S(2)}) collective-permute-start(bf16[1,32,2176]{2,1,0:T(8,128)(2,1)S(1)} %collective-permute-done.1.refs_2_), channel_id=1, source_target_pairs={{0,1},{1,0},{2,3},{3,2},{4,5},{5,4},{6,7},{7,6},{8,9},{9,8},{10,11... | collective-permute-start | bytes 417800 | tf_op jit(solution)/shard_map/ppermute | solution.py:279
  17.3 13.0 %collective-permute-start.13 = (bf16[2,32,2176]{2,1,0:T(8,128)(2,1)S(1)}, bf16[2,32,2176]{2,1,0:T(8,128)(2,1)S(1)}, u32[]{:S(2)}, u32[]{:S(2)}) collective-permute-start(bf16[2,32,2176]{2,1,0:T(8,128)(2,1)S(1)} %join.4), channel_id=1, source_target_pairs={{0,4},{1,5},{2,6},{3,7},{4,0},{5,1},{6,2},{7,3},{8,12},{9,13},{10,... | collective-permute-start | bytes 835592 | tf_op jit(solution)/shard_map/ppermute | solution.py:267
  19.6 10.9 %collective-permute-start.19 = (bf16[2,32,2176]{2,1,0:T(8,128)(2,1)S(1)}, bf16[2,32,2176]{2,1,0:T(8,128)(2,1)S(1)}, u32[]{:S(2)}, u32[]{:S(2)}) collective-permute-start(bf16[2,32,2176]{2,1,0:T(8,128)(2,1)S(1)} %collective-permute-done.4.refs_0_), channel_id=1, source_target_pairs={{0,2},{1,3},{2,0},{3,1},{4,6},{5,7},{6,4},{7,5},{8,10},{9,11},{10,... | collective-permute-start | bytes 835592 | tf_op jit(solution)/shard_map/ppermute | solution.py:276
  20.8 5.3 %collective-permute-start.7 = (bf16[1,32,2176]{2,1,0:T(8,128)(2,1)S(1)}, bf16[1,32,2176]{2,1,0:T(8,128)(2,1)S(1)}, u32[]{:S(2)}, u32[]{:S(2)}) collective-permute-start(bf16[1,32,2176]{2,1,0:T(8,128)(2,1)S(1)} %collective-permute-done.refs_1_), channel_id=1, source_target_pairs={{0,1},{1,0},{2,3},{3,2},{4,5},{5,4},{6,7},{7,6},{8,9},{9,8},{10,11... | collective-permute-start | bytes 417800 | tf_op jit(solution)/shard_map/ppermute | solution.py:279
  25.1 4.9 %collective-permute-start.15 = (bf16[1,32,2176]{2,1,0:T(8,128)(2,1)S(1)}, bf16[1,32,2176]{2,1,0:T(8,128)(2,1)S(1)}, u32[]{:S(2)}, u32[]{:S(2)}) collective-permute-start(bf16[1,32,2176]{2,1,0:T(8,128)(2,1)S(1)} %collective-permute-done.2.refs_3_), channel_id=1, source_target_pairs={{0,1},{1,0},{2,3},{3,2},{4,5},{5,4},{6,7},{7,6},{8,9},{9,8},{10,11... | collective-permute-start | bytes 417800 | tf_op jit(solution)/shard_map/ppermute | solution.py:279
  26.1 4.7 %collective-permute-start.11 = (bf16[1,32,2176]{2,1,0:T(8,128)(2,1)S(1)}, bf16[1,32,2176]{2,1,0:T(8,128)(2,1)S(1)}, u32[]{:S(2)}, u32[]{:S(2)}) collective-permute-start(bf16[1,32,2176]{2,1,0:T(8,128)(2,1)S(1)} %get-tuple-element.60.refs_0_), channel_id=1, source_target_pairs={{0,1},{1,0},{2,3},{3,2},{4,5},{5,4},{6,7},{7,6},{8,9},{9,8},{10,11... | collective-permute-start | bytes 417800 | tf_op jit(solution)/shard_map/ppermute | solution.py:279
  29.7 1.9 %collective-permute-start.10 = (bf16[1,32,2048]{2,1,0:T(8,128)(2,1)S(1)}, bf16[1,32,2048]{2,1,0:T(8,128)(2,1)S(1)}, u32[]{:S(2)}, u32[]{:S(2)}) collective-permute-start(bf16[1,32,2048]{2,1,0:T(8,128)(2,1)S(1)} %get-tuple-element.48), channel_id=1, source_target_pairs={{0,1},{1,0},{2,3},{3,2},{4,5},{5,4},{6,7},{7,6},{8,9},{9,8},{10,11... | collective-permute-start | bytes 393224 | tf_op jit(solution)/shard_map/ppermute | solution.py:279
  30.0 1.8 %collective-permute-start.16 = (bf16[1,32,2048]{2,1,0:T(8,128)(2,1)S(1)}, bf16[1,32,2048]{2,1,0:T(8,128)(2,1)S(1)}, u32[]{:S(2)}, u32[]{:S(2)}) collective-permute-start(bf16[1,32,2048]{2,1,0:T(8,128)(2,1)S(1)} %get-tuple-element.50), channel_id=1, source_target_pairs={{0,1},{1,0},{2,3},{3,2},{4,5},{5,4},{6,7},{7,6},{8,9},{9,8},{10,11... | collective-permute-start | bytes 393224 | tf_op jit(solution)/shard_map/ppermute | solution.py:279
  30.3 1.9 %collective-permute-start.17 = (bf16[1,32,2048]{2,1,0:T(8,128)(2,1)S(1)}, bf16[1,32,2048]{2,1,0:T(8,128)(2,1)S(1)}, u32[]{:S(2)}, u32[]{:S(2)}) collective-permute-start(bf16[1,32,2048]{2,1,0:T(8,128)(2,1)S(1)} %get-tuple-element.51), channel_id=1, source_target_pairs={{0,1},{1,0},{2,3},{3,2},{4,5},{5,4},{6,7},{7,6},{8,9},{9,8},{10,11... | collective-permute-start | bytes 393224 | tf_op jit(solution)/shard_map/ppermute | solution.py:279
  30.5 11.0 %collective-permute-start.27 = (bf16[3,32,2176]{2,1,0:T(8,128)(2,1)S(1)}, bf16[3,32,2176]{2,1,0:T(8,128)(2,1)S(1)}, u32[]{:S(2)}, u32[]{:S(2)}) collective-permute-start(bf16[3,32,2176]{2,1,0:T(8,128)(2,1)S(1)} %join.5), channel_id=1, source_target_pairs={{0,2},{1,3},{2,0},{3,1},{4,6},{5,7},{6,4},{7,5},{8,10},{9,11},{10,... | collective-permute-start | bytes 1253384 | tf_op jit(solution)/shard_map/ppermute | solution.py:276
  30.8 4.4 %collective-permute-start.14 = (bf16[2,32,2176]{2,1,0:T(8,128)(2,1)S(1)}, bf16[2,32,2176]{2,1,0:T(8,128)(2,1)S(1)}, u32[]{:S(2)}, u32[]{:S(2)}) collective-permute-start(bf16[2,32,2176]{2,1,0:T(8,128)(2,1)S(1)} %collective-permute-done.13.refs_1_.refs_2_), channel_id=1, source_target_pairs={{0,1},{1,0},{2,3},{3,2},{4,5},{5,4},{6,7},{7,6},{8,9},{9,8},{10,11... | collective-permute-start | bytes 835592 | tf_op jit(solution)/shard_map/ppermute | solution.py:279
  31.7 3.5 %collective-permute-start.20 = (bf16[2,32,2176]{2,1,0:T(8,128)(2,1)S(1)}, bf16[2,32,2176]{2,1,0:T(8,128)(2,1)S(1)}, u32[]{:S(2)}, u32[]{:S(2)}) collective-permute-start(bf16[2,32,2176]{2,1,0:T(8,128)(2,1)S(1)} %collective-permute-done.4.refs_0_), channel_id=1, source_target_pairs={{0,1},{1,0},{2,3},{3,2},{4,5},{5,4},{6,7},{7,6},{8,9},{9,8},{10,11... | collective-permute-start | bytes 835592 | tf_op jit(solution)/shard_map/ppermute | solution.py:279
  31.7 3.5 %collective-permute-start.21 = (bf16[2,32,2176]{2,1,0:T(8,128)(2,1)S(1)}, bf16[2,32,2176]{2,1,0:T(8,128)(2,1)S(1)}, u32[]{:S(2)}, u32[]{:S(2)}) collective-permute-start(bf16[2,32,2176]{2,1,0:T(8,128)(2,1)S(1)} %collective-permute-done.19.refs_1_), channel_id=1, source_target_pairs={{0,1},{1,0},{2,3},{3,2},{4,5},{5,4},{6,7},{7,6},{8,9},{9,8},{10,11... | collective-permute-start | bytes 835592 | tf_op jit(solution)/shard_map/ppermute | solution.py:279
  41.5 3.0 %collective-permute-start.28 = (bf16[3,32,2176]{2,1,0:T(8,128)(2,1)S(1)}, bf16[3,32,2176]{2,1,0:T(8,128)(2,1)S(1)}, u32[]{:S(2)}, u32[]{:S(2)}) collective-permute-start(bf16[3,32,2176]{2,1,0:T(8,128)(2,1)S(1)} %collective-permute-done.27.refs_4_), channel_id=1, source_target_pairs={{0,1},{1,0},{2,3},{3,2},{4,5},{5,4},{6,7},{7,6},{8,9},{9,8},{10,11... | collective-permute-start | bytes 1253384 | tf_op jit(solution)/shard_map/ppermute | solution.py:279
  42.7 13.6 %collective-permute-start.24 = (bf16[4,32,2048]{2,1,0:T(8,128)(2,1)S(1)}, bf16[4,32,2048]{2,1,0:T(8,128)(2,1)S(1)}, u32[]{:S(2)}, u32[]{:S(2)}) collective-permute-start(bf16[4,32,2048]{2,1,0:T(8,128)(2,1)S(1)} %total.7), channel_id=1, source_target_pairs={{0,2},{1,3},{2,0},{3,1},{4,6},{5,7},{6,4},{7,5},{8,10},{9,11},{10,... | collective-permute-start | bytes 1572872 | tf_op jit(solution)/shard_map/ppermute | solution.py:276
  50.6 5.8 %collective-permute-start.33 = (bf16[2,32,2048]{2,1,0:T(8,128)(2,1)S(1)}, bf16[2,32,2048]{2,1,0:T(8,128)(2,1)S(1)}, u32[]{:S(2)}, u32[]{:S(2)}) collective-permute-start(bf16[2,32,2048]{2,1,0:T(8,128)(2,1)S(1)} %get-tuple-element.66), channel_id=1, source_target_pairs={{0,1},{1,0},{2,3},{3,2},{4,5},{5,4},{6,7},{7,6},{8,9},{9,8},{10,11... | collective-permute-start | bytes 786440 | tf_op jit(solution)/shard_map/ppermute | solution.py:279
  50.9 8.0 %collective-permute-start.35 = (bf16[2,32,2048]{2,1,0:T(8,128)(2,1)S(1)}, bf16[2,32,2048]{2,1,0:T(8,128)(2,1)S(1)}, u32[]{:S(2)}, u32[]{:S(2)}) collective-permute-start(bf16[2,32,2048]{2,1,0:T(8,128)(2,1)S(1)} %get-tuple-element.67), channel_id=1, source_target_pairs={{0,1},{1,0},{2,3},{3,2},{4,5},{5,4},{6,7},{7,6},{8,9},{9,8},{10,11... | collective-permute-start | bytes 786440 | tf_op jit(solution)/shard_map/ppermute | solution.py:279
  51.9 9.9 %collective-permute-start.36 = (bf16[2,32,2048]{2,1,0:T(8,128)(2,1)S(1)}, bf16[2,32,2048]{2,1,0:T(8,128)(2,1)S(1)}, u32[]{:S(2)}, u32[]{:S(2)}) collective-permute-start(bf16[2,32,2048]{2,1,0:T(8,128)(2,1)S(1)} %total.8), channel_id=1, source_target_pairs={{0,2},{1,3},{2,0},{3,1},{4,6},{5,7},{6,4},{7,5},{8,10},{9,11},{10,... | collective-permute-start | bytes 786440 | tf_op jit(solution)/shard_map/ppermute | solution.py:276
  56.3 9.8 %collective-permute-start.30 = (bf16[2,32,2048]{2,1,0:T(8,128)(2,1)S(1)}, bf16[2,32,2048]{2,1,0:T(8,128)(2,1)S(1)}, u32[]{:S(2)}, u32[]{:S(2)}) collective-permute-start(bf16[2,32,2048]{2,1,0:T(8,128)(2,1)S(1)} %total.9), channel_id=1, source_target_pairs={{0,4},{1,5},{2,6},{3,7},{4,0},{5,1},{6,2},{7,3},{8,12},{9,13},{10,... | collective-permute-start | bytes 786440 | tf_op jit(solution)/shard_map/ppermute | solution.py:267
  56.5 11.0 %collective-permute-start.34 = (bf16[2,32,2048]{2,1,0:T(8,128)(2,1)S(1)}, bf16[2,32,2048]{2,1,0:T(8,128)(2,1)S(1)}, u32[]{:S(2)}, u32[]{:S(2)}) collective-permute-start(bf16[2,32,2048]{2,1,0:T(8,128)(2,1)S(1)} %total.11), channel_id=1, source_target_pairs={{0,2},{1,3},{2,0},{3,1},{4,6},{5,7},{6,4},{7,5},{8,10},{9,11},{10,... | collective-permute-start | bytes 786440 | tf_op jit(solution)/shard_map/ppermute | solution.py:276
  57.1 10.3 %collective-permute-start.32 = (bf16[2,32,2048]{2,1,0:T(8,128)(2,1)S(1)}, bf16[2,32,2048]{2,1,0:T(8,128)(2,1)S(1)}, u32[]{:S(2)}, u32[]{:S(2)}) collective-permute-start(bf16[2,32,2048]{2,1,0:T(8,128)(2,1)S(1)} %get-tuple-element.65), channel_id=1, source_target_pairs={{0,1},{1,0},{2,3},{3,2},{4,5},{5,4},{6,7},{7,6},{8,9},{9,8},{10,11... | collective-permute-start | bytes 786440 | tf_op jit(solution)/shard_map/ppermute | solution.py:279
  61.9 8.7 %collective-permute-start.38 = (bf16[1,32,2048]{2,1,0:T(8,128)(2,1)S(1)}, bf16[1,32,2048]{2,1,0:T(8,128)(2,1)S(1)}, u32[]{:S(2)}, u32[]{:S(2)}) collective-permute-start(bf16[1,32,2048]{2,1,0:T(8,128)(2,1)S(1)} %get-tuple-element.68), channel_id=1, source_target_pairs={{0,4},{1,5},{2,6},{3,7},{4,0},{5,1},{6,2},{7,3},{8,12},{9,13},{10,... | collective-permute-start | bytes 393224 | tf_op jit(solution)/shard_map/ppermute | solution.py:267
  62.0 15.4 %collective-permute-start.39 = (bf16[1,32,2048]{2,1,0:T(8,128)(2,1)S(1)}, bf16[1,32,2048]{2,1,0:T(8,128)(2,1)S(1)}, u32[]{:S(2)}, u32[]{:S(2)}) collective-permute-start(bf16[1,32,2048]{2,1,0:T(8,128)(2,1)S(1)} %get-tuple-element.69), channel_id=1, source_target_pairs={{0,8},{1,9},{2,10},{3,11},{4,12},{5,13},{6,14},{7,15},{8,0},{9,1},... | collective-permute-start | bytes 393224 | tf_op jit(solution)/shard_map/ppermute | solution.py:267
  67.5 13.8 %collective-permute-start.37 = (bf16[1,32,2048]{2,1,0:T(8,128)(2,1)S(1)}, bf16[1,32,2048]{2,1,0:T(8,128)(2,1)S(1)}, u32[]{:S(2)}, u32[]{:S(2)}) collective-permute-start(bf16[1,32,2048]{2,1,0:T(8,128)(2,1)S(1)} %total.13), channel_id=1, source_target_pairs={{0,12},{1,13},{2,14},{3,15},{4,8},{5,9},{6,10},{7,11},{8,4},{9,5},... | collective-permute-start | bytes 393224 | tf_op jit(solution)/shard_map/ppermute | solution.py:267
  70.6 13.6 %collective-permute-start.31 = (bf16[1,32,2048]{2,1,0:T(8,128)(2,1)S(1)}, bf16[1,32,2048]{2,1,0:T(8,128)(2,1)S(1)}, u32[]{:S(2)}, u32[]{:S(2)}) collective-permute-start(bf16[1,32,2048]{2,1,0:T(8,128)(2,1)S(1)} %total.10), channel_id=1, source_target_pairs={{0,12},{1,13},{2,14},{3,15},{4,8},{5,9},{6,10},{7,11},{8,4},{9,5},... | collective-permute-start | bytes 393224 | tf_op jit(solution)/shard_map/ppermute | solution.py:267
  (10 other events, 63.2 us)

commit v15 on v13

--- a/solution.py
+++ b/solution.py
@@ -281,14 +281,6 @@
     spans = []
     while line >> len(spans) > 2:
         spans.append(line >> len(spans))
-
-    def owner_of(p, piece):
-        if piece >= half:
-            p, piece = mirrored(p, 2), piece - half
-        for level in range(len(spans), 0, -1):
-            if piece >= 1 << (level - 1):
-                p, piece = mirrored(p, spans[level - 1]), piece - (1 << (level - 1))
-        return p
 
     payload = prepare(hidden_in, expert_ids, route_share, norm_gain, -(-owners // LANES) * LANES)
 
@@ -354,18 +346,11 @@
         mixed = terms[batch]
         if batch + 1 < batches:
             mixed[-1] = (None, [after(back[batch][0], sent[-1])])
-            mixed.append((None, [mirror(total(mixed, [(half, line)])[0], 2)]))
-            span, pieces = 4, half
-            while pieces > 1:
-                mixed.append((None, [mirror(total(mixed, [(pieces // 2, pieces)])[0], span)]))
-                span, pieces = span * 2, pieces // 2
-        else:
-            far_parts = total(mixed, [(j, j + 1) for j in range(half, line)])
-            mixed[-1] = (None, [after(mixed[-1][1][0], *far_parts), *mixed[-1][1][1:]])
-            parts = total(mixed, [(j, j + 1) for j in range(1, half)]) + far_parts
-            mixed += [
-                (None, [along_line(part, lambda p, j=j: owner_of(p, j))]) for j, part in enumerate(parts, 1)
-            ]
+        mixed.append((None, [mirror(total(mixed, [(half, line)])[0], 2)]))
+        span, pieces = 4, half
+        while pieces > 1:
+            mixed.append((None, [mirror(total(mixed, [(pieces // 2, pieces)])[0], span)]))
+            span, pieces = span * 2, pieces // 2
     return finish(hidden_in, terms)
 
 

time: 85.2 us -> 83.1 us (0.975)
  the two profiles are of different devices: /device:TPU:11 before, /device:TPU:0 now
where the time goes in v15:
time: 83.1 us; the launch traced here: 82.9 us
  starting transfers between devices  38.5 us (46%)
  waiting for transfers between devices  25.5 us (31%)
  Pallas kernels  18.8 us (23%)
    ppermute x8, starting transfers between devices, along_line(): lax.ppermute(rows, 'ep', [(i, place_of(i // 4) * 4 + i % 4) for i in rang...  23.4 us
    pallas_call x16, Pallas kernels, call(): pl.pallas_call(kernel, out_shape=shapes, in_specs=specs, out_specs=[VMEM]...  18.8 us
    ppermute x8, waiting for transfers between devices, along_line(): lax.ppermute(rows, 'ep', [(i, place_of(i // 4) * 4 + i % 4) for i in rang...  10.1 us
    ppermute x8, starting transfers between devices, to_mid(): return lax.ppermute(rows, 'ep', [(i, i ^ 2) for i in range(owners)])  9.86 us
    ppermute x8, waiting for transfers between devices, to_mid(): return lax.ppermute(rows, 'ep', [(i, i ^ 2) for i in range(owners)])  9.44 us
    ppermute x23, waiting for transfers between devices, to_core(): return lax.ppermute(rows, 'ep', [(i, i ^ 1) for i in range(owners)])  5.99 us
    ppermute x23, starting transfers between devices, to_core(): return lax.ppermute(rows, 'ep', [(i, i ^ 1) for i in range(owners)])  5.18 us
  transfers between devices with their start and end apart: 39, of which 17 were waited for; matrix products, arithmetic and copies ran while one was open for 0% of the time, Pallas kernels for 20%

profile of v15, /device:TPU:0, one launch (start us, length us, event | category | flops | bytes accessed | tf_op | source)
XLA Modules:
  0.0 82.9 jit_solution(3531893237289020990)
XLA Ops:
  0.0 1.2 %prepare.1 = (bf16[1,32,2176]{2,1,0:T(8,128)(2,1)S(1)}, bf16[1,32,2176]{2,1,0:T(8,128)(2,1)S(1)}) custom-call(bf16[2,32,2048]{2,1,0:T(8,128)(2,1)} %hidden_ref.1, s32[2,8,32]{2,1,0:T(8,128)} %bitcast.7, s32[2,8,32]{2,1,0:T(8,128)} %bitcast.8, f32[1,2048]{1,0:T(1,128)} %bitcast.9), custom_call_target="tpu_custom_call" | custom-call | tf_op jit(solution)/shard_map/prepare/pallas_call | solution.py:27
  1.2 3.0 %collective-permute-start.2 = (bf16[1,32,2176]{2,1,0:T(8,128)(2,1)S(1)}, bf16[1,32,2176]{2,1,0:T(8,128)(2,1)S(1)}, u32[]{:S(2)}, u32[]{:S(2)}) collective-permute-start(bf16[1,32,2176]{2,1,0:T(8,128)(2,1)S(1)} %get-tuple-element.57.refs_0_), channel_id=1, source_target_pairs={{0,2},{1,3},{2,0},{3,1},{4,6},{5,7},{6,4},{7,5},{8,10},{9,11},{10,... | collective-permute-start | bytes 417800 | tf_op jit(solution)/shard_map/ppermute | solution.py:276
  4.4 4.0 %collective-permute-start = (bf16[1,32,2176]{2,1,0:T(8,128)(2,1)S(1)}, bf16[1,32,2176]{2,1,0:T(8,128)(2,1)S(1)}, u32[]{:S(2)}, u32[]{:S(2)}) collective-permute-start(bf16[1,32,2176]{2,1,0:T(8,128)(2,1)S(1)} %get-tuple-element.43.refs_0_), channel_id=1, source_target_pairs={{0,12},{1,13},{2,14},{3,15},{4,8},{5,9},{6,10},{7,11},{8,4},{9,5},... | collective-permute-start | bytes 417800 | tf_op jit(solution)/shard_map/ppermute | solution.py:267
  8.4 3.8 %load.1 = (bf16[1,2048,768]{2,1,0:T(8,128)(2,1)S(1)}, bf16[1,2048,768]{2,1,0:T(8,128)(2,1)S(1)}, bf16[1,768,2048]{2,1,0:T(8,128)(2,1)S(1)}) custom-call(bf16[1,2048,768]{2,1,0:T(8,128)(2,1)} %refs_0_.1, bf16[1,2048,768]{2,1,0:T(8,128)(2,1)} %refs_1_.1, bf16[1,768,2048]{2,1,0:T(8,128)(2,1)} %refs_2_.1), custom_call_target="tpu_custom_call" | custom-call | tf_op jit(solution)/shard_map/load/pallas_call | solution.py:27
  12.2 2.1 %collective-permute-start.4 = (bf16[2,32,2176]{2,1,0:T(8,128)(2,1)S(1)}, bf16[2,32,2176]{2,1,0:T(8,128)(2,1)S(1)}, u32[]{:S(2)}, u32[]{:S(2)}) collective-permute-start(bf16[2,32,2176]{2,1,0:T(8,128)(2,1)S(1)} %join.3), channel_id=1, source_target_pairs={{0,4},{1,5},{2,6},{3,7},{4,0},{5,1},{6,2},{7,3},{8,12},{9,13},{10,... | collective-permute-start | bytes 835592 | tf_op jit(solution)/shard_map/ppermute | solution.py:267
  14.3 2.7 %collective-permute-start.3 = (bf16[1,32,2176]{2,1,0:T(8,128)(2,1)S(1)}, bf16[1,32,2176]{2,1,0:T(8,128)(2,1)S(1)}, u32[]{:S(2)}, u32[]{:S(2)}) collective-permute-start(bf16[1,32,2176]{2,1,0:T(8,128)(2,1)S(1)} %get-tuple-element.57.refs_0_), channel_id=1, source_target_pairs={{0,12},{1,13},{2,14},{3,15},{4,8},{5,9},{6,10},{7,11},{8,4},{9,5},... | collective-permute-start | bytes 417800 | tf_op jit(solution)/shard_map/ppermute | solution.py:267
  17.0 1.5 %collective-permute-start.5 = (bf16[1,32,2176]{2,1,0:T(8,128)(2,1)S(1)}, bf16[1,32,2176]{2,1,0:T(8,128)(2,1)S(1)}, u32[]{:S(2)}, u32[]{:S(2)}) collective-permute-start(bf16[1,32,2176]{2,1,0:T(8,128)(2,1)S(1)} %collective-permute-done.refs_1_), channel_id=1, source_target_pairs={{0,2},{1,3},{2,0},{3,1},{4,6},{5,7},{6,4},{7,5},{8,10},{9,11},{10,... | collective-permute-start | bytes 417800 | tf_op jit(solution)/shard_map/ppermute | solution.py:276
  19.0 4.8 %collective-permute-done.3.refs_1_.refs_0_ = bf16[1,32,2176]{2,1,0:T(8,128)(2,1)S(1)} collective-permute-done((bf16[1,32,2176]{2,1,0:T(8,128)(2,1)S(1)}, bf16[1,32,2176]{2,1,0:T(8,128)(2,1)S(1)}, u32[]{:S(2)}, u32[]{:S(2)}) %collective-permute-start.3) | collective-permute-done | bytes 139296 | tf_op jit(solution)/shard_map/ppermute | solution.py:267
  23.9 1.6 %collective-permute-start.19 = (bf16[2,32,2176]{2,1,0:T(8,128)(2,1)S(1)}, bf16[2,32,2176]{2,1,0:T(8,128)(2,1)S(1)}, u32[]{:S(2)}, u32[]{:S(2)}) collective-permute-start(bf16[2,32,2176]{2,1,0:T(8,128)(2,1)S(1)} %collective-permute-done.4.refs_0_), channel_id=1, source_target_pairs={{0,2},{1,3},{2,0},{3,1},{4,6},{5,7},{6,4},{7,5},{8,10},{9,11},{10,... | collective-permute-start | bytes 835592 | tf_op jit(solution)/shard_map/ppermute | solution.py:276
  26.1 0.8 collective-permute-done.7.refs_5_
  27.1 3.2 %ffn.3 = (bf16[2,2,32,2048]{3,2,1,0:T(8,128)(2,1)S(1)}, bf16[1,32,2048]{2,1,0:T(8,128)(2,1)S(1)}, bf16[1,32,2048]{2,1,0:T(8,128)(2,1)S(1)}, bf16[1,32,2048]{2,1,0:T(8,128)(2,1)S(1)}, bf16[1,32,2048]{2,1,0:T(8,128)(2,1)S(1)}) custom-call(s32[3,1,6]{2,1,0:T(1,128)S(1)} %bitcast.4, bf16[1,2048,768]{2,1,0:T(8,128)(2,1)S(1)} %get-tuple-element.35.gate_ref, ...), custom_call_target="tpu_custom_call" | custom-call | tf_op jit(solution)/shard_map/ffn/pallas_call | solution.py:27
  31.3 0.8 %collective-permute-start.27 = (bf16[3,32,2176]{2,1,0:T(8,128)(2,1)S(1)}, bf16[3,32,2176]{2,1,0:T(8,128)(2,1)S(1)}, u32[]{:S(2)}, u32[]{:S(2)}) collective-permute-start(bf16[3,32,2176]{2,1,0:T(8,128)(2,1)S(1)} %join.5), channel_id=1, source_target_pairs={{0,2},{1,3},{2,0},{3,1},{4,6},{5,7},{6,4},{7,5},{8,10},{9,11},{10,... | collective-permute-start | bytes 1253384 | tf_op jit(solution)/shard_map/ppermute | solution.py:276
  33.1 1.5 %collective-permute-done.18.refs_3_ = bf16[1,32,2048]{2,1,0:T(8,128)(2,1)S(1)} collective-permute-done((bf16[1,32,2048]{2,1,0:T(8,128)(2,1)S(1)}, bf16[1,32,2048]{2,1,0:T(8,128)(2,1)S(1)}, u32[]{:S(2)}, u32[]{:S(2)}) %collective-permute-start.18) | collective-permute-done | bytes 131104 | tf_op jit(solution)/shard_map/ppermute | solution.py:279
  34.9 1.1 %collective-permute-done.12.refs_6_ = bf16[1,32,2176]{2,1,0:T(8,128)(2,1)S(1)} collective-permute-done((bf16[1,32,2176]{2,1,0:T(8,128)(2,1)S(1)}, bf16[1,32,2176]{2,1,0:T(8,128)(2,1)S(1)}, u32[]{:S(2)}, u32[]{:S(2)}) %collective-permute-start.12) | collective-permute-done | bytes 139296 | tf_op jit(solution)/shard_map/ppermute | solution.py:279
  36.0 3.2 %ffn.4 = (bf16[2,2,32,2048]{3,2,1,0:T(8,128)(2,1)S(1)}, bf16[1,32,2048]{2,1,0:T(8,128)(2,1)S(1)}, bf16[1,32,2048]{2,1,0:T(8,128)(2,1)S(1)}, bf16[1,32,2048]{2,1,0:T(8,128)(2,1)S(1)}, bf16[1,32,2048]{2,1,0:T(8,128)(2,1)S(1)}) custom-call(s32[3,1,6]{2,1,0:T(1,128)S(1)} %bitcast.5, bf16[1,2048,768]{2,1,0:T(8,128)(2,1)S(1)} %get-tuple-element.35.gate_ref, ...), custom_call_target="tpu_custom_call" | custom-call | tf_op jit(solution)/shard_map/ffn/pallas_call | solution.py:27
  39.8 0.8 %collective-permute-done.22.refs_4_ = bf16[1,32,2048]{2,1,0:T(8,128)(2,1)S(1)} collective-permute-done((bf16[1,32,2048]{2,1,0:T(8,128)(2,1)S(1)}, bf16[1,32,2048]{2,1,0:T(8,128)(2,1)S(1)}, u32[]{:S(2)}, u32[]{:S(2)}) %collective-permute-start.22) | collective-permute-done | bytes 131104 | tf_op jit(solution)/shard_map/ppermute | solution.py:279
  41.0 2.0 %collective-permute-done.27.refs_4_ = bf16[3,32,2176]{2,1,0:T(8,128)(2,1)S(1)} collective-permute-done((bf16[3,32,2176]{2,1,0:T(8,128)(2,1)S(1)}, bf16[3,32,2176]{2,1,0:T(8,128)(2,1)S(1)}, u32[]{:S(2)}, u32[]{:S(2)}) %collective-permute-start.27) | collective-permute-done | bytes 417824 | tf_op jit(solution)/shard_map/ppermute | solution.py:276
  43.6 1.1 %collective-permute-start.24 = (bf16[4,32,2048]{2,1,0:T(8,128)(2,1)S(1)}, bf16[4,32,2048]{2,1,0:T(8,128)(2,1)S(1)}, u32[]{:S(2)}, u32[]{:S(2)}) collective-permute-start(bf16[4,32,2048]{2,1,0:T(8,128)(2,1)S(1)} %total.7), channel_id=1, source_target_pairs={{0,2},{1,3},{2,0},{3,1},{4,6},{5,7},{6,4},{7,5},{8,10},{9,11},{10,... | collective-permute-start | bytes 1572872 | tf_op jit(solution)/shard_map/ppermute | solution.py:276
  45.2 5.7 %ffn.5 = (bf16[2,4,32,2048]{3,2,1,0:T(8,128)(2,1)S(1)}, bf16[2,32,2048]{2,1,0:T(8,128)(2,1)S(1)}, bf16[2,32,2048]{2,1,0:T(8,128)(2,1)S(1)}, bf16[2,32,2048]{2,1,0:T(8,128)(2,1)S(1)}, bf16[2,32,2048]{2,1,0:T(8,128)(2,1)S(1)}) custom-call(s32[3,1,6]{2,1,0:T(1,128)S(1)} %bitcast.6, bf16[1,2048,768]{2,1,0:T(8,128)(2,1)S(1)} %get-tuple-element.35.gate_ref, ...), custom_call_target="tpu_custom_call" | custom-call | tf_op jit(solution)/shard_map/ffn/pallas_call | solution.py:27
  51.7 0.9 %collective-permute-done.29.refs_1_ = bf16[2,32,2048]{2,1,0:T(8,128)(2,1)S(1)} collective-permute-done((bf16[2,32,2048]{2,1,0:T(8,128)(2,1)S(1)}, bf16[2,32,2048]{2,1,0:T(8,128)(2,1)S(1)}, u32[]{:S(2)}, u32[]{:S(2)}) %collective-permute-start.29) | collective-permute-done | bytes 262176 | tf_op jit(solution)/shard_map/ppermute | solution.py:279
  52.6 1.1 %collective-permute-start.36 = (bf16[2,32,2048]{2,1,0:T(8,128)(2,1)S(1)}, bf16[2,32,2048]{2,1,0:T(8,128)(2,1)S(1)}, u32[]{:S(2)}, u32[]{:S(2)}) collective-permute-start(bf16[2,32,2048]{2,1,0:T(8,128)(2,1)S(1)} %total.8), channel_id=1, source_target_pairs={{0,2},{1,3},{2,0},{3,1},{4,6},{5,7},{6,4},{7,5},{8,10},{9,11},{10,... | collective-permute-start | bytes 786440 | tf_op jit(solution)/shard_map/ppermute | solution.py:276
  53.8 4.5 %collective-permute-done.24.refs_3_.refs_2_ = bf16[4,32,2048]{2,1,0:T(8,128)(2,1)S(1)} collective-permute-done((bf16[4,32,2048]{2,1,0:T(8,128)(2,1)S(1)}, bf16[4,32,2048]{2,1,0:T(8,128)(2,1)S(1)}, u32[]{:S(2)}, u32[]{:S(2)}) %collective-permute-start.24) | collective-permute-done | bytes 524320 | tf_op jit(solution)/shard_map/ppermute | solution.py:276
  58.4 2.0 %collective-permute-start.30 = (bf16[2,32,2048]{2,1,0:T(8,128)(2,1)S(1)}, bf16[2,32,2048]{2,1,0:T(8,128)(2,1)S(1)}, u32[]{:S(2)}, u32[]{:S(2)}) collective-permute-start(bf16[2,32,2048]{2,1,0:T(8,128)(2,1)S(1)} %total.9), channel_id=1, source_target_pairs={{0,4},{1,5},{2,6},{3,7},{4,0},{5,1},{6,2},{7,3},{8,12},{9,13},{10,... | collective-permute-start | bytes 786440 | tf_op jit(solution)/shard_map/ppermute | solution.py:267
  60.5 0.6 collective-permute-start.34
  61.1 2.8 %collective-permute-done.36.refs_2_ = bf16[2,32,2048]{2,1,0:T(8,128)(2,1)S(1)} collective-permute-done((bf16[2,32,2048]{2,1,0:T(8,128)(2,1)S(1)}, bf16[2,32,2048]{2,1,0:T(8,128)(2,1)S(1)}, u32[]{:S(2)}, u32[]{:S(2)}) %collective-permute-start.36) | collective-permute-done | bytes 262176 | tf_op jit(solution)/shard_map/ppermute | solution.py:276
  64.0 2.0 %collective-permute-start.37 = (bf16[2,32,2048]{2,1,0:T(8,128)(2,1)S(1)}, bf16[2,32,2048]{2,1,0:T(8,128)(2,1)S(1)}, u32[]{:S(2)}, u32[]{:S(2)}) collective-permute-start(bf16[2,32,2048]{2,1,0:T(8,128)(2,1)S(1)} %total.12), channel_id=1, source_target_pairs={{0,4},{1,5},{2,6},{3,7},{4,0},{5,1},{6,2},{7,3},{8,12},{9,13},{10,... | collective-permute-start | bytes 786440 | tf_op jit(solution)/shard_map/ppermute | solution.py:267
  66.3 4.2 %collective-permute-start.31 = (bf16[1,32,2048]{2,1,0:T(8,128)(2,1)S(1)}, bf16[1,32,2048]{2,1,0:T(8,128)(2,1)S(1)}, u32[]{:S(2)}, u32[]{:S(2)}) collective-permute-start(bf16[1,32,2048]{2,1,0:T(8,128)(2,1)S(1)} %total.10), channel_id=1, source_target_pairs={{0,12},{1,13},{2,14},{3,15},{4,8},{5,9},{6,10},{7,11},{8,4},{9,5},... | collective-permute-start | bytes 393224 | tf_op jit(solution)/shard_map/ppermute | solution.py:267
  70.5 2.0 %collective-permute-done.37.refs_3_.refs_8_ = bf16[2,32,2048]{2,1,0:T(8,128)(2,1)S(1)} collective-permute-done((bf16[2,32,2048]{2,1,0:T(8,128)(2,1)S(1)}, bf16[2,32,2048]{2,1,0:T(8,128)(2,1)S(1)}, u32[]{:S(2)}, u32[]{:S(2)}) %collective-permute-start.37) | collective-permute-done | bytes 262176 | tf_op jit(solution)/shard_map/ppermute | solution.py:267
  72.6 6.4 %collective-permute-start.38 = (bf16[1,32,2048]{2,1,0:T(8,128)(2,1)S(1)}, bf16[1,32,2048]{2,1,0:T(8,128)(2,1)S(1)}, u32[]{:S(2)}, u32[]{:S(2)}) collective-permute-start(bf16[1,32,2048]{2,1,0:T(8,128)(2,1)S(1)} %total.13), channel_id=1, source_target_pairs={{0,12},{1,13},{2,14},{3,15},{4,8},{5,9},{6,10},{7,11},{8,4},{9,5},... | collective-permute-start | bytes 393224 | tf_op jit(solution)/shard_map/ppermute | solution.py:267
  79.0 1.1 %collective-permute-done.31.refs_4_ = bf16[1,32,2048]{2,1,0:T(8,128)(2,1)S(1)} collective-permute-done((bf16[1,32,2048]{2,1,0:T(8,128)(2,1)S(1)}, bf16[1,32,2048]{2,1,0:T(8,128)(2,1)S(1)}, u32[]{:S(2)}, u32[]{:S(2)}) %collective-permute-start.31) | collective-permute-done | bytes 131104 | tf_op jit(solution)/shard_map/ppermute | solution.py:267
  80.0 2.0 %collective-permute-done.38.refs_9_ = bf16[1,32,2048]{2,1,0:T(8,128)(2,1)S(1)} collective-permute-done((bf16[1,32,2048]{2,1,0:T(8,128)(2,1)S(1)}, bf16[1,32,2048]{2,1,0:T(8,128)(2,1)S(1)}, u32[]{:S(2)}, u32[]{:S(2)}) %collective-permute-start.38) | collective-permute-done | bytes 131104 | tf_op jit(solution)/shard_map/ppermute | solution.py:267
  82.0 0.9 %finish.1 = bf16[2,32,2048]{2,1,0:T(8,128)(2,1)} custom-call(bf16[2,32,2048]{2,1,0:T(8,128)(2,1)S(1)} %copy-done, bf16[2,2,32,2048]{3,2,1,0:T(8,128)(2,1)S(1)} %get-tuple-element.44.refs_0_, bf16[1,32,2048]{2,1,0:T(8,128)(2,1)S(1)} %collective-permute-done.10.refs_1_, bf16[4,32,2048]{2,1,0:T(8,128)(2,1)S(1)} %collective-permute-done.24.refs_3_.refs_2_, ...), custom_call_target="tpu_custom_call" | custom-call | tf_op jit(solution)/shard_map/finish/pallas_call | solution.py:27
  (66 shorter events, 7.1 us)
Async XLA Ops:
  1.2 10.9 %collective-permute-start.2 = (bf16[1,32,2176]{2,1,0:T(8,128)(2,1)S(1)}, bf16[1,32,2176]{2,1,0:T(8,128)(2,1)S(1)}, u32[]{:S(2)}, u32[]{:S(2)}) collective-permute-start(bf16[1,32,2176]{2,1,0:T(8,128)(2,1)S(1)} %get-tuple-element.57.refs_0_), channel_id=1, source_target_pairs={{0,2},{1,3},{2,0},{3,1},{4,6},{5,7},{6,4},{7,5},{8,10},{9,11},{10,... | collective-permute-start | bytes 417800 | tf_op jit(solution)/shard_map/ppermute | solution.py:276
  4.3 7.9 %collective-permute-start.1 = (bf16[1,32,2176]{2,1,0:T(8,128)(2,1)S(1)}, bf16[1,32,2176]{2,1,0:T(8,128)(2,1)S(1)}, u32[]{:S(2)}, u32[]{:S(2)}) collective-permute-start(bf16[1,32,2176]{2,1,0:T(8,128)(2,1)S(1)} %get-tuple-element.43.refs_0_), channel_id=1, source_target_pairs={{0,2},{1,3},{2,0},{3,1},{4,6},{5,7},{6,4},{7,5},{8,10},{9,11},{10,... | collective-permute-start | bytes 417800 | tf_op jit(solution)/shard_map/ppermute | solution.py:276
  4.4 7.8 %collective-permute-start = (bf16[1,32,2176]{2,1,0:T(8,128)(2,1)S(1)}, bf16[1,32,2176]{2,1,0:T(8,128)(2,1)S(1)}, u32[]{:S(2)}, u32[]{:S(2)}) collective-permute-start(bf16[1,32,2176]{2,1,0:T(8,128)(2,1)S(1)} %get-tuple-element.43.refs_0_), channel_id=1, source_target_pairs={{0,12},{1,13},{2,14},{3,15},{4,8},{5,9},{6,10},{7,11},{8,4},{9,5},... | collective-permute-start | bytes 417800 | tf_op jit(solution)/shard_map/ppermute | solution.py:267
  12.2 11.6 %collective-permute-start.4 = (bf16[2,32,2176]{2,1,0:T(8,128)(2,1)S(1)}, bf16[2,32,2176]{2,1,0:T(8,128)(2,1)S(1)}, u32[]{:S(2)}, u32[]{:S(2)}) collective-permute-start(bf16[2,32,2176]{2,1,0:T(8,128)(2,1)S(1)} %join.3), channel_id=1, source_target_pairs={{0,4},{1,5},{2,6},{3,7},{4,0},{5,1},{6,2},{7,3},{8,12},{9,13},{10,... | collective-permute-start | bytes 835592 | tf_op jit(solution)/shard_map/ppermute | solution.py:267
  14.3 9.5 %collective-permute-start.3 = (bf16[1,32,2176]{2,1,0:T(8,128)(2,1)S(1)}, bf16[1,32,2176]{2,1,0:T(8,128)(2,1)S(1)}, u32[]{:S(2)}, u32[]{:S(2)}) collective-permute-start(bf16[1,32,2176]{2,1,0:T(8,128)(2,1)S(1)} %get-tuple-element.57.refs_0_), channel_id=1, source_target_pairs={{0,12},{1,13},{2,14},{3,15},{4,8},{5,9},{6,10},{7,11},{8,4},{9,5},... | collective-permute-start | bytes 417800 | tf_op jit(solution)/shard_map/ppermute | solution.py:267
  17.0 6.9 %collective-permute-start.5 = (bf16[1,32,2176]{2,1,0:T(8,128)(2,1)S(1)}, bf16[1,32,2176]{2,1,0:T(8,128)(2,1)S(1)}, u32[]{:S(2)}, u32[]{:S(2)}) collective-permute-start(bf16[1,32,2176]{2,1,0:T(8,128)(2,1)S(1)} %collective-permute-done.refs_1_), channel_id=1, source_target_pairs={{0,2},{1,3},{2,0},{3,1},{4,6},{5,7},{6,4},{7,5},{8,10},{9,11},{10,... | collective-permute-start | bytes 417800 | tf_op jit(solution)/shard_map/ppermute | solution.py:276
  18.5 7.0 %collective-permute-start.6 = (bf16[1,32,2176]{2,1,0:T(8,128)(2,1)S(1)}, bf16[1,32,2176]{2,1,0:T(8,128)(2,1)S(1)}, u32[]{:S(2)}, u32[]{:S(2)}) collective-permute-start(bf16[1,32,2176]{2,1,0:T(8,128)(2,1)S(1)} %get-tuple-element.43.refs_0_), channel_id=1, source_target_pairs={{0,1},{1,0},{2,3},{3,2},{4,5},{5,4},{6,7},{7,6},{8,9},{9,8},{10,11... | collective-permute-start | bytes 417800 | tf_op jit(solution)/shard_map/ppermute | solution.py:279
  18.5 7.6 %collective-permute-start.8 = (bf16[1,32,2176]{2,1,0:T(8,128)(2,1)S(1)}, bf16[1,32,2176]{2,1,0:T(8,128)(2,1)S(1)}, u32[]{:S(2)}, u32[]{:S(2)}) collective-permute-start(bf16[1,32,2176]{2,1,0:T(8,128)(2,1)S(1)} %collective-permute-done.1.refs_2_), channel_id=1, source_target_pairs={{0,1},{1,0},{2,3},{3,2},{4,5},{5,4},{6,7},{7,6},{8,9},{9,8},{10,11... | collective-permute-start | bytes 417800 | tf_op jit(solution)/shard_map/ppermute | solution.py:279
  23.8 7.1 %collective-permute-start.13 = (bf16[2,32,2176]{2,1,0:T(8,128)(2,1)S(1)}, bf16[2,32,2176]{2,1,0:T(8,128)(2,1)S(1)}, u32[]{:S(2)}, u32[]{:S(2)}) collective-permute-start(bf16[2,32,2176]{2,1,0:T(8,128)(2,1)S(1)} %join.4), channel_id=1, source_target_pairs={{0,4},{1,5},{2,6},{3,7},{4,0},{5,1},{6,2},{7,3},{8,12},{9,13},{10,... | collective-permute-start | bytes 835592 | tf_op jit(solution)/shard_map/ppermute | solution.py:267
  23.9 7.3 %collective-permute-start.19 = (bf16[2,32,2176]{2,1,0:T(8,128)(2,1)S(1)}, bf16[2,32,2176]{2,1,0:T(8,128)(2,1)S(1)}, u32[]{:S(2)}, u32[]{:S(2)}) collective-permute-start(bf16[2,32,2176]{2,1,0:T(8,128)(2,1)S(1)} %collective-permute-done.4.refs_0_), channel_id=1, source_target_pairs={{0,2},{1,3},{2,0},{3,1},{4,6},{5,7},{6,4},{7,5},{8,10},{9,11},{10,... | collective-permute-start | bytes 835592 | tf_op jit(solution)/shard_map/ppermute | solution.py:276
  26.0 4.7 %collective-permute-start.15 = (bf16[1,32,2176]{2,1,0:T(8,128)(2,1)S(1)}, bf16[1,32,2176]{2,1,0:T(8,128)(2,1)S(1)}, u32[]{:S(2)}, u32[]{:S(2)}) collective-permute-start(bf16[1,32,2176]{2,1,0:T(8,128)(2,1)S(1)} %collective-permute-done.2.refs_3_), channel_id=1, source_target_pairs={{0,1},{1,0},{2,3},{3,2},{4,5},{5,4},{6,7},{7,6},{8,9},{9,8},{10,11... | collective-permute-start | bytes 417800 | tf_op jit(solution)/shard_map/ppermute | solution.py:279
  26.9 5.2 %collective-permute-start.11 = (bf16[1,32,2176]{2,1,0:T(8,128)(2,1)S(1)}, bf16[1,32,2176]{2,1,0:T(8,128)(2,1)S(1)}, u32[]{:S(2)}, u32[]{:S(2)}) collective-permute-start(bf16[1,32,2176]{2,1,0:T(8,128)(2,1)S(1)} %get-tuple-element.57.refs_0_), channel_id=1, source_target_pairs={{0,1},{1,0},{2,3},{3,2},{4,5},{5,4},{6,7},{7,6},{8,9},{9,8},{10,11... | collective-permute-start | bytes 417800 | tf_op jit(solution)/shard_map/ppermute | solution.py:279
  30.3 2.0 %collective-permute-start.10 = (bf16[1,32,2048]{2,1,0:T(8,128)(2,1)S(1)}, bf16[1,32,2048]{2,1,0:T(8,128)(2,1)S(1)}, u32[]{:S(2)}, u32[]{:S(2)}) collective-permute-start(bf16[1,32,2048]{2,1,0:T(8,128)(2,1)S(1)} %get-tuple-element.45), channel_id=1, source_target_pairs={{0,1},{1,0},{2,3},{3,2},{4,5},{5,4},{6,7},{7,6},{8,9},{9,8},{10,11... | collective-permute-start | bytes 393224 | tf_op jit(solution)/shard_map/ppermute | solution.py:279
  30.7 1.9 %collective-permute-start.16 = (bf16[1,32,2048]{2,1,0:T(8,128)(2,1)S(1)}, bf16[1,32,2048]{2,1,0:T(8,128)(2,1)S(1)}, u32[]{:S(2)}, u32[]{:S(2)}) collective-permute-start(bf16[1,32,2048]{2,1,0:T(8,128)(2,1)S(1)} %get-tuple-element.47), channel_id=1, source_target_pairs={{0,1},{1,0},{2,3},{3,2},{4,5},{5,4},{6,7},{7,6},{8,9},{9,8},{10,11... | collective-permute-start | bytes 393224 | tf_op jit(solution)/shard_map/ppermute | solution.py:279
  30.9 1.9 %collective-permute-start.17 = (bf16[1,32,2048]{2,1,0:T(8,128)(2,1)S(1)}, bf16[1,32,2048]{2,1,0:T(8,128)(2,1)S(1)}, u32[]{:S(2)}, u32[]{:S(2)}) collective-permute-start(bf16[1,32,2048]{2,1,0:T(8,128)(2,1)S(1)} %get-tuple-element.48), channel_id=1, source_target_pairs={{0,1},{1,0},{2,3},{3,2},{4,5},{5,4},{6,7},{7,6},{8,9},{9,8},{10,11... | collective-permute-start | bytes 393224 | tf_op jit(solution)/shard_map/ppermute | solution.py:279
  31.3 11.8 %collective-permute-start.27 = (bf16[3,32,2176]{2,1,0:T(8,128)(2,1)S(1)}, bf16[3,32,2176]{2,1,0:T(8,128)(2,1)S(1)}, u32[]{:S(2)}, u32[]{:S(2)}) collective-permute-start(bf16[3,32,2176]{2,1,0:T(8,128)(2,1)S(1)} %join.5), channel_id=1, source_target_pairs={{0,2},{1,3},{2,0},{3,1},{4,6},{5,7},{6,4},{7,5},{8,10},{9,11},{10,... | collective-permute-start | bytes 1253384 | tf_op jit(solution)/shard_map/ppermute | solution.py:276
  32.1 3.9 %collective-permute-start.14 = (bf16[2,32,2176]{2,1,0:T(8,128)(2,1)S(1)}, bf16[2,32,2176]{2,1,0:T(8,128)(2,1)S(1)}, u32[]{:S(2)}, u32[]{:S(2)}) collective-permute-start(bf16[2,32,2176]{2,1,0:T(8,128)(2,1)S(1)} %collective-permute-done.13.refs_1_.refs_2_), channel_id=1, source_target_pairs={{0,1},{1,0},{2,3},{3,2},{4,5},{5,4},{6,7},{7,6},{8,9},{9,8},{10,11... | collective-permute-start | bytes 835592 | tf_op jit(solution)/shard_map/ppermute | solution.py:279
  32.3 3.7 %collective-permute-start.20 = (bf16[2,32,2176]{2,1,0:T(8,128)(2,1)S(1)}, bf16[2,32,2176]{2,1,0:T(8,128)(2,1)S(1)}, u32[]{:S(2)}, u32[]{:S(2)}) collective-permute-start(bf16[2,32,2176]{2,1,0:T(8,128)(2,1)S(1)} %collective-permute-done.4.refs_0_), channel_id=1, source_target_pairs={{0,1},{1,0},{2,3},{3,2},{4,5},{5,4},{6,7},{7,6},{8,9},{9,8},{10,11... | collective-permute-start | bytes 835592 | tf_op jit(solution)/shard_map/ppermute | solution.py:279
  32.6 3.4 %collective-permute-start.21 = (bf16[2,32,2176]{2,1,0:T(8,128)(2,1)S(1)}, bf16[2,32,2176]{2,1,0:T(8,128)(2,1)S(1)}, u32[]{:S(2)}, u32[]{:S(2)}) collective-permute-start(bf16[2,32,2176]{2,1,0:T(8,128)(2,1)S(1)} %collective-permute-done.19.refs_1_), channel_id=1, source_target_pairs={{0,1},{1,0},{2,3},{3,2},{4,5},{5,4},{6,7},{7,6},{8,9},{9,8},{10,11... | collective-permute-start | bytes 835592 | tf_op jit(solution)/shard_map/ppermute | solution.py:279
  32.8 1.8 %collective-permute-start.18 = (bf16[1,32,2048]{2,1,0:T(8,128)(2,1)S(1)}, bf16[1,32,2048]{2,1,0:T(8,128)(2,1)S(1)}, u32[]{:S(2)}, u32[]{:S(2)}) collective-permute-start(bf16[1,32,2048]{2,1,0:T(8,128)(2,1)S(1)} %get-tuple-element.49), channel_id=1, source_target_pairs={{0,1},{1,0},{2,3},{3,2},{4,5},{5,4},{6,7},{7,6},{8,9},{9,8},{10,11... | collective-permute-start | bytes 393224 | tf_op jit(solution)/shard_map/ppermute | solution.py:279
  43.1 2.1 %collective-permute-start.28 = (bf16[3,32,2176]{2,1,0:T(8,128)(2,1)S(1)}, bf16[3,32,2176]{2,1,0:T(8,128)(2,1)S(1)}, u32[]{:S(2)}, u32[]{:S(2)}) collective-permute-start(bf16[3,32,2176]{2,1,0:T(8,128)(2,1)S(1)} %collective-permute-done.27.refs_4_), channel_id=1, source_target_pairs={{0,1},{1,0},{2,3},{3,2},{4,5},{5,4},{6,7},{7,6},{8,9},{9,8},{10,11... | collective-permute-start | bytes 1253384 | tf_op jit(solution)/shard_map/ppermute | solution.py:279
  43.1 1.9 %collective-permute-start.25 = (bf16[1,32,2048]{2,1,0:T(8,128)(2,1)S(1)}, bf16[1,32,2048]{2,1,0:T(8,128)(2,1)S(1)}, u32[]{:S(2)}, u32[]{:S(2)}) collective-permute-start(bf16[1,32,2048]{2,1,0:T(8,128)(2,1)S(1)} %get-tuple-element.55), channel_id=1, source_target_pairs={{0,1},{1,0},{2,3},{3,2},{4,5},{5,4},{6,7},{7,6},{8,9},{9,8},{10,11... | collective-permute-start | bytes 393224 | tf_op jit(solution)/shard_map/ppermute | solution.py:279
  43.6 14.7 %collective-permute-start.24 = (bf16[4,32,2048]{2,1,0:T(8,128)(2,1)S(1)}, bf16[4,32,2048]{2,1,0:T(8,128)(2,1)S(1)}, u32[]{:S(2)}, u32[]{:S(2)}) collective-permute-start(bf16[4,32,2048]{2,1,0:T(8,128)(2,1)S(1)} %total.7), channel_id=1, source_target_pairs={{0,2},{1,3},{2,0},{3,1},{4,6},{5,7},{6,4},{7,5},{8,10},{9,11},{10,... | collective-permute-start | bytes 1572872 | tf_op jit(solution)/shard_map/ppermute | solution.py:276
  51.2 9.3 %collective-permute-start.33 = (bf16[2,32,2048]{2,1,0:T(8,128)(2,1)S(1)}, bf16[2,32,2048]{2,1,0:T(8,128)(2,1)S(1)}, u32[]{:S(2)}, u32[]{:S(2)}) collective-permute-start(bf16[2,32,2048]{2,1,0:T(8,128)(2,1)S(1)} %get-tuple-element.63), channel_id=1, source_target_pairs={{0,1},{1,0},{2,3},{3,2},{4,5},{5,4},{6,7},{7,6},{8,9},{9,8},{10,11... | collective-permute-start | bytes 786440 | tf_op jit(solution)/shard_map/ppermute | solution.py:279
  51.5 9.5 %collective-permute-start.35 = (bf16[2,32,2048]{2,1,0:T(8,128)(2,1)S(1)}, bf16[2,32,2048]{2,1,0:T(8,128)(2,1)S(1)}, u32[]{:S(2)}, u32[]{:S(2)}) collective-permute-start(bf16[2,32,2048]{2,1,0:T(8,128)(2,1)S(1)} %get-tuple-element.64), channel_id=1, source_target_pairs={{0,1},{1,0},{2,3},{3,2},{4,5},{5,4},{6,7},{7,6},{8,9},{9,8},{10,11... | collective-permute-start | bytes 786440 | tf_op jit(solution)/shard_map/ppermute | solution.py:279
  52.6 11.3 %collective-permute-start.36 = (bf16[2,32,2048]{2,1,0:T(8,128)(2,1)S(1)}, bf16[2,32,2048]{2,1,0:T(8,128)(2,1)S(1)}, u32[]{:S(2)}, u32[]{:S(2)}) collective-permute-start(bf16[2,32,2048]{2,1,0:T(8,128)(2,1)S(1)} %total.8), channel_id=1, source_target_pairs={{0,2},{1,3},{2,0},{3,1},{4,6},{5,7},{6,4},{7,5},{8,10},{9,11},{10,... | collective-permute-start | bytes 786440 | tf_op jit(solution)/shard_map/ppermute | solution.py:276
  53.8 16.8 %collective-permute-start.32 = (bf16[2,32,2048]{2,1,0:T(8,128)(2,1)S(1)}, bf16[2,32,2048]{2,1,0:T(8,128)(2,1)S(1)}, u32[]{:S(2)}, u32[]{:S(2)}) collective-permute-start(bf16[2,32,2048]{2,1,0:T(8,128)(2,1)S(1)} %get-tuple-element.62), channel_id=1, source_target_pairs={{0,1},{1,0},{2,3},{3,2},{4,5},{5,4},{6,7},{7,6},{8,9},{9,8},{10,11... | collective-permute-start | bytes 786440 | tf_op jit(solution)/shard_map/ppermute | solution.py:279
  58.4 7.8 %collective-permute-start.30 = (bf16[2,32,2048]{2,1,0:T(8,128)(2,1)S(1)}, bf16[2,32,2048]{2,1,0:T(8,128)(2,1)S(1)}, u32[]{:S(2)}, u32[]{:S(2)}) collective-permute-start(bf16[2,32,2048]{2,1,0:T(8,128)(2,1)S(1)} %total.9), channel_id=1, source_target_pairs={{0,4},{1,5},{2,6},{3,7},{4,0},{5,1},{6,2},{7,3},{8,12},{9,13},{10,... | collective-permute-start | bytes 786440 | tf_op jit(solution)/shard_map/ppermute | solution.py:267
  60.5 10.0 %collective-permute-start.34 = (bf16[2,32,2048]{2,1,0:T(8,128)(2,1)S(1)}, bf16[2,32,2048]{2,1,0:T(8,128)(2,1)S(1)}, u32[]{:S(2)}, u32[]{:S(2)}) collective-permute-start(bf16[2,32,2048]{2,1,0:T(8,128)(2,1)S(1)} %total.11), channel_id=1, source_target_pairs={{0,2},{1,3},{2,0},{3,1},{4,6},{5,7},{6,4},{7,5},{8,10},{9,11},{10,... | collective-permute-start | bytes 786440 | tf_op jit(solution)/shard_map/ppermute | solution.py:276
  64.0 8.5 %collective-permute-start.37 = (bf16[2,32,2048]{2,1,0:T(8,128)(2,1)S(1)}, bf16[2,32,2048]{2,1,0:T(8,128)(2,1)S(1)}, u32[]{:S(2)}, u32[]{:S(2)}) collective-permute-start(bf16[2,32,2048]{2,1,0:T(8,128)(2,1)S(1)} %total.12), channel_id=1, source_target_pairs={{0,4},{1,5},{2,6},{3,7},{4,0},{5,1},{6,2},{7,3},{8,12},{9,13},{10,... | collective-permute-start | bytes 786440 | tf_op jit(solution)/shard_map/ppermute | solution.py:267
  66.3 13.7 %collective-permute-start.31 = (bf16[1,32,2048]{2,1,0:T(8,128)(2,1)S(1)}, bf16[1,32,2048]{2,1,0:T(8,128)(2,1)S(1)}, u32[]{:S(2)}, u32[]{:S(2)}) collective-permute-start(bf16[1,32,2048]{2,1,0:T(8,128)(2,1)S(1)} %total.10), channel_id=1, source_target_pairs={{0,12},{1,13},{2,14},{3,15},{4,8},{5,9},{6,10},{7,11},{8,4},{9,5},... | collective-permute-start | bytes 393224 | tf_op jit(solution)/shard_map/ppermute | solution.py:267
  72.6 9.4 %collective-permute-start.38 = (bf16[1,32,2048]{2,1,0:T(8,128)(2,1)S(1)}, bf16[1,32,2048]{2,1,0:T(8,128)(2,1)S(1)}, u32[]{:S(2)}, u32[]{:S(2)}) collective-permute-start(bf16[1,32,2048]{2,1,0:T(8,128)(2,1)S(1)} %total.13), channel_id=1, source_target_pairs={{0,12},{1,13},{2,14},{3,15},{4,8},{5,9},{6,10},{7,11},{8,4},{9,5},... | collective-permute-start | bytes 393224 | tf_op jit(solution)/shard_map/ppermute | solution.py:267
  (9 other events, 56.7 us)

commit v16 on v15

--- a/solution.py
+++ b/solution.py
@@ -327,7 +327,7 @@
             xs += swap(xs)
             order += calls[0][1]
         else:
-            late = after(there[batch][-1], sent[-1])
+            late = after(there[batch][-1], sent[-1], *calls_before[-1][1][: SHARES // 2])
             xs = [*early[batch], late, *early_core[batch], to_core(late)]
             order += calls_before[-1][1][: SHARES // 2]
         mine, *other = ffn([after(xs[0], *order), *xs[1:]], table, weights)

time: 83.1 us -> 82.6 us (level)
  transfers between devices with their start and end apart: 39 -> 39, of which waited for: 17 -> 18; matrix products, arithmetic and copies ran while one was open for 0% -> 0% of each run, Pallas kernels for 20% -> 20%
where the time goes in v16:
time: 82.6 us; the launch traced here: 82.4 us
  starting transfers between devices  38.5 us (47%)
  waiting for transfers between devices  25 us (30%)
  Pallas kernels  18.8 us (23%)
    ppermute x8, starting transfers between devices, along_line(): lax.ppermute(rows, 'ep', [(i, place_of(i // 4) * 4 + i % 4) for i in rang...  23.4 us
    pallas_call x16, Pallas kernels, call(): pl.pallas_call(kernel, out_shape=shapes, in_specs=specs, out_specs=[VMEM]...  18.8 us
    ppermute x8, waiting for transfers between devices, along_line(): lax.ppermute(rows, 'ep', [(i, place_of(i // 4) * 4 + i % 4) for i in rang...  10.1 us
    ppermute x8, starting transfers between devices, to_mid(): return lax.ppermute(rows, 'ep', [(i, i ^ 2) for i in range(owners)])  9.86 us
    ppermute x8, waiting for transfers between devices, to_mid(): return lax.ppermute(rows, 'ep', [(i, i ^ 2) for i in range(owners)])  8.92 us
    ppermute x23, waiting for transfers between devices, to_core(): return lax.ppermute(rows, 'ep', [(i, i ^ 1) for i in range(owners)])  6 us
    ppermute x23, starting transfers between devices, to_core(): return lax.ppermute(rows, 'ep', [(i, i ^ 1) for i in range(owners)])  5.18 us
  transfers between devices with their start and end apart: 39, of which 18 were waited for; matrix products, arithmetic and copies ran while one was open for 0% of the time, Pallas kernels for 20%

profile of v16, /device:TPU:0, one launch (start us, length us, event | category | flops | bytes accessed | tf_op | source)
XLA Modules:
  0.0 82.4 jit_solution(10344324124298050197)
XLA Ops:
  0.0 1.2 %prepare.1 = (bf16[1,32,2176]{2,1,0:T(8,128)(2,1)S(1)}, bf16[1,32,2176]{2,1,0:T(8,128)(2,1)S(1)}) custom-call(bf16[2,32,2048]{2,1,0:T(8,128)(2,1)} %hidden_ref.1, s32[2,8,32]{2,1,0:T(8,128)} %bitcast.7, s32[2,8,32]{2,1,0:T(8,128)} %bitcast.8, f32[1,2048]{1,0:T(1,128)} %bitcast.9), custom_call_target="tpu_custom_call" | custom-call | tf_op jit(solution)/shard_map/prepare/pallas_call | solution.py:27
  1.2 3.0 %collective-permute-start.2 = (bf16[1,32,2176]{2,1,0:T(8,128)(2,1)S(1)}, bf16[1,32,2176]{2,1,0:T(8,128)(2,1)S(1)}, u32[]{:S(2)}, u32[]{:S(2)}) collective-permute-start(bf16[1,32,2176]{2,1,0:T(8,128)(2,1)S(1)} %get-tuple-element.57.refs_0_), channel_id=1, source_target_pairs={{0,2},{1,3},{2,0},{3,1},{4,6},{5,7},{6,4},{7,5},{8,10},{9,11},{10,... | collective-permute-start | bytes 417800 | tf_op jit(solution)/shard_map/ppermute | solution.py:276
  4.4 4.0 %collective-permute-start = (bf16[1,32,2176]{2,1,0:T(8,128)(2,1)S(1)}, bf16[1,32,2176]{2,1,0:T(8,128)(2,1)S(1)}, u32[]{:S(2)}, u32[]{:S(2)}) collective-permute-start(bf16[1,32,2176]{2,1,0:T(8,128)(2,1)S(1)} %get-tuple-element.43.refs_0_), channel_id=1, source_target_pairs={{0,12},{1,13},{2,14},{3,15},{4,8},{5,9},{6,10},{7,11},{8,4},{9,5},... | collective-permute-start | bytes 417800 | tf_op jit(solution)/shard_map/ppermute | solution.py:267
  8.4 3.8 %load.1 = (bf16[1,2048,768]{2,1,0:T(8,128)(2,1)S(1)}, bf16[1,2048,768]{2,1,0:T(8,128)(2,1)S(1)}, bf16[1,768,2048]{2,1,0:T(8,128)(2,1)S(1)}) custom-call(bf16[1,2048,768]{2,1,0:T(8,128)(2,1)} %refs_0_.1, bf16[1,2048,768]{2,1,0:T(8,128)(2,1)} %refs_1_.1, bf16[1,768,2048]{2,1,0:T(8,128)(2,1)} %refs_2_.1), custom_call_target="tpu_custom_call" | custom-call | tf_op jit(solution)/shard_map/load/pallas_call | solution.py:27
  12.2 2.1 %collective-permute-start.4 = (bf16[2,32,2176]{2,1,0:T(8,128)(2,1)S(1)}, bf16[2,32,2176]{2,1,0:T(8,128)(2,1)S(1)}, u32[]{:S(2)}, u32[]{:S(2)}) collective-permute-start(bf16[2,32,2176]{2,1,0:T(8,128)(2,1)S(1)} %join.3), channel_id=1, source_target_pairs={{0,4},{1,5},{2,6},{3,7},{4,0},{5,1},{6,2},{7,3},{8,12},{9,13},{10,... | collective-permute-start | bytes 835592 | tf_op jit(solution)/shard_map/ppermute | solution.py:267
  14.3 2.7 %collective-permute-start.3 = (bf16[1,32,2176]{2,1,0:T(8,128)(2,1)S(1)}, bf16[1,32,2176]{2,1,0:T(8,128)(2,1)S(1)}, u32[]{:S(2)}, u32[]{:S(2)}) collective-permute-start(bf16[1,32,2176]{2,1,0:T(8,128)(2,1)S(1)} %get-tuple-element.57.refs_0_), channel_id=1, source_target_pairs={{0,12},{1,13},{2,14},{3,15},{4,8},{5,9},{6,10},{7,11},{8,4},{9,5},... | collective-permute-start | bytes 417800 | tf_op jit(solution)/shard_map/ppermute | solution.py:267
  17.0 1.5 %collective-permute-start.5 = (bf16[1,32,2176]{2,1,0:T(8,128)(2,1)S(1)}, bf16[1,32,2176]{2,1,0:T(8,128)(2,1)S(1)}, u32[]{:S(2)}, u32[]{:S(2)}) collective-permute-start(bf16[1,32,2176]{2,1,0:T(8,128)(2,1)S(1)} %collective-permute-done.refs_1_), channel_id=1, source_target_pairs={{0,2},{1,3},{2,0},{3,1},{4,6},{5,7},{6,4},{7,5},{8,10},{9,11},{10,... | collective-permute-start | bytes 417800 | tf_op jit(solution)/shard_map/ppermute | solution.py:276
  19.0 4.8 %collective-permute-done.3.refs_1_.refs_0_ = bf16[1,32,2176]{2,1,0:T(8,128)(2,1)S(1)} collective-permute-done((bf16[1,32,2176]{2,1,0:T(8,128)(2,1)S(1)}, bf16[1,32,2176]{2,1,0:T(8,128)(2,1)S(1)}, u32[]{:S(2)}, u32[]{:S(2)}) %collective-permute-start.3) | collective-permute-done | bytes 139296 | tf_op jit(solution)/shard_map/ppermute | solution.py:267
  23.9 1.6 %collective-permute-start.19 = (bf16[2,32,2176]{2,1,0:T(8,128)(2,1)S(1)}, bf16[2,32,2176]{2,1,0:T(8,128)(2,1)S(1)}, u32[]{:S(2)}, u32[]{:S(2)}) collective-permute-start(bf16[2,32,2176]{2,1,0:T(8,128)(2,1)S(1)} %collective-permute-done.4.refs_0_), channel_id=1, source_target_pairs={{0,2},{1,3},{2,0},{3,1},{4,6},{5,7},{6,4},{7,5},{8,10},{9,11},{10,... | collective-permute-start | bytes 835592 | tf_op jit(solution)/shard_map/ppermute | solution.py:276
  26.1 0.8 collective-permute-done.7.refs_5_
  27.1 3.2 %ffn.3 = (bf16[2,2,32,2048]{3,2,1,0:T(8,128)(2,1)S(1)}, bf16[1,32,2048]{2,1,0:T(8,128)(2,1)S(1)}, bf16[1,32,2048]{2,1,0:T(8,128)(2,1)S(1)}, bf16[1,32,2048]{2,1,0:T(8,128)(2,1)S(1)}, bf16[1,32,2048]{2,1,0:T(8,128)(2,1)S(1)}) custom-call(s32[3,1,6]{2,1,0:T(1,128)S(1)} %bitcast.4, bf16[1,2048,768]{2,1,0:T(8,128)(2,1)S(1)} %get-tuple-element.35.gate_ref, ...), custom_call_target="tpu_custom_call" | custom-call | tf_op jit(solution)/shard_map/ffn/pallas_call | solution.py:27
  31.3 0.8 %collective-permute-start.27 = (bf16[3,32,2176]{2,1,0:T(8,128)(2,1)S(1)}, bf16[3,32,2176]{2,1,0:T(8,128)(2,1)S(1)}, u32[]{:S(2)}, u32[]{:S(2)}) collective-permute-start(bf16[3,32,2176]{2,1,0:T(8,128)(2,1)S(1)} %join.5), channel_id=1, source_target_pairs={{0,2},{1,3},{2,0},{3,1},{4,6},{5,7},{6,4},{7,5},{8,10},{9,11},{10,... | collective-permute-start | bytes 1253384 | tf_op jit(solution)/shard_map/ppermute | solution.py:276
  33.1 1.5 %collective-permute-done.18.refs_3_ = bf16[1,32,2048]{2,1,0:T(8,128)(2,1)S(1)} collective-permute-done((bf16[1,32,2048]{2,1,0:T(8,128)(2,1)S(1)}, bf16[1,32,2048]{2,1,0:T(8,128)(2,1)S(1)}, u32[]{:S(2)}, u32[]{:S(2)}) %collective-permute-start.18) | collective-permute-done | bytes 131104 | tf_op jit(solution)/shard_map/ppermute | solution.py:279
  34.9 1.1 %collective-permute-done.12.refs_6_ = bf16[1,32,2176]{2,1,0:T(8,128)(2,1)S(1)} collective-permute-done((bf16[1,32,2176]{2,1,0:T(8,128)(2,1)S(1)}, bf16[1,32,2176]{2,1,0:T(8,128)(2,1)S(1)}, u32[]{:S(2)}, u32[]{:S(2)}) %collective-permute-start.12) | collective-permute-done | bytes 139296 | tf_op jit(solution)/shard_map/ppermute | solution.py:279
  36.0 3.2 %ffn.4 = (bf16[2,2,32,2048]{3,2,1,0:T(8,128)(2,1)S(1)}, bf16[1,32,2048]{2,1,0:T(8,128)(2,1)S(1)}, bf16[1,32,2048]{2,1,0:T(8,128)(2,1)S(1)}, bf16[1,32,2048]{2,1,0:T(8,128)(2,1)S(1)}, bf16[1,32,2048]{2,1,0:T(8,128)(2,1)S(1)}) custom-call(s32[3,1,6]{2,1,0:T(1,128)S(1)} %bitcast.5, bf16[1,2048,768]{2,1,0:T(8,128)(2,1)S(1)} %get-tuple-element.35.gate_ref, ...), custom_call_target="tpu_custom_call" | custom-call | tf_op jit(solution)/shard_map/ffn/pallas_call | solution.py:27
  41.4 1.7 %collective-permute-done.27.refs_4_ = bf16[3,32,2176]{2,1,0:T(8,128)(2,1)S(1)} collective-permute-done((bf16[3,32,2176]{2,1,0:T(8,128)(2,1)S(1)}, bf16[3,32,2176]{2,1,0:T(8,128)(2,1)S(1)}, u32[]{:S(2)}, u32[]{:S(2)}) %collective-permute-start.27) | collective-permute-done | bytes 417824 | tf_op jit(solution)/shard_map/ppermute | solution.py:276
  43.1 1.1 %collective-permute-start.24 = (bf16[4,32,2048]{2,1,0:T(8,128)(2,1)S(1)}, bf16[4,32,2048]{2,1,0:T(8,128)(2,1)S(1)}, u32[]{:S(2)}, u32[]{:S(2)}) collective-permute-start(bf16[4,32,2048]{2,1,0:T(8,128)(2,1)S(1)} %total.7), channel_id=1, source_target_pairs={{0,2},{1,3},{2,0},{3,1},{4,6},{5,7},{6,4},{7,5},{8,10},{9,11},{10,... | collective-permute-start | bytes 1572872 | tf_op jit(solution)/shard_map/ppermute | solution.py:276
  44.2 0.7 collective-permute-done.28.refs_9_
  44.8 5.7 %ffn.5 = (bf16[2,4,32,2048]{3,2,1,0:T(8,128)(2,1)S(1)}, bf16[2,32,2048]{2,1,0:T(8,128)(2,1)S(1)}, bf16[2,32,2048]{2,1,0:T(8,128)(2,1)S(1)}, bf16[2,32,2048]{2,1,0:T(8,128)(2,1)S(1)}, bf16[2,32,2048]{2,1,0:T(8,128)(2,1)S(1)}) custom-call(s32[3,1,6]{2,1,0:T(1,128)S(1)} %bitcast.6, bf16[1,2048,768]{2,1,0:T(8,128)(2,1)S(1)} %get-tuple-element.35.gate_ref, ...), custom_call_target="tpu_custom_call" | custom-call | tf_op jit(solution)/shard_map/ffn/pallas_call | solution.py:27
  51.3 0.9 %collective-permute-done.29.refs_1_ = bf16[2,32,2048]{2,1,0:T(8,128)(2,1)S(1)} collective-permute-done((bf16[2,32,2048]{2,1,0:T(8,128)(2,1)S(1)}, bf16[2,32,2048]{2,1,0:T(8,128)(2,1)S(1)}, u32[]{:S(2)}, u32[]{:S(2)}) %collective-permute-start.29) | collective-permute-done | bytes 262176 | tf_op jit(solution)/shard_map/ppermute | solution.py:279
  52.2 1.1 %collective-permute-start.36 = (bf16[2,32,2048]{2,1,0:T(8,128)(2,1)S(1)}, bf16[2,32,2048]{2,1,0:T(8,128)(2,1)S(1)}, u32[]{:S(2)}, u32[]{:S(2)}) collective-permute-start(bf16[2,32,2048]{2,1,0:T(8,128)(2,1)S(1)} %total.8), channel_id=1, source_target_pairs={{0,2},{1,3},{2,0},{3,1},{4,6},{5,7},{6,4},{7,5},{8,10},{9,11},{10,... | collective-permute-start | bytes 786440 | tf_op jit(solution)/shard_map/ppermute | solution.py:276
  53.4 4.4 %collective-permute-done.24.refs_3_.refs_2_ = bf16[4,32,2048]{2,1,0:T(8,128)(2,1)S(1)} collective-permute-done((bf16[4,32,2048]{2,1,0:T(8,128)(2,1)S(1)}, bf16[4,32,2048]{2,1,0:T(8,128)(2,1)S(1)}, u32[]{:S(2)}, u32[]{:S(2)}) %collective-permute-start.24) | collective-permute-done | bytes 524320 | tf_op jit(solution)/shard_map/ppermute | solution.py:276
  57.9 2.0 %collective-permute-start.30 = (bf16[2,32,2048]{2,1,0:T(8,128)(2,1)S(1)}, bf16[2,32,2048]{2,1,0:T(8,128)(2,1)S(1)}, u32[]{:S(2)}, u32[]{:S(2)}) collective-permute-start(bf16[2,32,2048]{2,1,0:T(8,128)(2,1)S(1)} %total.9), channel_id=1, source_target_pairs={{0,4},{1,5},{2,6},{3,7},{4,0},{5,1},{6,2},{7,3},{8,12},{9,13},{10,... | collective-permute-start | bytes 786440 | tf_op jit(solution)/shard_map/ppermute | solution.py:267
  60.0 0.6 collective-permute-start.34
  60.6 2.8 %collective-permute-done.36.refs_2_ = bf16[2,32,2048]{2,1,0:T(8,128)(2,1)S(1)} collective-permute-done((bf16[2,32,2048]{2,1,0:T(8,128)(2,1)S(1)}, bf16[2,32,2048]{2,1,0:T(8,128)(2,1)S(1)}, u32[]{:S(2)}, u32[]{:S(2)}) %collective-permute-start.36) | collective-permute-done | bytes 262176 | tf_op jit(solution)/shard_map/ppermute | solution.py:276
  63.5 2.0 %collective-permute-start.37 = (bf16[2,32,2048]{2,1,0:T(8,128)(2,1)S(1)}, bf16[2,32,2048]{2,1,0:T(8,128)(2,1)S(1)}, u32[]{:S(2)}, u32[]{:S(2)}) collective-permute-start(bf16[2,32,2048]{2,1,0:T(8,128)(2,1)S(1)} %total.12), channel_id=1, source_target_pairs={{0,4},{1,5},{2,6},{3,7},{4,0},{5,1},{6,2},{7,3},{8,12},{9,13},{10,... | collective-permute-start | bytes 786440 | tf_op jit(solution)/shard_map/ppermute | solution.py:267
  65.8 4.2 %collective-permute-start.31 = (bf16[1,32,2048]{2,1,0:T(8,128)(2,1)S(1)}, bf16[1,32,2048]{2,1,0:T(8,128)(2,1)S(1)}, u32[]{:S(2)}, u32[]{:S(2)}) collective-permute-start(bf16[1,32,2048]{2,1,0:T(8,128)(2,1)S(1)} %total.10), channel_id=1, source_target_pairs={{0,12},{1,13},{2,14},{3,15},{4,8},{5,9},{6,10},{7,11},{8,4},{9,5},... | collective-permute-start | bytes 393224 | tf_op jit(solution)/shard_map/ppermute | solution.py:267
  70.0 2.0 %collective-permute-done.37.refs_3_.refs_8_ = bf16[2,32,2048]{2,1,0:T(8,128)(2,1)S(1)} collective-permute-done((bf16[2,32,2048]{2,1,0:T(8,128)(2,1)S(1)}, bf16[2,32,2048]{2,1,0:T(8,128)(2,1)S(1)}, u32[]{:S(2)}, u32[]{:S(2)}) %collective-permute-start.37) | collective-permute-done | bytes 262176 | tf_op jit(solution)/shard_map/ppermute | solution.py:267
  72.1 6.4 %collective-permute-start.38 = (bf16[1,32,2048]{2,1,0:T(8,128)(2,1)S(1)}, bf16[1,32,2048]{2,1,0:T(8,128)(2,1)S(1)}, u32[]{:S(2)}, u32[]{:S(2)}) collective-permute-start(bf16[1,32,2048]{2,1,0:T(8,128)(2,1)S(1)} %total.13), channel_id=1, source_target_pairs={{0,12},{1,13},{2,14},{3,15},{4,8},{5,9},{6,10},{7,11},{8,4},{9,5},... | collective-permute-start | bytes 393224 | tf_op jit(solution)/shard_map/ppermute | solution.py:267
  78.5 1.1 %collective-permute-done.31.refs_4_ = bf16[1,32,2048]{2,1,0:T(8,128)(2,1)S(1)} collective-permute-done((bf16[1,32,2048]{2,1,0:T(8,128)(2,1)S(1)}, bf16[1,32,2048]{2,1,0:T(8,128)(2,1)S(1)}, u32[]{:S(2)}, u32[]{:S(2)}) %collective-permute-start.31) | collective-permute-done | bytes 131104 | tf_op jit(solution)/shard_map/ppermute | solution.py:267
  79.5 2.0 %collective-permute-done.38.refs_9_ = bf16[1,32,2048]{2,1,0:T(8,128)(2,1)S(1)} collective-permute-done((bf16[1,32,2048]{2,1,0:T(8,128)(2,1)S(1)}, bf16[1,32,2048]{2,1,0:T(8,128)(2,1)S(1)}, u32[]{:S(2)}, u32[]{:S(2)}) %collective-permute-start.38) | collective-permute-done | bytes 131104 | tf_op jit(solution)/shard_map/ppermute | solution.py:267
  81.5 0.9 %finish.1 = bf16[2,32,2048]{2,1,0:T(8,128)(2,1)} custom-call(bf16[2,32,2048]{2,1,0:T(8,128)(2,1)S(1)} %copy-done, bf16[2,2,32,2048]{3,2,1,0:T(8,128)(2,1)S(1)} %get-tuple-element.44.refs_0_, bf16[1,32,2048]{2,1,0:T(8,128)(2,1)S(1)} %collective-permute-done.10.refs_1_, bf16[4,32,2048]{2,1,0:T(8,128)(2,1)S(1)} %collective-permute-done.24.refs_3_.refs_2_, ...), custom_call_target="tpu_custom_call" | custom-call | tf_op jit(solution)/shard_map/finish/pallas_call | solution.py:27
  (66 shorter events, 7.3 us)
Async XLA Ops:
  1.2 10.9 %collective-permute-start.2 = (bf16[1,32,2176]{2,1,0:T(8,128)(2,1)S(1)}, bf16[1,32,2176]{2,1,0:T(8,128)(2,1)S(1)}, u32[]{:S(2)}, u32[]{:S(2)}) collective-permute-start(bf16[1,32,2176]{2,1,0:T(8,128)(2,1)S(1)} %get-tuple-element.57.refs_0_), channel_id=1, source_target_pairs={{0,2},{1,3},{2,0},{3,1},{4,6},{5,7},{6,4},{7,5},{8,10},{9,11},{10,... | collective-permute-start | bytes 417800 | tf_op jit(solution)/shard_map/ppermute | solution.py:276
  4.3 7.9 %collective-permute-start.1 = (bf16[1,32,2176]{2,1,0:T(8,128)(2,1)S(1)}, bf16[1,32,2176]{2,1,0:T(8,128)(2,1)S(1)}, u32[]{:S(2)}, u32[]{:S(2)}) collective-permute-start(bf16[1,32,2176]{2,1,0:T(8,128)(2,1)S(1)} %get-tuple-element.43.refs_0_), channel_id=1, source_target_pairs={{0,2},{1,3},{2,0},{3,1},{4,6},{5,7},{6,4},{7,5},{8,10},{9,11},{10,... | collective-permute-start | bytes 417800 | tf_op jit(solution)/shard_map/ppermute | solution.py:276
  4.4 7.8 %collective-permute-start = (bf16[1,32,2176]{2,1,0:T(8,128)(2,1)S(1)}, bf16[1,32,2176]{2,1,0:T(8,128)(2,1)S(1)}, u32[]{:S(2)}, u32[]{:S(2)}) collective-permute-start(bf16[1,32,2176]{2,1,0:T(8,128)(2,1)S(1)} %get-tuple-element.43.refs_0_), channel_id=1, source_target_pairs={{0,12},{1,13},{2,14},{3,15},{4,8},{5,9},{6,10},{7,11},{8,4},{9,5},... | collective-permute-start | bytes 417800 | tf_op jit(solution)/shard_map/ppermute | solution.py:267
  12.2 11.6 %collective-permute-start.4 = (bf16[2,32,2176]{2,1,0:T(8,128)(2,1)S(1)}, bf16[2,32,2176]{2,1,0:T(8,128)(2,1)S(1)}, u32[]{:S(2)}, u32[]{:S(2)}) collective-permute-start(bf16[2,32,2176]{2,1,0:T(8,128)(2,1)S(1)} %join.3), channel_id=1, source_target_pairs={{0,4},{1,5},{2,6},{3,7},{4,0},{5,1},{6,2},{7,3},{8,12},{9,13},{10,... | collective-permute-start | bytes 835592 | tf_op jit(solution)/shard_map/ppermute | solution.py:267
  14.3 9.5 %collective-permute-start.3 = (bf16[1,32,2176]{2,1,0:T(8,128)(2,1)S(1)}, bf16[1,32,2176]{2,1,0:T(8,128)(2,1)S(1)}, u32[]{:S(2)}, u32[]{:S(2)}) collective-permute-start(bf16[1,32,2176]{2,1,0:T(8,128)(2,1)S(1)} %get-tuple-element.57.refs_0_), channel_id=1, source_target_pairs={{0,12},{1,13},{2,14},{3,15},{4,8},{5,9},{6,10},{7,11},{8,4},{9,5},... | collective-permute-start | bytes 417800 | tf_op jit(solution)/shard_map/ppermute | solution.py:267
  17.0 6.9 %collective-permute-start.5 = (bf16[1,32,2176]{2,1,0:T(8,128)(2,1)S(1)}, bf16[1,32,2176]{2,1,0:T(8,128)(2,1)S(1)}, u32[]{:S(2)}, u32[]{:S(2)}) collective-permute-start(bf16[1,32,2176]{2,1,0:T(8,128)(2,1)S(1)} %collective-permute-done.refs_1_), channel_id=1, source_target_pairs={{0,2},{1,3},{2,0},{3,1},{4,6},{5,7},{6,4},{7,5},{8,10},{9,11},{10,... | collective-permute-start | bytes 417800 | tf_op jit(solution)/shard_map/ppermute | solution.py:276
  18.5 7.0 %collective-permute-start.6 = (bf16[1,32,2176]{2,1,0:T(8,128)(2,1)S(1)}, bf16[1,32,2176]{2,1,0:T(8,128)(2,1)S(1)}, u32[]{:S(2)}, u32[]{:S(2)}) collective-permute-start(bf16[1,32,2176]{2,1,0:T(8,128)(2,1)S(1)} %get-tuple-element.43.refs_0_), channel_id=1, source_target_pairs={{0,1},{1,0},{2,3},{3,2},{4,5},{5,4},{6,7},{7,6},{8,9},{9,8},{10,11... | collective-permute-start | bytes 417800 | tf_op jit(solution)/shard_map/ppermute | solution.py:279
  18.5 7.6 %collective-permute-start.8 = (bf16[1,32,2176]{2,1,0:T(8,128)(2,1)S(1)}, bf16[1,32,2176]{2,1,0:T(8,128)(2,1)S(1)}, u32[]{:S(2)}, u32[]{:S(2)}) collective-permute-start(bf16[1,32,2176]{2,1,0:T(8,128)(2,1)S(1)} %collective-permute-done.1.refs_2_), channel_id=1, source_target_pairs={{0,1},{1,0},{2,3},{3,2},{4,5},{5,4},{6,7},{7,6},{8,9},{9,8},{10,11... | collective-permute-start | bytes 417800 | tf_op jit(solution)/shard_map/ppermute | solution.py:279
  23.8 7.1 %collective-permute-start.13 = (bf16[2,32,2176]{2,1,0:T(8,128)(2,1)S(1)}, bf16[2,32,2176]{2,1,0:T(8,128)(2,1)S(1)}, u32[]{:S(2)}, u32[]{:S(2)}) collective-permute-start(bf16[2,32,2176]{2,1,0:T(8,128)(2,1)S(1)} %join.4), channel_id=1, source_target_pairs={{0,4},{1,5},{2,6},{3,7},{4,0},{5,1},{6,2},{7,3},{8,12},{9,13},{10,... | collective-permute-start | bytes 835592 | tf_op jit(solution)/shard_map/ppermute | solution.py:267
  23.9 7.3 %collective-permute-start.19 = (bf16[2,32,2176]{2,1,0:T(8,128)(2,1)S(1)}, bf16[2,32,2176]{2,1,0:T(8,128)(2,1)S(1)}, u32[]{:S(2)}, u32[]{:S(2)}) collective-permute-start(bf16[2,32,2176]{2,1,0:T(8,128)(2,1)S(1)} %collective-permute-done.4.refs_0_), channel_id=1, source_target_pairs={{0,2},{1,3},{2,0},{3,1},{4,6},{5,7},{6,4},{7,5},{8,10},{9,11},{10,... | collective-permute-start | bytes 835592 | tf_op jit(solution)/shard_map/ppermute | solution.py:276
  26.0 4.7 %collective-permute-start.15 = (bf16[1,32,2176]{2,1,0:T(8,128)(2,1)S(1)}, bf16[1,32,2176]{2,1,0:T(8,128)(2,1)S(1)}, u32[]{:S(2)}, u32[]{:S(2)}) collective-permute-start(bf16[1,32,2176]{2,1,0:T(8,128)(2,1)S(1)} %collective-permute-done.2.refs_3_), channel_id=1, source_target_pairs={{0,1},{1,0},{2,3},{3,2},{4,5},{5,4},{6,7},{7,6},{8,9},{9,8},{10,11... | collective-permute-start | bytes 417800 | tf_op jit(solution)/shard_map/ppermute | solution.py:279
  26.9 5.2 %collective-permute-start.11 = (bf16[1,32,2176]{2,1,0:T(8,128)(2,1)S(1)}, bf16[1,32,2176]{2,1,0:T(8,128)(2,1)S(1)}, u32[]{:S(2)}, u32[]{:S(2)}) collective-permute-start(bf16[1,32,2176]{2,1,0:T(8,128)(2,1)S(1)} %get-tuple-element.57.refs_0_), channel_id=1, source_target_pairs={{0,1},{1,0},{2,3},{3,2},{4,5},{5,4},{6,7},{7,6},{8,9},{9,8},{10,11... | collective-permute-start | bytes 417800 | tf_op jit(solution)/shard_map/ppermute | solution.py:279
  30.3 2.0 %collective-permute-start.10 = (bf16[1,32,2048]{2,1,0:T(8,128)(2,1)S(1)}, bf16[1,32,2048]{2,1,0:T(8,128)(2,1)S(1)}, u32[]{:S(2)}, u32[]{:S(2)}) collective-permute-start(bf16[1,32,2048]{2,1,0:T(8,128)(2,1)S(1)} %get-tuple-element.45), channel_id=1, source_target_pairs={{0,1},{1,0},{2,3},{3,2},{4,5},{5,4},{6,7},{7,6},{8,9},{9,8},{10,11... | collective-permute-start | bytes 393224 | tf_op jit(solution)/shard_map/ppermute | solution.py:279
  30.7 1.9 %collective-permute-start.16 = (bf16[1,32,2048]{2,1,0:T(8,128)(2,1)S(1)}, bf16[1,32,2048]{2,1,0:T(8,128)(2,1)S(1)}, u32[]{:S(2)}, u32[]{:S(2)}) collective-permute-start(bf16[1,32,2048]{2,1,0:T(8,128)(2,1)S(1)} %get-tuple-element.47), channel_id=1, source_target_pairs={{0,1},{1,0},{2,3},{3,2},{4,5},{5,4},{6,7},{7,6},{8,9},{9,8},{10,11... | collective-permute-start | bytes 393224 | tf_op jit(solution)/shard_map/ppermute | solution.py:279
  30.9 1.9 %collective-permute-start.17 = (bf16[1,32,2048]{2,1,0:T(8,128)(2,1)S(1)}, bf16[1,32,2048]{2,1,0:T(8,128)(2,1)S(1)}, u32[]{:S(2)}, u32[]{:S(2)}) collective-permute-start(bf16[1,32,2048]{2,1,0:T(8,128)(2,1)S(1)} %get-tuple-element.48), channel_id=1, source_target_pairs={{0,1},{1,0},{2,3},{3,2},{4,5},{5,4},{6,7},{7,6},{8,9},{9,8},{10,11... | collective-permute-start | bytes 393224 | tf_op jit(solution)/shard_map/ppermute | solution.py:279
  31.3 11.8 %collective-permute-start.27 = (bf16[3,32,2176]{2,1,0:T(8,128)(2,1)S(1)}, bf16[3,32,2176]{2,1,0:T(8,128)(2,1)S(1)}, u32[]{:S(2)}, u32[]{:S(2)}) collective-permute-start(bf16[3,32,2176]{2,1,0:T(8,128)(2,1)S(1)} %join.5), channel_id=1, source_target_pairs={{0,2},{1,3},{2,0},{3,1},{4,6},{5,7},{6,4},{7,5},{8,10},{9,11},{10,... | collective-permute-start | bytes 1253384 | tf_op jit(solution)/shard_map/ppermute | solution.py:276
  32.1 3.9 %collective-permute-start.14 = (bf16[2,32,2176]{2,1,0:T(8,128)(2,1)S(1)}, bf16[2,32,2176]{2,1,0:T(8,128)(2,1)S(1)}, u32[]{:S(2)}, u32[]{:S(2)}) collective-permute-start(bf16[2,32,2176]{2,1,0:T(8,128)(2,1)S(1)} %collective-permute-done.13.refs_1_.refs_2_), channel_id=1, source_target_pairs={{0,1},{1,0},{2,3},{3,2},{4,5},{5,4},{6,7},{7,6},{8,9},{9,8},{10,11... | collective-permute-start | bytes 835592 | tf_op jit(solution)/shard_map/ppermute | solution.py:279
  32.3 3.7 %collective-permute-start.20 = (bf16[2,32,2176]{2,1,0:T(8,128)(2,1)S(1)}, bf16[2,32,2176]{2,1,0:T(8,128)(2,1)S(1)}, u32[]{:S(2)}, u32[]{:S(2)}) collective-permute-start(bf16[2,32,2176]{2,1,0:T(8,128)(2,1)S(1)} %collective-permute-done.4.refs_0_), channel_id=1, source_target_pairs={{0,1},{1,0},{2,3},{3,2},{4,5},{5,4},{6,7},{7,6},{8,9},{9,8},{10,11... | collective-permute-start | bytes 835592 | tf_op jit(solution)/shard_map/ppermute | solution.py:279
  32.6 3.4 %collective-permute-start.21 = (bf16[2,32,2176]{2,1,0:T(8,128)(2,1)S(1)}, bf16[2,32,2176]{2,1,0:T(8,128)(2,1)S(1)}, u32[]{:S(2)}, u32[]{:S(2)}) collective-permute-start(bf16[2,32,2176]{2,1,0:T(8,128)(2,1)S(1)} %collective-permute-done.19.refs_1_), channel_id=1, source_target_pairs={{0,1},{1,0},{2,3},{3,2},{4,5},{5,4},{6,7},{7,6},{8,9},{9,8},{10,11... | collective-permute-start | bytes 835592 | tf_op jit(solution)/shard_map/ppermute | solution.py:279
  32.8 1.8 %collective-permute-start.18 = (bf16[1,32,2048]{2,1,0:T(8,128)(2,1)S(1)}, bf16[1,32,2048]{2,1,0:T(8,128)(2,1)S(1)}, u32[]{:S(2)}, u32[]{:S(2)}) collective-permute-start(bf16[1,32,2048]{2,1,0:T(8,128)(2,1)S(1)} %get-tuple-element.49), channel_id=1, source_target_pairs={{0,1},{1,0},{2,3},{3,2},{4,5},{5,4},{6,7},{7,6},{8,9},{9,8},{10,11... | collective-permute-start | bytes 393224 | tf_op jit(solution)/shard_map/ppermute | solution.py:279
  43.1 1.8 %collective-permute-start.28 = (bf16[3,32,2176]{2,1,0:T(8,128)(2,1)S(1)}, bf16[3,32,2176]{2,1,0:T(8,128)(2,1)S(1)}, u32[]{:S(2)}, u32[]{:S(2)}) collective-permute-start(bf16[3,32,2176]{2,1,0:T(8,128)(2,1)S(1)} %collective-permute-done.27.refs_4_), channel_id=1, source_target_pairs={{0,1},{1,0},{2,3},{3,2},{4,5},{5,4},{6,7},{7,6},{8,9},{9,8},{10,11... | collective-permute-start | bytes 1253384 | tf_op jit(solution)/shard_map/ppermute | solution.py:279
  43.1 14.7 %collective-permute-start.24 = (bf16[4,32,2048]{2,1,0:T(8,128)(2,1)S(1)}, bf16[4,32,2048]{2,1,0:T(8,128)(2,1)S(1)}, u32[]{:S(2)}, u32[]{:S(2)}) collective-permute-start(bf16[4,32,2048]{2,1,0:T(8,128)(2,1)S(1)} %total.7), channel_id=1, source_target_pairs={{0,2},{1,3},{2,0},{3,1},{4,6},{5,7},{6,4},{7,5},{8,10},{9,11},{10,... | collective-permute-start | bytes 1572872 | tf_op jit(solution)/shard_map/ppermute | solution.py:276
  50.6 1.6 %collective-permute-start.29 = (bf16[2,32,2048]{2,1,0:T(8,128)(2,1)S(1)}, bf16[2,32,2048]{2,1,0:T(8,128)(2,1)S(1)}, u32[]{:S(2)}, u32[]{:S(2)}) collective-permute-start(bf16[2,32,2048]{2,1,0:T(8,128)(2,1)S(1)} %get-tuple-element.60), channel_id=1, source_target_pairs={{0,1},{1,0},{2,3},{3,2},{4,5},{5,4},{6,7},{7,6},{8,9},{9,8},{10,11... | collective-permute-start | bytes 786440 | tf_op jit(solution)/shard_map/ppermute | solution.py:279
  50.8 9.1 %collective-permute-start.33 = (bf16[2,32,2048]{2,1,0:T(8,128)(2,1)S(1)}, bf16[2,32,2048]{2,1,0:T(8,128)(2,1)S(1)}, u32[]{:S(2)}, u32[]{:S(2)}) collective-permute-start(bf16[2,32,2048]{2,1,0:T(8,128)(2,1)S(1)} %get-tuple-element.63), channel_id=1, source_target_pairs={{0,1},{1,0},{2,3},{3,2},{4,5},{5,4},{6,7},{7,6},{8,9},{9,8},{10,11... | collective-permute-start | bytes 786440 | tf_op jit(solution)/shard_map/ppermute | solution.py:279
  51.1 9.4 %collective-permute-start.35 = (bf16[2,32,2048]{2,1,0:T(8,128)(2,1)S(1)}, bf16[2,32,2048]{2,1,0:T(8,128)(2,1)S(1)}, u32[]{:S(2)}, u32[]{:S(2)}) collective-permute-start(bf16[2,32,2048]{2,1,0:T(8,128)(2,1)S(1)} %get-tuple-element.64), channel_id=1, source_target_pairs={{0,1},{1,0},{2,3},{3,2},{4,5},{5,4},{6,7},{7,6},{8,9},{9,8},{10,11... | collective-permute-start | bytes 786440 | tf_op jit(solution)/shard_map/ppermute | solution.py:279
  52.2 11.2 %collective-permute-start.36 = (bf16[2,32,2048]{2,1,0:T(8,128)(2,1)S(1)}, bf16[2,32,2048]{2,1,0:T(8,128)(2,1)S(1)}, u32[]{:S(2)}, u32[]{:S(2)}) collective-permute-start(bf16[2,32,2048]{2,1,0:T(8,128)(2,1)S(1)} %total.8), channel_id=1, source_target_pairs={{0,2},{1,3},{2,0},{3,1},{4,6},{5,7},{6,4},{7,5},{8,10},{9,11},{10,... | collective-permute-start | bytes 786440 | tf_op jit(solution)/shard_map/ppermute | solution.py:276
  53.4 16.6 %collective-permute-start.32 = (bf16[2,32,2048]{2,1,0:T(8,128)(2,1)S(1)}, bf16[2,32,2048]{2,1,0:T(8,128)(2,1)S(1)}, u32[]{:S(2)}, u32[]{:S(2)}) collective-permute-start(bf16[2,32,2048]{2,1,0:T(8,128)(2,1)S(1)} %get-tuple-element.62), channel_id=1, source_target_pairs={{0,1},{1,0},{2,3},{3,2},{4,5},{5,4},{6,7},{7,6},{8,9},{9,8},{10,11... | collective-permute-start | bytes 786440 | tf_op jit(solution)/shard_map/ppermute | solution.py:279
  57.9 7.8 %collective-permute-start.30 = (bf16[2,32,2048]{2,1,0:T(8,128)(2,1)S(1)}, bf16[2,32,2048]{2,1,0:T(8,128)(2,1)S(1)}, u32[]{:S(2)}, u32[]{:S(2)}) collective-permute-start(bf16[2,32,2048]{2,1,0:T(8,128)(2,1)S(1)} %total.9), channel_id=1, source_target_pairs={{0,4},{1,5},{2,6},{3,7},{4,0},{5,1},{6,2},{7,3},{8,12},{9,13},{10,... | collective-permute-start | bytes 786440 | tf_op jit(solution)/shard_map/ppermute | solution.py:267
  60.0 10.0 %collective-permute-start.34 = (bf16[2,32,2048]{2,1,0:T(8,128)(2,1)S(1)}, bf16[2,32,2048]{2,1,0:T(8,128)(2,1)S(1)}, u32[]{:S(2)}, u32[]{:S(2)}) collective-permute-start(bf16[2,32,2048]{2,1,0:T(8,128)(2,1)S(1)} %total.11), channel_id=1, source_target_pairs={{0,2},{1,3},{2,0},{3,1},{4,6},{5,7},{6,4},{7,5},{8,10},{9,11},{10,... | collective-permute-start | bytes 786440 | tf_op jit(solution)/shard_map/ppermute | solution.py:276
  63.5 8.5 %collective-permute-start.37 = (bf16[2,32,2048]{2,1,0:T(8,128)(2,1)S(1)}, bf16[2,32,2048]{2,1,0:T(8,128)(2,1)S(1)}, u32[]{:S(2)}, u32[]{:S(2)}) collective-permute-start(bf16[2,32,2048]{2,1,0:T(8,128)(2,1)S(1)} %total.12), channel_id=1, source_target_pairs={{0,4},{1,5},{2,6},{3,7},{4,0},{5,1},{6,2},{7,3},{8,12},{9,13},{10,... | collective-permute-start | bytes 786440 | tf_op jit(solution)/shard_map/ppermute | solution.py:267
  65.8 13.7 %collective-permute-start.31 = (bf16[1,32,2048]{2,1,0:T(8,128)(2,1)S(1)}, bf16[1,32,2048]{2,1,0:T(8,128)(2,1)S(1)}, u32[]{:S(2)}, u32[]{:S(2)}) collective-permute-start(bf16[1,32,2048]{2,1,0:T(8,128)(2,1)S(1)} %total.10), channel_id=1, source_target_pairs={{0,12},{1,13},{2,14},{3,15},{4,8},{5,9},{6,10},{7,11},{8,4},{9,5},... | collective-permute-start | bytes 393224 | tf_op jit(solution)/shard_map/ppermute | solution.py:267
  72.1 9.4 %collective-permute-start.38 = (bf16[1,32,2048]{2,1,0:T(8,128)(2,1)S(1)}, bf16[1,32,2048]{2,1,0:T(8,128)(2,1)S(1)}, u32[]{:S(2)}, u32[]{:S(2)}) collective-permute-start(bf16[1,32,2048]{2,1,0:T(8,128)(2,1)S(1)} %total.13), channel_id=1, source_target_pairs={{0,12},{1,13},{2,14},{3,15},{4,8},{5,9},{6,10},{7,11},{8,4},{9,5},... | collective-permute-start | bytes 393224 | tf_op jit(solution)/shard_map/ppermute | solution.py:267
  (9 other events, 56.2 us)
